TPU v7x, 32 devices: a whole 2x2x4 slice. The times are simulated.
32 devices in a mesh: row: 8 (over z, y), col: 4 (over x, core).
Axes of the slice: x: 2, y: 2, z: 4, core: 2. Of those that a mesh axis runs over, the one named last changes fastest.
Arguments:
- points: float32 [8192, 16], P(('row', 'col')), may hold values from -6 to 6
- inv_lengths: float32 [16], replicated, may hold values from 0.35 to 0.7
- signal_level: float32 [1], replicated, may hold values from 0.5 to 2
- noise_level: float32 [1], replicated, may hold values from 0.05 to 0.5
- right_sides: float32 [8192, 32], P(('row', 'col')), may hold values from -6 to 6
- block_counts: int32 [32], P(('row', 'col')), may hold values from 1 to 256, 6144 in all
Outputs:
- solution: float32 [8192, 32], P(('row', 'col'))
- residual: float32 [8192, 32], P(('row', 'col'))
Inputs may be any that keep to these rules, and one draw needn't show every extreme that they name: `block_counts`: each block of 256 slots holds its valid points first; the slots after them are padding.
All inputs are finite; a program needn't handle non-finite values.
Results may differ from a plain program's by a relative error of at most 0.012.
The roundings to bfloat16 on the way count: a program that leaves them out, or rounds other values in their place, can miss the bound.
Values may be sent and summed in bfloat16 or wider, within the bound.
No kernel may reach another device: no remote copies, remote signals or barrier semaphores. Data moves between devices by JAX's collectives and lax.ppermute only.
A program may use at most 64 MiB of HBM per device.

v0:
```python
import math

import jax
import jax.numpy as jnp
from jax import lax
from jax.sharding import PartitionSpec as P

ITERS = 2


def kernel_tile(scaled_rows, square_rows, scaled_cols, square_cols, signal):
    inner_product = lax.dot_general(
        scaled_rows,
        scaled_cols,
        (((1,), (1,)), ((), ())),
        precision=lax.Precision.HIGHEST,
        preferred_element_type=jnp.float32,
    )
    distance = square_rows[:, None] + square_cols[None, :] - 2.0 * inner_product
    return (signal * jnp.exp(-0.5 * distance)).astype(jnp.bfloat16)


def gather_rows(direction):
    return lax.all_gather(direction, "col", axis=0, tiled=True)


def column_norm(residual):
    return lax.psum(jnp.sum(residual * residual, axis=0), ("row", "col"))


def column_sweep(scaled_rows, square_rows, scaled_cols, square_cols, direction, signal):
    feat_count = scaled_rows.shape[1]
    zero_rows = jnp.zeros((scaled_rows.shape[0], direction.shape[1]), jnp.float32)
    running = zero_rows
    piece = lax.all_gather(direction, "row", axis=0, tiled=True)
    piece_rows = piece.shape[0]
    sub_rows = math.gcd(piece_rows, 512)
    pieces_count = piece_rows // sub_rows

    def advance(carried, parts):
        scaled_part, square_part, dir_part = parts
        kernel_block = kernel_tile(scaled_rows, square_rows, scaled_part, square_part, signal)
        return (carried + jnp.dot(kernel_block, dir_part, preferred_element_type=jnp.float32), None)

    running, unused = lax.scan(
        advance,
        running,
        (
            scaled_cols.reshape(pieces_count, sub_rows, feat_count),
            square_cols.reshape(pieces_count, sub_rows),
            piece.reshape(pieces_count, sub_rows, piece.shape[1]),
        ),
    )
    return running


def body(points, inv_lengths, signal_level, noise_level, right_sides, block_counts):
    block_rows = points.shape[0]
    signal = signal_level[0]
    noise_var = noise_level[0]
    scaled_own = points * inv_lengths[None, :]
    scaled_rows = lax.all_gather(scaled_own, "col", axis=0, tiled=True)
    square_rows = jnp.sum(scaled_rows * scaled_rows, axis=1)
    scaled_cols = lax.all_gather(scaled_own, "row", axis=0, tiled=True)
    square_cols = jnp.sum(scaled_cols * scaled_cols, axis=1)
    slots = jnp.arange(block_rows, dtype=jnp.int32)
    valid_rows = (slots < block_counts[0]).astype(jnp.float32)[:, None]
    residual = valid_rows * right_sides
    solution = jnp.zeros_like(residual)
    direction = residual.astype(jnp.bfloat16)
    norm_now = column_norm(residual)
    for iteration in range(ITERS):
        dir_float = direction.astype(jnp.float32)
        forward = column_sweep(
            scaled_rows, square_rows, scaled_cols, square_cols, direction, signal
        )
        row_dirs = gather_rows(direction)
        reduced = lax.psum_scatter(forward, "col", scatter_dimension=0, tiled=True)
        applied = valid_rows * reduced + noise_var * dir_float
        local_sum = noise_var * jnp.sum(dir_float * dir_float, axis=0) + jnp.sum(
            row_dirs.astype(jnp.float32) * forward, axis=0
        )
        curvature = lax.psum(local_sum, ("row", "col"))
        applied, curvature = (applied, curvature)
        dir_float = direction.astype(jnp.float32)
        step_size = norm_now / curvature
        solution = solution + step_size * dir_float
        residual = residual - step_size * applied
        if iteration + 1 < ITERS:
            norm_next = column_norm(residual)
            direction = (residual + norm_next / norm_now * dir_float).astype(jnp.bfloat16)
            norm_now = norm_next
    return (solution, residual)


def solution(mesh):
    in_specs = (P(("row", "col"), None), P(), P(), P(), P(("row", "col"), None), P(("row", "col")))
    out_specs = (P(("row", "col"), None), P(("row", "col"), None))
    return jax.shard_map(body, mesh=mesh, in_specs=in_specs, out_specs=out_specs, check_vma=False)
```

profile of v0, /device:TPU:0, one launch (start us, length us, event | category | flops | bytes accessed | tf_op | source)
XLA Modules:
  0.0 279.5 jit_solution(3296214072854860885)
XLA Ops:
  7.2 0.0 reduce-scatter.3.cloned.1.call-start
  7.2 0.8 broadcast_multiply_fusion
  8.0 6.2 %all_gather.19 = f32[1024,16]{0,1:T(8,128)S(1)} all-gather(f32[256,16]{0,1:T(8,128)S(1)} %broadcast_multiply_fusion), channel_id=1, replica_groups=mesh['row'=8,'col'=4] {'col'}, dimensions={0}, use_global_device_ids=true | all-gather | bytes 81920 | tf_op jit(solution)/shard_map/all_gather | solution.py:62
  14.2 31.4 %all_gather.20 = f32[2048,16]{0,1:T(8,128)S(1)} all-gather(f32[256,16]{0,1:T(8,128)S(1)} %broadcast_multiply_fusion), channel_id=1, replica_groups=mesh['row'=8,'col'=4] {'row'}, dimensions={0}, use_global_device_ids=true | all-gather | bytes 147456 | tf_op jit(solution)/shard_map/all_gather | solution.py:64
  46.2 0.9 fusion.25
  47.1 30.5 %all_gather.21 = bf16[2048,32]{0,1:T(8,128)(2,1)S(1)} all-gather(bf16[256,32]{0,1:T(8,128)(2,1)S(1)} %get-tuple-element.213), channel_id=1, replica_groups=mesh['row'=8,'col'=4] {'row'}, dimensions={0}, use_global_device_ids=true | all-gather | bytes 147456 | tf_op jit(solution)/shard_map/all_gather | solution.py:35
  77.6 0.3 copy.14
  78.0 0.0 copy-start.2
  78.0 13.5 %while.22 = (s32[]{:T(128)}, f32[1024,32]{0,1:T(8,128)S(1)}, f32[]{:T(128)}, f32[1024]{0:T(1024)S(1)}, f32[4,512]{1,0:T(4,128)S(1)}, /*index=5*/f32[4,512,16]{1,...) while((s32[]{:T(128)}, f32[1024,32]{0,1:T(8,128)S(1)}, ...), condition=%wide.region_6.7_spmd.clone, body=%wide.region_5.6_spmd.clone.sunk | while | flops 137428992 | bytes 2599039 | solution.py:45
  78.0 2.9 %fusion.51 = bf16[1024,512]{1,0:T(8,128)(2,1)S(1)} fusion(f32[1024,16]{0,1:T(8,128)S(1)} %get-tuple-element.341, f32[512]{0:T(512)S(1)} %bitcast.80, f32[1024]{0:T(1024)S(1)} %get-tuple-element.338, f32[]{:T(128)} %get-tuple-element.337, f32[4,512,16]{1,2,0:T(8,128)S(1)} %get-tuple-element.340, s32[]{:T(128)} %get-tuple-element.325), kind=kOutput, calls=%fused_computation.4.clone.1 | convolution fusion | flops 103809024 | bytes 1153032 | tf_op jit(solution)/shard_map/while/body/eval_jaxpr/dot_general | solution.py:12
  80.9 0.4 convolution_add_fusion.4
  81.4 2.9 %fusion.51 = bf16[1024,512]{1,0:T(8,128)(2,1)S(1)} fusion(f32[1024,16]{0,1:T(8,128)S(1)} %get-tuple-element.341, f32[512]{0:T(512)S(1)} %bitcast.80, f32[1024]{0:T(1024)S(1)} %get-tuple-element.338, f32[]{:T(128)} %get-tuple-element.337, f32[4,512,16]{1,2,0:T(8,128)S(1)} %get-tuple-element.340, s32[]{:T(128)} %get-tuple-element.325), kind=kOutput, calls=%fused_computation.4.clone.1 | convolution fusion | flops 103809024 | bytes 1153032 | tf_op jit(solution)/shard_map/while/body/eval_jaxpr/dot_general | solution.py:12
  84.3 0.4 convolution_add_fusion.4
  84.7 2.9 %fusion.51 = bf16[1024,512]{1,0:T(8,128)(2,1)S(1)} fusion(f32[1024,16]{0,1:T(8,128)S(1)} %get-tuple-element.341, f32[512]{0:T(512)S(1)} %bitcast.80, f32[1024]{0:T(1024)S(1)} %get-tuple-element.338, f32[]{:T(128)} %get-tuple-element.337, f32[4,512,16]{1,2,0:T(8,128)S(1)} %get-tuple-element.340, s32[]{:T(128)} %get-tuple-element.325), kind=kOutput, calls=%fused_computation.4.clone.1 | convolution fusion | flops 103809024 | bytes 1153032 | tf_op jit(solution)/shard_map/while/body/eval_jaxpr/dot_general | solution.py:12
  87.7 0.4 convolution_add_fusion.4
  88.1 2.9 %fusion.51 = bf16[1024,512]{1,0:T(8,128)(2,1)S(1)} fusion(f32[1024,16]{0,1:T(8,128)S(1)} %get-tuple-element.341, f32[512]{0:T(512)S(1)} %bitcast.80, f32[1024]{0:T(1024)S(1)} %get-tuple-element.338, f32[]{:T(128)} %get-tuple-element.337, f32[4,512,16]{1,2,0:T(8,128)S(1)} %get-tuple-element.340, s32[]{:T(128)} %get-tuple-element.325), kind=kOutput, calls=%fused_computation.4.clone.1 | convolution fusion | flops 103809024 | bytes 1153032 | tf_op jit(solution)/shard_map/while/body/eval_jaxpr/dot_general | solution.py:12
  91.0 0.4 convolution_add_fusion.4
  91.5 0.0 copy-start.1
  91.5 0.6 copy-done.1
  92.1 0.0 reduce-scatter.3.cloned.1.call-update
  92.1 0.0 reduce-scatter.5.cloned.1.call-start
  92.2 5.2 %all_gather.18 = bf16[1024,32]{0,1:T(8,128)(2,1)S(1)} all-gather(bf16[256,32]{0,1:T(8,128)(2,1)S(1)} %get-tuple-element.213), channel_id=1, replica_groups=mesh['row'=8,'col'=4] {'col'}, dimensions={0}, use_global_device_ids=true | all-gather | bytes 81920 | tf_op jit(solution)/shard_map/all_gather | solution.py:24
  97.4 1.0 multiply_reduce_fusion.1
  99.1 39.6 %all-reduce = (f32[32]{0:T(128)S(1)}, f32[32]{0:T(128)S(1)}) all-reduce(f32[32]{0:T(128)S(1)} %get-tuple-element.214, f32[32]{0:T(128)S(1)} %multiply_add_fusion.1), channel_id=1, replica_groups=mesh['row'=8,'col'=4] {'row','col'}, use_global_device_ids=true, to_apply=%region_1.0 | all-reduce | flops 64 | bytes 512 | tf_op jit(solution)/shard_map/psum | solution.py:28
  138.7 0.0 reduce-scatter.3.cloned.1.call-done
  138.7 0.0 copy-done.2
  138.7 0.9 multiply_reduce_fusion.4
  139.7 40.7 %psum.30 = f32[32]{0:T(128)S(1)} all-reduce(f32[32]{0:T(128)S(1)} %get-tuple-element.210), channel_id=1, replica_groups=mesh['row'=8,'col'=4] {'row','col'}, use_global_device_ids=true, to_apply=%region_11.12 | all-reduce | flops 32 | bytes 256 | tf_op jit(solution)/shard_map/psum | solution.py:28
  180.4 0.2 fusion.20
  180.6 30.7 %all_gather.23 = bf16[2048,32]{0,1:T(8,128)(2,1)S(1)} all-gather(bf16[256,32]{0,1:T(8,128)(2,1)S(1)} %get-tuple-element.209), channel_id=1, replica_groups=mesh['row'=8,'col'=4] {'row'}, dimensions={0}, use_global_device_ids=true | all-gather | bytes 147456 | tf_op jit(solution)/shard_map/all_gather | solution.py:35
  211.3 5.3 %all_gather.22 = bf16[1024,32]{0,1:T(8,128)(2,1)S(1)} all-gather(bf16[256,32]{0,1:T(8,128)(2,1)S(1)} %get-tuple-element.209), channel_id=1, replica_groups=mesh['row'=8,'col'=4] {'col'}, dimensions={0}, use_global_device_ids=true | all-gather | bytes 81920 | tf_op jit(solution)/shard_map/all_gather | solution.py:24
  216.6 0.3 copy.15
  216.9 13.5 %while.23 = (s32[]{:T(128)}, f32[1024,32]{0,1:T(8,128)S(1)}, f32[]{:T(128)}, f32[1024]{0:T(1024)S(1)}, f32[4,512]{1,0:T(4,128)S(1)}, /*index=5*/f32[4,512,16]{1,...) while((s32[]{:T(128)}, f32[1024,32]{0,1:T(8,128)S(1)}, ...), condition=%wide.region_14.15_spmd.clone, body=%wide.region_13.14_spmd.clone.sunk | while | flops 137428992 | bytes 2599039 | solution.py:45
  216.9 2.9 %fusion.56 = bf16[1024,512]{1,0:T(8,128)(2,1)S(1)} fusion(f32[1024,16]{0,1:T(8,128)S(1)} %get-tuple-element.371, f32[512]{0:T(512)S(1)} %bitcast.81, f32[1024]{0:T(1024)S(1)} %get-tuple-element.368, f32[]{:T(128)} %get-tuple-element.367, f32[4,512,16]{1,2,0:T(8,128)S(1)} %get-tuple-element.370, s32[]{:T(128)} %get-tuple-element.355), kind=kOutput, calls=%fused_computation.17.clone.1 | convolution fusion | flops 103809024 | bytes 1153032 | tf_op jit(solution)/shard_map/while/body/eval_jaxpr/dot_general | solution.py:12
  219.8 0.4 convolution_add_fusion.5
  220.3 2.9 %fusion.56 = bf16[1024,512]{1,0:T(8,128)(2,1)S(1)} fusion(f32[1024,16]{0,1:T(8,128)S(1)} %get-tuple-element.371, f32[512]{0:T(512)S(1)} %bitcast.81, f32[1024]{0:T(1024)S(1)} %get-tuple-element.368, f32[]{:T(128)} %get-tuple-element.367, f32[4,512,16]{1,2,0:T(8,128)S(1)} %get-tuple-element.370, s32[]{:T(128)} %get-tuple-element.355), kind=kOutput, calls=%fused_computation.17.clone.1 | convolution fusion | flops 103809024 | bytes 1153032 | tf_op jit(solution)/shard_map/while/body/eval_jaxpr/dot_general | solution.py:12
  223.2 0.4 convolution_add_fusion.5
  223.7 2.9 %fusion.56 = bf16[1024,512]{1,0:T(8,128)(2,1)S(1)} fusion(f32[1024,16]{0,1:T(8,128)S(1)} %get-tuple-element.371, f32[512]{0:T(512)S(1)} %bitcast.81, f32[1024]{0:T(1024)S(1)} %get-tuple-element.368, f32[]{:T(128)} %get-tuple-element.367, f32[4,512,16]{1,2,0:T(8,128)S(1)} %get-tuple-element.370, s32[]{:T(128)} %get-tuple-element.355), kind=kOutput, calls=%fused_computation.17.clone.1 | convolution fusion | flops 103809024 | bytes 1153032 | tf_op jit(solution)/shard_map/while/body/eval_jaxpr/dot_general | solution.py:12
  226.6 0.4 convolution_add_fusion.5
  227.0 2.9 %fusion.56 = bf16[1024,512]{1,0:T(8,128)(2,1)S(1)} fusion(f32[1024,16]{0,1:T(8,128)S(1)} %get-tuple-element.371, f32[512]{0:T(512)S(1)} %bitcast.81, f32[1024]{0:T(1024)S(1)} %get-tuple-element.368, f32[]{:T(128)} %get-tuple-element.367, f32[4,512,16]{1,2,0:T(8,128)S(1)} %get-tuple-element.370, s32[]{:T(128)} %get-tuple-element.355), kind=kOutput, calls=%fused_computation.17.clone.1 | convolution fusion | flops 103809024 | bytes 1153032 | tf_op jit(solution)/shard_map/while/body/eval_jaxpr/dot_general | solution.py:12
  229.9 0.4 convolution_add_fusion.5
  230.4 0.0 copy-start
  230.4 0.6 copy-done
  231.0 0.0 reduce-scatter.5.cloned.1.call-update
  231.0 1.0 multiply_reduce_fusion
  232.1 39.1 %psum.31 = f32[32]{0:T(128)S(1)} all-reduce(f32[32]{0:T(128)S(1)} %multiply_add_fusion), channel_id=1, replica_groups=mesh['row'=8,'col'=4] {'row','col'}, use_global_device_ids=true, to_apply=%region_16.17 | all-reduce | flops 32 | bytes 256 | tf_op jit(solution)/shard_map/psum | solution.py:83
  271.2 0.0 reduce-scatter.5.cloned.1.call-done
  271.2 1.5 fusion.24
  (20 shorter events, 0.2 us)
Async XLA Ops:
  7.2 131.6 %reduce-scatter.3.cloned.1.call-start = ((), (), s32[]{:S(2)}) async-start(), calls=%async_computation.2 | async-start | bytes 163840 | tf_op jit(solution)/shard_map/reduce_scatter | solution.py:78
  78.0 60.8 %copy-start.2 = (f32[256,32]{0,1:T(8,128)S(1)}, f32[256,32]{0,1:T(8,128)}, u32[]{:S(2)}) copy-start(f32[256,32]{0,1:T(8,128)} %param.14) | copy-start | bytes 98308
  91.5 0.6 copy-start.1
  92.1 179.1 %reduce-scatter.5.cloned.1.call-start = ((), (), s32[]{:S(2)}) async-start(), calls=%async_computation.3 | async-start | bytes 163840 | tf_op jit(solution)/shard_map/reduce_scatter | solution.py:78
  230.4 0.6 copy-start
Sparse Core Ops, SparseCore 0:
  92.2 20.4 reduce-scatter.2
  231.2 20.0 reduce-scatter.4
where the time goes:
time: 280 us
  blocking collectives  229 us (82%)
  matrix products  26.6 us (10%)
  between operations  15.5 us (6%)
  other arithmetic  6.38 us (2%)
    psum x2, blocking collectives, column_norm(): return lax.psum(jnp.sum(residual * residual, axis=0), ('row', 'col'))  80.3 us
    all_gather x2, blocking collectives, column_sweep(): piece = lax.all_gather(direction, 'row', axis=0, tiled=True)  61.2 us
    psum x1, blocking collectives, body(): curvature = lax.psum(local_sum, ('row', 'col'))  39.1 us
    all_gather x1, blocking collectives, body(): scaled_cols = lax.all_gather(scaled_own, 'row', axis=0, tiled=True)  31.4 us
    dot_general x8, matrix products, kernel_tile(): lax.dot_general(scaled_rows, scaled_cols, (((1,), (1,)), ((), ())), preci...  23.2 us
    all_gather x2, blocking collectives, gather_rows(): return lax.all_gather(direction, 'col', axis=0, tiled=True)  10.6 us
    all_gather x1, blocking collectives, body(): scaled_rows = lax.all_gather(scaled_own, 'col', axis=0, tiled=True)  6.18 us
  transfers between devices with their start and end apart: 2, of which 0 were waited for; matrix products, arithmetic and copies ran while one was open for 1% of the time, Pallas kernels for 0%

commit v1 on v0

v1 whole, which is shorter than its diff:
```python
import functools
import math

import jax
import jax.numpy as jnp
from jax import lax
from jax.experimental import pallas as pl
from jax.experimental.pallas import tpu as pltpu
from jax.sharding import PartitionSpec as P

AXES = ("row", "col")
LOG2E = 1.0 / math.log(2.0)
FAR = 64.0
KEEP_BYTES = 20 * 2**20
COPIES = 4
F32, BF16 = jnp.float32, jnp.bfloat16
VMEM = pl.BlockSpec(memory_space=pltpu.VMEM)


def swap(array, bit, count):
    return lax.ppermute(array, AXES, [(i, i ^ bit) for i in range(count)])


def three_parts(wide):
    high = wide.astype(BF16)
    rest = wide - high.astype(F32)
    middle = rest.astype(BF16)
    return high, middle, (rest - middle.astype(F32)).astype(BF16)


def features(scaled, level, left):
    high, middle, low = three_parts(scaled)
    half = -0.5 * jnp.sum(scaled * scaled, axis=0, keepdims=True)
    if not left:
        half = half + level
    halves = [part.astype(F32) for part in three_parts(half)]
    ones = [jnp.ones_like(half)] * 3
    tail = (halves + ones if left else ones + halves) + [jnp.zeros((10, half.shape[1]), F32)]
    parts = [high, high, middle, high, low, middle] if left else [high, middle, high, low, high, middle]
    return jnp.concatenate(parts + [jnp.concatenate(tail, axis=0).astype(BF16)], axis=0)


def feature_rows(feat):
    return 6 * feat + 16


def prepare_kernel(points_ref, inv_ref, right_ref, count_ref, sent_ref):
    feat, slots = points_ref.shape
    valid = lax.broadcasted_iota(jnp.int32, (1, slots), 1) < count_ref[0]
    scaled = points_ref[...] * inv_ref[...] * math.sqrt(LOG2E)
    sent_ref[0, :feat, :] = jnp.where(valid, scaled, FAR)
    sent_ref[0, feat:, :] = jnp.where(valid, right_ref[...], 0.0)


def fill_right(near_ref, signal_ref, right_ref, feat):
    blocks, slots = right_ref.shape[1] // near_ref.shape[2], near_ref.shape[2]
    for b in range(blocks):
        level = jnp.log(jnp.full((1, slots), signal_ref[0], F32)) * LOG2E
        right_ref[:, b * slots : (b + 1) * slots] = features(near_ref[b, :feat, :], level, False)


def entries(left, right):
    powers = lax.dot_general(left, right, (((0,), (0,)), ((), ())), preferred_element_type=F32)
    return jnp.exp2(powers).astype(BF16)


def apply_kernel(feat, group, keep, near_ref, far_ref, signal_ref, so_far_ref, *refs):
    if keep:
        kept_ref, out_ref, right_ref, left_ref, dirs_ref = refs
    else:
        out_ref, right_ref, left_ref, dirs_ref = refs
    slots = far_ref.shape[2]
    fill_right(near_ref, signal_ref, right_ref, feat)
    out_ref[...] = so_far_ref[...]

    def step(g, carry):
        for b in range(group):
            place = slice(b * slots, (b + 1) * slots)
            left_ref[:, place] = features(far_ref[g * group + b, :feat, :], None, True)
            dirs_ref[:, place] = far_ref[g * group + b, feat:, :].astype(BF16)
        block = entries(left_ref[...], right_ref[...])
        if keep:
            kept_ref[g] = block
        out_ref[...] += jnp.dot(dirs_ref[...], block, preferred_element_type=F32)
        return carry

    lax.fori_loop(0, far_ref.shape[0] // group, step, 0)


def apply_first(near, far, signal, so_far, copies, feat, group, keep):
    slots, probes = far.shape[2], far.shape[1] - feat
    wide, steps = group * slots, far.shape[0] // group
    outs = [jax.ShapeDtypeStruct((probes, copies * slots), F32)]
    if keep:
        outs = [pltpu.VMEM((steps, wide, copies * slots), BF16)] + outs
    done = pl.pallas_call(
        functools.partial(apply_kernel, feat, group, keep),
        out_shape=outs,
        in_specs=[VMEM, VMEM, pl.BlockSpec(memory_space=pltpu.SMEM), VMEM],
        out_specs=[VMEM] * len(outs),
        scratch_shapes=[
            pltpu.VMEM((feature_rows(feat), copies * slots), BF16),
            pltpu.VMEM((feature_rows(feat), wide), BF16),
            pltpu.VMEM((probes, wide), BF16),
        ],
        compiler_params=pltpu.CompilerParams(vmem_limit_bytes=(16 if keep else 40) * 2**20),
        cost_estimate=pl.CostEstimate(
            flops=2 * copies * slots * far.shape[0] * slots * 256, bytes_accessed=far.size * 4, transcendentals=0
        ),
    )(near, far, signal, so_far)
    return (done[0], done[1]) if keep else (None, done[0])


def image_kernel(feat, copies, near_ref, noise_ref, product_ref, image_ref):
    slots = near_ref.shape[2]
    for b in range(copies):
        direction = near_ref[b, feat:, :].astype(BF16).astype(F32)
        image_ref[b] = product_ref[:, b * slots : (b + 1) * slots] + noise_ref[0] * direction


def second_kernel(feat, group, keep, copies, signal_ref, noise_ref, *refs):
    points, images, refs = refs[:4], refs[4:8], refs[8:]
    if keep:
        kept, refs = refs[:4], refs[4:]
    (partial_ref, solution_ref, residual_ref, own_dir_ref, own_image_ref, norm_ref, product_ref, dirs_ref) = refs[:8]
    if not keep:
        right_ref, left_ref = refs[8:]
    slots, probes = images[0].shape[2], images[0].shape[1]
    pairs = list(zip(points, images))

    def over_blocks(visit, start):
        carry = start
        for x_ref, w_ref in pairs:
            carry = lax.fori_loop(0, x_ref.shape[0], functools.partial(visit, x_ref, w_ref), carry, unroll=True if x_ref.shape[0] <= 8 else 8)
        return carry

    def column(total):
        return jnp.sum(total, axis=1, keepdims=True)

    zero = jnp.zeros((probes, slots), F32)

    def sums(x_ref, w_ref, b, carry):
        norm, curve = carry
        right = x_ref[b, feat:, :]
        return norm + right * right, curve + right.astype(BF16).astype(F32) * w_ref[b]

    norm, curve = over_blocks(sums, (zero, zero))
    norm_now = column(norm)
    step_size = norm_now / column(curve)

    def next_sum(x_ref, w_ref, b, norm):
        residual = x_ref[b, feat:, :] - step_size * w_ref[b]
        return norm + residual * residual

    norm_next = column(over_blocks(next_sum, zero))
    ratio = norm_next / norm_now

    def direct(x_ref, w_ref, b):
        right = x_ref[b, feat:, :]
        first = right.astype(BF16).astype(F32)
        residual = right - step_size * w_ref[b]
        return residual, first, (residual + ratio * first).astype(BF16)

    product_ref[...] = jnp.zeros_like(product_ref)
    if not keep:
        fill_right(points[0], signal_ref, right_ref, feat)
    for piece, (x_ref, w_ref) in enumerate(pairs):

        def step(g, carry, piece=piece, x_ref=x_ref, w_ref=w_ref):
            for b in range(group):
                place = slice(b * slots, (b + 1) * slots)
                dirs_ref[:, place] = direct(x_ref, w_ref, g * group + b)[2]
                if not keep:
                    left_ref[:, place] = features(x_ref[g * group + b, :feat, :], None, True)
            block = kept[piece][g] if keep else entries(left_ref[...], right_ref[...])
            product_ref[...] += jnp.dot(dirs_ref[...], block, preferred_element_type=F32)
            return carry

        lax.fori_loop(0, x_ref.shape[0] // group, step, 0)

    total = zero
    for b in range(copies):
        residual, first, direction = direct(points[0], images[0], b)
        direction = direction.astype(F32)
        image = product_ref[:, b * slots : (b + 1) * slots] + noise_ref[0] * direction
        total = total + direction * image
        if b == 0:
            solution_ref[...] = step_size * first
            residual_ref[...] = residual
            own_dir_ref[...] = direction
            own_image_ref[...] = image
    partial_ref[...] = jnp.broadcast_to(column(total), partial_ref.shape)
    norm_ref[...] = jnp.broadcast_to(norm_next, norm_ref.shape)


def second(signal, noise, points, images, kept, copies, feat, group):
    keep = kept is not None
    slots, probes = images[0].shape[2], images[0].shape[1]
    own = jax.ShapeDtypeStruct((probes, slots), F32)
    small = jax.ShapeDtypeStruct((probes, 128), F32)
    wide = group * slots
    scratch = [pltpu.VMEM((probes, copies * slots), F32), pltpu.VMEM((probes, wide), BF16)]
    if not keep:
        scratch += [pltpu.VMEM((feature_rows(feat), copies * slots), BF16), pltpu.VMEM((feature_rows(feat), wide), BF16)]
    smem = pl.BlockSpec(memory_space=pltpu.SMEM)
    return pl.pallas_call(
        functools.partial(second_kernel, feat, group, keep, copies),
        out_shape=[small, own, own, own, own, small],
        in_specs=[smem, smem] + [VMEM] * (12 if keep else 8),
        out_specs=[VMEM] * 6,
        scratch_shapes=scratch,
        compiler_params=pltpu.CompilerParams(vmem_limit_bytes=(16 if keep else 48) * 2**20),
    )(signal, noise, *points, *images, *(kept or ()))


def finish_kernel(curve_ref, norm_ref, solution_ref, residual_ref, direction_ref, image_ref, out_ref, left_ref):
    step_size = norm_ref[:, :1] / curve_ref[:, :1]
    out_ref[...] = solution_ref[...] + step_size * direction_ref[...]
    left_ref[...] = residual_ref[...] - step_size * image_ref[...]


def spread(own, bits, count):
    held = own
    for bit in bits[:-2]:
        held = jnp.concatenate([held, swap(held, bit, count)], axis=0)
    across = swap(held, bits[-2], count)
    return held, swap(held, bits[-1], count), across, swap(across, bits[-1], count)


def body(count, points, inv_lengths, signal_level, noise_level, right_sides, block_counts):
    slots, feat = points.shape
    probes = right_sides.shape[1]
    copies = COPIES
    while copies > 1 and (copies * 4 > count or copies * count * slots * slots * 2 > KEEP_BYTES):
        copies //= 2
    keep = copies * count * slots * slots * 2 <= KEEP_BYTES
    group = math.gcd(count // 4, 8)
    bits = [1 << k for k in reversed(range(count.bit_length() - 1))]
    later = bits[copies.bit_length() - 1 :]
    smem = pl.BlockSpec(memory_space=pltpu.SMEM)
    own = pl.pallas_call(
        prepare_kernel,
        out_shape=jax.ShapeDtypeStruct((1, feat + probes, slots), F32),
        in_specs=[VMEM, VMEM, VMEM, smem],
        out_specs=VMEM,
    )(points.T, inv_lengths[:, None], right_sides.T, block_counts)
    pieces = spread(own, bits, count)
    near = pieces[0][:copies]
    kept = []
    product = jnp.zeros((probes, copies * slots), F32)
    for piece in pieces:
        block, product = apply_first(near, piece, signal_level, product, copies, feat, group, keep)
        kept.append(block)
    image = pl.pallas_call(
        functools.partial(image_kernel, feat, copies),
        out_shape=jax.ShapeDtypeStruct((copies, probes, slots), F32),
        in_specs=[VMEM, smem, VMEM],
        out_specs=VMEM,
    )(near, noise_level, product)
    images = spread(image, later, count)
    partial, solution, residual, direction, own_image, norm = second(
        signal_level, noise_level, pieces, images, kept if keep else None, copies, feat, group
    )
    for bit in reversed(later):
        partial = partial + swap(partial, bit, count)
    done = jax.ShapeDtypeStruct((probes, slots), F32)
    solution, residual = pl.pallas_call(
        finish_kernel,
        out_shape=[done, done],
        in_specs=[VMEM] * 6,
        out_specs=[VMEM] * 2,
    )(partial, norm, solution, residual, direction, own_image)
    return solution.T, residual.T


def solution(mesh):
    count = math.prod(mesh.shape[axis] for axis in AXES)
    rows = P(AXES, None)
    return jax.shard_map(
        functools.partial(body, count),
        mesh=mesh,
        in_specs=(rows, P(), P(), P(), rows, P(AXES)),
        out_specs=(rows, rows),
        check_vma=False,
    )
```

time: 280 us -> 94.4 us (0.34)
  blocking collectives: 229 us -> 0 us
  waiting for transfers between devices: 0.04 us -> 33.3 us
  matrix products: 26.6 us -> 0 us
  local copies, waits for them, and re-layouts: 1.89 us -> 21.7 us
  Pallas kernels: 0 us -> 16.1 us
  starting transfers between devices: 0.08 us -> 16.1 us
  between operations: 15.5 us -> 2.67 us
    psum x3 -> x0, blocking collectives: 119 us -> none  [the longest x2 80.3 us: column_norm(): return lax.psum(jnp.sum(residual * residual, axis=0), ('row', 'col'))]
    all_gather x6 -> x0, blocking collectives: 109 us -> none  [the longest x2 61.2 us: column_sweep(): piece = lax.all_gather(direction, 'row', axis=0, tiled=True)]
    ppermute x0 -> x13, waiting for transfers between devices: none -> 33.3 us  [swap(): return lax.ppermute(array, AXES, [(i, i ^ bit) for i in range(count)])]
    dot_general x16 -> x0, matrix products: 26.6 us -> none  [the longest x8 23.2 us: kernel_tile(): lax.dot_general(scaled_rows, scaled_cols, (((1,), (1,)), ((), ())), preci...]
    unnamed x8 -> x30, local copies, waits for them, and re-layouts: 1.81 us -> 20.3 us
    pallas_call x0 -> x8, Pallas kernels: none -> 16.1 us  [the longest x4 7.92 us: apply_first(): pl.pallas_call(functools.partial(apply_kernel, feat, group, keep), out_sh...]
    ppermute x0 -> x13, starting transfers between devices: none -> 16.1 us  [swap(): return lax.ppermute(array, AXES, [(i, i ^ bit) for i in range(count)])]
    reduce_sum x7 -> x0, other arithmetic: 4.1 us -> none  [the longest x2 2.05 us: body(): jnp.sum(row_dirs.astype(jnp.float32) * forward, axis=0)]
  transfers between devices with their start and end apart: 2 -> 13, of which waited for: 0 -> 10; matrix products, arithmetic and copies ran while one was open for 1% -> 0% of each run, Pallas kernels for 0% -> 6%
where the time goes in v1:
time: 94.4 us; the launch traced here: 93.8 us
  waiting for transfers between devices  33.3 us (35%)
  local copies, waits for them, and re-layouts  21.7 us (23%)
  Pallas kernels  16.1 us (17%)
  starting transfers between devices  16.1 us (17%)
  other arithmetic  3.97 us (4%)
  between operations  2.67 us (3%)
    ppermute x13, waiting for transfers between devices, swap(): return lax.ppermute(array, AXES, [(i, i ^ bit) for i in range(count)])  33.3 us
    unnamed x30, local copies, waits for them, and re-layouts  20.3 us
    ppermute x13, starting transfers between devices, swap(): return lax.ppermute(array, AXES, [(i, i ^ bit) for i in range(count)])  16.1 us
    pallas_call x4, Pallas kernels, apply_first(): pl.pallas_call(functools.partial(apply_kernel, feat, group, keep), out_sh...  7.92 us
    pallas_call x1, Pallas kernels, second(): pl.pallas_call(functools.partial(second_kernel, feat, group, keep, copies...  3.46 us
    concatenate x4, other arithmetic, spread(): held = jnp.concatenate([held, swap(held, bit, count)], axis=0)  3.36 us
  transfers between devices with their start and end apart: 13, of which 10 were waited for; matrix products, arithmetic and copies ran while one was open for 0% of the time, Pallas kernels for 6%

profile of v1, /device:TPU:0, one launch (start us, length us, event | category | flops | bytes accessed | tf_op | source)
XLA Modules:
  0.0 93.8 jit_solution(2052845065714251089)
XLA Ops:
  1.3 1.3 %copy.8.inv_ref = f32[16,1]{1,0:T(8,128)} copy(f32[16,1]{0,1:T(1,128)} %bitcast.7) | data formatting | bytes 128 | tf_op jit(solution)/shard_map/broadcast_in_dim | solution.py:246
  2.6 1.5 %shard_map.77 = f32[1,48,256]{2,1,0:T(8,128)} custom-call(f32[16,256]{1,0:T(8,128)} %bitcast.6, f32[16,1]{1,0:T(8,128)} %copy.8.inv_ref, f32[32,256]{1,0:T(8,128)} %bitcast.5, s32[1]{0:T(128)S(6)} %copy.11.count_ref), custom_call_target="tpu_custom_call" | custom-call | tf_op jit(solution)/shard_map/pallas_call | solution.py:241
  4.1 4.0 %collective-permute-start = (f32[1,48,256]{2,1,0:T(8,128)}, f32[1,48,256]{2,1,0:T(8,128)S(1)}, u32[]{:S(2)}, u32[]{:S(2)}) collective-permute-start(f32[1,48,256]{2,1,0:T(8,128)} %shard_map.77), channel_id=1, source_target_pairs={{0,16},{1,17},{2,18},{3,19},{4,20},{5,21},{6,22},{7,23},{8,24},{9,... | collective-permute-start | bytes 147464 | tf_op jit(solution)/shard_map/ppermute | solution.py:21
  8.1 2.8 %collective-permute-done = f32[1,48,256]{2,1,0:T(8,128)S(1)} collective-permute-done((f32[1,48,256]{2,1,0:T(8,128)}, f32[1,48,256]{2,1,0:T(8,128)S(1)}, u32[]{:S(2)}, u32[]{:S(2)}) %collective-permute-start) | collective-permute-done | bytes 49184 | tf_op jit(solution)/shard_map/ppermute | solution.py:21
  10.9 0.8 pad_maximum_fusion.3
  11.7 1.4 %collective-permute-start.1 = (f32[2,48,256]{2,1,0:T(8,128)S(1)}, f32[2,48,256]{2,1,0:T(8,128)S(1)}, u32[]{:S(2)}, u32[]{:S(2)}) collective-permute-start(f32[2,48,256]{2,1,0:T(8,128)S(1)} %pad_maximum_fusion.3), channel_id=1, source_target_pairs={{0,8},{1,9},{2,10},{3,11},{4,12},{5,13},{6,14},{7,15},{8,0},{9,1},... | collective-permute-start | bytes 294920 | tf_op jit(solution)/shard_map/ppermute | solution.py:21
  13.1 3.2 %collective-permute-done.1 = f32[2,48,256]{2,1,0:T(8,128)S(1)} collective-permute-done((f32[2,48,256]{2,1,0:T(8,128)S(1)}, f32[2,48,256]{2,1,0:T(8,128)S(1)}, u32[]{:S(2)}, u32[]{:S(2)}) %collective-permute-start.1) | collective-permute-done | bytes 98336 | tf_op jit(solution)/shard_map/ppermute | solution.py:21
  16.4 0.8 pad_maximum_fusion.2.near_ref
  17.2 1.8 %collective-permute-start.2 = (f32[4,48,256]{2,1,0:T(8,128)S(1)}, f32[4,48,256]{2,1,0:T(8,128)S(1)}, u32[]{:S(2)}, u32[]{:S(2)}) collective-permute-start(f32[4,48,256]{2,1,0:T(8,128)S(1)} %pad_maximum_fusion.2.near_ref), channel_id=1, source_target_pairs={{0,4},{1,5},{2,6},{3,7},{4,0},{5,1},{6,2},{7,3},{8,12},{9,13},{10,... | collective-permute-start | bytes 589832 | tf_op jit(solution)/shard_map/ppermute | solution.py:21
  19.0 3.9 %collective-permute-done.2 = f32[4,48,256]{2,1,0:T(8,128)S(1)} collective-permute-done((f32[4,48,256]{2,1,0:T(8,128)S(1)}, f32[4,48,256]{2,1,0:T(8,128)S(1)}, u32[]{:S(2)}, u32[]{:S(2)}) %collective-permute-start.2) | collective-permute-done | bytes 196640 | tf_op jit(solution)/shard_map/ppermute | solution.py:21
  22.9 0.8 pad_maximum_fusion.far_ref.refs_0_
  23.7 1.8 %collective-permute-start.4 = (f32[8,48,256]{2,1,0:T(8,128)S(1)}, f32[8,48,256]{2,1,0:T(8,128)S(1)}, u32[]{:S(2)}, u32[]{:S(2)}) collective-permute-start(f32[8,48,256]{2,1,0:T(8,128)S(1)} %pad_maximum_fusion.far_ref.refs_0_), channel_id=1, source_target_pairs={{0,2},{1,3},{2,0},{3,1},{4,6},{5,7},{6,4},{7,5},{8,10},{9,11},{10,... | collective-permute-start | bytes 1179656 | tf_op jit(solution)/shard_map/ppermute | solution.py:21
  25.5 6.1 %collective-permute-done.4.far_ref.refs_2_ = f32[8,48,256]{2,1,0:T(8,128)S(1)} collective-permute-done((f32[8,48,256]{2,1,0:T(8,128)S(1)}, f32[8,48,256]{2,1,0:T(8,128)S(1)}, u32[]{:S(2)}, u32[]{:S(2)}) %collective-permute-start.4) | collective-permute-done | bytes 393248 | tf_op jit(solution)/shard_map/ppermute | solution.py:21
  32.9 2.0 %shard_map.78 = (bf16[1,2048,1024]{2,1,0:T(8,128)(2,1)S(1)}, f32[32,1024]{1,0:T(8,128)S(1)}) custom-call(f32[4,48,256]{2,1,0:T(8,128)S(1)} %pad_maximum_fusion.2.near_ref, f32[8,48,256]{2,1,0:T(8,128)S(1)} %pad_maximum_fusion.far_ref.refs_0_, f32[1]{0:T(128)S(6)} %copy.9.signal_ref, f32[32,1024]{1,0:T(8,128)S(1)} %broadcast_in_dim.7.so_far_ref), custom_call_target="tpu_custom_call" | custom-call | flops 1073741824 | bytes 393216 | tf_op jit(solution)/shard_map/pallas_call | solution.py:96
  34.9 0.0 copy-start
  34.9 2.0 %copy-done = bf16[1,2048,1024]{2,1,0:T(8,128)(2,1)} copy-done((bf16[1,2048,1024]{2,1,0:T(8,128)(2,1)}, bf16[1,2048,1024]{2,1,0:T(8,128)(2,1)S(1)}, u32[]{:S(2)}) %copy-start) | copy-done | bytes 4194328
  36.9 2.0 %shard_map.79 = (bf16[1,2048,1024]{2,1,0:T(8,128)(2,1)S(1)}, f32[32,1024]{1,0:T(8,128)S(1)}) custom-call(f32[4,48,256]{2,1,0:T(8,128)S(1)} %pad_maximum_fusion.2.near_ref, f32[8,48,256]{2,1,0:T(8,128)S(1)} %collective-permute-done.3.far_ref.refs_1_, f32[1]{0:T(128)S(6)} %copy.9.signal_ref, f32[32,1024]{1,0:T(8,128)S(1)} %get-tuple-element.18.so_far_ref), custom_call_target="tpu_custom_call" | custom-call | flops 1073741824 | bytes 393216 | tf_op jit(solution)/shard_map/pallas_call | solution.py:96
  38.9 2.0 %copy-done.2 = bf16[1,2048,1024]{2,1,0:T(8,128)(2,1)} copy-done((bf16[1,2048,1024]{2,1,0:T(8,128)(2,1)}, bf16[1,2048,1024]{2,1,0:T(8,128)(2,1)S(1)}, u32[]{:S(2)}) %copy-start.2) | copy-done | bytes 4194328
  40.9 2.0 %shard_map.80 = (bf16[1,2048,1024]{2,1,0:T(8,128)(2,1)S(1)}, f32[32,1024]{1,0:T(8,128)S(1)}) custom-call(f32[4,48,256]{2,1,0:T(8,128)S(1)} %pad_maximum_fusion.2.near_ref, f32[8,48,256]{2,1,0:T(8,128)S(1)} %collective-permute-done.4.far_ref.refs_2_, f32[1]{0:T(128)S(6)} %copy.9.signal_ref, f32[32,1024]{1,0:T(8,128)S(1)} %get-tuple-element.19.so_far_ref), custom_call_target="tpu_custom_call" | custom-call | flops 1073741824 | bytes 393216 | tf_op jit(solution)/shard_map/pallas_call | solution.py:96
  42.9 2.0 %copy-done.4 = bf16[1,2048,1024]{2,1,0:T(8,128)(2,1)} copy-done((bf16[1,2048,1024]{2,1,0:T(8,128)(2,1)}, bf16[1,2048,1024]{2,1,0:T(8,128)(2,1)S(1)}, u32[]{:S(2)}) %copy-start.4) | copy-done | bytes 4194328
  44.9 2.0 %shard_map.81 = (bf16[1,2048,1024]{2,1,0:T(8,128)(2,1)S(1)}, f32[32,1024]{1,0:T(8,128)S(1)}) custom-call(f32[4,48,256]{2,1,0:T(8,128)S(1)} %pad_maximum_fusion.2.near_ref, f32[8,48,256]{2,1,0:T(8,128)S(1)} %collective-permute-done.5.far_ref.refs_3_, f32[1]{0:T(128)S(6)} %copy.9.signal_ref, f32[32,1024]{1,0:T(8,128)S(1)} %get-tuple-element.20.so_far_ref), custom_call_target="tpu_custom_call" | custom-call | flops 1073741824 | bytes 393216 | tf_op jit(solution)/shard_map/pallas_call | solution.py:96
  46.9 1.9 %copy-done.6 = bf16[1,2048,1024]{2,1,0:T(8,128)(2,1)} copy-done((bf16[1,2048,1024]{2,1,0:T(8,128)(2,1)}, bf16[1,2048,1024]{2,1,0:T(8,128)(2,1)S(1)}, u32[]{:S(2)}) %copy-start.6) | copy-done | bytes 4194328
  48.8 0.6 copy-done.9
  49.4 1.7 %shard_map.82 = f32[4,32,256]{2,1,0:T(8,128)} custom-call(f32[4,48,256]{2,1,0:T(8,128)} %copy-done.8, f32[1]{0:T(128)S(6)} %copy.10.noise_ref, f32[32,1024]{1,0:T(8,128)} %copy-done.9), custom_call_target="tpu_custom_call" | custom-call | tf_op jit(solution)/shard_map/pallas_call | solution.py:254
  51.1 1.7 %collective-permute-start.6 = (f32[4,32,256]{2,1,0:T(8,128)}, f32[4,32,256]{2,1,0:T(8,128)S(1)}, u32[]{:S(2)}, u32[]{:S(2)}) collective-permute-start(f32[4,32,256]{2,1,0:T(8,128)} %shard_map.82), channel_id=1, source_target_pairs={{0,4},{1,5},{2,6},{3,7},{4,0},{5,1},{6,2},{7,3},{8,12},{9,13},{10,... | collective-permute-start | bytes 393224 | tf_op jit(solution)/shard_map/ppermute | solution.py:21
  52.8 4.4 %collective-permute-done.6 = f32[4,32,256]{2,1,0:T(8,128)S(1)} collective-permute-done((f32[4,32,256]{2,1,0:T(8,128)}, f32[4,32,256]{2,1,0:T(8,128)S(1)}, u32[]{:S(2)}, u32[]{:S(2)}) %collective-permute-start.6) | collective-permute-done | bytes 131104 | tf_op jit(solution)/shard_map/ppermute | solution.py:21
  57.2 0.9 pad_maximum_fusion.1.refs_4_
  58.2 1.8 %collective-permute-start.8 = (f32[8,32,256]{2,1,0:T(8,128)S(1)}, f32[8,32,256]{2,1,0:T(8,128)S(1)}, u32[]{:S(2)}, u32[]{:S(2)}) collective-permute-start(f32[8,32,256]{2,1,0:T(8,128)S(1)} %pad_maximum_fusion.1.refs_4_), channel_id=1, source_target_pairs={{0,2},{1,3},{2,0},{3,1},{4,6},{5,7},{6,4},{7,5},{8,10},{9,11},{10,... | collective-permute-start | bytes 786440 | tf_op jit(solution)/shard_map/ppermute | solution.py:21
  59.9 6.2 %collective-permute-done.8.refs_6_ = f32[8,32,256]{2,1,0:T(8,128)S(1)} collective-permute-done((f32[8,32,256]{2,1,0:T(8,128)S(1)}, f32[8,32,256]{2,1,0:T(8,128)S(1)}, u32[]{:S(2)}, u32[]{:S(2)}) %collective-permute-start.8) | collective-permute-done | bytes 262176 | tf_op jit(solution)/shard_map/ppermute | solution.py:21
  66.2 1.5 %collective-permute-done.9.refs_7_ = f32[8,32,256]{2,1,0:T(8,128)S(1)} collective-permute-done((f32[8,32,256]{2,1,0:T(8,128)S(1)}, f32[8,32,256]{2,1,0:T(8,128)S(1)}, u32[]{:S(2)}, u32[]{:S(2)}) %collective-permute-start.9) | collective-permute-done | bytes 262176 | tf_op jit(solution)/shard_map/ppermute | solution.py:21
  67.7 2.2 %copy-done.1 = bf16[1,2048,1024]{2,1,0:T(8,128)(2,1)S(1)} copy-done((bf16[1,2048,1024]{2,1,0:T(8,128)(2,1)S(1)}, bf16[1,2048,1024]{2,1,0:T(8,128)(2,1)}, u32[]{:S(2)}) %copy-start.1) | copy-done | bytes 4194328
  69.9 2.2 %copy-done.3 = bf16[1,2048,1024]{2,1,0:T(8,128)(2,1)S(1)} copy-done((bf16[1,2048,1024]{2,1,0:T(8,128)(2,1)S(1)}, bf16[1,2048,1024]{2,1,0:T(8,128)(2,1)}, u32[]{:S(2)}) %copy-start.3) | copy-done | bytes 4194328
  72.1 2.2 %copy-done.5 = bf16[1,2048,1024]{2,1,0:T(8,128)(2,1)S(1)} copy-done((bf16[1,2048,1024]{2,1,0:T(8,128)(2,1)S(1)}, bf16[1,2048,1024]{2,1,0:T(8,128)(2,1)}, u32[]{:S(2)}) %copy-start.5) | copy-done | bytes 4194328
  74.3 2.2 %copy-done.7 = bf16[1,2048,1024]{2,1,0:T(8,128)(2,1)S(1)} copy-done((bf16[1,2048,1024]{2,1,0:T(8,128)(2,1)S(1)}, bf16[1,2048,1024]{2,1,0:T(8,128)(2,1)}, u32[]{:S(2)}) %copy-start.7) | copy-done | bytes 4194328
  76.5 3.5 %shard_map.83 = (f32[32,128]{1,0:T(8,128)S(1)}, f32[32,256]{1,0:T(8,128)S(1)}, f32[32,256]{1,0:T(8,128)S(1)}, f32[32,256]{1,0:T(8,128)S(1)}, f32[32,256]{1,0:T(8,128)S(1)}, /*index=5*/f32[32,128]{1,0:T(8,128)S(1)}) custom-call(f32[1]{0:T(128)S(6)} %copy.9.signal_ref, f32[1]{0:T(128)S(6)} %copy.10.noise_ref, ...), custom_call_target="tpu_custom_call" | custom-call | tf_op jit(solution)/shard_map/pallas_call | solution.py:206
  79.9 0.6 copy-done.10
  80.5 0.6 copy-done.11
  81.1 0.6 copy-done.12
  81.7 0.6 copy-done.13
  82.3 0.6 copy-done.14
  82.9 0.1 collective-permute-start.10
  83.1 1.0 %collective-permute-done.10 = f32[32,128]{1,0:T(8,128)S(1)} collective-permute-done((f32[32,128]{1,0:T(8,128)S(1)}, f32[32,128]{1,0:T(8,128)S(1)}, u32[]{:S(2)}, u32[]{:S(2)}) %collective-permute-start.10) | collective-permute-done | bytes 16416 | tf_op jit(solution)/shard_map/ppermute | solution.py:21
  84.1 1.7 %collective-permute-start.11 = (f32[32,128]{1,0:T(8,128)S(1)}, f32[32,128]{1,0:T(8,128)S(1)}, u32[]{:S(2)}, u32[]{:S(2)}) collective-permute-start(f32[32,128]{1,0:T(8,128)S(1)} %add.9), channel_id=1, source_target_pairs={{0,2},{1,3},{2,0},{3,1},{4,6},{5,7},{6,4},{7,5},{8,10},{9,11},{10,... | collective-permute-start | bytes 49160 | tf_op jit(solution)/shard_map/ppermute | solution.py:21
  85.8 2.0 %collective-permute-done.11 = f32[32,128]{1,0:T(8,128)S(1)} collective-permute-done((f32[32,128]{1,0:T(8,128)S(1)}, f32[32,128]{1,0:T(8,128)S(1)}, u32[]{:S(2)}, u32[]{:S(2)}) %collective-permute-start.11) | collective-permute-done | bytes 16416 | tf_op jit(solution)/shard_map/ppermute | solution.py:21
  87.9 1.7 %collective-permute-start.12 = (f32[32,128]{1,0:T(8,128)S(1)}, f32[32,128]{1,0:T(8,128)S(1)}, u32[]{:S(2)}, u32[]{:S(2)}) collective-permute-start(f32[32,128]{1,0:T(8,128)S(1)} %add.10), channel_id=1, source_target_pairs={{0,4},{1,5},{2,6},{3,7},{4,0},{5,1},{6,2},{7,3},{8,12},{9,13},{10,... | collective-permute-start | bytes 49160 | tf_op jit(solution)/shard_map/ppermute | solution.py:21
  89.6 2.0 %collective-permute-done.12 = f32[32,128]{1,0:T(8,128)S(1)} collective-permute-done((f32[32,128]{1,0:T(8,128)S(1)}, f32[32,128]{1,0:T(8,128)S(1)}, u32[]{:S(2)}, u32[]{:S(2)}) %collective-permute-start.12) | collective-permute-done | bytes 16416 | tf_op jit(solution)/shard_map/ppermute | solution.py:21
  91.6 0.6 add.11.curve_ref
  92.2 1.5 %shard_map.84 = (f32[32,256]{1,0:T(8,128)}, f32[32,256]{1,0:T(8,128)}) custom-call(f32[32,128]{1,0:T(8,128)} %add.11.curve_ref, f32[32,128]{1,0:T(8,128)} %copy-done.14, f32[32,256]{1,0:T(8,128)} %copy-done.10, f32[32,256]{1,0:T(8,128)} %copy-done.11, f32[32,256]{1,0:T(8,128)} %copy-done.12, f32[32,256]{1,0:T(8,128)} %copy-done.13), custom_call_target="tpu_custom_call" | custom-call | tf_op jit(solution)/shard_map/pallas_call | solution.py:267
  (25 shorter events, 0.1 us)
Async XLA Ops:
  4.1 6.8 %collective-permute-start = (f32[1,48,256]{2,1,0:T(8,128)}, f32[1,48,256]{2,1,0:T(8,128)S(1)}, u32[]{:S(2)}, u32[]{:S(2)}) collective-permute-start(f32[1,48,256]{2,1,0:T(8,128)} %shard_map.77), channel_id=1, source_target_pairs={{0,16},{1,17},{2,18},{3,19},{4,20},{5,21},{6,22},{7,23},{8,24},{9,... | collective-permute-start | bytes 147464 | tf_op jit(solution)/shard_map/ppermute | solution.py:21
  11.7 4.6 %collective-permute-start.1 = (f32[2,48,256]{2,1,0:T(8,128)S(1)}, f32[2,48,256]{2,1,0:T(8,128)S(1)}, u32[]{:S(2)}, u32[]{:S(2)}) collective-permute-start(f32[2,48,256]{2,1,0:T(8,128)S(1)} %pad_maximum_fusion.3), channel_id=1, source_target_pairs={{0,8},{1,9},{2,10},{3,11},{4,12},{5,13},{6,14},{7,15},{8,0},{9,1},... | collective-permute-start | bytes 294920 | tf_op jit(solution)/shard_map/ppermute | solution.py:21
  17.2 27.7 %copy-start.8 = (f32[4,48,256]{2,1,0:T(8,128)}, f32[4,48,256]{2,1,0:T(8,128)S(1)}, u32[]{:S(2)}) copy-start(f32[4,48,256]{2,1,0:T(8,128)S(1)} %pad_maximum_fusion.2.near_ref) | copy-start | bytes 589828
  17.2 5.7 %collective-permute-start.2 = (f32[4,48,256]{2,1,0:T(8,128)S(1)}, f32[4,48,256]{2,1,0:T(8,128)S(1)}, u32[]{:S(2)}, u32[]{:S(2)}) collective-permute-start(f32[4,48,256]{2,1,0:T(8,128)S(1)} %pad_maximum_fusion.2.near_ref), channel_id=1, source_target_pairs={{0,4},{1,5},{2,6},{3,7},{4,0},{5,1},{6,2},{7,3},{8,12},{9,13},{10,... | collective-permute-start | bytes 589832 | tf_op jit(solution)/shard_map/ppermute | solution.py:21
  23.7 7.8 %collective-permute-start.4 = (f32[8,48,256]{2,1,0:T(8,128)S(1)}, f32[8,48,256]{2,1,0:T(8,128)S(1)}, u32[]{:S(2)}, u32[]{:S(2)}) collective-permute-start(f32[8,48,256]{2,1,0:T(8,128)S(1)} %pad_maximum_fusion.far_ref.refs_0_), channel_id=1, source_target_pairs={{0,2},{1,3},{2,0},{3,1},{4,6},{5,7},{6,4},{7,5},{8,10},{9,11},{10,... | collective-permute-start | bytes 1179656 | tf_op jit(solution)/shard_map/ppermute | solution.py:21
  25.5 11.3 %collective-permute-start.3 = (f32[8,48,256]{2,1,0:T(8,128)S(1)}, f32[8,48,256]{2,1,0:T(8,128)S(1)}, u32[]{:S(2)}, u32[]{:S(2)}) collective-permute-start(f32[8,48,256]{2,1,0:T(8,128)S(1)} %pad_maximum_fusion.far_ref.refs_0_), channel_id=1, source_target_pairs={{0,1},{1,0},{2,3},{3,2},{4,5},{5,4},{6,7},{7,6},{8,9},{9,8},{10,11... | collective-permute-start | bytes 1179656 | tf_op jit(solution)/shard_map/ppermute | solution.py:21
  31.6 13.3 %collective-permute-start.5 = (f32[8,48,256]{2,1,0:T(8,128)S(1)}, f32[8,48,256]{2,1,0:T(8,128)S(1)}, u32[]{:S(2)}, u32[]{:S(2)}) collective-permute-start(f32[8,48,256]{2,1,0:T(8,128)S(1)} %collective-permute-done.4.far_ref.refs_2_), channel_id=1, source_target_pairs={{0,1},{1,0},{2,3},{3,2},{4,5},{5,4},{6,7},{7,6},{8,9},{9,8},{10,11... | collective-permute-start | bytes 1179656 | tf_op jit(solution)/shard_map/ppermute | solution.py:21
  34.9 2.0 %copy-start = (bf16[1,2048,1024]{2,1,0:T(8,128)(2,1)}, bf16[1,2048,1024]{2,1,0:T(8,128)(2,1)S(1)}, u32[]{:S(2)}) copy-start(bf16[1,2048,1024]{2,1,0:T(8,128)(2,1)S(1)} %get-tuple-element.22.refs_8_) | copy-start | bytes 12582916
  38.8 2.0 %copy-start.2 = (bf16[1,2048,1024]{2,1,0:T(8,128)(2,1)}, bf16[1,2048,1024]{2,1,0:T(8,128)(2,1)S(1)}, u32[]{:S(2)}) copy-start(bf16[1,2048,1024]{2,1,0:T(8,128)(2,1)S(1)} %get-tuple-element.23.refs_9_) | copy-start | bytes 12582916
  42.9 2.0 %copy-start.4 = (bf16[1,2048,1024]{2,1,0:T(8,128)(2,1)}, bf16[1,2048,1024]{2,1,0:T(8,128)(2,1)S(1)}, u32[]{:S(2)}) copy-start(bf16[1,2048,1024]{2,1,0:T(8,128)(2,1)S(1)} %get-tuple-element.24.refs_10_) | copy-start | bytes 12582916
  46.9 1.9 %copy-start.6 = (bf16[1,2048,1024]{2,1,0:T(8,128)(2,1)}, bf16[1,2048,1024]{2,1,0:T(8,128)(2,1)S(1)}, u32[]{:S(2)}) copy-start(bf16[1,2048,1024]{2,1,0:T(8,128)(2,1)S(1)} %get-tuple-element.25.refs_11_) | copy-start | bytes 12582916
  48.8 0.6 copy-start.9
  51.1 6.1 %collective-permute-start.6 = (f32[4,32,256]{2,1,0:T(8,128)}, f32[4,32,256]{2,1,0:T(8,128)S(1)}, u32[]{:S(2)}, u32[]{:S(2)}) collective-permute-start(f32[4,32,256]{2,1,0:T(8,128)} %shard_map.82), channel_id=1, source_target_pairs={{0,4},{1,5},{2,6},{3,7},{4,0},{5,1},{6,2},{7,3},{8,12},{9,13},{10,... | collective-permute-start | bytes 393224 | tf_op jit(solution)/shard_map/ppermute | solution.py:21
  58.2 8.0 %collective-permute-start.8 = (f32[8,32,256]{2,1,0:T(8,128)S(1)}, f32[8,32,256]{2,1,0:T(8,128)S(1)}, u32[]{:S(2)}, u32[]{:S(2)}) collective-permute-start(f32[8,32,256]{2,1,0:T(8,128)S(1)} %pad_maximum_fusion.1.refs_4_), channel_id=1, source_target_pairs={{0,2},{1,3},{2,0},{3,1},{4,6},{5,7},{6,4},{7,5},{8,10},{9,11},{10,... | collective-permute-start | bytes 786440 | tf_op jit(solution)/shard_map/ppermute | solution.py:21
  59.9 6.2 %collective-permute-start.7 = (f32[8,32,256]{2,1,0:T(8,128)S(1)}, f32[8,32,256]{2,1,0:T(8,128)S(1)}, u32[]{:S(2)}, u32[]{:S(2)}) collective-permute-start(f32[8,32,256]{2,1,0:T(8,128)S(1)} %pad_maximum_fusion.1.refs_4_), channel_id=1, source_target_pairs={{0,1},{1,0},{2,3},{3,2},{4,5},{5,4},{6,7},{7,6},{8,9},{9,8},{10,11... | collective-permute-start | bytes 786440 | tf_op jit(solution)/shard_map/ppermute | solution.py:21
  66.2 1.5 %collective-permute-start.9 = (f32[8,32,256]{2,1,0:T(8,128)S(1)}, f32[8,32,256]{2,1,0:T(8,128)S(1)}, u32[]{:S(2)}, u32[]{:S(2)}) collective-permute-start(f32[8,32,256]{2,1,0:T(8,128)S(1)} %collective-permute-done.8.refs_6_), channel_id=1, source_target_pairs={{0,1},{1,0},{2,3},{3,2},{4,5},{5,4},{6,7},{7,6},{8,9},{9,8},{10,11... | collective-permute-start | bytes 786440 | tf_op jit(solution)/shard_map/ppermute | solution.py:21
  67.7 2.2 %copy-start.1 = (bf16[1,2048,1024]{2,1,0:T(8,128)(2,1)S(1)}, bf16[1,2048,1024]{2,1,0:T(8,128)(2,1)}, u32[]{:S(2)}) copy-start(bf16[1,2048,1024]{2,1,0:T(8,128)(2,1)} %copy-done) | copy-start | bytes 12582916
  69.9 2.2 %copy-start.3 = (bf16[1,2048,1024]{2,1,0:T(8,128)(2,1)S(1)}, bf16[1,2048,1024]{2,1,0:T(8,128)(2,1)}, u32[]{:S(2)}) copy-start(bf16[1,2048,1024]{2,1,0:T(8,128)(2,1)} %copy-done.2) | copy-start | bytes 12582916
  72.1 2.2 %copy-start.5 = (bf16[1,2048,1024]{2,1,0:T(8,128)(2,1)S(1)}, bf16[1,2048,1024]{2,1,0:T(8,128)(2,1)}, u32[]{:S(2)}) copy-start(bf16[1,2048,1024]{2,1,0:T(8,128)(2,1)} %copy-done.4) | copy-start | bytes 12582916
  74.3 2.2 %copy-start.7 = (bf16[1,2048,1024]{2,1,0:T(8,128)(2,1)S(1)}, bf16[1,2048,1024]{2,1,0:T(8,128)(2,1)}, u32[]{:S(2)}) copy-start(bf16[1,2048,1024]{2,1,0:T(8,128)(2,1)} %copy-done.6) | copy-start | bytes 12582916
  79.9 0.6 copy-start.10
  80.5 0.6 copy-start.11
  81.1 0.6 copy-start.12
  81.7 0.6 copy-start.13
  82.3 0.6 copy-start.14
  82.9 1.2 %collective-permute-start.10 = (f32[32,128]{1,0:T(8,128)S(1)}, f32[32,128]{1,0:T(8,128)S(1)}, u32[]{:S(2)}, u32[]{:S(2)}) collective-permute-start(f32[32,128]{1,0:T(8,128)S(1)} %get-tuple-element.26), channel_id=1, source_target_pairs={{0,1},{1,0},{2,3},{3,2},{4,5},{5,4},{6,7},{7,6},{8,9},{9,8},{10,11... | collective-permute-start | bytes 49160 | tf_op jit(solution)/shard_map/ppermute | solution.py:21
  84.1 3.7 %collective-permute-start.11 = (f32[32,128]{1,0:T(8,128)S(1)}, f32[32,128]{1,0:T(8,128)S(1)}, u32[]{:S(2)}, u32[]{:S(2)}) collective-permute-start(f32[32,128]{1,0:T(8,128)S(1)} %add.9), channel_id=1, source_target_pairs={{0,2},{1,3},{2,0},{3,1},{4,6},{5,7},{6,4},{7,5},{8,10},{9,11},{10,... | collective-permute-start | bytes 49160 | tf_op jit(solution)/shard_map/ppermute | solution.py:21
  87.9 3.7 %collective-permute-start.12 = (f32[32,128]{1,0:T(8,128)S(1)}, f32[32,128]{1,0:T(8,128)S(1)}, u32[]{:S(2)}, u32[]{:S(2)}) collective-permute-start(f32[32,128]{1,0:T(8,128)S(1)} %add.10), channel_id=1, source_target_pairs={{0,4},{1,5},{2,6},{3,7},{4,0},{5,1},{6,2},{7,3},{8,12},{9,13},{10,... | collective-permute-start | bytes 49160 | tf_op jit(solution)/shard_map/ppermute | solution.py:21

commit v2 on v1

--- a/solution.py
+++ b/solution.py
@@ -15,6 +15,11 @@
 COPIES = 4
 F32, BF16 = jnp.float32, jnp.bfloat16
 VMEM = pl.BlockSpec(memory_space=pltpu.VMEM)
+SMEM = pl.BlockSpec(memory_space=pltpu.SMEM)
+
+
+def stay(array):
+    return pltpu.with_memory_space_constraint(array, pltpu.VMEM)
 
 
 def swap(array, bit, count):
@@ -47,7 +52,11 @@
 def prepare_kernel(points_ref, inv_ref, right_ref, count_ref, sent_ref):
     feat, slots = points_ref.shape
     valid = lax.broadcasted_iota(jnp.int32, (1, slots), 1) < count_ref[0]
-    scaled = points_ref[...] * inv_ref[...] * math.sqrt(LOG2E)
+    row = lax.broadcasted_iota(jnp.int32, (feat, slots), 0)
+    inverse = jnp.zeros((feat, slots), F32)
+    for f in range(feat):
+        inverse = jnp.where(row == f, inv_ref[f], inverse)
+    scaled = points_ref[...] * inverse * math.sqrt(LOG2E)
     sent_ref[0, :feat, :] = jnp.where(valid, scaled, FAR)
     sent_ref[0, feat:, :] = jnp.where(valid, right_ref[...], 0.0)
 
@@ -64,14 +73,17 @@
     return jnp.exp2(powers).astype(BF16)
 
 
-def apply_kernel(feat, group, keep, near_ref, far_ref, signal_ref, so_far_ref, *refs):
-    if keep:
-        kept_ref, out_ref, right_ref, left_ref, dirs_ref = refs
+def apply_kernel(feat, group, keep, last, near_ref, far_ref, signal_ref, noise_ref, so_far_ref, *refs):
+    if keep:
+        kept_ref, out_ref, right_ref, left_ref, dirs_ref, sum_ref = refs
     else:
-        out_ref, right_ref, left_ref, dirs_ref = refs
+        out_ref, right_ref, left_ref, dirs_ref, sum_ref = refs
     slots = far_ref.shape[2]
     fill_right(near_ref, signal_ref, right_ref, feat)
-    out_ref[...] = so_far_ref[...]
+    if so_far_ref is None:
+        sum_ref[...] = jnp.zeros_like(sum_ref)
+    else:
+        sum_ref[...] = so_far_ref[...]
 
     def step(g, carry):
         for b in range(group):
@@ -81,41 +93,44 @@
         block = entries(left_ref[...], right_ref[...])
         if keep:
             kept_ref[g] = block
-        out_ref[...] += jnp.dot(dirs_ref[...], block, preferred_element_type=F32)
+        sum_ref[...] += jnp.dot(dirs_ref[...], block, preferred_element_type=F32)
         return carry
 
     lax.fori_loop(0, far_ref.shape[0] // group, step, 0)
-
-
-def apply_first(near, far, signal, so_far, copies, feat, group, keep):
-    slots, probes = far.shape[2], far.shape[1] - feat
+    if not last:
+        out_ref[...] = sum_ref[...]
+        return
+    for b in range(near_ref.shape[0]):
+        direction = near_ref[b, feat:, :].astype(BF16).astype(F32)
+        out_ref[b] = sum_ref[:, b * slots : (b + 1) * slots] + noise_ref[0] * direction
+
+
+def apply_first(near, far, signal, noise, so_far, feat, group, keep, last):
+    copies, slots, probes = near.shape[0], far.shape[2], far.shape[1] - feat
     wide, steps = group * slots, far.shape[0] // group
-    outs = [jax.ShapeDtypeStruct((probes, copies * slots), F32)]
+    outs = [pltpu.VMEM((copies, probes, slots) if last else (probes, copies * slots), F32)]
     if keep:
         outs = [pltpu.VMEM((steps, wide, copies * slots), BF16)] + outs
+    kernel = functools.partial(apply_kernel, feat, group, keep, last)
+    if so_far is None:
+        kernel = functools.partial(lambda inner, *refs: inner(*refs[:4], None, *refs[4:]), kernel)
     done = pl.pallas_call(
-        functools.partial(apply_kernel, feat, group, keep),
+        kernel,
         out_shape=outs,
-        in_specs=[VMEM, VMEM, pl.BlockSpec(memory_space=pltpu.SMEM), VMEM],
+        in_specs=[VMEM, VMEM, SMEM, SMEM] + ([] if so_far is None else [VMEM]),
         out_specs=[VMEM] * len(outs),
         scratch_shapes=[
             pltpu.VMEM((feature_rows(feat), copies * slots), BF16),
             pltpu.VMEM((feature_rows(feat), wide), BF16),
             pltpu.VMEM((probes, wide), BF16),
+            pltpu.VMEM((probes, copies * slots), F32),
         ],
         compiler_params=pltpu.CompilerParams(vmem_limit_bytes=(16 if keep else 40) * 2**20),
         cost_estimate=pl.CostEstimate(
             flops=2 * copies * slots * far.shape[0] * slots * 256, bytes_accessed=far.size * 4, transcendentals=0
         ),
-    )(near, far, signal, so_far)
+    )(*([stay(near), stay(far)] if keep else [near, far]), signal, noise, *([] if so_far is None else [stay(so_far)]))
     return (done[0], done[1]) if keep else (None, done[0])
-
-
-def image_kernel(feat, copies, near_ref, noise_ref, product_ref, image_ref):
-    slots = near_ref.shape[2]
-    for b in range(copies):
-        direction = near_ref[b, feat:, :].astype(BF16).astype(F32)
-        image_ref[b] = product_ref[:, b * slots : (b + 1) * slots] + noise_ref[0] * direction
 
 
 def second_kernel(feat, group, keep, copies, signal_ref, noise_ref, *refs):
@@ -196,17 +211,16 @@
 def second(signal, noise, points, images, kept, copies, feat, group):
     keep = kept is not None
     slots, probes = images[0].shape[2], images[0].shape[1]
-    own = jax.ShapeDtypeStruct((probes, slots), F32)
-    small = jax.ShapeDtypeStruct((probes, 128), F32)
-    wide = group * slots
+    own, small, wide = pltpu.VMEM((probes, slots), F32), pltpu.VMEM((probes, 128), F32), group * slots
     scratch = [pltpu.VMEM((probes, copies * slots), F32), pltpu.VMEM((probes, wide), BF16)]
-    if not keep:
+    if keep:
+        points, images, kept = ([stay(piece) for piece in pieces] for pieces in (points, images, kept))
+    else:
         scratch += [pltpu.VMEM((feature_rows(feat), copies * slots), BF16), pltpu.VMEM((feature_rows(feat), wide), BF16)]
-    smem = pl.BlockSpec(memory_space=pltpu.SMEM)
     return pl.pallas_call(
         functools.partial(second_kernel, feat, group, keep, copies),
         out_shape=[small, own, own, own, own, small],
-        in_specs=[smem, smem] + [VMEM] * (12 if keep else 8),
+        in_specs=[SMEM, SMEM] + [VMEM] * (12 if keep else 8),
         out_specs=[VMEM] * 6,
         scratch_shapes=scratch,
         compiler_params=pltpu.CompilerParams(vmem_limit_bytes=(16 if keep else 48) * 2**20),
@@ -219,12 +233,10 @@
     left_ref[...] = residual_ref[...] - step_size * image_ref[...]
 
 
-def spread(own, bits, count):
-    held = own
-    for bit in bits[:-2]:
+def gather(held, bits, count):
+    for bit in bits:
         held = jnp.concatenate([held, swap(held, bit, count)], axis=0)
-    across = swap(held, bits[-2], count)
-    return held, swap(held, bits[-1], count), across, swap(across, bits[-1], count)
+    return held
 
 
 def body(count, points, inv_lengths, signal_level, noise_level, right_sides, block_counts):
@@ -237,27 +249,29 @@
     group = math.gcd(count // 4, 8)
     bits = [1 << k for k in reversed(range(count.bit_length() - 1))]
     later = bits[copies.bit_length() - 1 :]
-    smem = pl.BlockSpec(memory_space=pltpu.SMEM)
     own = pl.pallas_call(
         prepare_kernel,
-        out_shape=jax.ShapeDtypeStruct((1, feat + probes, slots), F32),
-        in_specs=[VMEM, VMEM, VMEM, smem],
+        out_shape=pltpu.VMEM((1, feat + probes, slots), F32),
+        in_specs=[VMEM, SMEM, VMEM, SMEM],
         out_specs=VMEM,
-    )(points.T, inv_lengths[:, None], right_sides.T, block_counts)
-    pieces = spread(own, bits, count)
-    near = pieces[0][:copies]
-    kept = []
-    product = jnp.zeros((probes, copies * slots), F32)
-    for piece in pieces:
-        block, product = apply_first(near, piece, signal_level, product, copies, feat, group, keep)
-        kept.append(block)
-    image = pl.pallas_call(
-        functools.partial(image_kernel, feat, copies),
-        out_shape=jax.ShapeDtypeStruct((copies, probes, slots), F32),
-        in_specs=[VMEM, smem, VMEM],
-        out_specs=VMEM,
-    )(near, noise_level, product)
-    images = spread(image, later, count)
+    )(points.T, inv_lengths, right_sides.T, block_counts)
+    first = functools.partial(apply_first, feat=feat, group=group, keep=keep)
+
+    held = gather(own, bits[:-2], count)
+    near = held[:copies]
+    across, beside = swap(held, bits[-2], count), swap(held, bits[-1], count)
+    kept_held, product = first(near, held, signal_level, noise_level, None, last=False)
+    kept_beside, product = first(near, beside, signal_level, noise_level, product, last=False)
+    across, product = lax.optimization_barrier((across, product))
+    beyond = swap(across, bits[-1], count)
+    kept_across, product = first(near, across, signal_level, noise_level, product, last=False)
+    kept_beyond, image = first(near, beyond, signal_level, noise_level, product, last=True)
+    pieces = [held, beside, across, beyond]
+    kept = [kept_held, kept_beside, kept_across, kept_beyond]
+
+    held = gather(image, later[:-2], count)
+    across, beside = swap(held, bits[-2], count), swap(held, bits[-1], count)
+    images = [held, beside, across, swap(across, bits[-1], count)]
     partial, solution, residual, direction, own_image, norm = second(
         signal_level, noise_level, pieces, images, kept if keep else None, copies, feat, group
     )
@@ -269,7 +283,7 @@
         out_shape=[done, done],
         in_specs=[VMEM] * 6,
         out_specs=[VMEM] * 2,
-    )(partial, norm, solution, residual, direction, own_image)
+    )(*[stay(array) for array in (partial, norm, solution, residual, direction, own_image)])
     return solution.T, residual.T
 
 

time: 94.4 us -> 63.5 us (0.67)
  local copies, waits for them, and re-layouts: 21.7 us -> 0.02 us
  other arithmetic: 3.97 us -> 0.06 us
  Pallas kernels: 16.1 us -> 12.9 us
  waiting for transfers between devices: 33.3 us -> 31.3 us
    unnamed x30 -> x1, local copies, waits for them, and re-layouts: 20.3 us -> 0.01 us
    concatenate x4 -> x3, other arithmetic: 3.36 us -> 0.05 us  [gather(): held = jnp.concatenate([held, swap(held, bit, count)], axis=0)]
    pallas_call x6 -> x5, Pallas kernels: 11.1 us -> 8.75 us  [the longest x4 7.93 us: apply_first(): pl.pallas_call(kernel, out_shape=outs, in_specs=[VMEM, VMEM, SMEM, SMEM]...]
    ppermute x13, waiting for transfers between devices: 33.3 us -> 31.3 us  [swap(): return lax.ppermute(array, AXES, [(i, i ^ bit) for i in range(count)])]
    broadcast_in_dim x2 -> x0, local copies, waits for them, and re-layouts: 1.34 us -> none  [the longest x1 1.33 us: body(): inv_lengths[:, None]]
  transfers between devices with their start and end apart: 13 -> 13, of which waited for: 10 -> 10; matrix products, arithmetic and copies ran while one was open for 0% -> 0% of each run, Pallas kernels for 6% -> 9%
where the time goes in v2:
time: 63.5 us; the launch traced here: 63.2 us
  waiting for transfers between devices  31.3 us (49%)
  starting transfers between devices  16.3 us (26%)
  Pallas kernels  12.9 us (20%)
  between operations  2.64 us (4%)
    ppermute x13, waiting for transfers between devices, swap(): return lax.ppermute(array, AXES, [(i, i ^ bit) for i in range(count)])  31.3 us
    ppermute x13, starting transfers between devices, swap(): return lax.ppermute(array, AXES, [(i, i ^ bit) for i in range(count)])  16.3 us
    pallas_call x4, Pallas kernels, apply_first(): pl.pallas_call(kernel, out_shape=outs, in_specs=[VMEM, VMEM, SMEM, SMEM]...  7.93 us
    pallas_call x1, Pallas kernels, second(): pl.pallas_call(functools.partial(second_kernel, feat, group, keep, copies...  3.46 us
  transfers between devices with their start and end apart: 13, of which 10 were waited for; matrix products, arithmetic and copies ran while one was open for 0% of the time, Pallas kernels for 9%

profile of v2, /device:TPU:0, one launch (start us, length us, event | category | flops | bytes accessed | tf_op | source)
XLA Modules:
  0.0 63.2 jit_solution(14025324502579284422)
XLA Ops:
  1.3 0.8 %shard_map.77 = f32[1,48,256]{2,1,0:T(8,128)S(1)} custom-call(f32[16,256]{1,0:T(8,128)} %bitcast.5, f32[16]{0:T(128)} %inv_ref.1, f32[32,256]{1,0:T(8,128)} %bitcast.4, s32[1]{0:T(128)S(6)} %copy.11.count_ref), custom_call_target="tpu_custom_call" | custom-call | tf_op jit(solution)/shard_map/pallas_call | solution.py:252
  2.1 4.1 %collective-permute-start = (f32[1,48,256]{2,1,0:T(8,128)S(1)}, f32[1,48,256]{2,1,0:T(8,128)S(1)}, u32[]{:S(2)}, u32[]{:S(2)}) collective-permute-start(f32[1,48,256]{2,1,0:T(8,128)S(1)} %shard_map.77), channel_id=1, source_target_pairs={{0,16},{1,17},{2,18},{3,19},{4,20},{5,21},{6,22},{7,23},{8,24},{9,... | collective-permute-start | bytes 147464 | tf_op jit(solution)/shard_map/ppermute | solution.py:26
  6.2 2.6 %collective-permute-done = f32[1,48,256]{2,1,0:T(8,128)S(1)} collective-permute-done((f32[1,48,256]{2,1,0:T(8,128)S(1)}, f32[1,48,256]{2,1,0:T(8,128)S(1)}, u32[]{:S(2)}, u32[]{:S(2)}) %collective-permute-start) | collective-permute-done | bytes 49184 | tf_op jit(solution)/shard_map/ppermute | solution.py:26
  8.8 1.4 %collective-permute-start.1 = (f32[2,48,256]{2,1,0:T(8,128)S(1)}, f32[2,48,256]{2,1,0:T(8,128)S(1)}, u32[]{:S(2)}, u32[]{:S(2)}) collective-permute-start(f32[2,48,256]{2,1,0:T(8,128)S(1)} %pad_maximum_fusion.2), channel_id=1, source_target_pairs={{0,8},{1,9},{2,10},{3,11},{4,12},{5,13},{6,14},{7,15},{8,0},{9,1},... | collective-permute-start | bytes 294920 | tf_op jit(solution)/shard_map/ppermute | solution.py:26
  10.3 3.2 %collective-permute-done.1 = f32[2,48,256]{2,1,0:T(8,128)S(1)} collective-permute-done((f32[2,48,256]{2,1,0:T(8,128)S(1)}, f32[2,48,256]{2,1,0:T(8,128)S(1)}, u32[]{:S(2)}, u32[]{:S(2)}) %collective-permute-start.1) | collective-permute-done | bytes 98336 | tf_op jit(solution)/shard_map/ppermute | solution.py:26
  13.5 1.8 %collective-permute-start.2 = (f32[4,48,256]{2,1,0:T(8,128)S(1)}, f32[4,48,256]{2,1,0:T(8,128)S(1)}, u32[]{:S(2)}, u32[]{:S(2)}) collective-permute-start(f32[4,48,256]{2,1,0:T(8,128)S(1)} %pad_maximum_fusion.1.refs_0_.near_ref), channel_id=1, source_target_pairs={{0,4},{1,5},{2,6},{3,7},{4,0},{5,1},{6,2},{7,3},{8,12},{9,13},{10,... | collective-permute-start | bytes 589832 | tf_op jit(solution)/shard_map/ppermute | solution.py:26
  15.3 3.9 %collective-permute-done.2 = f32[4,48,256]{2,1,0:T(8,128)S(1)} collective-permute-done((f32[4,48,256]{2,1,0:T(8,128)S(1)}, f32[4,48,256]{2,1,0:T(8,128)S(1)}, u32[]{:S(2)}, u32[]{:S(2)}) %collective-permute-start.2) | collective-permute-done | bytes 196640 | tf_op jit(solution)/shard_map/ppermute | solution.py:26
  19.3 0.1 collective-permute-start.3
  19.4 1.8 %collective-permute-start.4 = (f32[8,48,256]{2,1,0:T(8,128)S(1)}, f32[8,48,256]{2,1,0:T(8,128)S(1)}, u32[]{:S(2)}, u32[]{:S(2)}) collective-permute-start(f32[8,48,256]{2,1,0:T(8,128)S(1)} %pad_maximum_fusion.refs_1_.refs_0_), channel_id=1, source_target_pairs={{0,2},{1,3},{2,0},{3,1},{4,6},{5,7},{6,4},{7,5},{8,10},{9,11},{10,... | collective-permute-start | bytes 1179656 | tf_op jit(solution)/shard_map/ppermute | solution.py:26
  22.4 2.0 %shard_map.78 = (bf16[1,2048,1024]{2,1,0:T(8,128)(2,1)S(1)}, f32[32,1024]{1,0:T(8,128)S(1)}) custom-call(f32[4,48,256]{2,1,0:T(8,128)S(1)} %pad_maximum_fusion.1.refs_0_.near_ref, f32[8,48,256]{2,1,0:T(8,128)S(1)} %pad_maximum_fusion.refs_1_.refs_0_, f32[1]{0:T(128)S(6)} %copy.9.refs_2_.signal_ref, f32[1]{0:T(128)S(6)} %copy.10.refs_3_.noise_ref), custom_call_target="tpu_custom_call" | custom-call | flops 1073741824 | bytes 393216 | tf_op jit(solution)/shard_map/pallas_call | solution.py:117
  24.4 0.0 collective-permute-done.3.far_ref.refs_1_
  24.4 2.0 %shard_map.79 = (bf16[1,2048,1024]{2,1,0:T(8,128)(2,1)S(1)}, f32[32,1024]{1,0:T(8,128)S(1)}) custom-call(f32[4,48,256]{2,1,0:T(8,128)S(1)} %pad_maximum_fusion.1.refs_0_.near_ref, f32[8,48,256]{2,1,0:T(8,128)S(1)} %collective-permute-done.3.far_ref.refs_1_, f32[1]{0:T(128)S(6)} %copy.9.refs_2_.signal_ref, f32[1]{0:T(128)S(6)} %copy.10.refs_3_.noise_ref, ...), custom_call_target="tpu_custom_call" | custom-call | flops 1073741824 | bytes 393216 | tf_op jit(solution)/shard_map/pallas_call | solution.py:117
  26.4 4.5 %collective-permute-done.4.far_ref.refs_2_ = f32[8,48,256]{2,1,0:T(8,128)S(1)} collective-permute-done((f32[8,48,256]{2,1,0:T(8,128)S(1)}, f32[8,48,256]{2,1,0:T(8,128)S(1)}, u32[]{:S(2)}, u32[]{:S(2)}) %collective-permute-start.4) | collective-permute-done | bytes 393248 | tf_op jit(solution)/shard_map/ppermute | solution.py:26
  30.9 0.0 collective-permute-start.5
  30.9 2.0 %shard_map.80 = (bf16[1,2048,1024]{2,1,0:T(8,128)(2,1)S(1)}, f32[32,1024]{1,0:T(8,128)S(1)}) custom-call(f32[4,48,256]{2,1,0:T(8,128)S(1)} %pad_maximum_fusion.1.refs_0_.near_ref, f32[8,48,256]{2,1,0:T(8,128)S(1)} %collective-permute-done.4.far_ref.refs_2_, f32[1]{0:T(128)S(6)} %copy.9.refs_2_.signal_ref, f32[1]{0:T(128)S(6)} %copy.10.refs_3_.noise_ref, ...), custom_call_target="tpu_custom_call" | custom-call | flops 1073741824 | bytes 393216 | tf_op jit(solution)/shard_map/pallas_call | solution.py:117
  32.9 0.0 collective-permute-done.5.far_ref.refs_3_
  32.9 2.0 %shard_map.81 = (bf16[1,2048,1024]{2,1,0:T(8,128)(2,1)S(1)}, f32[4,32,256]{2,1,0:T(8,128)S(1)}) custom-call(f32[4,48,256]{2,1,0:T(8,128)S(1)} %pad_maximum_fusion.1.refs_0_.near_ref, f32[8,48,256]{2,1,0:T(8,128)S(1)} %collective-permute-done.5.far_ref.refs_3_, f32[1]{0:T(128)S(6)} %copy.9.refs_2_.signal_ref, f32[1]{0:T(128)S(6)} %copy.10.refs_3_.noise_ref, ...), custom_call_target="tpu_custom_call" | custom-call | flops 1073741824 | bytes 393216 | tf_op jit(solution)/shard_map/pallas_call | solution.py:117
  34.9 1.8 %collective-permute-start.6 = (f32[4,32,256]{2,1,0:T(8,128)S(1)}, f32[4,32,256]{2,1,0:T(8,128)S(1)}, u32[]{:S(2)}, u32[]{:S(2)}) collective-permute-start(f32[4,32,256]{2,1,0:T(8,128)S(1)} %get-tuple-element.25), channel_id=1, source_target_pairs={{0,4},{1,5},{2,6},{3,7},{4,0},{5,1},{6,2},{7,3},{8,12},{9,13},{10,... | collective-permute-start | bytes 393224 | tf_op jit(solution)/shard_map/ppermute | solution.py:26
  36.6 4.2 %collective-permute-done.6 = f32[4,32,256]{2,1,0:T(8,128)S(1)} collective-permute-done((f32[4,32,256]{2,1,0:T(8,128)S(1)}, f32[4,32,256]{2,1,0:T(8,128)S(1)}, u32[]{:S(2)}, u32[]{:S(2)}) %collective-permute-start.6) | collective-permute-done | bytes 131104 | tf_op jit(solution)/shard_map/ppermute | solution.py:26
  40.8 1.8 %collective-permute-start.8 = (f32[8,32,256]{2,1,0:T(8,128)S(1)}, f32[8,32,256]{2,1,0:T(8,128)S(1)}, u32[]{:S(2)}, u32[]{:S(2)}) collective-permute-start(f32[8,32,256]{2,1,0:T(8,128)S(1)} %constant_dynamic-update-slice_fusion.refs_4_), channel_id=1, source_target_pairs={{0,2},{1,3},{2,0},{3,1},{4,6},{5,7},{6,4},{7,5},{8,10},{9,11},{10,... | collective-permute-start | bytes 786440 | tf_op jit(solution)/shard_map/ppermute | solution.py:26
  42.6 0.0 collective-permute-start.7
  42.6 6.2 %collective-permute-done.8.refs_6_ = f32[8,32,256]{2,1,0:T(8,128)S(1)} collective-permute-done((f32[8,32,256]{2,1,0:T(8,128)S(1)}, f32[8,32,256]{2,1,0:T(8,128)S(1)}, u32[]{:S(2)}, u32[]{:S(2)}) %collective-permute-start.8) | collective-permute-done | bytes 262176 | tf_op jit(solution)/shard_map/ppermute | solution.py:26
  48.8 0.0 collective-permute-start.9
  48.8 0.0 collective-permute-done.7.refs_5_
  48.8 1.5 %collective-permute-done.9.refs_7_ = f32[8,32,256]{2,1,0:T(8,128)S(1)} collective-permute-done((f32[8,32,256]{2,1,0:T(8,128)S(1)}, f32[8,32,256]{2,1,0:T(8,128)S(1)}, u32[]{:S(2)}, u32[]{:S(2)}) %collective-permute-start.9) | collective-permute-done | bytes 262176 | tf_op jit(solution)/shard_map/ppermute | solution.py:26
  50.4 3.5 %shard_map.82 = (f32[32,128]{1,0:T(8,128)S(1)}, f32[32,256]{1,0:T(8,128)S(1)}, f32[32,256]{1,0:T(8,128)S(1)}, f32[32,256]{1,0:T(8,128)S(1)}, f32[32,256]{1,0:T(8,128)S(1)}, /*index=5*/f32[32,128]{1,0:T(8,128)S(1)}) custom-call(f32[1]{0:T(128)S(6)} %copy.9.refs_2_.signal_ref, f32[1]{0:T(128)S(6)} %copy.10.refs_3_.noise_ref, ...), custom_call_target="tpu_custom_call" | custom-call | tf_op jit(solution)/shard_map/pallas_call | solution.py:220
  53.8 0.1 collective-permute-start.10
  54.0 1.0 %collective-permute-done.10 = f32[32,128]{1,0:T(8,128)S(1)} collective-permute-done((f32[32,128]{1,0:T(8,128)S(1)}, f32[32,128]{1,0:T(8,128)S(1)}, u32[]{:S(2)}, u32[]{:S(2)}) %collective-permute-start.10) | collective-permute-done | bytes 16416 | tf_op jit(solution)/shard_map/ppermute | solution.py:26
  55.0 1.7 %collective-permute-start.11 = (f32[32,128]{1,0:T(8,128)S(1)}, f32[32,128]{1,0:T(8,128)S(1)}, u32[]{:S(2)}, u32[]{:S(2)}) collective-permute-start(f32[32,128]{1,0:T(8,128)S(1)} %add.9), channel_id=1, source_target_pairs={{0,2},{1,3},{2,0},{3,1},{4,6},{5,7},{6,4},{7,5},{8,10},{9,11},{10,... | collective-permute-start | bytes 49160 | tf_op jit(solution)/shard_map/ppermute | solution.py:26
  56.7 2.0 %collective-permute-done.11 = f32[32,128]{1,0:T(8,128)S(1)} collective-permute-done((f32[32,128]{1,0:T(8,128)S(1)}, f32[32,128]{1,0:T(8,128)S(1)}, u32[]{:S(2)}, u32[]{:S(2)}) %collective-permute-start.11) | collective-permute-done | bytes 16416 | tf_op jit(solution)/shard_map/ppermute | solution.py:26
  58.8 1.7 %collective-permute-start.12 = (f32[32,128]{1,0:T(8,128)S(1)}, f32[32,128]{1,0:T(8,128)S(1)}, u32[]{:S(2)}, u32[]{:S(2)}) collective-permute-start(f32[32,128]{1,0:T(8,128)S(1)} %add.10), channel_id=1, source_target_pairs={{0,4},{1,5},{2,6},{3,7},{4,0},{5,1},{6,2},{7,3},{8,12},{9,13},{10,... | collective-permute-start | bytes 49160 | tf_op jit(solution)/shard_map/ppermute | solution.py:26
  60.5 2.0 %collective-permute-done.12 = f32[32,128]{1,0:T(8,128)S(1)} collective-permute-done((f32[32,128]{1,0:T(8,128)S(1)}, f32[32,128]{1,0:T(8,128)S(1)}, u32[]{:S(2)}, u32[]{:S(2)}) %collective-permute-start.12) | collective-permute-done | bytes 16416 | tf_op jit(solution)/shard_map/ppermute | solution.py:26
  62.5 0.7 %shard_map.83 = (f32[32,256]{1,0:T(8,128)}, f32[32,256]{1,0:T(8,128)}) custom-call(f32[32,128]{1,0:T(8,128)S(1)} %add.11.curve_ref, f32[32,128]{1,0:T(8,128)S(1)} %get-tuple-element.31.norm_ref, f32[32,256]{1,0:T(8,128)S(1)} %get-tuple-element.32.solution_ref, f32[32,256]{1,0:T(8,128)S(1)} %get-tuple-element.33.residual_ref, ...), custom_call_target="tpu_custom_call" | custom-call | tf_op jit(solution)/shard_map/pallas_call | solution.py:281
  (8 shorter events, 0.1 us)
Async XLA Ops:
  2.1 6.7 %collective-permute-start = (f32[1,48,256]{2,1,0:T(8,128)S(1)}, f32[1,48,256]{2,1,0:T(8,128)S(1)}, u32[]{:S(2)}, u32[]{:S(2)}) collective-permute-start(f32[1,48,256]{2,1,0:T(8,128)S(1)} %shard_map.77), channel_id=1, source_target_pairs={{0,16},{1,17},{2,18},{3,19},{4,20},{5,21},{6,22},{7,23},{8,24},{9,... | collective-permute-start | bytes 147464 | tf_op jit(solution)/shard_map/ppermute | solution.py:26
  8.8 4.7 %collective-permute-start.1 = (f32[2,48,256]{2,1,0:T(8,128)S(1)}, f32[2,48,256]{2,1,0:T(8,128)S(1)}, u32[]{:S(2)}, u32[]{:S(2)}) collective-permute-start(f32[2,48,256]{2,1,0:T(8,128)S(1)} %pad_maximum_fusion.2), channel_id=1, source_target_pairs={{0,8},{1,9},{2,10},{3,11},{4,12},{5,13},{6,14},{7,15},{8,0},{9,1},... | collective-permute-start | bytes 294920 | tf_op jit(solution)/shard_map/ppermute | solution.py:26
  13.5 5.7 %collective-permute-start.2 = (f32[4,48,256]{2,1,0:T(8,128)S(1)}, f32[4,48,256]{2,1,0:T(8,128)S(1)}, u32[]{:S(2)}, u32[]{:S(2)}) collective-permute-start(f32[4,48,256]{2,1,0:T(8,128)S(1)} %pad_maximum_fusion.1.refs_0_.near_ref), channel_id=1, source_target_pairs={{0,4},{1,5},{2,6},{3,7},{4,0},{5,1},{6,2},{7,3},{8,12},{9,13},{10,... | collective-permute-start | bytes 589832 | tf_op jit(solution)/shard_map/ppermute | solution.py:26
  19.3 5.1 %collective-permute-start.3 = (f32[8,48,256]{2,1,0:T(8,128)S(1)}, f32[8,48,256]{2,1,0:T(8,128)S(1)}, u32[]{:S(2)}, u32[]{:S(2)}) collective-permute-start(f32[8,48,256]{2,1,0:T(8,128)S(1)} %pad_maximum_fusion.refs_1_.refs_0_), channel_id=1, source_target_pairs={{0,1},{1,0},{2,3},{3,2},{4,5},{5,4},{6,7},{7,6},{8,9},{9,8},{10,11... | collective-permute-start | bytes 1179656 | tf_op jit(solution)/shard_map/ppermute | solution.py:26
  19.4 11.5 %collective-permute-start.4 = (f32[8,48,256]{2,1,0:T(8,128)S(1)}, f32[8,48,256]{2,1,0:T(8,128)S(1)}, u32[]{:S(2)}, u32[]{:S(2)}) collective-permute-start(f32[8,48,256]{2,1,0:T(8,128)S(1)} %pad_maximum_fusion.refs_1_.refs_0_), channel_id=1, source_target_pairs={{0,2},{1,3},{2,0},{3,1},{4,6},{5,7},{6,4},{7,5},{8,10},{9,11},{10,... | collective-permute-start | bytes 1179656 | tf_op jit(solution)/shard_map/ppermute | solution.py:26
  30.9 2.0 %collective-permute-start.5 = (f32[8,48,256]{2,1,0:T(8,128)S(1)}, f32[8,48,256]{2,1,0:T(8,128)S(1)}, u32[]{:S(2)}, u32[]{:S(2)}) collective-permute-start(f32[8,48,256]{2,1,0:T(8,128)S(1)} %collective-permute-done.4.far_ref.refs_2_), channel_id=1, source_target_pairs={{0,1},{1,0},{2,3},{3,2},{4,5},{5,4},{6,7},{7,6},{8,9},{9,8},{10,11... | collective-permute-start | bytes 1179656 | tf_op jit(solution)/shard_map/ppermute | solution.py:26
  34.9 6.0 %collective-permute-start.6 = (f32[4,32,256]{2,1,0:T(8,128)S(1)}, f32[4,32,256]{2,1,0:T(8,128)S(1)}, u32[]{:S(2)}, u32[]{:S(2)}) collective-permute-start(f32[4,32,256]{2,1,0:T(8,128)S(1)} %get-tuple-element.25), channel_id=1, source_target_pairs={{0,4},{1,5},{2,6},{3,7},{4,0},{5,1},{6,2},{7,3},{8,12},{9,13},{10,... | collective-permute-start | bytes 393224 | tf_op jit(solution)/shard_map/ppermute | solution.py:26
  40.8 8.0 %collective-permute-start.8 = (f32[8,32,256]{2,1,0:T(8,128)S(1)}, f32[8,32,256]{2,1,0:T(8,128)S(1)}, u32[]{:S(2)}, u32[]{:S(2)}) collective-permute-start(f32[8,32,256]{2,1,0:T(8,128)S(1)} %constant_dynamic-update-slice_fusion.refs_4_), channel_id=1, source_target_pairs={{0,2},{1,3},{2,0},{3,1},{4,6},{5,7},{6,4},{7,5},{8,10},{9,11},{10,... | collective-permute-start | bytes 786440 | tf_op jit(solution)/shard_map/ppermute | solution.py:26
  42.6 6.2 %collective-permute-start.7 = (f32[8,32,256]{2,1,0:T(8,128)S(1)}, f32[8,32,256]{2,1,0:T(8,128)S(1)}, u32[]{:S(2)}, u32[]{:S(2)}) collective-permute-start(f32[8,32,256]{2,1,0:T(8,128)S(1)} %constant_dynamic-update-slice_fusion.refs_4_), channel_id=1, source_target_pairs={{0,1},{1,0},{2,3},{3,2},{4,5},{5,4},{6,7},{7,6},{8,9},{9,8},{10,11... | collective-permute-start | bytes 786440 | tf_op jit(solution)/shard_map/ppermute | solution.py:26
  48.8 1.5 %collective-permute-start.9 = (f32[8,32,256]{2,1,0:T(8,128)S(1)}, f32[8,32,256]{2,1,0:T(8,128)S(1)}, u32[]{:S(2)}, u32[]{:S(2)}) collective-permute-start(f32[8,32,256]{2,1,0:T(8,128)S(1)} %collective-permute-done.8.refs_6_), channel_id=1, source_target_pairs={{0,1},{1,0},{2,3},{3,2},{4,5},{5,4},{6,7},{7,6},{8,9},{9,8},{10,11... | collective-permute-start | bytes 786440 | tf_op jit(solution)/shard_map/ppermute | solution.py:26
  53.8 1.2 %collective-permute-start.10 = (f32[32,128]{1,0:T(8,128)S(1)}, f32[32,128]{1,0:T(8,128)S(1)}, u32[]{:S(2)}, u32[]{:S(2)}) collective-permute-start(f32[32,128]{1,0:T(8,128)S(1)} %get-tuple-element.30), channel_id=1, source_target_pairs={{0,1},{1,0},{2,3},{3,2},{4,5},{5,4},{6,7},{7,6},{8,9},{9,8},{10,11... | collective-permute-start | bytes 49160 | tf_op jit(solution)/shard_map/ppermute | solution.py:26
  55.0 3.7 %collective-permute-start.11 = (f32[32,128]{1,0:T(8,128)S(1)}, f32[32,128]{1,0:T(8,128)S(1)}, u32[]{:S(2)}, u32[]{:S(2)}) collective-permute-start(f32[32,128]{1,0:T(8,128)S(1)} %add.9), channel_id=1, source_target_pairs={{0,2},{1,3},{2,0},{3,1},{4,6},{5,7},{6,4},{7,5},{8,10},{9,11},{10,... | collective-permute-start | bytes 49160 | tf_op jit(solution)/shard_map/ppermute | solution.py:26
  58.8 3.7 %collective-permute-start.12 = (f32[32,128]{1,0:T(8,128)S(1)}, f32[32,128]{1,0:T(8,128)S(1)}, u32[]{:S(2)}, u32[]{:S(2)}) collective-permute-start(f32[32,128]{1,0:T(8,128)S(1)} %add.10), channel_id=1, source_target_pairs={{0,4},{1,5},{2,6},{3,7},{4,0},{5,1},{6,2},{7,3},{8,12},{9,13},{10,... | collective-permute-start | bytes 49160 | tf_op jit(solution)/shard_map/ppermute | solution.py:26

commit v3 on v2

--- a/solution.py
+++ b/solution.py
@@ -13,6 +13,7 @@
 FAR = 64.0
 KEEP_BYTES = 20 * 2**20
 COPIES = 4
+PIECES = 8
 F32, BF16 = jnp.float32, jnp.bfloat16
 VMEM = pl.BlockSpec(memory_space=pltpu.VMEM)
 SMEM = pl.BlockSpec(memory_space=pltpu.SMEM)
@@ -73,30 +74,34 @@
     return jnp.exp2(powers).astype(BF16)
 
 
-def apply_kernel(feat, group, keep, last, near_ref, far_ref, signal_ref, noise_ref, so_far_ref, *refs):
-    if keep:
-        kept_ref, out_ref, right_ref, left_ref, dirs_ref, sum_ref = refs
+def apply_kernel(feat, group, keep, begin, last, count, near_ref, signal_ref, noise_ref, *refs):
+    far, refs = refs[:count], refs[count:]
+    if begin:
+        right_ref, refs = refs[-4], refs[:-4] + refs[-3:]
     else:
-        out_ref, right_ref, left_ref, dirs_ref, sum_ref = refs
-    slots = far_ref.shape[2]
-    fill_right(near_ref, signal_ref, right_ref, feat)
-    if so_far_ref is None:
+        right_ref, so_far_ref, refs = refs[0], refs[1], refs[2:]
+    kept, refs = (refs[:count], refs[count:]) if keep else ((), refs)
+    out_ref, left_ref, dirs_ref, sum_ref = refs
+    slots = near_ref.shape[2]
+    if begin:
+        fill_right(near_ref, signal_ref, right_ref, feat)
         sum_ref[...] = jnp.zeros_like(sum_ref)
     else:
         sum_ref[...] = so_far_ref[...]
-
-    def step(g, carry):
-        for b in range(group):
-            place = slice(b * slots, (b + 1) * slots)
-            left_ref[:, place] = features(far_ref[g * group + b, :feat, :], None, True)
-            dirs_ref[:, place] = far_ref[g * group + b, feat:, :].astype(BF16)
-        block = entries(left_ref[...], right_ref[...])
-        if keep:
-            kept_ref[g] = block
-        sum_ref[...] += jnp.dot(dirs_ref[...], block, preferred_element_type=F32)
-        return carry
-
-    lax.fori_loop(0, far_ref.shape[0] // group, step, 0)
+    for piece, far_ref in enumerate(far):
+
+        def step(g, carry, piece=piece, far_ref=far_ref):
+            for b in range(group):
+                place = slice(b * slots, (b + 1) * slots)
+                left_ref[:, place] = features(far_ref[g * group + b, :feat, :], None, True)
+                dirs_ref[:, place] = far_ref[g * group + b, feat:, :].astype(BF16)
+            block = entries(left_ref[...], right_ref[...])
+            if keep:
+                kept[piece][g] = block
+            sum_ref[...] += jnp.dot(dirs_ref[...], block, preferred_element_type=F32)
+            return carry
+
+        lax.fori_loop(0, far_ref.shape[0] // group, step, 0)
     if not last:
         out_ref[...] = sum_ref[...]
         return
@@ -105,38 +110,44 @@
         out_ref[b] = sum_ref[:, b * slots : (b + 1) * slots] + noise_ref[0] * direction
 
 
-def apply_first(near, far, signal, noise, so_far, feat, group, keep, last):
-    copies, slots, probes = near.shape[0], far.shape[2], far.shape[1] - feat
-    wide, steps = group * slots, far.shape[0] // group
+def apply_first(near, far, signal, noise, so_far, feat, group, keep, last=False):
+    copies, slots, probes = near.shape[0], near.shape[2], near.shape[1] - feat
+    wide, steps, begin = group * slots, far[0].shape[0] // group, so_far is None
     outs = [pltpu.VMEM((copies, probes, slots) if last else (probes, copies * slots), F32)]
     if keep:
-        outs = [pltpu.VMEM((steps, wide, copies * slots), BF16)] + outs
-    kernel = functools.partial(apply_kernel, feat, group, keep, last)
-    if so_far is None:
-        kernel = functools.partial(lambda inner, *refs: inner(*refs[:4], None, *refs[4:]), kernel)
+        outs = [pltpu.VMEM((steps, wide, copies * slots), BF16)] * len(far) + outs
+    if begin:
+        outs = outs + [pltpu.VMEM((feature_rows(feat), copies * slots), BF16)]
+    arrays = [near, *far, *([] if begin else so_far)]
+    if keep:
+        arrays = [stay(array) for array in arrays]
     done = pl.pallas_call(
-        kernel,
+        functools.partial(apply_kernel, feat, group, keep, begin, last, len(far)),
         out_shape=outs,
-        in_specs=[VMEM, VMEM, SMEM, SMEM] + ([] if so_far is None else [VMEM]),
+        in_specs=[VMEM, SMEM, SMEM] + [VMEM] * (len(arrays) - 1),
         out_specs=[VMEM] * len(outs),
         scratch_shapes=[
-            pltpu.VMEM((feature_rows(feat), copies * slots), BF16),
             pltpu.VMEM((feature_rows(feat), wide), BF16),
             pltpu.VMEM((probes, wide), BF16),
             pltpu.VMEM((probes, copies * slots), F32),
         ],
         compiler_params=pltpu.CompilerParams(vmem_limit_bytes=(16 if keep else 40) * 2**20),
         cost_estimate=pl.CostEstimate(
-            flops=2 * copies * slots * far.shape[0] * slots * 256, bytes_accessed=far.size * 4, transcendentals=0
+            flops=2 * copies * slots * len(far) * far[0].shape[0] * slots * 256,
+            bytes_accessed=far[0].size * 4,
+            transcendentals=0,
         ),
-    )(*([stay(near), stay(far)] if keep else [near, far]), signal, noise, *([] if so_far is None else [stay(so_far)]))
-    return (done[0], done[1]) if keep else (None, done[0])
+    )(arrays[0], signal, noise, *arrays[1:])
+    kept, rest = (done[: len(far)], done[len(far) :]) if keep else ([None] * len(far), done)
+    if begin:
+        return kept, (rest[1], rest[0])
+    return kept, rest[0] if last else (so_far[0], rest[0])
 
 
 def second_kernel(feat, group, keep, copies, signal_ref, noise_ref, *refs):
-    points, images, refs = refs[:4], refs[4:8], refs[8:]
+    points, images, refs = refs[:PIECES], refs[PIECES : 2 * PIECES], refs[2 * PIECES :]
     if keep:
-        kept, refs = refs[:4], refs[4:]
+        kept, refs = refs[:PIECES], refs[PIECES:]
     (partial_ref, solution_ref, residual_ref, own_dir_ref, own_image_ref, norm_ref, product_ref, dirs_ref) = refs[:8]
     if not keep:
         right_ref, left_ref = refs[8:]
@@ -220,7 +231,7 @@
     return pl.pallas_call(
         functools.partial(second_kernel, feat, group, keep, copies),
         out_shape=[small, own, own, own, own, small],
-        in_specs=[SMEM, SMEM] + [VMEM] * (12 if keep else 8),
+        in_specs=[SMEM, SMEM] + [VMEM] * (3 * PIECES if keep else 2 * PIECES),
         out_specs=[VMEM] * 6,
         scratch_shapes=scratch,
         compiler_params=pltpu.CompilerParams(vmem_limit_bytes=(16 if keep else 48) * 2**20),
@@ -243,12 +254,13 @@
     slots, feat = points.shape
     probes = right_sides.shape[1]
     copies = COPIES
-    while copies > 1 and (copies * 4 > count or copies * count * slots * slots * 2 > KEEP_BYTES):
+    while copies > 1 and (copies * PIECES > count or copies * count * slots * slots * 2 > KEEP_BYTES):
         copies //= 2
     keep = copies * count * slots * slots * 2 <= KEEP_BYTES
-    group = math.gcd(count // 4, 8)
+    group = math.gcd(count // PIECES, 8)
     bits = [1 << k for k in reversed(range(count.bit_length() - 1))]
     later = bits[copies.bit_length() - 1 :]
+    one, two, core = bits[-3:]
     own = pl.pallas_call(
         prepare_kernel,
         out_shape=pltpu.VMEM((1, feat + probes, slots), F32),
@@ -257,21 +269,26 @@
     )(points.T, inv_lengths, right_sides.T, block_counts)
     first = functools.partial(apply_first, feat=feat, group=group, keep=keep)
 
-    held = gather(own, bits[:-2], count)
+    held = gather(own, bits[:-3], count)
     near = held[:copies]
-    across, beside = swap(held, bits[-2], count), swap(held, bits[-1], count)
-    kept_held, product = first(near, held, signal_level, noise_level, None, last=False)
-    kept_beside, product = first(near, beside, signal_level, noise_level, product, last=False)
-    across, product = lax.optimization_barrier((across, product))
-    beyond = swap(across, bits[-1], count)
-    kept_across, product = first(near, across, signal_level, noise_level, product, last=False)
-    kept_beyond, image = first(near, beyond, signal_level, noise_level, product, last=True)
-    pieces = [held, beside, across, beyond]
-    kept = [kept_held, kept_beside, kept_across, kept_beyond]
-
-    held = gather(image, later[:-2], count)
-    across, beside = swap(held, bits[-2], count), swap(held, bits[-1], count)
-    images = [held, beside, across, swap(across, bits[-1], count)]
+    beside, up, over, corner = (swap(held, bit, count) for bit in (core, one, two, one | two))
+    kept_0, product = first(near, [held, beside], signal_level, noise_level, None)
+    up, product = lax.optimization_barrier((up, product))
+    up_beside = swap(up, core, count)
+    kept_1, product = first(near, [up], signal_level, noise_level, product)
+    over, product = lax.optimization_barrier((over, product))
+    over_beside = swap(over, core, count)
+    kept_2, product = first(near, [up_beside, over], signal_level, noise_level, product)
+    corner, product = lax.optimization_barrier((corner, product))
+    corner_beside = swap(corner, core, count)
+    kept_3, product = first(near, [over_beside, corner], signal_level, noise_level, product)
+    kept_4, image = first(near, [corner_beside], signal_level, noise_level, product, last=True)
+    pieces = [held, beside, up, up_beside, over, over_beside, corner, corner_beside]
+    kept = [*kept_0, *kept_1, *kept_2, *kept_3, *kept_4]
+
+    held = gather(image, later[:-3], count)
+    direct = [held] + [swap(held, bit, count) for bit in (one, two, one | two)]
+    images = [array for piece in direct for array in (piece, swap(piece, core, count))]
     partial, solution, residual, direction, own_image, norm = second(
         signal_level, noise_level, pieces, images, kept if keep else None, copies, feat, group
     )

time: 63.5 us -> 56.8 us (0.89)
  waiting for transfers between devices: 31.3 us -> 21.8 us
  starting transfers between devices: 16.3 us -> 19 us
    ppermute x13 -> x19, waiting for transfers between devices: 31.3 us -> 21.8 us  [swap(): return lax.ppermute(array, AXES, [(i, i ^ bit) for i in range(count)])]
    ppermute x13 -> x19, starting transfers between devices: 16.3 us -> 19 us  [swap(): return lax.ppermute(array, AXES, [(i, i ^ bit) for i in range(count)])]
    pallas_call x4 -> x5, Pallas kernels: 7.93 us -> 8.02 us  [apply_first(): pl.pallas_call(functools.partial(apply_kernel, feat, group, keep, begin,...]
  transfers between devices with their start and end apart: 13 -> 19, of which waited for: 10 -> 11; matrix products, arithmetic and copies ran while one was open for 0% -> 0% of each run, Pallas kernels for 9% -> 12%
where the time goes in v3:
time: 56.8 us; the launch traced here: 56.5 us
  waiting for transfers between devices  21.8 us (38%)
  starting transfers between devices  19 us (33%)
  Pallas kernels  13 us (23%)
  between operations  2.64 us (5%)
    ppermute x19, waiting for transfers between devices, swap(): return lax.ppermute(array, AXES, [(i, i ^ bit) for i in range(count)])  21.8 us
    ppermute x19, starting transfers between devices, swap(): return lax.ppermute(array, AXES, [(i, i ^ bit) for i in range(count)])  19 us
    pallas_call x5, Pallas kernels, apply_first(): pl.pallas_call(functools.partial(apply_kernel, feat, group, keep, begin,...  8.02 us
    pallas_call x1, Pallas kernels, second(): pl.pallas_call(functools.partial(second_kernel, feat, group, keep, copies...  3.46 us
  transfers between devices with their start and end apart: 19, of which 11 were waited for; matrix products, arithmetic and copies ran while one was open for 0% of the time, Pallas kernels for 12%

profile of v3, /device:TPU:0, one launch (start us, length us, event | category | flops | bytes accessed | tf_op | source)
XLA Modules:
  0.0 56.5 jit_solution(11422649756702061037)
XLA Ops:
  1.3 0.8 %shard_map.77 = f32[1,48,256]{2,1,0:T(8,128)S(1)} custom-call(f32[16,256]{1,0:T(8,128)} %bitcast.5, f32[16]{0:T(128)} %inv_ref.1, f32[32,256]{1,0:T(8,128)} %bitcast.4, s32[1]{0:T(128)S(6)} %copy.10.count_ref), custom_call_target="tpu_custom_call" | custom-call | tf_op jit(solution)/shard_map/pallas_call | solution.py:264
  2.1 4.1 %collective-permute-start = (f32[1,48,256]{2,1,0:T(8,128)S(1)}, f32[1,48,256]{2,1,0:T(8,128)S(1)}, u32[]{:S(2)}, u32[]{:S(2)}) collective-permute-start(f32[1,48,256]{2,1,0:T(8,128)S(1)} %shard_map.77), channel_id=1, source_target_pairs={{0,16},{1,17},{2,18},{3,19},{4,20},{5,21},{6,22},{7,23},{8,24},{9,... | collective-permute-start | bytes 147464 | tf_op jit(solution)/shard_map/ppermute | solution.py:27
  6.2 2.6 %collective-permute-done = f32[1,48,256]{2,1,0:T(8,128)S(1)} collective-permute-done((f32[1,48,256]{2,1,0:T(8,128)S(1)}, f32[1,48,256]{2,1,0:T(8,128)S(1)}, u32[]{:S(2)}, u32[]{:S(2)}) %collective-permute-start) | collective-permute-done | bytes 49184 | tf_op jit(solution)/shard_map/ppermute | solution.py:27
  8.8 1.4 %collective-permute-start.1 = (f32[2,48,256]{2,1,0:T(8,128)S(1)}, f32[2,48,256]{2,1,0:T(8,128)S(1)}, u32[]{:S(2)}, u32[]{:S(2)}) collective-permute-start(f32[2,48,256]{2,1,0:T(8,128)S(1)} %pad_maximum_fusion.1), channel_id=1, source_target_pairs={{0,8},{1,9},{2,10},{3,11},{4,12},{5,13},{6,14},{7,15},{8,0},{9,1},... | collective-permute-start | bytes 294920 | tf_op jit(solution)/shard_map/ppermute | solution.py:27
  10.3 3.2 %collective-permute-done.1 = f32[2,48,256]{2,1,0:T(8,128)S(1)} collective-permute-done((f32[2,48,256]{2,1,0:T(8,128)S(1)}, f32[2,48,256]{2,1,0:T(8,128)S(1)}, u32[]{:S(2)}, u32[]{:S(2)}) %collective-permute-start.1) | collective-permute-done | bytes 98336 | tf_op jit(solution)/shard_map/ppermute | solution.py:27
  13.5 0.1 collective-permute-start.2
  13.6 1.8 %collective-permute-start.3 = (f32[4,48,256]{2,1,0:T(8,128)S(1)}, f32[4,48,256]{2,1,0:T(8,128)S(1)}, u32[]{:S(2)}, u32[]{:S(2)}) collective-permute-start(f32[4,48,256]{2,1,0:T(8,128)S(1)} %pad_maximum_fusion.near_ref.refs_0_), channel_id=1, source_target_pairs={{0,4},{1,5},{2,6},{3,7},{4,0},{5,1},{6,2},{7,3},{8,12},{9,13},{10,... | collective-permute-start | bytes 589832 | tf_op jit(solution)/shard_map/ppermute | solution.py:27
  16.7 1.6 %collective-permute-start.5 = (f32[4,48,256]{2,1,0:T(8,128)S(1)}, f32[4,48,256]{2,1,0:T(8,128)S(1)}, u32[]{:S(2)}, u32[]{:S(2)}) collective-permute-start(f32[4,48,256]{2,1,0:T(8,128)S(1)} %pad_maximum_fusion.near_ref.refs_0_), channel_id=1, source_target_pairs={{0,2},{1,3},{2,0},{3,1},{4,6},{5,7},{6,4},{7,5},{8,10},{9,11},{10,... | collective-permute-start | bytes 589832 | tf_op jit(solution)/shard_map/ppermute | solution.py:27
  18.2 0.0 collective-permute-done.2.refs_1_
  18.2 2.0 %shard_map.78 = (bf16[1,1024,1024]{2,1,0:T(8,128)(2,1)S(1)}, bf16[1,1024,1024]{2,1,0:T(8,128)(2,1)S(1)}, f32[32,1024]{1,0:T(8,128)S(1)}, bf16[112,1024]{1,0:T(8,128)(2,1)S(1)}) custom-call(f32[4,48,256]{2,1,0:T(8,128)S(1)} %pad_maximum_fusion.near_ref.refs_0_, f32[1]{0:T(128)S(6)} %copy.8.signal_ref, f32[1]{0:T(128)S(6)} %copy.9.noise_ref, ...), custom_call_target="tpu_custom_call" | custom-call | flops 1073741824 | bytes 196608 | tf_op jit(solution)/shard_map/pallas_call | solution.py:124
  20.2 0.7 %collective-permute-done.3.refs_0_.refs_2_ = f32[4,48,256]{2,1,0:T(8,128)S(1)} collective-permute-done((f32[4,48,256]{2,1,0:T(8,128)S(1)}, f32[4,48,256]{2,1,0:T(8,128)S(1)}, u32[]{:S(2)}, u32[]{:S(2)}) %collective-permute-start.3) | collective-permute-done | bytes 196640 | tf_op jit(solution)/shard_map/ppermute | solution.py:27
  20.9 0.0 collective-permute-start.4
  20.9 2.7 %collective-permute-start.7 = (f32[4,48,256]{2,1,0:T(8,128)S(1)}, f32[4,48,256]{2,1,0:T(8,128)S(1)}, u32[]{:S(2)}, u32[]{:S(2)}) collective-permute-start(f32[4,48,256]{2,1,0:T(8,128)S(1)} %pad_maximum_fusion.near_ref.refs_0_), channel_id=1, source_target_pairs={{0,6},{1,7},{2,4},{3,5},{4,2},{5,3},{6,0},{7,1},{8,14},{9,15},{10,... | collective-permute-start | bytes 589832 | tf_op jit(solution)/shard_map/ppermute | solution.py:27
  23.6 1.1 %shard_map.79 = (bf16[1,1024,1024]{2,1,0:T(8,128)(2,1)S(1)}, f32[32,1024]{1,0:T(8,128)S(1)}) custom-call(f32[4,48,256]{2,1,0:T(8,128)S(1)} %pad_maximum_fusion.near_ref.refs_0_, f32[1]{0:T(128)S(6)} %copy.8.signal_ref, f32[1]{0:T(128)S(6)} %copy.9.noise_ref, f32[4,48,256]{2,1,0:T(8,128)S(1)} %collective-permute-done.3.refs_0_.refs_2_, ...), custom_call_target="tpu_custom_call" | custom-call | flops 536870912 | bytes 196608 | tf_op jit(solution)/shard_map/pallas_call | solution.py:124
  24.6 0.0 collective-permute-done.5.refs_1_.refs_4_
  24.6 0.3 collective-permute-start.6
  24.9 0.0 collective-permute-done.4.refs_0_.refs_3_
  24.9 2.0 %shard_map.80 = (bf16[1,1024,1024]{2,1,0:T(8,128)(2,1)S(1)}, bf16[1,1024,1024]{2,1,0:T(8,128)(2,1)S(1)}, f32[32,1024]{1,0:T(8,128)S(1)}) custom-call(f32[4,48,256]{2,1,0:T(8,128)S(1)} %pad_maximum_fusion.near_ref.refs_0_, f32[1]{0:T(128)S(6)} %copy.8.signal_ref, f32[1]{0:T(128)S(6)} %copy.9.noise_ref, ...), custom_call_target="tpu_custom_call" | custom-call | flops 1073741824 | bytes 196608 | tf_op jit(solution)/shard_map/pallas_call | solution.py:124
  26.9 2.2 %collective-permute-done.7.refs_1_.refs_6_ = f32[4,48,256]{2,1,0:T(8,128)S(1)} collective-permute-done((f32[4,48,256]{2,1,0:T(8,128)S(1)}, f32[4,48,256]{2,1,0:T(8,128)S(1)}, u32[]{:S(2)}, u32[]{:S(2)}) %collective-permute-start.7) | collective-permute-done | bytes 196640 | tf_op jit(solution)/shard_map/ppermute | solution.py:27
  29.1 0.0 collective-permute-start.8
  29.1 0.0 collective-permute-done.6.refs_0_.refs_5_
  29.1 2.0 %shard_map.81 = (bf16[1,1024,1024]{2,1,0:T(8,128)(2,1)S(1)}, bf16[1,1024,1024]{2,1,0:T(8,128)(2,1)S(1)}, f32[32,1024]{1,0:T(8,128)S(1)}) custom-call(f32[4,48,256]{2,1,0:T(8,128)S(1)} %pad_maximum_fusion.near_ref.refs_0_, f32[1]{0:T(128)S(6)} %copy.8.signal_ref, f32[1]{0:T(128)S(6)} %copy.9.noise_ref, ...), custom_call_target="tpu_custom_call" | custom-call | flops 1073741824 | bytes 196608 | tf_op jit(solution)/shard_map/pallas_call | solution.py:124
  31.1 0.0 collective-permute-done.8.refs_0_.refs_7_
  31.1 1.1 %shard_map.82 = (bf16[1,1024,1024]{2,1,0:T(8,128)(2,1)S(1)}, f32[4,32,256]{2,1,0:T(8,128)S(1)}) custom-call(f32[4,48,256]{2,1,0:T(8,128)S(1)} %pad_maximum_fusion.near_ref.refs_0_, f32[1]{0:T(128)S(6)} %copy.8.signal_ref, f32[1]{0:T(128)S(6)} %copy.9.noise_ref, f32[4,48,256]{2,1,0:T(8,128)S(1)} %collective-permute-done.8.refs_0_.refs_7_, ...), custom_call_target="tpu_custom_call" | custom-call | flops 536870912 | bytes 196608 | tf_op jit(solution)/shard_map/pallas_call | solution.py:124
  32.2 2.7 %collective-permute-start.14 = (f32[4,32,256]{2,1,0:T(8,128)S(1)}, f32[4,32,256]{2,1,0:T(8,128)S(1)}, u32[]{:S(2)}, u32[]{:S(2)}) collective-permute-start(f32[4,32,256]{2,1,0:T(8,128)S(1)} %get-tuple-element.47.refs_8_), channel_id=1, source_target_pairs={{0,6},{1,7},{2,4},{3,5},{4,2},{5,3},{6,0},{7,1},{8,14},{9,15},{10,... | collective-permute-start | bytes 393224 | tf_op jit(solution)/shard_map/ppermute | solution.py:27
  34.9 0.5 collective-permute-start.12
  35.4 0.3 collective-permute-start.10
  35.7 0.0 collective-permute-start.9
  35.7 3.7 %collective-permute-done.14.refs_14_ = f32[4,32,256]{2,1,0:T(8,128)S(1)} collective-permute-done((f32[4,32,256]{2,1,0:T(8,128)S(1)}, f32[4,32,256]{2,1,0:T(8,128)S(1)}, u32[]{:S(2)}, u32[]{:S(2)}) %collective-permute-start.14) | collective-permute-done | bytes 131104 | tf_op jit(solution)/shard_map/ppermute | solution.py:27
  39.4 0.0 collective-permute-start.15
  39.4 2.7 %collective-permute-done.12.refs_12_ = f32[4,32,256]{2,1,0:T(8,128)S(1)} collective-permute-done((f32[4,32,256]{2,1,0:T(8,128)S(1)}, f32[4,32,256]{2,1,0:T(8,128)S(1)}, u32[]{:S(2)}, u32[]{:S(2)}) %collective-permute-start.12) | collective-permute-done | bytes 131104 | tf_op jit(solution)/shard_map/ppermute | solution.py:27
  42.1 0.0 collective-permute-start.13
  42.1 0.0 collective-permute-done.10.refs_10_
  42.1 0.5 collective-permute-start.11
  42.7 0.0 collective-permute-done.9.refs_9_
  42.7 0.0 collective-permute-done.15.refs_15_
  42.7 0.8 %collective-permute-done.13.refs_13_ = f32[4,32,256]{2,1,0:T(8,128)S(1)} collective-permute-done((f32[4,32,256]{2,1,0:T(8,128)S(1)}, f32[4,32,256]{2,1,0:T(8,128)S(1)}, u32[]{:S(2)}, u32[]{:S(2)}) %collective-permute-start.13) | collective-permute-done | bytes 131104 | tf_op jit(solution)/shard_map/ppermute | solution.py:27
  43.5 0.2 collective-permute-done.11.refs_11_
  43.7 3.5 %shard_map.83 = (f32[32,128]{1,0:T(8,128)S(1)}, f32[32,256]{1,0:T(8,128)S(1)}, f32[32,256]{1,0:T(8,128)S(1)}, f32[32,256]{1,0:T(8,128)S(1)}, f32[32,256]{1,0:T(8,128)S(1)}, /*index=5*/f32[32,128]{1,0:T(8,128)S(1)}) custom-call(f32[1]{0:T(128)S(6)} %copy.8.signal_ref, f32[1]{0:T(128)S(6)} %copy.9.noise_ref, ...), custom_call_target="tpu_custom_call" | custom-call | tf_op jit(solution)/shard_map/pallas_call | solution.py:231
  47.1 0.3 collective-permute-start.16
  47.5 0.9 %collective-permute-done.16 = f32[32,128]{1,0:T(8,128)S(1)} collective-permute-done((f32[32,128]{1,0:T(8,128)S(1)}, f32[32,128]{1,0:T(8,128)S(1)}, u32[]{:S(2)}, u32[]{:S(2)}) %collective-permute-start.16) | collective-permute-done | bytes 16416 | tf_op jit(solution)/shard_map/ppermute | solution.py:27
  48.3 1.5 %collective-permute-start.17 = (f32[32,128]{1,0:T(8,128)S(1)}, f32[32,128]{1,0:T(8,128)S(1)}, u32[]{:S(2)}, u32[]{:S(2)}) collective-permute-start(f32[32,128]{1,0:T(8,128)S(1)} %add.9), channel_id=1, source_target_pairs={{0,2},{1,3},{2,0},{3,1},{4,6},{5,7},{6,4},{7,5},{8,10},{9,11},{10,... | collective-permute-start | bytes 49160 | tf_op jit(solution)/shard_map/ppermute | solution.py:27
  49.8 2.2 %collective-permute-done.17 = f32[32,128]{1,0:T(8,128)S(1)} collective-permute-done((f32[32,128]{1,0:T(8,128)S(1)}, f32[32,128]{1,0:T(8,128)S(1)}, u32[]{:S(2)}, u32[]{:S(2)}) %collective-permute-start.17) | collective-permute-done | bytes 16416 | tf_op jit(solution)/shard_map/ppermute | solution.py:27
  52.1 1.2 %collective-permute-start.18 = (f32[32,128]{1,0:T(8,128)S(1)}, f32[32,128]{1,0:T(8,128)S(1)}, u32[]{:S(2)}, u32[]{:S(2)}) collective-permute-start(f32[32,128]{1,0:T(8,128)S(1)} %add.10), channel_id=1, source_target_pairs={{0,4},{1,5},{2,6},{3,7},{4,0},{5,1},{6,2},{7,3},{8,12},{9,13},{10,... | collective-permute-start | bytes 49160 | tf_op jit(solution)/shard_map/ppermute | solution.py:27
  53.3 2.5 %collective-permute-done.18 = f32[32,128]{1,0:T(8,128)S(1)} collective-permute-done((f32[32,128]{1,0:T(8,128)S(1)}, f32[32,128]{1,0:T(8,128)S(1)}, u32[]{:S(2)}, u32[]{:S(2)}) %collective-permute-start.18) | collective-permute-done | bytes 16416 | tf_op jit(solution)/shard_map/ppermute | solution.py:27
  55.8 0.7 %shard_map.84 = (f32[32,256]{1,0:T(8,128)}, f32[32,256]{1,0:T(8,128)}) custom-call(f32[32,128]{1,0:T(8,128)S(1)} %add.11.curve_ref, f32[32,128]{1,0:T(8,128)S(1)} %get-tuple-element.57.norm_ref, f32[32,256]{1,0:T(8,128)S(1)} %get-tuple-element.58.solution_ref, f32[32,256]{1,0:T(8,128)S(1)} %get-tuple-element.59.residual_ref, ...), custom_call_target="tpu_custom_call" | custom-call | tf_op jit(solution)/shard_map/pallas_call | solution.py:298
  (5 shorter events, 0.0 us)
Async XLA Ops:
  2.1 6.7 %collective-permute-start = (f32[1,48,256]{2,1,0:T(8,128)S(1)}, f32[1,48,256]{2,1,0:T(8,128)S(1)}, u32[]{:S(2)}, u32[]{:S(2)}) collective-permute-start(f32[1,48,256]{2,1,0:T(8,128)S(1)} %shard_map.77), channel_id=1, source_target_pairs={{0,16},{1,17},{2,18},{3,19},{4,20},{5,21},{6,22},{7,23},{8,24},{9,... | collective-permute-start | bytes 147464 | tf_op jit(solution)/shard_map/ppermute | solution.py:27
  8.8 4.7 %collective-permute-start.1 = (f32[2,48,256]{2,1,0:T(8,128)S(1)}, f32[2,48,256]{2,1,0:T(8,128)S(1)}, u32[]{:S(2)}, u32[]{:S(2)}) collective-permute-start(f32[2,48,256]{2,1,0:T(8,128)S(1)} %pad_maximum_fusion.1), channel_id=1, source_target_pairs={{0,8},{1,9},{2,10},{3,11},{4,12},{5,13},{6,14},{7,15},{8,0},{9,1},... | collective-permute-start | bytes 294920 | tf_op jit(solution)/shard_map/ppermute | solution.py:27
  13.5 4.7 %collective-permute-start.2 = (f32[4,48,256]{2,1,0:T(8,128)S(1)}, f32[4,48,256]{2,1,0:T(8,128)S(1)}, u32[]{:S(2)}, u32[]{:S(2)}) collective-permute-start(f32[4,48,256]{2,1,0:T(8,128)S(1)} %pad_maximum_fusion.near_ref.refs_0_), channel_id=1, source_target_pairs={{0,1},{1,0},{2,3},{3,2},{4,5},{5,4},{6,7},{7,6},{8,9},{9,8},{10,11... | collective-permute-start | bytes 589832 | tf_op jit(solution)/shard_map/ppermute | solution.py:27
  13.6 7.3 %collective-permute-start.3 = (f32[4,48,256]{2,1,0:T(8,128)S(1)}, f32[4,48,256]{2,1,0:T(8,128)S(1)}, u32[]{:S(2)}, u32[]{:S(2)}) collective-permute-start(f32[4,48,256]{2,1,0:T(8,128)S(1)} %pad_maximum_fusion.near_ref.refs_0_), channel_id=1, source_target_pairs={{0,4},{1,5},{2,6},{3,7},{4,0},{5,1},{6,2},{7,3},{8,12},{9,13},{10,... | collective-permute-start | bytes 589832 | tf_op jit(solution)/shard_map/ppermute | solution.py:27
  16.7 8.0 %collective-permute-start.5 = (f32[4,48,256]{2,1,0:T(8,128)S(1)}, f32[4,48,256]{2,1,0:T(8,128)S(1)}, u32[]{:S(2)}, u32[]{:S(2)}) collective-permute-start(f32[4,48,256]{2,1,0:T(8,128)S(1)} %pad_maximum_fusion.near_ref.refs_0_), channel_id=1, source_target_pairs={{0,2},{1,3},{2,0},{3,1},{4,6},{5,7},{6,4},{7,5},{8,10},{9,11},{10,... | collective-permute-start | bytes 589832 | tf_op jit(solution)/shard_map/ppermute | solution.py:27
  20.9 4.0 %collective-permute-start.4 = (f32[4,48,256]{2,1,0:T(8,128)S(1)}, f32[4,48,256]{2,1,0:T(8,128)S(1)}, u32[]{:S(2)}, u32[]{:S(2)}) collective-permute-start(f32[4,48,256]{2,1,0:T(8,128)S(1)} %collective-permute-done.3.refs_0_.refs_2_), channel_id=1, source_target_pairs={{0,1},{1,0},{2,3},{3,2},{4,5},{5,4},{6,7},{7,6},{8,9},{9,8},{10,11... | collective-permute-start | bytes 589832 | tf_op jit(solution)/shard_map/ppermute | solution.py:27
  20.9 8.2 %collective-permute-start.7 = (f32[4,48,256]{2,1,0:T(8,128)S(1)}, f32[4,48,256]{2,1,0:T(8,128)S(1)}, u32[]{:S(2)}, u32[]{:S(2)}) collective-permute-start(f32[4,48,256]{2,1,0:T(8,128)S(1)} %pad_maximum_fusion.near_ref.refs_0_), channel_id=1, source_target_pairs={{0,6},{1,7},{2,4},{3,5},{4,2},{5,3},{6,0},{7,1},{8,14},{9,15},{10,... | collective-permute-start | bytes 589832 | tf_op jit(solution)/shard_map/ppermute | solution.py:27
  24.6 4.5 %collective-permute-start.6 = (f32[4,48,256]{2,1,0:T(8,128)S(1)}, f32[4,48,256]{2,1,0:T(8,128)S(1)}, u32[]{:S(2)}, u32[]{:S(2)}) collective-permute-start(f32[4,48,256]{2,1,0:T(8,128)S(1)} %collective-permute-done.5.refs_1_.refs_4_), channel_id=1, source_target_pairs={{0,1},{1,0},{2,3},{3,2},{4,5},{5,4},{6,7},{7,6},{8,9},{9,8},{10,11... | collective-permute-start | bytes 589832 | tf_op jit(solution)/shard_map/ppermute | solution.py:27
  29.1 2.0 %collective-permute-start.8 = (f32[4,48,256]{2,1,0:T(8,128)S(1)}, f32[4,48,256]{2,1,0:T(8,128)S(1)}, u32[]{:S(2)}, u32[]{:S(2)}) collective-permute-start(f32[4,48,256]{2,1,0:T(8,128)S(1)} %collective-permute-done.7.refs_1_.refs_6_), channel_id=1, source_target_pairs={{0,1},{1,0},{2,3},{3,2},{4,5},{5,4},{6,7},{7,6},{8,9},{9,8},{10,11... | collective-permute-start | bytes 589832 | tf_op jit(solution)/shard_map/ppermute | solution.py:27
  32.2 7.2 %collective-permute-start.14 = (f32[4,32,256]{2,1,0:T(8,128)S(1)}, f32[4,32,256]{2,1,0:T(8,128)S(1)}, u32[]{:S(2)}, u32[]{:S(2)}) collective-permute-start(f32[4,32,256]{2,1,0:T(8,128)S(1)} %get-tuple-element.47.refs_8_), channel_id=1, source_target_pairs={{0,6},{1,7},{2,4},{3,5},{4,2},{5,3},{6,0},{7,1},{8,14},{9,15},{10,... | collective-permute-start | bytes 393224 | tf_op jit(solution)/shard_map/ppermute | solution.py:27
  34.9 7.3 %collective-permute-start.12 = (f32[4,32,256]{2,1,0:T(8,128)S(1)}, f32[4,32,256]{2,1,0:T(8,128)S(1)}, u32[]{:S(2)}, u32[]{:S(2)}) collective-permute-start(f32[4,32,256]{2,1,0:T(8,128)S(1)} %get-tuple-element.47.refs_8_), channel_id=1, source_target_pairs={{0,2},{1,3},{2,0},{3,1},{4,6},{5,7},{6,4},{7,5},{8,10},{9,11},{10,... | collective-permute-start | bytes 393224 | tf_op jit(solution)/shard_map/ppermute | solution.py:27
  35.4 6.7 %collective-permute-start.10 = (f32[4,32,256]{2,1,0:T(8,128)S(1)}, f32[4,32,256]{2,1,0:T(8,128)S(1)}, u32[]{:S(2)}, u32[]{:S(2)}) collective-permute-start(f32[4,32,256]{2,1,0:T(8,128)S(1)} %get-tuple-element.47.refs_8_), channel_id=1, source_target_pairs={{0,4},{1,5},{2,6},{3,7},{4,0},{5,1},{6,2},{7,3},{8,12},{9,13},{10,... | collective-permute-start | bytes 393224 | tf_op jit(solution)/shard_map/ppermute | solution.py:27
  35.7 6.9 %collective-permute-start.9 = (f32[4,32,256]{2,1,0:T(8,128)S(1)}, f32[4,32,256]{2,1,0:T(8,128)S(1)}, u32[]{:S(2)}, u32[]{:S(2)}) collective-permute-start(f32[4,32,256]{2,1,0:T(8,128)S(1)} %get-tuple-element.47.refs_8_), channel_id=1, source_target_pairs={{0,1},{1,0},{2,3},{3,2},{4,5},{5,4},{6,7},{7,6},{8,9},{9,8},{10,11... | collective-permute-start | bytes 393224 | tf_op jit(solution)/shard_map/ppermute | solution.py:27
  39.4 3.2 %collective-permute-start.15 = (f32[4,32,256]{2,1,0:T(8,128)S(1)}, f32[4,32,256]{2,1,0:T(8,128)S(1)}, u32[]{:S(2)}, u32[]{:S(2)}) collective-permute-start(f32[4,32,256]{2,1,0:T(8,128)S(1)} %collective-permute-done.14.refs_14_), channel_id=1, source_target_pairs={{0,1},{1,0},{2,3},{3,2},{4,5},{5,4},{6,7},{7,6},{8,9},{9,8},{10,11... | collective-permute-start | bytes 393224 | tf_op jit(solution)/shard_map/ppermute | solution.py:27
  42.1 1.3 %collective-permute-start.13 = (f32[4,32,256]{2,1,0:T(8,128)S(1)}, f32[4,32,256]{2,1,0:T(8,128)S(1)}, u32[]{:S(2)}, u32[]{:S(2)}) collective-permute-start(f32[4,32,256]{2,1,0:T(8,128)S(1)} %collective-permute-done.12.refs_12_), channel_id=1, source_target_pairs={{0,1},{1,0},{2,3},{3,2},{4,5},{5,4},{6,7},{7,6},{8,9},{9,8},{10,11... | collective-permute-start | bytes 393224 | tf_op jit(solution)/shard_map/ppermute | solution.py:27
  42.1 1.5 %collective-permute-start.11 = (f32[4,32,256]{2,1,0:T(8,128)S(1)}, f32[4,32,256]{2,1,0:T(8,128)S(1)}, u32[]{:S(2)}, u32[]{:S(2)}) collective-permute-start(f32[4,32,256]{2,1,0:T(8,128)S(1)} %collective-permute-done.10.refs_10_), channel_id=1, source_target_pairs={{0,1},{1,0},{2,3},{3,2},{4,5},{5,4},{6,7},{7,6},{8,9},{9,8},{10,11... | collective-permute-start | bytes 393224 | tf_op jit(solution)/shard_map/ppermute | solution.py:27
  47.1 1.2 %collective-permute-start.16 = (f32[32,128]{1,0:T(8,128)S(1)}, f32[32,128]{1,0:T(8,128)S(1)}, u32[]{:S(2)}, u32[]{:S(2)}) collective-permute-start(f32[32,128]{1,0:T(8,128)S(1)} %get-tuple-element.56), channel_id=1, source_target_pairs={{0,1},{1,0},{2,3},{3,2},{4,5},{5,4},{6,7},{7,6},{8,9},{9,8},{10,11... | collective-permute-start | bytes 49160 | tf_op jit(solution)/shard_map/ppermute | solution.py:27
  48.3 3.7 %collective-permute-start.17 = (f32[32,128]{1,0:T(8,128)S(1)}, f32[32,128]{1,0:T(8,128)S(1)}, u32[]{:S(2)}, u32[]{:S(2)}) collective-permute-start(f32[32,128]{1,0:T(8,128)S(1)} %add.9), channel_id=1, source_target_pairs={{0,2},{1,3},{2,0},{3,1},{4,6},{5,7},{6,4},{7,5},{8,10},{9,11},{10,... | collective-permute-start | bytes 49160 | tf_op jit(solution)/shard_map/ppermute | solution.py:27
  52.1 3.7 %collective-permute-start.18 = (f32[32,128]{1,0:T(8,128)S(1)}, f32[32,128]{1,0:T(8,128)S(1)}, u32[]{:S(2)}, u32[]{:S(2)}) collective-permute-start(f32[32,128]{1,0:T(8,128)S(1)} %add.10), channel_id=1, source_target_pairs={{0,4},{1,5},{2,6},{3,7},{4,0},{5,1},{6,2},{7,3},{8,12},{9,13},{10,... | collective-permute-start | bytes 49160 | tf_op jit(solution)/shard_map/ppermute | solution.py:27

commit v4 on v3

--- a/solution.py
+++ b/solution.py
@@ -16,7 +16,6 @@
 PIECES = 8
 F32, BF16 = jnp.float32, jnp.bfloat16
 VMEM = pl.BlockSpec(memory_space=pltpu.VMEM)
-SMEM = pl.BlockSpec(memory_space=pltpu.SMEM)
 
 
 def stay(array):
@@ -62,11 +61,20 @@
     sent_ref[0, feat:, :] = jnp.where(valid, right_ref[...], 0.0)
 
 
-def fill_right(near_ref, signal_ref, right_ref, feat):
+def prepare(points, inv_lengths, right_sides, block_counts):
+    smem = pl.BlockSpec(memory_space=pltpu.SMEM)
+    return pl.pallas_call(
+        prepare_kernel,
+        out_shape=pltpu.VMEM((1, points.shape[1] + right_sides.shape[1], points.shape[0]), F32),
+        in_specs=[VMEM, smem, VMEM, smem],
+        out_specs=VMEM,
+    )(points.T, inv_lengths, right_sides.T, block_counts)
+
+
+def fill_right(near_ref, levels_ref, right_ref, feat):
     blocks, slots = right_ref.shape[1] // near_ref.shape[2], near_ref.shape[2]
     for b in range(blocks):
-        level = jnp.log(jnp.full((1, slots), signal_ref[0], F32)) * LOG2E
-        right_ref[:, b * slots : (b + 1) * slots] = features(near_ref[b, :feat, :], level, False)
+        right_ref[:, b * slots : (b + 1) * slots] = features(near_ref[b, :feat, :], levels_ref[0:1, :], False)
 
 
 def entries(left, right):
@@ -74,7 +82,7 @@
     return jnp.exp2(powers).astype(BF16)
 
 
-def apply_kernel(feat, group, keep, begin, last, count, near_ref, signal_ref, noise_ref, *refs):
+def apply_kernel(feat, group, keep, begin, last, count, near_ref, levels_ref, *refs):
     far, refs = refs[:count], refs[count:]
     if begin:
         right_ref, refs = refs[-4], refs[:-4] + refs[-3:]
@@ -84,7 +92,7 @@
     out_ref, left_ref, dirs_ref, sum_ref = refs
     slots = near_ref.shape[2]
     if begin:
-        fill_right(near_ref, signal_ref, right_ref, feat)
+        fill_right(near_ref, levels_ref, right_ref, feat)
         sum_ref[...] = jnp.zeros_like(sum_ref)
     else:
         sum_ref[...] = so_far_ref[...]
@@ -107,10 +115,10 @@
         return
     for b in range(near_ref.shape[0]):
         direction = near_ref[b, feat:, :].astype(BF16).astype(F32)
-        out_ref[b] = sum_ref[:, b * slots : (b + 1) * slots] + noise_ref[0] * direction
-
-
-def apply_first(near, far, signal, noise, so_far, feat, group, keep, last=False):
+        out_ref[b] = sum_ref[:, b * slots : (b + 1) * slots] + levels_ref[1:2, :] * direction
+
+
+def apply_first(near, far, levels, so_far, feat, group, keep, last=False):
     copies, slots, probes = near.shape[0], near.shape[2], near.shape[1] - feat
     wide, steps, begin = group * slots, far[0].shape[0] // group, so_far is None
     outs = [pltpu.VMEM((copies, probes, slots) if last else (probes, copies * slots), F32)]
@@ -118,13 +126,13 @@
         outs = [pltpu.VMEM((steps, wide, copies * slots), BF16)] * len(far) + outs
     if begin:
         outs = outs + [pltpu.VMEM((feature_rows(feat), copies * slots), BF16)]
-    arrays = [near, *far, *([] if begin else so_far)]
+    arrays = [near, levels, *far, *([] if begin else so_far)]
     if keep:
         arrays = [stay(array) for array in arrays]
     done = pl.pallas_call(
         functools.partial(apply_kernel, feat, group, keep, begin, last, len(far)),
         out_shape=outs,
-        in_specs=[VMEM, SMEM, SMEM] + [VMEM] * (len(arrays) - 1),
+        in_specs=[VMEM] * len(arrays),
         out_specs=[VMEM] * len(outs),
         scratch_shapes=[
             pltpu.VMEM((feature_rows(feat), wide), BF16),
@@ -137,14 +145,14 @@
             bytes_accessed=far[0].size * 4,
             transcendentals=0,
         ),
-    )(arrays[0], signal, noise, *arrays[1:])
+    )(*arrays)
     kept, rest = (done[: len(far)], done[len(far) :]) if keep else ([None] * len(far), done)
     if begin:
         return kept, (rest[1], rest[0])
     return kept, rest[0] if last else (so_far[0], rest[0])
 
 
-def second_kernel(feat, group, keep, copies, signal_ref, noise_ref, *refs):
+def second_kernel(feat, group, keep, copies, levels_ref, *refs):
     points, images, refs = refs[:PIECES], refs[PIECES : 2 * PIECES], refs[2 * PIECES :]
     if keep:
         kept, refs = refs[:PIECES], refs[PIECES:]
@@ -189,7 +197,7 @@
 
     product_ref[...] = jnp.zeros_like(product_ref)
     if not keep:
-        fill_right(points[0], signal_ref, right_ref, feat)
+        fill_right(points[0], levels_ref, right_ref, feat)
     for piece, (x_ref, w_ref) in enumerate(pairs):
 
         def step(g, carry, piece=piece, x_ref=x_ref, w_ref=w_ref):
@@ -208,7 +216,7 @@
     for b in range(copies):
         residual, first, direction = direct(points[0], images[0], b)
         direction = direction.astype(F32)
-        image = product_ref[:, b * slots : (b + 1) * slots] + noise_ref[0] * direction
+        image = product_ref[:, b * slots : (b + 1) * slots] + levels_ref[1:2, :] * direction
         total = total + direction * image
         if b == 0:
             solution_ref[...] = step_size * first
@@ -219,23 +227,24 @@
     norm_ref[...] = jnp.broadcast_to(norm_next, norm_ref.shape)
 
 
-def second(signal, noise, points, images, kept, copies, feat, group):
+def second(levels, points, images, kept, copies, feat, group):
     keep = kept is not None
     slots, probes = images[0].shape[2], images[0].shape[1]
     own, small, wide = pltpu.VMEM((probes, slots), F32), pltpu.VMEM((probes, 128), F32), group * slots
     scratch = [pltpu.VMEM((probes, copies * slots), F32), pltpu.VMEM((probes, wide), BF16)]
     if keep:
+        levels = stay(levels)
         points, images, kept = ([stay(piece) for piece in pieces] for pieces in (points, images, kept))
     else:
         scratch += [pltpu.VMEM((feature_rows(feat), copies * slots), BF16), pltpu.VMEM((feature_rows(feat), wide), BF16)]
     return pl.pallas_call(
         functools.partial(second_kernel, feat, group, keep, copies),
         out_shape=[small, own, own, own, own, small],
-        in_specs=[SMEM, SMEM] + [VMEM] * (3 * PIECES if keep else 2 * PIECES),
+        in_specs=[VMEM] * (3 * PIECES + 1 if keep else 2 * PIECES + 1),
         out_specs=[VMEM] * 6,
         scratch_shapes=scratch,
         compiler_params=pltpu.CompilerParams(vmem_limit_bytes=(16 if keep else 48) * 2**20),
-    )(signal, noise, *points, *images, *(kept or ()))
+    )(levels, *points, *images, *(kept or ()))
 
 
 def finish_kernel(curve_ref, norm_ref, solution_ref, residual_ref, direction_ref, image_ref, out_ref, left_ref):
@@ -245,8 +254,18 @@
 
 
 def gather(held, bits, count):
-    for bit in bits:
-        held = jnp.concatenate([held, swap(held, bit, count)], axis=0)
+    for at in range(0, len(bits), 2):
+        pair = bits[at : at + 2]
+        flips = pair if len(pair) == 1 else [pair[0], pair[1], sum(pair)]
+        held = jnp.concatenate([held] + [swap(held, flip, count) for flip in flips], axis=0)
+    return held
+
+
+def total(held, bits, count):
+    for at in range(0, len(bits), 2):
+        pair = bits[at : at + 2]
+        flips = pair if len(pair) == 1 else [pair[0], pair[1], sum(pair)]
+        held = sum([swap(held, flip, count) for flip in flips], held)
     return held
 
 
@@ -261,39 +280,38 @@
     bits = [1 << k for k in reversed(range(count.bit_length() - 1))]
     later = bits[copies.bit_length() - 1 :]
     one, two, core = bits[-3:]
-    own = pl.pallas_call(
-        prepare_kernel,
-        out_shape=pltpu.VMEM((1, feat + probes, slots), F32),
-        in_specs=[VMEM, SMEM, VMEM, SMEM],
-        out_specs=VMEM,
-    )(points.T, inv_lengths, right_sides.T, block_counts)
+    own = prepare(points, inv_lengths, right_sides, block_counts)
+    own, signal_level, noise_level = lax.optimization_barrier((own, signal_level, noise_level))
+    levels = jnp.stack([jnp.log(signal_level[0]) * LOG2E, noise_level[0]])
+    levels = jnp.broadcast_to(levels[:, None], (2, slots))
     first = functools.partial(apply_first, feat=feat, group=group, keep=keep)
 
     held = gather(own, bits[:-3], count)
+    held, levels = lax.optimization_barrier((held, levels))
     near = held[:copies]
-    beside, up, over, corner = (swap(held, bit, count) for bit in (core, one, two, one | two))
-    kept_0, product = first(near, [held, beside], signal_level, noise_level, None)
+    beside, up, over = (swap(held, bit, count) for bit in (core, one, two))
+    kept_0, product = first(near, [held, beside], levels, None)
     up, product = lax.optimization_barrier((up, product))
-    up_beside = swap(up, core, count)
-    kept_1, product = first(near, [up], signal_level, noise_level, product)
+    corner, up_beside = swap(up, two, count), swap(up, core, count)
+    kept_1, product = first(near, [up], levels, product)
     over, product = lax.optimization_barrier((over, product))
     over_beside = swap(over, core, count)
-    kept_2, product = first(near, [up_beside, over], signal_level, noise_level, product)
+    kept_2, product = first(near, [up_beside, over], levels, product)
     corner, product = lax.optimization_barrier((corner, product))
     corner_beside = swap(corner, core, count)
-    kept_3, product = first(near, [over_beside, corner], signal_level, noise_level, product)
-    kept_4, image = first(near, [corner_beside], signal_level, noise_level, product, last=True)
+    kept_3, product = first(near, [over_beside, corner], levels, product)
+    kept_4, image = first(near, [corner_beside], levels, product, last=True)
     pieces = [held, beside, up, up_beside, over, over_beside, corner, corner_beside]
     kept = [*kept_0, *kept_1, *kept_2, *kept_3, *kept_4]
 
     held = gather(image, later[:-3], count)
-    direct = [held] + [swap(held, bit, count) for bit in (one, two, one | two)]
-    images = [array for piece in direct for array in (piece, swap(piece, core, count))]
+    up, over, corner = (swap(held, bit, count) for bit in (one, two, one | two))
+    beside, up_beside, over_beside, corner_beside = (swap(array, core, count) for array in (held, up, over, corner))
+    images = [held, beside, up, up_beside, over, over_beside, corner, corner_beside]
     partial, solution, residual, direction, own_image, norm = second(
-        signal_level, noise_level, pieces, images, kept if keep else None, copies, feat, group
+        levels, pieces, images, kept if keep else None, copies, feat, group
     )
-    for bit in reversed(later):
-        partial = partial + swap(partial, bit, count)
+    partial = total(partial + swap(partial, core, count), later[:-1][::-1], count)
     done = jax.ShapeDtypeStruct((probes, slots), F32)
     solution, residual = pl.pallas_call(
         finish_kernel,

time: 56.8 us -> 54 us (0.951)
  waiting for transfers between devices: 21.8 us -> 19.3 us
    ppermute x19 -> x21, waiting for transfers between devices: 21.8 us -> 19.3 us  [swap(): return lax.ppermute(array, AXES, [(i, i ^ bit) for i in range(count)])]
    ppermute x19 -> x21, starting transfers between devices: 19 us -> 18.5 us  [swap(): return lax.ppermute(array, AXES, [(i, i ^ bit) for i in range(count)])]
  transfers between devices with their start and end apart: 19 -> 21, of which waited for: 11 -> 13; matrix products, arithmetic and copies ran while one was open for 0% -> 0% of each run, Pallas kernels for 12% -> 13%
where the time goes in v4:
time: 54 us; the launch traced here: 53.8 us
  waiting for transfers between devices  19.3 us (36%)
  starting transfers between devices  18.5 us (34%)
  Pallas kernels  13.1 us (24%)
  between operations  2.68 us (5%)
    ppermute x21, waiting for transfers between devices, swap(): return lax.ppermute(array, AXES, [(i, i ^ bit) for i in range(count)])  19.3 us
    ppermute x21, starting transfers between devices, swap(): return lax.ppermute(array, AXES, [(i, i ^ bit) for i in range(count)])  18.5 us
    pallas_call x5, Pallas kernels, apply_first(): pl.pallas_call(functools.partial(apply_kernel, feat, group, keep, begin,...  8.08 us
    pallas_call x1, Pallas kernels, second(): pl.pallas_call(functools.partial(second_kernel, feat, group, keep, copies...  3.52 us
  transfers between devices with their start and end apart: 21, of which 13 were waited for; matrix products, arithmetic and copies ran while one was open for 0% of the time, Pallas kernels for 13%

profile of v4, /device:TPU:0, one launch (start us, length us, event | category | flops | bytes accessed | tf_op | source)
XLA Modules:
  0.0 53.8 jit_solution(12202286398845890708)
XLA Ops:
  1.3 0.8 %shard_map.77 = f32[1,48,256]{2,1,0:T(8,128)S(1)} custom-call(f32[16,256]{1,0:T(8,128)} %bitcast.5, f32[16]{0:T(128)} %inv_ref.1, f32[32,256]{1,0:T(8,128)} %bitcast.4, s32[1]{0:T(128)S(6)} %copy.10.count_ref), custom_call_target="tpu_custom_call" | custom-call | tf_op jit(solution)/shard_map/pallas_call | solution.py:66
  2.1 5.1 %collective-permute-start.2 = (f32[1,48,256]{2,1,0:T(8,128)S(1)}, f32[1,48,256]{2,1,0:T(8,128)S(1)}, u32[]{:S(2)}, u32[]{:S(2)}) collective-permute-start(f32[1,48,256]{2,1,0:T(8,128)S(1)} %shard_map.77), channel_id=1, source_target_pairs={{0,24},{1,25},{2,26},{3,27},{4,28},{5,29},{6,30},{7,31},{8,16},{9,... | collective-permute-start | bytes 147464 | tf_op jit(solution)/shard_map/ppermute | solution.py:26
  7.2 0.0 collective-permute-start.1
  7.2 0.6 %collective-permute-start = (f32[1,48,256]{2,1,0:T(8,128)S(1)}, f32[1,48,256]{2,1,0:T(8,128)S(1)}, u32[]{:S(2)}, u32[]{:S(2)}) collective-permute-start(f32[1,48,256]{2,1,0:T(8,128)S(1)} %shard_map.77), channel_id=1, source_target_pairs={{0,16},{1,17},{2,18},{3,19},{4,20},{5,21},{6,22},{7,23},{8,24},{9,... | collective-permute-start | bytes 147464 | tf_op jit(solution)/shard_map/ppermute | solution.py:26
  9.2 0.1 pad_maximum_fusion.1
  9.3 0.2 collective-permute-done.2
  9.5 1.8 %collective-permute-done.1 = f32[1,48,256]{2,1,0:T(8,128)S(1)} collective-permute-done((f32[1,48,256]{2,1,0:T(8,128)S(1)}, f32[1,48,256]{2,1,0:T(8,128)S(1)}, u32[]{:S(2)}, u32[]{:S(2)}) %collective-permute-start.1) | collective-permute-done | bytes 49184 | tf_op jit(solution)/shard_map/ppermute | solution.py:26
  11.3 1.2 %collective-permute-done = f32[1,48,256]{2,1,0:T(8,128)S(1)} collective-permute-done((f32[1,48,256]{2,1,0:T(8,128)S(1)}, f32[1,48,256]{2,1,0:T(8,128)S(1)}, u32[]{:S(2)}, u32[]{:S(2)}) %collective-permute-start) | collective-permute-done | bytes 49184 | tf_op jit(solution)/shard_map/ppermute | solution.py:26
  12.5 0.1 broadcast_in_dim.2.levels_ref
  12.6 0.0 collective-permute-start.3
  12.6 1.6 %collective-permute-start.4 = (f32[4,48,256]{2,1,0:T(8,128)S(1)}, f32[4,48,256]{2,1,0:T(8,128)S(1)}, u32[]{:S(2)}, u32[]{:S(2)}) collective-permute-start(f32[4,48,256]{2,1,0:T(8,128)S(1)} %pad_maximum_fusion.near_ref.refs_0_), channel_id=1, source_target_pairs={{0,4},{1,5},{2,6},{3,7},{4,0},{5,1},{6,2},{7,3},{8,12},{9,13},{10,... | collective-permute-start | bytes 589832 | tf_op jit(solution)/shard_map/ppermute | solution.py:26
  14.2 1.5 %collective-permute-start.6 = (f32[4,48,256]{2,1,0:T(8,128)S(1)}, f32[4,48,256]{2,1,0:T(8,128)S(1)}, u32[]{:S(2)}, u32[]{:S(2)}) collective-permute-start(f32[4,48,256]{2,1,0:T(8,128)S(1)} %pad_maximum_fusion.near_ref.refs_0_), channel_id=1, source_target_pairs={{0,2},{1,3},{2,0},{3,1},{4,6},{5,7},{6,4},{7,5},{8,10},{9,11},{10,... | collective-permute-start | bytes 589832 | tf_op jit(solution)/shard_map/ppermute | solution.py:26
  15.7 0.0 collective-permute-done.3.refs_1_
  15.7 2.0 %shard_map.78 = (bf16[1,1024,1024]{2,1,0:T(8,128)(2,1)S(1)}, bf16[1,1024,1024]{2,1,0:T(8,128)(2,1)S(1)}, f32[32,1024]{1,0:T(8,128)S(1)}, bf16[112,1024]{1,0:T(8,128)(2,1)S(1)}) custom-call(f32[4,48,256]{2,1,0:T(8,128)S(1)} %pad_maximum_fusion.near_ref.refs_0_, f32[2,256]{1,0:T(2,128)S(1)} %broadcast_in_dim.2.levels_ref, ...), custom_call_target="tpu_custom_call" | custom-call | flops 1073741824 | bytes 196608 | tf_op jit(solution)/shard_map/pallas_call | solution.py:132
  17.6 2.3 %collective-permute-done.4.refs_0_.refs_2_ = f32[4,48,256]{2,1,0:T(8,128)S(1)} collective-permute-done((f32[4,48,256]{2,1,0:T(8,128)S(1)}, f32[4,48,256]{2,1,0:T(8,128)S(1)}, u32[]{:S(2)}, u32[]{:S(2)}) %collective-permute-start.4) | collective-permute-done | bytes 196640 | tf_op jit(solution)/shard_map/ppermute | solution.py:26
  19.9 0.0 collective-permute-start.5
  19.9 1.5 %collective-permute-start.8 = (f32[4,48,256]{2,1,0:T(8,128)S(1)}, f32[4,48,256]{2,1,0:T(8,128)S(1)}, u32[]{:S(2)}, u32[]{:S(2)}) collective-permute-start(f32[4,48,256]{2,1,0:T(8,128)S(1)} %collective-permute-done.4.refs_0_.refs_2_), channel_id=1, source_target_pairs={{0,2},{1,3},{2,0},{3,1},{4,6},{5,7},{6,4},{7,5},{8,10},{9,11},{10,... | collective-permute-start | bytes 589832 | tf_op jit(solution)/shard_map/ppermute | solution.py:26
  21.4 1.1 %shard_map.79 = (bf16[1,1024,1024]{2,1,0:T(8,128)(2,1)S(1)}, f32[32,1024]{1,0:T(8,128)S(1)}) custom-call(f32[4,48,256]{2,1,0:T(8,128)S(1)} %pad_maximum_fusion.near_ref.refs_0_, f32[2,256]{1,0:T(2,128)S(1)} %broadcast_in_dim.2.levels_ref, f32[4,48,256]{2,1,0:T(8,128)S(1)} %collective-permute-done.4.refs_0_.refs_2_, ...), custom_call_target="tpu_custom_call" | custom-call | flops 536870912 | bytes 196608 | tf_op jit(solution)/shard_map/pallas_call | solution.py:132
  22.5 0.0 collective-permute-done.6.refs_1_.refs_4_
  22.5 0.3 collective-permute-start.7
  22.8 0.0 collective-permute-done.5.refs_0_.refs_3_
  22.8 2.0 %shard_map.80 = (bf16[1,1024,1024]{2,1,0:T(8,128)(2,1)S(1)}, bf16[1,1024,1024]{2,1,0:T(8,128)(2,1)S(1)}, f32[32,1024]{1,0:T(8,128)S(1)}) custom-call(f32[4,48,256]{2,1,0:T(8,128)S(1)} %pad_maximum_fusion.near_ref.refs_0_, f32[2,256]{1,0:T(2,128)S(1)} %broadcast_in_dim.2.levels_ref, f32[4,48,256]{2,1,0:T(8,128)S(1)} %collective-permute-done.5.refs_0_.refs_3_, ...), custom_call_target="tpu_custom_call" | custom-call | flops 1073741824 | bytes 196608 | tf_op jit(solution)/shard_map/pallas_call | solution.py:132
  24.8 2.5 %collective-permute-done.8.refs_1_.refs_6_ = f32[4,48,256]{2,1,0:T(8,128)S(1)} collective-permute-done((f32[4,48,256]{2,1,0:T(8,128)S(1)}, f32[4,48,256]{2,1,0:T(8,128)S(1)}, u32[]{:S(2)}, u32[]{:S(2)}) %collective-permute-start.8) | collective-permute-done | bytes 196640 | tf_op jit(solution)/shard_map/ppermute | solution.py:26
  27.2 2.0 %shard_map.81 = (bf16[1,1024,1024]{2,1,0:T(8,128)(2,1)S(1)}, bf16[1,1024,1024]{2,1,0:T(8,128)(2,1)S(1)}, f32[32,1024]{1,0:T(8,128)S(1)}) custom-call(f32[4,48,256]{2,1,0:T(8,128)S(1)} %pad_maximum_fusion.near_ref.refs_0_, f32[2,256]{1,0:T(2,128)S(1)} %broadcast_in_dim.2.levels_ref, f32[4,48,256]{2,1,0:T(8,128)S(1)} %collective-permute-done.7.refs_0_.refs_5_, ...), custom_call_target="tpu_custom_call" | custom-call | flops 1073741824 | bytes 196608 | tf_op jit(solution)/shard_map/pallas_call | solution.py:132
  29.2 0.0 collective-permute-done.9.refs_0_.refs_7_
  29.3 1.1 %shard_map.82 = (bf16[1,1024,1024]{2,1,0:T(8,128)(2,1)S(1)}, f32[4,32,256]{2,1,0:T(8,128)S(1)}) custom-call(f32[4,48,256]{2,1,0:T(8,128)S(1)} %pad_maximum_fusion.near_ref.refs_0_, f32[2,256]{1,0:T(2,128)S(1)} %broadcast_in_dim.2.levels_ref, f32[4,48,256]{2,1,0:T(8,128)S(1)} %collective-permute-done.9.refs_0_.refs_7_, ...), custom_call_target="tpu_custom_call" | custom-call | flops 536870912 | bytes 196608 | tf_op jit(solution)/shard_map/pallas_call | solution.py:132
  30.3 2.5 %collective-permute-start.15 = (f32[4,32,256]{2,1,0:T(8,128)S(1)}, f32[4,32,256]{2,1,0:T(8,128)S(1)}, u32[]{:S(2)}, u32[]{:S(2)}) collective-permute-start(f32[4,32,256]{2,1,0:T(8,128)S(1)} %get-tuple-element.57.refs_8_), channel_id=1, source_target_pairs={{0,6},{1,7},{2,4},{3,5},{4,2},{5,3},{6,0},{7,1},{8,14},{9,15},{10,... | collective-permute-start | bytes 393224 | tf_op jit(solution)/shard_map/ppermute | solution.py:26
  32.8 0.5 %collective-permute-start.13 = (f32[4,32,256]{2,1,0:T(8,128)S(1)}, f32[4,32,256]{2,1,0:T(8,128)S(1)}, u32[]{:S(2)}, u32[]{:S(2)}) collective-permute-start(f32[4,32,256]{2,1,0:T(8,128)S(1)} %get-tuple-element.57.refs_8_), channel_id=1, source_target_pairs={{0,2},{1,3},{2,0},{3,1},{4,6},{5,7},{6,4},{7,5},{8,10},{9,11},{10,... | collective-permute-start | bytes 393224 | tf_op jit(solution)/shard_map/ppermute | solution.py:26
  33.4 0.5 collective-permute-start.11
  33.9 3.7 %collective-permute-done.15.refs_14_ = f32[4,32,256]{2,1,0:T(8,128)S(1)} collective-permute-done((f32[4,32,256]{2,1,0:T(8,128)S(1)}, f32[4,32,256]{2,1,0:T(8,128)S(1)}, u32[]{:S(2)}, u32[]{:S(2)}) %collective-permute-start.15) | collective-permute-done | bytes 131104 | tf_op jit(solution)/shard_map/ppermute | solution.py:26
  37.6 0.0 collective-permute-start.16
  37.6 2.5 %collective-permute-done.13.refs_12_ = f32[4,32,256]{2,1,0:T(8,128)S(1)} collective-permute-done((f32[4,32,256]{2,1,0:T(8,128)S(1)}, f32[4,32,256]{2,1,0:T(8,128)S(1)}, u32[]{:S(2)}, u32[]{:S(2)}) %collective-permute-start.13) | collective-permute-done | bytes 131104 | tf_op jit(solution)/shard_map/ppermute | solution.py:26
  40.1 0.0 collective-permute-start.14
  40.1 0.0 collective-permute-done.11.refs_10_
  40.1 0.5 collective-permute-start.12
  40.6 0.0 collective-permute-done.10.refs_9_
  40.6 0.8 %collective-permute-done.14.refs_13_ = f32[4,32,256]{2,1,0:T(8,128)S(1)} collective-permute-done((f32[4,32,256]{2,1,0:T(8,128)S(1)}, f32[4,32,256]{2,1,0:T(8,128)S(1)}, u32[]{:S(2)}, u32[]{:S(2)}) %collective-permute-start.14) | collective-permute-done | bytes 131104 | tf_op jit(solution)/shard_map/ppermute | solution.py:26
  41.5 0.2 collective-permute-done.12.refs_11_
  41.6 3.5 %shard_map.83 = (f32[32,128]{1,0:T(8,128)S(1)}, f32[32,256]{1,0:T(8,128)S(1)}, f32[32,256]{1,0:T(8,128)S(1)}, f32[32,256]{1,0:T(8,128)S(1)}, f32[32,256]{1,0:T(8,128)S(1)}, /*index=5*/f32[32,128]{1,0:T(8,128)S(1)}) custom-call(f32[2,256]{1,0:T(2,128)S(1)} %broadcast_in_dim.2.levels_ref, f32[4,48,256]{2,1,0:T(8,128)S(1)} %pad_maximum_fusion.near_ref.refs_0_, ...), custom_call_target="tpu_custom_call" | custom-call | tf_op jit(solution)/shard_map/pallas_call | solution.py:240
  45.2 0.3 collective-permute-start.17
  45.5 0.9 %collective-permute-done.17 = f32[32,128]{1,0:T(8,128)S(1)} collective-permute-done((f32[32,128]{1,0:T(8,128)S(1)}, f32[32,128]{1,0:T(8,128)S(1)}, u32[]{:S(2)}, u32[]{:S(2)}) %collective-permute-start.17) | collective-permute-done | bytes 16416 | tf_op jit(solution)/shard_map/ppermute | solution.py:26
  46.4 2.2 %collective-permute-start.20 = (f32[32,128]{1,0:T(8,128)S(1)}, f32[32,128]{1,0:T(8,128)S(1)}, u32[]{:S(2)}, u32[]{:S(2)}) collective-permute-start(f32[32,128]{1,0:T(8,128)S(1)} %add.12), channel_id=1, source_target_pairs={{0,6},{1,7},{2,4},{3,5},{4,2},{5,3},{6,0},{7,1},{8,14},{9,15},{10,... | collective-permute-start | bytes 49160 | tf_op jit(solution)/shard_map/ppermute | solution.py:26
  48.5 0.8 %collective-permute-start.19 = (f32[32,128]{1,0:T(8,128)S(1)}, f32[32,128]{1,0:T(8,128)S(1)}, u32[]{:S(2)}, u32[]{:S(2)}) collective-permute-start(f32[32,128]{1,0:T(8,128)S(1)} %add.12), channel_id=1, source_target_pairs={{0,4},{1,5},{2,6},{3,7},{4,0},{5,1},{6,2},{7,3},{8,12},{9,13},{10,... | collective-permute-start | bytes 49160 | tf_op jit(solution)/shard_map/ppermute | solution.py:26
  49.3 0.5 collective-permute-start.18
  49.8 1.1 %collective-permute-done.20 = f32[32,128]{1,0:T(8,128)S(1)} collective-permute-done((f32[32,128]{1,0:T(8,128)S(1)}, f32[32,128]{1,0:T(8,128)S(1)}, u32[]{:S(2)}, u32[]{:S(2)}) %collective-permute-start.20) | collective-permute-done | bytes 16416 | tf_op jit(solution)/shard_map/ppermute | solution.py:26
  51.0 1.3 %collective-permute-done.19 = f32[32,128]{1,0:T(8,128)S(1)} collective-permute-done((f32[32,128]{1,0:T(8,128)S(1)}, f32[32,128]{1,0:T(8,128)S(1)}, u32[]{:S(2)}, u32[]{:S(2)}) %collective-permute-start.19) | collective-permute-done | bytes 16416 | tf_op jit(solution)/shard_map/ppermute | solution.py:26
  52.3 0.8 %collective-permute-done.18 = f32[32,128]{1,0:T(8,128)S(1)} collective-permute-done((f32[32,128]{1,0:T(8,128)S(1)}, f32[32,128]{1,0:T(8,128)S(1)}, u32[]{:S(2)}, u32[]{:S(2)}) %collective-permute-start.18) | collective-permute-done | bytes 16416 | tf_op jit(solution)/shard_map/ppermute | solution.py:26
  53.1 0.7 %shard_map.84 = (f32[32,256]{1,0:T(8,128)}, f32[32,256]{1,0:T(8,128)}) custom-call(f32[32,128]{1,0:T(8,128)S(1)} %add_add_fusion.curve_ref, f32[32,128]{1,0:T(8,128)S(1)} %get-tuple-element.67.norm_ref, f32[32,256]{1,0:T(8,128)S(1)} %get-tuple-element.68.solution_ref, f32[32,256]{1,0:T(8,128)S(1)} %get-tuple-element.69.residual_ref, ...), custom_call_target="tpu_custom_call" | custom-call | tf_op jit(solution)/shard_map/pallas_call | solution.py:316
  (7 shorter events, 0.0 us)
Async XLA Ops:
  2.1 7.4 %collective-permute-start.2 = (f32[1,48,256]{2,1,0:T(8,128)S(1)}, f32[1,48,256]{2,1,0:T(8,128)S(1)}, u32[]{:S(2)}, u32[]{:S(2)}) collective-permute-start(f32[1,48,256]{2,1,0:T(8,128)S(1)} %shard_map.77), channel_id=1, source_target_pairs={{0,24},{1,25},{2,26},{3,27},{4,28},{5,29},{6,30},{7,31},{8,16},{9,... | collective-permute-start | bytes 147464 | tf_op jit(solution)/shard_map/ppermute | solution.py:26
  7.2 4.1 %collective-permute-start.1 = (f32[1,48,256]{2,1,0:T(8,128)S(1)}, f32[1,48,256]{2,1,0:T(8,128)S(1)}, u32[]{:S(2)}, u32[]{:S(2)}) collective-permute-start(f32[1,48,256]{2,1,0:T(8,128)S(1)} %shard_map.77), channel_id=1, source_target_pairs={{0,8},{1,9},{2,10},{3,11},{4,12},{5,13},{6,14},{7,15},{8,0},{9,1},... | collective-permute-start | bytes 147464 | tf_op jit(solution)/shard_map/ppermute | solution.py:26
  7.2 5.3 %collective-permute-start = (f32[1,48,256]{2,1,0:T(8,128)S(1)}, f32[1,48,256]{2,1,0:T(8,128)S(1)}, u32[]{:S(2)}, u32[]{:S(2)}) collective-permute-start(f32[1,48,256]{2,1,0:T(8,128)S(1)} %shard_map.77), channel_id=1, source_target_pairs={{0,16},{1,17},{2,18},{3,19},{4,20},{5,21},{6,22},{7,23},{8,24},{9,... | collective-permute-start | bytes 147464 | tf_op jit(solution)/shard_map/ppermute | solution.py:26
  12.6 3.1 %collective-permute-start.3 = (f32[4,48,256]{2,1,0:T(8,128)S(1)}, f32[4,48,256]{2,1,0:T(8,128)S(1)}, u32[]{:S(2)}, u32[]{:S(2)}) collective-permute-start(f32[4,48,256]{2,1,0:T(8,128)S(1)} %pad_maximum_fusion.near_ref.refs_0_), channel_id=1, source_target_pairs={{0,1},{1,0},{2,3},{3,2},{4,5},{5,4},{6,7},{7,6},{8,9},{9,8},{10,11... | collective-permute-start | bytes 589832 | tf_op jit(solution)/shard_map/ppermute | solution.py:26
  12.6 7.3 %collective-permute-start.4 = (f32[4,48,256]{2,1,0:T(8,128)S(1)}, f32[4,48,256]{2,1,0:T(8,128)S(1)}, u32[]{:S(2)}, u32[]{:S(2)}) collective-permute-start(f32[4,48,256]{2,1,0:T(8,128)S(1)} %pad_maximum_fusion.near_ref.refs_0_), channel_id=1, source_target_pairs={{0,4},{1,5},{2,6},{3,7},{4,0},{5,1},{6,2},{7,3},{8,12},{9,13},{10,... | collective-permute-start | bytes 589832 | tf_op jit(solution)/shard_map/ppermute | solution.py:26
  14.2 8.3 %collective-permute-start.6 = (f32[4,48,256]{2,1,0:T(8,128)S(1)}, f32[4,48,256]{2,1,0:T(8,128)S(1)}, u32[]{:S(2)}, u32[]{:S(2)}) collective-permute-start(f32[4,48,256]{2,1,0:T(8,128)S(1)} %pad_maximum_fusion.near_ref.refs_0_), channel_id=1, source_target_pairs={{0,2},{1,3},{2,0},{3,1},{4,6},{5,7},{6,4},{7,5},{8,10},{9,11},{10,... | collective-permute-start | bytes 589832 | tf_op jit(solution)/shard_map/ppermute | solution.py:26
  19.9 2.9 %collective-permute-start.5 = (f32[4,48,256]{2,1,0:T(8,128)S(1)}, f32[4,48,256]{2,1,0:T(8,128)S(1)}, u32[]{:S(2)}, u32[]{:S(2)}) collective-permute-start(f32[4,48,256]{2,1,0:T(8,128)S(1)} %collective-permute-done.4.refs_0_.refs_2_), channel_id=1, source_target_pairs={{0,1},{1,0},{2,3},{3,2},{4,5},{5,4},{6,7},{7,6},{8,9},{9,8},{10,11... | collective-permute-start | bytes 589832 | tf_op jit(solution)/shard_map/ppermute | solution.py:26
  19.9 7.3 %collective-permute-start.8 = (f32[4,48,256]{2,1,0:T(8,128)S(1)}, f32[4,48,256]{2,1,0:T(8,128)S(1)}, u32[]{:S(2)}, u32[]{:S(2)}) collective-permute-start(f32[4,48,256]{2,1,0:T(8,128)S(1)} %collective-permute-done.4.refs_0_.refs_2_), channel_id=1, source_target_pairs={{0,2},{1,3},{2,0},{3,1},{4,6},{5,7},{6,4},{7,5},{8,10},{9,11},{10,... | collective-permute-start | bytes 589832 | tf_op jit(solution)/shard_map/ppermute | solution.py:26
  22.5 4.7 %collective-permute-start.7 = (f32[4,48,256]{2,1,0:T(8,128)S(1)}, f32[4,48,256]{2,1,0:T(8,128)S(1)}, u32[]{:S(2)}, u32[]{:S(2)}) collective-permute-start(f32[4,48,256]{2,1,0:T(8,128)S(1)} %collective-permute-done.6.refs_1_.refs_4_), channel_id=1, source_target_pairs={{0,1},{1,0},{2,3},{3,2},{4,5},{5,4},{6,7},{7,6},{8,9},{9,8},{10,11... | collective-permute-start | bytes 589832 | tf_op jit(solution)/shard_map/ppermute | solution.py:26
  27.2 2.0 %collective-permute-start.9 = (f32[4,48,256]{2,1,0:T(8,128)S(1)}, f32[4,48,256]{2,1,0:T(8,128)S(1)}, u32[]{:S(2)}, u32[]{:S(2)}) collective-permute-start(f32[4,48,256]{2,1,0:T(8,128)S(1)} %collective-permute-done.8.refs_1_.refs_6_), channel_id=1, source_target_pairs={{0,1},{1,0},{2,3},{3,2},{4,5},{5,4},{6,7},{7,6},{8,9},{9,8},{10,11... | collective-permute-start | bytes 589832 | tf_op jit(solution)/shard_map/ppermute | solution.py:26
  30.3 7.3 %collective-permute-start.15 = (f32[4,32,256]{2,1,0:T(8,128)S(1)}, f32[4,32,256]{2,1,0:T(8,128)S(1)}, u32[]{:S(2)}, u32[]{:S(2)}) collective-permute-start(f32[4,32,256]{2,1,0:T(8,128)S(1)} %get-tuple-element.57.refs_8_), channel_id=1, source_target_pairs={{0,6},{1,7},{2,4},{3,5},{4,2},{5,3},{6,0},{7,1},{8,14},{9,15},{10,... | collective-permute-start | bytes 393224 | tf_op jit(solution)/shard_map/ppermute | solution.py:26
  32.8 7.3 %collective-permute-start.13 = (f32[4,32,256]{2,1,0:T(8,128)S(1)}, f32[4,32,256]{2,1,0:T(8,128)S(1)}, u32[]{:S(2)}, u32[]{:S(2)}) collective-permute-start(f32[4,32,256]{2,1,0:T(8,128)S(1)} %get-tuple-element.57.refs_8_), channel_id=1, source_target_pairs={{0,2},{1,3},{2,0},{3,1},{4,6},{5,7},{6,4},{7,5},{8,10},{9,11},{10,... | collective-permute-start | bytes 393224 | tf_op jit(solution)/shard_map/ppermute | solution.py:26
  33.4 6.7 %collective-permute-start.11 = (f32[4,32,256]{2,1,0:T(8,128)S(1)}, f32[4,32,256]{2,1,0:T(8,128)S(1)}, u32[]{:S(2)}, u32[]{:S(2)}) collective-permute-start(f32[4,32,256]{2,1,0:T(8,128)S(1)} %get-tuple-element.57.refs_8_), channel_id=1, source_target_pairs={{0,4},{1,5},{2,6},{3,7},{4,0},{5,1},{6,2},{7,3},{8,12},{9,13},{10,... | collective-permute-start | bytes 393224 | tf_op jit(solution)/shard_map/ppermute | solution.py:26
  33.9 6.7 %collective-permute-start.10 = (f32[4,32,256]{2,1,0:T(8,128)S(1)}, f32[4,32,256]{2,1,0:T(8,128)S(1)}, u32[]{:S(2)}, u32[]{:S(2)}) collective-permute-start(f32[4,32,256]{2,1,0:T(8,128)S(1)} %get-tuple-element.57.refs_8_), channel_id=1, source_target_pairs={{0,1},{1,0},{2,3},{3,2},{4,5},{5,4},{6,7},{7,6},{8,9},{9,8},{10,11... | collective-permute-start | bytes 393224 | tf_op jit(solution)/shard_map/ppermute | solution.py:26
  37.6 3.0 %collective-permute-start.16 = (f32[4,32,256]{2,1,0:T(8,128)S(1)}, f32[4,32,256]{2,1,0:T(8,128)S(1)}, u32[]{:S(2)}, u32[]{:S(2)}) collective-permute-start(f32[4,32,256]{2,1,0:T(8,128)S(1)} %collective-permute-done.15.refs_14_), channel_id=1, source_target_pairs={{0,1},{1,0},{2,3},{3,2},{4,5},{5,4},{6,7},{7,6},{8,9},{9,8},{10,11... | collective-permute-start | bytes 393224 | tf_op jit(solution)/shard_map/ppermute | solution.py:26
  40.1 1.3 %collective-permute-start.14 = (f32[4,32,256]{2,1,0:T(8,128)S(1)}, f32[4,32,256]{2,1,0:T(8,128)S(1)}, u32[]{:S(2)}, u32[]{:S(2)}) collective-permute-start(f32[4,32,256]{2,1,0:T(8,128)S(1)} %collective-permute-done.13.refs_12_), channel_id=1, source_target_pairs={{0,1},{1,0},{2,3},{3,2},{4,5},{5,4},{6,7},{7,6},{8,9},{9,8},{10,11... | collective-permute-start | bytes 393224 | tf_op jit(solution)/shard_map/ppermute | solution.py:26
  40.1 1.5 %collective-permute-start.12 = (f32[4,32,256]{2,1,0:T(8,128)S(1)}, f32[4,32,256]{2,1,0:T(8,128)S(1)}, u32[]{:S(2)}, u32[]{:S(2)}) collective-permute-start(f32[4,32,256]{2,1,0:T(8,128)S(1)} %collective-permute-done.11.refs_10_), channel_id=1, source_target_pairs={{0,1},{1,0},{2,3},{3,2},{4,5},{5,4},{6,7},{7,6},{8,9},{9,8},{10,11... | collective-permute-start | bytes 393224 | tf_op jit(solution)/shard_map/ppermute | solution.py:26
  45.2 1.2 %collective-permute-start.17 = (f32[32,128]{1,0:T(8,128)S(1)}, f32[32,128]{1,0:T(8,128)S(1)}, u32[]{:S(2)}, u32[]{:S(2)}) collective-permute-start(f32[32,128]{1,0:T(8,128)S(1)} %get-tuple-element.66), channel_id=1, source_target_pairs={{0,1},{1,0},{2,3},{3,2},{4,5},{5,4},{6,7},{7,6},{8,9},{9,8},{10,11... | collective-permute-start | bytes 49160 | tf_op jit(solution)/shard_map/ppermute | solution.py:26
  46.4 4.6 %collective-permute-start.20 = (f32[32,128]{1,0:T(8,128)S(1)}, f32[32,128]{1,0:T(8,128)S(1)}, u32[]{:S(2)}, u32[]{:S(2)}) collective-permute-start(f32[32,128]{1,0:T(8,128)S(1)} %add.12), channel_id=1, source_target_pairs={{0,6},{1,7},{2,4},{3,5},{4,2},{5,3},{6,0},{7,1},{8,14},{9,15},{10,... | collective-permute-start | bytes 49160 | tf_op jit(solution)/shard_map/ppermute | solution.py:26
  48.5 3.7 %collective-permute-start.19 = (f32[32,128]{1,0:T(8,128)S(1)}, f32[32,128]{1,0:T(8,128)S(1)}, u32[]{:S(2)}, u32[]{:S(2)}) collective-permute-start(f32[32,128]{1,0:T(8,128)S(1)} %add.12), channel_id=1, source_target_pairs={{0,4},{1,5},{2,6},{3,7},{4,0},{5,1},{6,2},{7,3},{8,12},{9,13},{10,... | collective-permute-start | bytes 49160 | tf_op jit(solution)/shard_map/ppermute | solution.py:26
  49.3 3.7 %collective-permute-start.18 = (f32[32,128]{1,0:T(8,128)S(1)}, f32[32,128]{1,0:T(8,128)S(1)}, u32[]{:S(2)}, u32[]{:S(2)}) collective-permute-start(f32[32,128]{1,0:T(8,128)S(1)} %add.12), channel_id=1, source_target_pairs={{0,2},{1,3},{2,0},{3,1},{4,6},{5,7},{6,4},{7,5},{8,10},{9,11},{10,... | collective-permute-start | bytes 49160 | tf_op jit(solution)/shard_map/ppermute | solution.py:26

commit v5 on v4

--- a/solution.py
+++ b/solution.py
@@ -26,46 +26,56 @@
     return lax.ppermute(array, AXES, [(i, i ^ bit) for i in range(count)])
 
 
+def two_parts(wide):
+    high = wide.astype(BF16)
+    return high, (wide - high.astype(F32)).astype(BF16)
+
+
 def three_parts(wide):
-    high = wide.astype(BF16)
-    rest = wide - high.astype(F32)
-    middle = rest.astype(BF16)
-    return high, middle, (rest - middle.astype(F32)).astype(BF16)
-
-
-def features(scaled, level, left):
-    high, middle, low = three_parts(scaled)
+    high, _ = two_parts(wide)
+    return high, *two_parts(wide - high.astype(F32))
+
+
+def features(parts, level, left):
+    feat = parts.shape[0] // 2
+    high, low = parts[:feat], parts[feat:]
+    scaled = high.astype(F32) + low.astype(F32)
     half = -0.5 * jnp.sum(scaled * scaled, axis=0, keepdims=True)
     if not left:
         half = half + level
     halves = [part.astype(F32) for part in three_parts(half)]
     ones = [jnp.ones_like(half)] * 3
     tail = (halves + ones if left else ones + halves) + [jnp.zeros((10, half.shape[1]), F32)]
-    parts = [high, high, middle, high, low, middle] if left else [high, middle, high, low, high, middle]
-    return jnp.concatenate(parts + [jnp.concatenate(tail, axis=0).astype(BF16)], axis=0)
+    rows = [high, high, low, low] if left else [high, low, high, low]
+    return jnp.concatenate(rows + [jnp.concatenate(tail, axis=0).astype(BF16)], axis=0)
 
 
 def feature_rows(feat):
-    return 6 * feat + 16
+    return 4 * feat + 16
 
 
 def prepare_kernel(points_ref, inv_ref, right_ref, count_ref, sent_ref):
     feat, slots = points_ref.shape
+    probes = right_ref.shape[0]
     valid = lax.broadcasted_iota(jnp.int32, (1, slots), 1) < count_ref[0]
     row = lax.broadcasted_iota(jnp.int32, (feat, slots), 0)
     inverse = jnp.zeros((feat, slots), F32)
     for f in range(feat):
         inverse = jnp.where(row == f, inv_ref[f], inverse)
     scaled = points_ref[...] * inverse * math.sqrt(LOG2E)
-    sent_ref[0, :feat, :] = jnp.where(valid, scaled, FAR)
-    sent_ref[0, feat:, :] = jnp.where(valid, right_ref[...], 0.0)
+    high, low = two_parts(jnp.where(valid, scaled, FAR))
+    direction, rest = two_parts(jnp.where(valid, right_ref[...], 0.0))
+    sent_ref[0, :feat, :] = high
+    sent_ref[0, feat : 2 * feat, :] = low
+    sent_ref[0, 2 * feat : 2 * feat + probes, :] = direction
+    sent_ref[0, 2 * feat + probes :, :] = rest
 
 
 def prepare(points, inv_lengths, right_sides, block_counts):
     smem = pl.BlockSpec(memory_space=pltpu.SMEM)
     return pl.pallas_call(
         prepare_kernel,
-        out_shape=pltpu.VMEM((1, points.shape[1] + right_sides.shape[1], points.shape[0]), F32),
+        out_shape=pltpu.VMEM((1, 2 * points.shape[1] + 2 * right_sides.shape[1], points.shape[0]), BF16),
         in_specs=[VMEM, smem, VMEM, smem],
         out_specs=VMEM,
     )(points.T, inv_lengths, right_sides.T, block_counts)
@@ -74,7 +84,7 @@
 def fill_right(near_ref, levels_ref, right_ref, feat):
     blocks, slots = right_ref.shape[1] // near_ref.shape[2], near_ref.shape[2]
     for b in range(blocks):
-        right_ref[:, b * slots : (b + 1) * slots] = features(near_ref[b, :feat, :], levels_ref[0:1, :], False)
+        right_ref[:, b * slots : (b + 1) * slots] = features(near_ref[b, : 2 * feat, :], levels_ref[0:1, :], False)
 
 
 def entries(left, right):
@@ -89,8 +99,11 @@
     else:
         right_ref, so_far_ref, refs = refs[0], refs[1], refs[2:]
     kept, refs = (refs[:count], refs[count:]) if keep else ((), refs)
+    own_ref = None
+    if last:
+        own_ref, refs = refs[1], refs[:1] + refs[2:]
     out_ref, left_ref, dirs_ref, sum_ref = refs
-    slots = near_ref.shape[2]
+    slots, probes = near_ref.shape[2], dirs_ref.shape[0]
     if begin:
         fill_right(near_ref, levels_ref, right_ref, feat)
         sum_ref[...] = jnp.zeros_like(sum_ref)
@@ -101,8 +114,8 @@
         def step(g, carry, piece=piece, far_ref=far_ref):
             for b in range(group):
                 place = slice(b * slots, (b + 1) * slots)
-                left_ref[:, place] = features(far_ref[g * group + b, :feat, :], None, True)
-                dirs_ref[:, place] = far_ref[g * group + b, feat:, :].astype(BF16)
+                left_ref[:, place] = features(far_ref[g * group + b, : 2 * feat, :], None, True)
+                dirs_ref[:, place] = far_ref[g * group + b, 2 * feat :, :]
             block = entries(left_ref[...], right_ref[...])
             if keep:
                 kept[piece][g] = block
@@ -113,15 +126,33 @@
     if not last:
         out_ref[...] = sum_ref[...]
         return
+    images, rests = [], []
+    norm = curve = jnp.zeros((probes, slots), F32)
     for b in range(near_ref.shape[0]):
-        direction = near_ref[b, feat:, :].astype(BF16).astype(F32)
-        out_ref[b] = sum_ref[:, b * slots : (b + 1) * slots] + levels_ref[1:2, :] * direction
+        direction = near_ref[b, 2 * feat : 2 * feat + probes, :].astype(F32)
+        rest = near_ref[b, 2 * feat + probes :, :].astype(F32)
+        image = sum_ref[:, b * slots : (b + 1) * slots] + levels_ref[1:2, :] * direction
+        norm = norm + (direction + rest) * (direction + rest)
+        curve = curve + direction * image
+        images.append(image)
+        rests.append(rest)
+    own_ref[...] = images[0]
+    norm, curve = (jnp.sum(each, axis=1, keepdims=True) for each in (norm, curve))
+    slope = jnp.where(norm > 0.0, curve / norm, 0.0)
+    for b, (image, rest) in enumerate(zip(images, rests)):
+        out_ref[0, b * probes : (b + 1) * probes, :] = image - slope * rest
+    lane = lax.broadcasted_iota(jnp.int32, (probes, 128), 1)
+    both = jnp.where(lane == 0, norm, jnp.where(lane == 1, curve, 0.0))
+    flat = jnp.concatenate([both, jnp.zeros((128 - probes, 128), F32)], axis=0).T
+    out_ref[0, len(images) * probes :, :] = jnp.concatenate([flat[:8], jnp.zeros((8, slots - 128), F32)], axis=1)
 
 
 def apply_first(near, far, levels, so_far, feat, group, keep, last=False):
-    copies, slots, probes = near.shape[0], near.shape[2], near.shape[1] - feat
+    copies, slots, probes = near.shape[0], near.shape[2], far[0].shape[1] - 2 * feat
     wide, steps, begin = group * slots, far[0].shape[0] // group, so_far is None
-    outs = [pltpu.VMEM((copies, probes, slots) if last else (probes, copies * slots), F32)]
+    outs = [pltpu.VMEM((1, copies * probes + 8, slots) if last else (probes, copies * slots), F32)]
+    if last:
+        outs = outs + [pltpu.VMEM((probes, slots), F32)]
     if keep:
         outs = [pltpu.VMEM((steps, wide, copies * slots), BF16)] * len(far) + outs
     if begin:
@@ -149,51 +180,52 @@
     kept, rest = (done[: len(far)], done[len(far) :]) if keep else ([None] * len(far), done)
     if begin:
         return kept, (rest[1], rest[0])
-    return kept, rest[0] if last else (so_far[0], rest[0])
-
-
-def second_kernel(feat, group, keep, copies, levels_ref, *refs):
+    return kept, rest if last else (so_far[0], rest[0])
+
+
+def second_kernel(feat, group, keep, copies, levels_ref, own_ref, own_image_in_ref, *refs):
     points, images, refs = refs[:PIECES], refs[PIECES : 2 * PIECES], refs[2 * PIECES :]
     if keep:
         kept, refs = refs[:PIECES], refs[PIECES:]
     (partial_ref, solution_ref, residual_ref, own_dir_ref, own_image_ref, norm_ref, product_ref, dirs_ref) = refs[:8]
     if not keep:
         right_ref, left_ref = refs[8:]
-    slots, probes = images[0].shape[2], images[0].shape[1]
+    slots, probes = images[0].shape[2], own_image_in_ref.shape[0]
     pairs = list(zip(points, images))
 
     def over_blocks(visit, start):
         carry = start
         for x_ref, w_ref in pairs:
-            carry = lax.fori_loop(0, x_ref.shape[0], functools.partial(visit, x_ref, w_ref), carry, unroll=True if x_ref.shape[0] <= 8 else 8)
+            blocks = x_ref.shape[0]
+            carry = lax.fori_loop(0, blocks, functools.partial(visit, x_ref, w_ref), carry, unroll=min(blocks, 8))
         return carry
 
-    def column(total):
-        return jnp.sum(total, axis=1, keepdims=True)
-
-    zero = jnp.zeros((probes, slots), F32)
-
-    def sums(x_ref, w_ref, b, carry):
-        norm, curve = carry
-        right = x_ref[b, feat:, :]
-        return norm + right * right, curve + right.astype(BF16).astype(F32) * w_ref[b]
-
-    norm, curve = over_blocks(sums, (zero, zero))
-    norm_now = column(norm)
-    step_size = norm_now / column(curve)
+    def column(wide):
+        return jnp.sum(wide, axis=1, keepdims=True)
+
+    def residual_of(x_ref, w_ref, b):
+        first = x_ref[b, 2 * feat :, :].astype(F32)
+        image = w_ref[b // copies, pl.ds(pl.multiple_of(b % copies * probes, probes), probes), :]
+        return first - step_size * image, first
+
+    sums = jnp.zeros((8, 128), F32)
+    for w_ref in images:
+        for g in range(w_ref.shape[0]):
+            sums = sums + w_ref[g, copies * probes :, :128]
+    sums = jnp.concatenate([sums, jnp.zeros((120, 128), F32)], axis=0).T[:probes]
+    norm_now = sums[:, 0:1]
+    step_size = norm_now / sums[:, 1:2]
 
     def next_sum(x_ref, w_ref, b, norm):
-        residual = x_ref[b, feat:, :] - step_size * w_ref[b]
+        residual, _ = residual_of(x_ref, w_ref, b)
         return norm + residual * residual
 
-    norm_next = column(over_blocks(next_sum, zero))
+    norm_next = column(over_blocks(next_sum, jnp.zeros((probes, slots), F32)))
     ratio = norm_next / norm_now
 
     def direct(x_ref, w_ref, b):
-        right = x_ref[b, feat:, :]
-        first = right.astype(BF16).astype(F32)
-        residual = right - step_size * w_ref[b]
-        return residual, first, (residual + ratio * first).astype(BF16)
+        residual, first = residual_of(x_ref, w_ref, b)
+        return (residual + ratio * first).astype(BF16)
 
     product_ref[...] = jnp.zeros_like(product_ref)
     if not keep:
@@ -203,48 +235,49 @@
         def step(g, carry, piece=piece, x_ref=x_ref, w_ref=w_ref):
             for b in range(group):
                 place = slice(b * slots, (b + 1) * slots)
-                dirs_ref[:, place] = direct(x_ref, w_ref, g * group + b)[2]
+                dirs_ref[:, place] = direct(x_ref, w_ref, g * group + b)
                 if not keep:
-                    left_ref[:, place] = features(x_ref[g * group + b, :feat, :], None, True)
+                    left_ref[:, place] = features(x_ref[g * group + b, : 2 * feat, :], None, True)
             block = kept[piece][g] if keep else entries(left_ref[...], right_ref[...])
             product_ref[...] += jnp.dot(dirs_ref[...], block, preferred_element_type=F32)
             return carry
 
         lax.fori_loop(0, x_ref.shape[0] // group, step, 0)
 
-    total = zero
+    curve = jnp.zeros((probes, slots), F32)
     for b in range(copies):
-        residual, first, direction = direct(points[0], images[0], b)
-        direction = direction.astype(F32)
-        image = product_ref[:, b * slots : (b + 1) * slots] + levels_ref[1:2, :] * direction
-        total = total + direction * image
-        if b == 0:
-            solution_ref[...] = step_size * first
-            residual_ref[...] = residual
-            own_dir_ref[...] = direction
-            own_image_ref[...] = image
-    partial_ref[...] = jnp.broadcast_to(column(total), partial_ref.shape)
+        direction = direct(points[0], images[0], b).astype(F32)
+        curve = curve + direction * (product_ref[:, b * slots : (b + 1) * slots] + levels_ref[1:2, :] * direction)
+    first = own_ref[0, 2 * feat : 2 * feat + probes, :].astype(F32)
+    right = first + own_ref[0, 2 * feat + probes :, :].astype(F32)
+    residual = right - step_size * own_image_in_ref[...]
+    direction = (residual + ratio * first).astype(BF16).astype(F32)
+    solution_ref[...] = step_size * first
+    residual_ref[...] = residual
+    own_dir_ref[...] = direction
+    own_image_ref[...] = product_ref[:, :slots] + levels_ref[1:2, :] * direction
+    partial_ref[...] = jnp.broadcast_to(column(curve), partial_ref.shape)
     norm_ref[...] = jnp.broadcast_to(norm_next, norm_ref.shape)
 
 
-def second(levels, points, images, kept, copies, feat, group):
+def second(levels, own, own_image, points, images, kept, copies, feat, group):
     keep = kept is not None
-    slots, probes = images[0].shape[2], images[0].shape[1]
-    own, small, wide = pltpu.VMEM((probes, slots), F32), pltpu.VMEM((probes, 128), F32), group * slots
+    slots, probes = own_image.shape[1], own_image.shape[0]
+    one, small, wide = pltpu.VMEM((probes, slots), F32), pltpu.VMEM((probes, 128), F32), group * slots
     scratch = [pltpu.VMEM((probes, copies * slots), F32), pltpu.VMEM((probes, wide), BF16)]
+    arrays = [levels, own, own_image, *points, *images, *(kept or ())]
     if keep:
-        levels = stay(levels)
-        points, images, kept = ([stay(piece) for piece in pieces] for pieces in (points, images, kept))
+        arrays = [stay(array) for array in arrays]
     else:
         scratch += [pltpu.VMEM((feature_rows(feat), copies * slots), BF16), pltpu.VMEM((feature_rows(feat), wide), BF16)]
     return pl.pallas_call(
         functools.partial(second_kernel, feat, group, keep, copies),
-        out_shape=[small, own, own, own, own, small],
-        in_specs=[VMEM] * (3 * PIECES + 1 if keep else 2 * PIECES + 1),
+        out_shape=[small, one, one, one, one, small],
+        in_specs=[VMEM] * len(arrays),
         out_specs=[VMEM] * 6,
         scratch_shapes=scratch,
         compiler_params=pltpu.CompilerParams(vmem_limit_bytes=(16 if keep else 48) * 2**20),
-    )(levels, *points, *images, *(kept or ()))
+    )(*arrays)
 
 
 def finish_kernel(curve_ref, norm_ref, solution_ref, residual_ref, direction_ref, image_ref, out_ref, left_ref):
@@ -289,6 +322,7 @@
     held = gather(own, bits[:-3], count)
     held, levels = lax.optimization_barrier((held, levels))
     near = held[:copies]
+    held = held[:, : 2 * feat + probes]
     beside, up, over = (swap(held, bit, count) for bit in (core, one, two))
     kept_0, product = first(near, [held, beside], levels, None)
     up, product = lax.optimization_barrier((up, product))
@@ -300,7 +334,7 @@
     corner, product = lax.optimization_barrier((corner, product))
     corner_beside = swap(corner, core, count)
     kept_3, product = first(near, [over_beside, corner], levels, product)
-    kept_4, image = first(near, [corner_beside], levels, product, last=True)
+    kept_4, (image, own_image) = first(near, [corner_beside], levels, product, last=True)
     pieces = [held, beside, up, up_beside, over, over_beside, corner, corner_beside]
     kept = [*kept_0, *kept_1, *kept_2, *kept_3, *kept_4]
 
@@ -308,8 +342,8 @@
     up, over, corner = (swap(held, bit, count) for bit in (one, two, one | two))
     beside, up_beside, over_beside, corner_beside = (swap(array, core, count) for array in (held, up, over, corner))
     images = [held, beside, up, up_beside, over, over_beside, corner, corner_beside]
-    partial, solution, residual, direction, own_image, norm = second(
-        levels, pieces, images, kept if keep else None, copies, feat, group
+    partial, solution, residual, direction, second_image, norm = second(
+        levels, own, own_image, pieces, images, kept if keep else None, copies, feat, group
     )
     partial = total(partial + swap(partial, core, count), later[:-1][::-1], count)
     done = jax.ShapeDtypeStruct((probes, slots), F32)
@@ -318,7 +352,7 @@
         out_shape=[done, done],
         in_specs=[VMEM] * 6,
         out_specs=[VMEM] * 2,
-    )(*[stay(array) for array in (partial, norm, solution, residual, direction, own_image)])
+    )(*[stay(array) for array in (partial, norm, solution, residual, direction, second_image)])
     return solution.T, residual.T
 
 

time: 54 us -> 51.9 us (0.961)
  waiting for transfers between devices: 19.3 us -> 16.8 us
    ppermute x21, waiting for transfers between devices: 19.3 us -> 16.8 us  [swap(): return lax.ppermute(array, AXES, [(i, i ^ bit) for i in range(count)])]
  transfers between devices with their start and end apart: 21 -> 21, of which waited for: 13 -> 13; matrix products, arithmetic and copies ran while one was open for 0% -> 0% of each run, Pallas kernels for 13% -> 14%
where the time goes in v5:
time: 51.9 us; the launch traced here: 51.6 us
  starting transfers between devices  18.5 us (36%)
  waiting for transfers between devices  16.8 us (32%)
  Pallas kernels  13.4 us (26%)
  between operations  2.68 us (5%)
    ppermute x21, starting transfers between devices, swap(): return lax.ppermute(array, AXES, [(i, i ^ bit) for i in range(count)])  18.5 us
    ppermute x21, waiting for transfers between devices, swap(): return lax.ppermute(array, AXES, [(i, i ^ bit) for i in range(count)])  16.8 us
    pallas_call x5, Pallas kernels, apply_first(): pl.pallas_call(functools.partial(apply_kernel, feat, group, keep, begin,...  8.25 us
    pallas_call x1, Pallas kernels, second(): pl.pallas_call(functools.partial(second_kernel, feat, group, keep, copies...  3.58 us
  transfers between devices with their start and end apart: 21, of which 13 were waited for; matrix products, arithmetic and copies ran while one was open for 0% of the time, Pallas kernels for 14%

profile of v5, /device:TPU:0, one launch (start us, length us, event | category | flops | bytes accessed | tf_op | source)
XLA Modules:
  0.0 51.6 jit_solution(136085173068089188)
XLA Ops:
  1.3 0.8 %shard_map.77.own_ref = bf16[1,96,256]{2,1,0:T(8,128)(2,1)S(1)} custom-call(f32[16,256]{1,0:T(8,128)} %bitcast.5, f32[16]{0:T(128)} %inv_ref.1, f32[32,256]{1,0:T(8,128)} %bitcast.4, s32[1]{0:T(128)S(6)} %copy.10.count_ref), custom_call_target="tpu_custom_call" | custom-call | tf_op jit(solution)/shard_map/pallas_call | solution.py:76
  2.1 5.1 %collective-permute-start.2 = (bf16[1,96,256]{2,1,0:T(8,128)(2,1)S(1)}, bf16[1,96,256]{2,1,0:T(8,128)(2,1)S(1)}, u32[]{:S(2)}, u32[]{:S(2)}) collective-permute-start(bf16[1,96,256]{2,1,0:T(8,128)(2,1)S(1)} %shard_map.77.own_ref), channel_id=1, source_target_pairs={{0,24},{1,25},{2,26},{3,27},{4,28},{5,29},{6,30},{7,31},{8,16},{9,... | collective-permute-start | bytes 147464 | tf_op jit(solution)/shard_map/ppermute | solution.py:26
  7.2 0.0 collective-permute-start.1
  7.2 0.6 %collective-permute-start = (bf16[1,96,256]{2,1,0:T(8,128)(2,1)S(1)}, bf16[1,96,256]{2,1,0:T(8,128)(2,1)S(1)}, u32[]{:S(2)}, u32[]{:S(2)}) collective-permute-start(bf16[1,96,256]{2,1,0:T(8,128)(2,1)S(1)} %shard_map.77.own_ref), channel_id=1, source_target_pairs={{0,16},{1,17},{2,18},{3,19},{4,20},{5,21},{6,22},{7,23},{8,24},{9,... | collective-permute-start | bytes 147464 | tf_op jit(solution)/shard_map/ppermute | solution.py:26
  9.2 0.1 pad_maximum_fusion.1
  9.3 0.2 collective-permute-done.2
  9.5 1.8 %collective-permute-done.1 = bf16[1,96,256]{2,1,0:T(8,128)(2,1)S(1)} collective-permute-done((bf16[1,96,256]{2,1,0:T(8,128)(2,1)S(1)}, bf16[1,96,256]{2,1,0:T(8,128)(2,1)S(1)}, u32[]{:S(2)}, u32[]{:S(2)}) %collective-permute-start.1) | collective-permute-done | bytes 49184 | tf_op jit(solution)/shard_map/ppermute | solution.py:26
  11.3 1.2 %collective-permute-done = bf16[1,96,256]{2,1,0:T(8,128)(2,1)S(1)} collective-permute-done((bf16[1,96,256]{2,1,0:T(8,128)(2,1)S(1)}, bf16[1,96,256]{2,1,0:T(8,128)(2,1)S(1)}, u32[]{:S(2)}, u32[]{:S(2)}) %collective-permute-start) | collective-permute-done | bytes 49184 | tf_op jit(solution)/shard_map/ppermute | solution.py:26
  12.5 0.1 broadcast_in_dim.2.levels_ref
  12.6 0.1 collective-permute-start.4
  12.7 1.6 %collective-permute-start.3 = (bf16[4,64,256]{2,1,0:T(8,128)(2,1)S(1)}, bf16[4,64,256]{2,1,0:T(8,128)(2,1)S(1)}, u32[]{:S(2)}, u32[]{:S(2)}) collective-permute-start(bf16[4,64,256]{2,1,0:T(8,128)(2,1)S(1)} %slice.3.refs_0_), channel_id=1, source_target_pairs={{0,4},{1,5},{2,6},{3,7},{4,0},{5,1},{6,2},{7,3},{8,12},{9,13},{10,... | collective-permute-start | bytes 393224 | tf_op jit(solution)/shard_map/ppermute | solution.py:26
  14.3 1.5 %collective-permute-start.6 = (bf16[4,64,256]{2,1,0:T(8,128)(2,1)S(1)}, bf16[4,64,256]{2,1,0:T(8,128)(2,1)S(1)}, u32[]{:S(2)}, u32[]{:S(2)}) collective-permute-start(bf16[4,64,256]{2,1,0:T(8,128)(2,1)S(1)} %slice.3.refs_0_), channel_id=1, source_target_pairs={{0,2},{1,3},{2,0},{3,1},{4,6},{5,7},{6,4},{7,5},{8,10},{9,11},{10,... | collective-permute-start | bytes 393224 | tf_op jit(solution)/shard_map/ppermute | solution.py:26
  15.8 2.0 %shard_map.78 = (bf16[1,1024,1024]{2,1,0:T(8,128)(2,1)S(1)}, bf16[1,1024,1024]{2,1,0:T(8,128)(2,1)S(1)}, f32[32,1024]{1,0:T(8,128)S(1)}, bf16[80,1024]{1,0:T(8,128)(2,1)S(1)}) custom-call(bf16[4,96,256]{2,1,0:T(8,128)(2,1)S(1)} %pad_maximum_fusion.near_ref, f32[2,256]{1,0:T(2,128)S(1)} %broadcast_in_dim.2.levels_ref, bf16[4,64,256]{2,1,0:T(8,128)(2,1)S(1)} %slice.3.refs_0_, ...), custom_call_target="tpu_custom_call" | custom-call | flops 1073741824 | bytes 262144 | tf_op jit(solution)/shard_map/pallas_call | solution.py:163
  17.8 0.9 %collective-permute-done.3.refs_0_.refs_2_ = bf16[4,64,256]{2,1,0:T(8,128)(2,1)S(1)} collective-permute-done((bf16[4,64,256]{2,1,0:T(8,128)(2,1)S(1)}, bf16[4,64,256]{2,1,0:T(8,128)(2,1)S(1)}, u32[]{:S(2)}, u32[]{:S(2)}) %collective-permute-start.3) | collective-permute-done | bytes 131104 | tf_op jit(solution)/shard_map/ppermute | solution.py:26
  18.6 0.0 collective-permute-start.7
  18.6 1.5 %collective-permute-start.5 = (bf16[4,64,256]{2,1,0:T(8,128)(2,1)S(1)}, bf16[4,64,256]{2,1,0:T(8,128)(2,1)S(1)}, u32[]{:S(2)}, u32[]{:S(2)}) collective-permute-start(bf16[4,64,256]{2,1,0:T(8,128)(2,1)S(1)} %collective-permute-done.3.refs_0_.refs_2_), channel_id=1, source_target_pairs={{0,2},{1,3},{2,0},{3,1},{4,6},{5,7},{6,4},{7,5},{8,10},{9,11},{10,... | collective-permute-start | bytes 393224 | tf_op jit(solution)/shard_map/ppermute | solution.py:26
  20.1 1.1 %shard_map.79 = (bf16[1,1024,1024]{2,1,0:T(8,128)(2,1)S(1)}, f32[32,1024]{1,0:T(8,128)S(1)}) custom-call(bf16[4,96,256]{2,1,0:T(8,128)(2,1)S(1)} %pad_maximum_fusion.near_ref, f32[2,256]{1,0:T(2,128)S(1)} %broadcast_in_dim.2.levels_ref, bf16[4,64,256]{2,1,0:T(8,128)(2,1)S(1)} %collective-permute-done.3.refs_0_.refs_2_, ...), custom_call_target="tpu_custom_call" | custom-call | flops 536870912 | bytes 262144 | tf_op jit(solution)/shard_map/pallas_call | solution.py:163
  21.2 0.0 collective-permute-done.6.refs_1_.refs_4_
  21.2 0.3 collective-permute-start.9
  21.5 0.0 collective-permute-done.7.refs_0_.refs_3_
  21.5 2.0 %shard_map.80 = (bf16[1,1024,1024]{2,1,0:T(8,128)(2,1)S(1)}, bf16[1,1024,1024]{2,1,0:T(8,128)(2,1)S(1)}, f32[32,1024]{1,0:T(8,128)S(1)}) custom-call(bf16[4,96,256]{2,1,0:T(8,128)(2,1)S(1)} %pad_maximum_fusion.near_ref, f32[2,256]{1,0:T(2,128)S(1)} %broadcast_in_dim.2.levels_ref, bf16[4,64,256]{2,1,0:T(8,128)(2,1)S(1)} %collective-permute-done.7.refs_0_.refs_3_, ...), custom_call_target="tpu_custom_call" | custom-call | flops 1073741824 | bytes 262144 | tf_op jit(solution)/shard_map/pallas_call | solution.py:163
  23.5 1.0 %collective-permute-done.5.refs_1_.refs_6_ = bf16[4,64,256]{2,1,0:T(8,128)(2,1)S(1)} collective-permute-done((bf16[4,64,256]{2,1,0:T(8,128)(2,1)S(1)}, bf16[4,64,256]{2,1,0:T(8,128)(2,1)S(1)}, u32[]{:S(2)}, u32[]{:S(2)}) %collective-permute-start.5) | collective-permute-done | bytes 131104 | tf_op jit(solution)/shard_map/ppermute | solution.py:26
  24.5 2.0 %shard_map.81 = (bf16[1,1024,1024]{2,1,0:T(8,128)(2,1)S(1)}, bf16[1,1024,1024]{2,1,0:T(8,128)(2,1)S(1)}, f32[32,1024]{1,0:T(8,128)S(1)}) custom-call(bf16[4,96,256]{2,1,0:T(8,128)(2,1)S(1)} %pad_maximum_fusion.near_ref, f32[2,256]{1,0:T(2,128)S(1)} %broadcast_in_dim.2.levels_ref, bf16[4,64,256]{2,1,0:T(8,128)(2,1)S(1)} %collective-permute-done.9.refs_0_.refs_5_, ...), custom_call_target="tpu_custom_call" | custom-call | flops 1073741824 | bytes 262144 | tf_op jit(solution)/shard_map/pallas_call | solution.py:163
  26.5 0.0 collective-permute-done.8.refs_0_.refs_7_
  26.5 1.2 %shard_map.82 = (bf16[1,1024,1024]{2,1,0:T(8,128)(2,1)S(1)}, f32[1,136,256]{2,1,0:T(8,128)S(1)}, f32[32,256]{1,0:T(8,128)S(1)}) custom-call(bf16[4,96,256]{2,1,0:T(8,128)(2,1)S(1)} %pad_maximum_fusion.near_ref, f32[2,256]{1,0:T(2,128)S(1)} %broadcast_in_dim.2.levels_ref, bf16[4,64,256]{2,1,0:T(8,128)(2,1)S(1)} %collective-permute-done.8.refs_0_.refs_7_, ...), custom_call_target="tpu_custom_call" | custom-call | flops 536870912 | bytes 262144 | tf_op jit(solution)/shard_map/pallas_call | solution.py:163
  27.8 2.5 %collective-permute-start.15 = (f32[1,136,256]{2,1,0:T(8,128)S(1)}, f32[1,136,256]{2,1,0:T(8,128)S(1)}, u32[]{:S(2)}, u32[]{:S(2)}) collective-permute-start(f32[1,136,256]{2,1,0:T(8,128)S(1)} %get-tuple-element.59.refs_8_), channel_id=1, source_target_pairs={{0,6},{1,7},{2,4},{3,5},{4,2},{5,3},{6,0},{7,1},{8,14},{9,15},{10,... | collective-permute-start | bytes 417800 | tf_op jit(solution)/shard_map/ppermute | solution.py:26
  30.2 0.5 %collective-permute-start.13 = (f32[1,136,256]{2,1,0:T(8,128)S(1)}, f32[1,136,256]{2,1,0:T(8,128)S(1)}, u32[]{:S(2)}, u32[]{:S(2)}) collective-permute-start(f32[1,136,256]{2,1,0:T(8,128)S(1)} %get-tuple-element.59.refs_8_), channel_id=1, source_target_pairs={{0,2},{1,3},{2,0},{3,1},{4,6},{5,7},{6,4},{7,5},{8,10},{9,11},{10,... | collective-permute-start | bytes 417800 | tf_op jit(solution)/shard_map/ppermute | solution.py:26
  30.8 0.5 collective-permute-start.11
  31.3 0.0 collective-permute-start.10
  31.3 3.9 %collective-permute-done.15.refs_14_ = f32[1,136,256]{2,1,0:T(8,128)S(1)} collective-permute-done((f32[1,136,256]{2,1,0:T(8,128)S(1)}, f32[1,136,256]{2,1,0:T(8,128)S(1)}, u32[]{:S(2)}, u32[]{:S(2)}) %collective-permute-start.15) | collective-permute-done | bytes 139296 | tf_op jit(solution)/shard_map/ppermute | solution.py:26
  35.1 0.0 collective-permute-start.16
  35.2 2.7 %collective-permute-done.13.refs_12_ = f32[1,136,256]{2,1,0:T(8,128)S(1)} collective-permute-done((f32[1,136,256]{2,1,0:T(8,128)S(1)}, f32[1,136,256]{2,1,0:T(8,128)S(1)}, u32[]{:S(2)}, u32[]{:S(2)}) %collective-permute-start.13) | collective-permute-done | bytes 139296 | tf_op jit(solution)/shard_map/ppermute | solution.py:26
  37.8 0.0 collective-permute-done.11.refs_10_
  37.8 0.5 collective-permute-start.12
  38.4 0.0 collective-permute-done.10.refs_9_
  38.4 0.0 collective-permute-done.16.refs_15_
  38.4 0.8 %collective-permute-done.14.refs_13_ = f32[1,136,256]{2,1,0:T(8,128)S(1)} collective-permute-done((f32[1,136,256]{2,1,0:T(8,128)S(1)}, f32[1,136,256]{2,1,0:T(8,128)S(1)}, u32[]{:S(2)}, u32[]{:S(2)}) %collective-permute-start.14) | collective-permute-done | bytes 139296 | tf_op jit(solution)/shard_map/ppermute | solution.py:26
  39.2 0.2 collective-permute-done.12.refs_11_
  39.4 3.6 %shard_map.83 = (f32[32,128]{1,0:T(8,128)S(1)}, f32[32,256]{1,0:T(8,128)S(1)}, f32[32,256]{1,0:T(8,128)S(1)}, f32[32,256]{1,0:T(8,128)S(1)}, f32[32,256]{1,0:T(8,128)S(1)}, /*index=5*/f32[32,128]{1,0:T(8,128)S(1)}) custom-call(f32[2,256]{1,0:T(2,128)S(1)} %broadcast_in_dim.2.levels_ref, bf16[1,96,256]{2,1,0:T(8,128)(2,1)S(1)} %shard_map.77.own_ref, ...), custom_call_target="tpu_custom_call" | custom-call | tf_op jit(solution)/shard_map/pallas_call | solution.py:273
  43.0 0.3 collective-permute-start.17
  43.3 0.9 %collective-permute-done.17 = f32[32,128]{1,0:T(8,128)S(1)} collective-permute-done((f32[32,128]{1,0:T(8,128)S(1)}, f32[32,128]{1,0:T(8,128)S(1)}, u32[]{:S(2)}, u32[]{:S(2)}) %collective-permute-start.17) | collective-permute-done | bytes 16416 | tf_op jit(solution)/shard_map/ppermute | solution.py:26
  44.2 2.2 %collective-permute-start.20 = (f32[32,128]{1,0:T(8,128)S(1)}, f32[32,128]{1,0:T(8,128)S(1)}, u32[]{:S(2)}, u32[]{:S(2)}) collective-permute-start(f32[32,128]{1,0:T(8,128)S(1)} %add.12), channel_id=1, source_target_pairs={{0,6},{1,7},{2,4},{3,5},{4,2},{5,3},{6,0},{7,1},{8,14},{9,15},{10,... | collective-permute-start | bytes 49160 | tf_op jit(solution)/shard_map/ppermute | solution.py:26
  46.3 0.8 %collective-permute-start.19 = (f32[32,128]{1,0:T(8,128)S(1)}, f32[32,128]{1,0:T(8,128)S(1)}, u32[]{:S(2)}, u32[]{:S(2)}) collective-permute-start(f32[32,128]{1,0:T(8,128)S(1)} %add.12), channel_id=1, source_target_pairs={{0,4},{1,5},{2,6},{3,7},{4,0},{5,1},{6,2},{7,3},{8,12},{9,13},{10,... | collective-permute-start | bytes 49160 | tf_op jit(solution)/shard_map/ppermute | solution.py:26
  47.1 0.5 %collective-permute-start.18 = (f32[32,128]{1,0:T(8,128)S(1)}, f32[32,128]{1,0:T(8,128)S(1)}, u32[]{:S(2)}, u32[]{:S(2)}) collective-permute-start(f32[32,128]{1,0:T(8,128)S(1)} %add.12), channel_id=1, source_target_pairs={{0,2},{1,3},{2,0},{3,1},{4,6},{5,7},{6,4},{7,5},{8,10},{9,11},{10,... | collective-permute-start | bytes 49160 | tf_op jit(solution)/shard_map/ppermute | solution.py:26
  47.7 1.1 %collective-permute-done.20 = f32[32,128]{1,0:T(8,128)S(1)} collective-permute-done((f32[32,128]{1,0:T(8,128)S(1)}, f32[32,128]{1,0:T(8,128)S(1)}, u32[]{:S(2)}, u32[]{:S(2)}) %collective-permute-start.20) | collective-permute-done | bytes 16416 | tf_op jit(solution)/shard_map/ppermute | solution.py:26
  48.8 1.3 %collective-permute-done.19 = f32[32,128]{1,0:T(8,128)S(1)} collective-permute-done((f32[32,128]{1,0:T(8,128)S(1)}, f32[32,128]{1,0:T(8,128)S(1)}, u32[]{:S(2)}, u32[]{:S(2)}) %collective-permute-start.19) | collective-permute-done | bytes 16416 | tf_op jit(solution)/shard_map/ppermute | solution.py:26
  50.1 0.8 %collective-permute-done.18 = f32[32,128]{1,0:T(8,128)S(1)} collective-permute-done((f32[32,128]{1,0:T(8,128)S(1)}, f32[32,128]{1,0:T(8,128)S(1)}, u32[]{:S(2)}, u32[]{:S(2)}) %collective-permute-start.18) | collective-permute-done | bytes 16416 | tf_op jit(solution)/shard_map/ppermute | solution.py:26
  50.9 0.7 %shard_map.84 = (f32[32,256]{1,0:T(8,128)}, f32[32,256]{1,0:T(8,128)}) custom-call(f32[32,128]{1,0:T(8,128)S(1)} %add_add_fusion.curve_ref, f32[32,128]{1,0:T(8,128)S(1)} %get-tuple-element.69.norm_ref, f32[32,256]{1,0:T(8,128)S(1)} %get-tuple-element.70.solution_ref, f32[32,256]{1,0:T(8,128)S(1)} %get-tuple-element.71.residual_ref, ...), custom_call_target="tpu_custom_call" | custom-call | tf_op jit(solution)/shard_map/pallas_call | solution.py:350
  (8 shorter events, 0.1 us)
Async XLA Ops:
  2.1 7.4 %collective-permute-start.2 = (bf16[1,96,256]{2,1,0:T(8,128)(2,1)S(1)}, bf16[1,96,256]{2,1,0:T(8,128)(2,1)S(1)}, u32[]{:S(2)}, u32[]{:S(2)}) collective-permute-start(bf16[1,96,256]{2,1,0:T(8,128)(2,1)S(1)} %shard_map.77.own_ref), channel_id=1, source_target_pairs={{0,24},{1,25},{2,26},{3,27},{4,28},{5,29},{6,30},{7,31},{8,16},{9,... | collective-permute-start | bytes 147464 | tf_op jit(solution)/shard_map/ppermute | solution.py:26
  7.2 4.1 %collective-permute-start.1 = (bf16[1,96,256]{2,1,0:T(8,128)(2,1)S(1)}, bf16[1,96,256]{2,1,0:T(8,128)(2,1)S(1)}, u32[]{:S(2)}, u32[]{:S(2)}) collective-permute-start(bf16[1,96,256]{2,1,0:T(8,128)(2,1)S(1)} %shard_map.77.own_ref), channel_id=1, source_target_pairs={{0,8},{1,9},{2,10},{3,11},{4,12},{5,13},{6,14},{7,15},{8,0},{9,1},... | collective-permute-start | bytes 147464 | tf_op jit(solution)/shard_map/ppermute | solution.py:26
  7.2 5.3 %collective-permute-start = (bf16[1,96,256]{2,1,0:T(8,128)(2,1)S(1)}, bf16[1,96,256]{2,1,0:T(8,128)(2,1)S(1)}, u32[]{:S(2)}, u32[]{:S(2)}) collective-permute-start(bf16[1,96,256]{2,1,0:T(8,128)(2,1)S(1)} %shard_map.77.own_ref), channel_id=1, source_target_pairs={{0,16},{1,17},{2,18},{3,19},{4,20},{5,21},{6,22},{7,23},{8,24},{9,... | collective-permute-start | bytes 147464 | tf_op jit(solution)/shard_map/ppermute | solution.py:26
  12.6 3.2 %collective-permute-start.4 = (bf16[4,64,256]{2,1,0:T(8,128)(2,1)S(1)}, bf16[4,64,256]{2,1,0:T(8,128)(2,1)S(1)}, u32[]{:S(2)}, u32[]{:S(2)}) collective-permute-start(bf16[4,64,256]{2,1,0:T(8,128)(2,1)S(1)} %slice.3.refs_0_), channel_id=1, source_target_pairs={{0,1},{1,0},{2,3},{3,2},{4,5},{5,4},{6,7},{7,6},{8,9},{9,8},{10,11... | collective-permute-start | bytes 393224 | tf_op jit(solution)/shard_map/ppermute | solution.py:26
  12.7 5.9 %collective-permute-start.3 = (bf16[4,64,256]{2,1,0:T(8,128)(2,1)S(1)}, bf16[4,64,256]{2,1,0:T(8,128)(2,1)S(1)}, u32[]{:S(2)}, u32[]{:S(2)}) collective-permute-start(bf16[4,64,256]{2,1,0:T(8,128)(2,1)S(1)} %slice.3.refs_0_), channel_id=1, source_target_pairs={{0,4},{1,5},{2,6},{3,7},{4,0},{5,1},{6,2},{7,3},{8,12},{9,13},{10,... | collective-permute-start | bytes 393224 | tf_op jit(solution)/shard_map/ppermute | solution.py:26
  14.3 6.9 %collective-permute-start.6 = (bf16[4,64,256]{2,1,0:T(8,128)(2,1)S(1)}, bf16[4,64,256]{2,1,0:T(8,128)(2,1)S(1)}, u32[]{:S(2)}, u32[]{:S(2)}) collective-permute-start(bf16[4,64,256]{2,1,0:T(8,128)(2,1)S(1)} %slice.3.refs_0_), channel_id=1, source_target_pairs={{0,2},{1,3},{2,0},{3,1},{4,6},{5,7},{6,4},{7,5},{8,10},{9,11},{10,... | collective-permute-start | bytes 393224 | tf_op jit(solution)/shard_map/ppermute | solution.py:26
  18.6 2.9 %collective-permute-start.7 = (bf16[4,64,256]{2,1,0:T(8,128)(2,1)S(1)}, bf16[4,64,256]{2,1,0:T(8,128)(2,1)S(1)}, u32[]{:S(2)}, u32[]{:S(2)}) collective-permute-start(bf16[4,64,256]{2,1,0:T(8,128)(2,1)S(1)} %collective-permute-done.3.refs_0_.refs_2_), channel_id=1, source_target_pairs={{0,1},{1,0},{2,3},{3,2},{4,5},{5,4},{6,7},{7,6},{8,9},{9,8},{10,11... | collective-permute-start | bytes 393224 | tf_op jit(solution)/shard_map/ppermute | solution.py:26
  18.6 5.9 %collective-permute-start.5 = (bf16[4,64,256]{2,1,0:T(8,128)(2,1)S(1)}, bf16[4,64,256]{2,1,0:T(8,128)(2,1)S(1)}, u32[]{:S(2)}, u32[]{:S(2)}) collective-permute-start(bf16[4,64,256]{2,1,0:T(8,128)(2,1)S(1)} %collective-permute-done.3.refs_0_.refs_2_), channel_id=1, source_target_pairs={{0,2},{1,3},{2,0},{3,1},{4,6},{5,7},{6,4},{7,5},{8,10},{9,11},{10,... | collective-permute-start | bytes 393224 | tf_op jit(solution)/shard_map/ppermute | solution.py:26
  21.2 3.3 %collective-permute-start.9 = (bf16[4,64,256]{2,1,0:T(8,128)(2,1)S(1)}, bf16[4,64,256]{2,1,0:T(8,128)(2,1)S(1)}, u32[]{:S(2)}, u32[]{:S(2)}) collective-permute-start(bf16[4,64,256]{2,1,0:T(8,128)(2,1)S(1)} %collective-permute-done.6.refs_1_.refs_4_), channel_id=1, source_target_pairs={{0,1},{1,0},{2,3},{3,2},{4,5},{5,4},{6,7},{7,6},{8,9},{9,8},{10,11... | collective-permute-start | bytes 393224 | tf_op jit(solution)/shard_map/ppermute | solution.py:26
  24.5 2.0 %collective-permute-start.8 = (bf16[4,64,256]{2,1,0:T(8,128)(2,1)S(1)}, bf16[4,64,256]{2,1,0:T(8,128)(2,1)S(1)}, u32[]{:S(2)}, u32[]{:S(2)}) collective-permute-start(bf16[4,64,256]{2,1,0:T(8,128)(2,1)S(1)} %collective-permute-done.5.refs_1_.refs_6_), channel_id=1, source_target_pairs={{0,1},{1,0},{2,3},{3,2},{4,5},{5,4},{6,7},{7,6},{8,9},{9,8},{10,11... | collective-permute-start | bytes 393224 | tf_op jit(solution)/shard_map/ppermute | solution.py:26
  27.8 7.4 %collective-permute-start.15 = (f32[1,136,256]{2,1,0:T(8,128)S(1)}, f32[1,136,256]{2,1,0:T(8,128)S(1)}, u32[]{:S(2)}, u32[]{:S(2)}) collective-permute-start(f32[1,136,256]{2,1,0:T(8,128)S(1)} %get-tuple-element.59.refs_8_), channel_id=1, source_target_pairs={{0,6},{1,7},{2,4},{3,5},{4,2},{5,3},{6,0},{7,1},{8,14},{9,15},{10,... | collective-permute-start | bytes 417800 | tf_op jit(solution)/shard_map/ppermute | solution.py:26
  30.2 7.6 %collective-permute-start.13 = (f32[1,136,256]{2,1,0:T(8,128)S(1)}, f32[1,136,256]{2,1,0:T(8,128)S(1)}, u32[]{:S(2)}, u32[]{:S(2)}) collective-permute-start(f32[1,136,256]{2,1,0:T(8,128)S(1)} %get-tuple-element.59.refs_8_), channel_id=1, source_target_pairs={{0,2},{1,3},{2,0},{3,1},{4,6},{5,7},{6,4},{7,5},{8,10},{9,11},{10,... | collective-permute-start | bytes 417800 | tf_op jit(solution)/shard_map/ppermute | solution.py:26
  30.8 7.1 %collective-permute-start.11 = (f32[1,136,256]{2,1,0:T(8,128)S(1)}, f32[1,136,256]{2,1,0:T(8,128)S(1)}, u32[]{:S(2)}, u32[]{:S(2)}) collective-permute-start(f32[1,136,256]{2,1,0:T(8,128)S(1)} %get-tuple-element.59.refs_8_), channel_id=1, source_target_pairs={{0,4},{1,5},{2,6},{3,7},{4,0},{5,1},{6,2},{7,3},{8,12},{9,13},{10,... | collective-permute-start | bytes 417800 | tf_op jit(solution)/shard_map/ppermute | solution.py:26
  31.3 7.1 %collective-permute-start.10 = (f32[1,136,256]{2,1,0:T(8,128)S(1)}, f32[1,136,256]{2,1,0:T(8,128)S(1)}, u32[]{:S(2)}, u32[]{:S(2)}) collective-permute-start(f32[1,136,256]{2,1,0:T(8,128)S(1)} %get-tuple-element.59.refs_8_), channel_id=1, source_target_pairs={{0,1},{1,0},{2,3},{3,2},{4,5},{5,4},{6,7},{7,6},{8,9},{9,8},{10,11... | collective-permute-start | bytes 417800 | tf_op jit(solution)/shard_map/ppermute | solution.py:26
  35.1 3.2 %collective-permute-start.16 = (f32[1,136,256]{2,1,0:T(8,128)S(1)}, f32[1,136,256]{2,1,0:T(8,128)S(1)}, u32[]{:S(2)}, u32[]{:S(2)}) collective-permute-start(f32[1,136,256]{2,1,0:T(8,128)S(1)} %collective-permute-done.15.refs_14_), channel_id=1, source_target_pairs={{0,1},{1,0},{2,3},{3,2},{4,5},{5,4},{6,7},{7,6},{8,9},{9,8},{10,11... | collective-permute-start | bytes 417800 | tf_op jit(solution)/shard_map/ppermute | solution.py:26
  37.8 1.4 %collective-permute-start.14 = (f32[1,136,256]{2,1,0:T(8,128)S(1)}, f32[1,136,256]{2,1,0:T(8,128)S(1)}, u32[]{:S(2)}, u32[]{:S(2)}) collective-permute-start(f32[1,136,256]{2,1,0:T(8,128)S(1)} %collective-permute-done.13.refs_12_), channel_id=1, source_target_pairs={{0,1},{1,0},{2,3},{3,2},{4,5},{5,4},{6,7},{7,6},{8,9},{9,8},{10,11... | collective-permute-start | bytes 417800 | tf_op jit(solution)/shard_map/ppermute | solution.py:26
  37.8 1.6 %collective-permute-start.12 = (f32[1,136,256]{2,1,0:T(8,128)S(1)}, f32[1,136,256]{2,1,0:T(8,128)S(1)}, u32[]{:S(2)}, u32[]{:S(2)}) collective-permute-start(f32[1,136,256]{2,1,0:T(8,128)S(1)} %collective-permute-done.11.refs_10_), channel_id=1, source_target_pairs={{0,1},{1,0},{2,3},{3,2},{4,5},{5,4},{6,7},{7,6},{8,9},{9,8},{10,11... | collective-permute-start | bytes 417800 | tf_op jit(solution)/shard_map/ppermute | solution.py:26
  43.0 1.2 %collective-permute-start.17 = (f32[32,128]{1,0:T(8,128)S(1)}, f32[32,128]{1,0:T(8,128)S(1)}, u32[]{:S(2)}, u32[]{:S(2)}) collective-permute-start(f32[32,128]{1,0:T(8,128)S(1)} %get-tuple-element.68), channel_id=1, source_target_pairs={{0,1},{1,0},{2,3},{3,2},{4,5},{5,4},{6,7},{7,6},{8,9},{9,8},{10,11... | collective-permute-start | bytes 49160 | tf_op jit(solution)/shard_map/ppermute | solution.py:26
  44.2 4.6 %collective-permute-start.20 = (f32[32,128]{1,0:T(8,128)S(1)}, f32[32,128]{1,0:T(8,128)S(1)}, u32[]{:S(2)}, u32[]{:S(2)}) collective-permute-start(f32[32,128]{1,0:T(8,128)S(1)} %add.12), channel_id=1, source_target_pairs={{0,6},{1,7},{2,4},{3,5},{4,2},{5,3},{6,0},{7,1},{8,14},{9,15},{10,... | collective-permute-start | bytes 49160 | tf_op jit(solution)/shard_map/ppermute | solution.py:26
  46.3 3.7 %collective-permute-start.19 = (f32[32,128]{1,0:T(8,128)S(1)}, f32[32,128]{1,0:T(8,128)S(1)}, u32[]{:S(2)}, u32[]{:S(2)}) collective-permute-start(f32[32,128]{1,0:T(8,128)S(1)} %add.12), channel_id=1, source_target_pairs={{0,4},{1,5},{2,6},{3,7},{4,0},{5,1},{6,2},{7,3},{8,12},{9,13},{10,... | collective-permute-start | bytes 49160 | tf_op jit(solution)/shard_map/ppermute | solution.py:26
  47.1 3.7 %collective-permute-start.18 = (f32[32,128]{1,0:T(8,128)S(1)}, f32[32,128]{1,0:T(8,128)S(1)}, u32[]{:S(2)}, u32[]{:S(2)}) collective-permute-start(f32[32,128]{1,0:T(8,128)S(1)} %add.12), channel_id=1, source_target_pairs={{0,2},{1,3},{2,0},{3,1},{4,6},{5,7},{6,4},{7,5},{8,10},{9,11},{10,... | collective-permute-start | bytes 49160 | tf_op jit(solution)/shard_map/ppermute | solution.py:26

commit v6 on v5

--- a/solution.py
+++ b/solution.py
@@ -14,6 +14,7 @@
 KEEP_BYTES = 20 * 2**20
 COPIES = 4
 PIECES = 8
+TAIL = 16
 F32, BF16 = jnp.float32, jnp.bfloat16
 VMEM = pl.BlockSpec(memory_space=pltpu.VMEM)
 
@@ -126,32 +127,40 @@
     if not last:
         out_ref[...] = sum_ref[...]
         return
-    images, rests = [], []
+    images, rights = [], []
     norm = curve = jnp.zeros((probes, slots), F32)
     for b in range(near_ref.shape[0]):
         direction = near_ref[b, 2 * feat : 2 * feat + probes, :].astype(F32)
-        rest = near_ref[b, 2 * feat + probes :, :].astype(F32)
+        right = direction + near_ref[b, 2 * feat + probes :, :].astype(F32)
         image = sum_ref[:, b * slots : (b + 1) * slots] + levels_ref[1:2, :] * direction
-        norm = norm + (direction + rest) * (direction + rest)
+        norm = norm + right * right
         curve = curve + direction * image
         images.append(image)
-        rests.append(rest)
+        rights.append(right)
     own_ref[...] = images[0]
     norm, curve = (jnp.sum(each, axis=1, keepdims=True) for each in (norm, curve))
-    slope = jnp.where(norm > 0.0, curve / norm, 0.0)
-    for b, (image, rest) in enumerate(zip(images, rests)):
-        out_ref[0, b * probes : (b + 1) * probes, :] = image - slope * rest
+    usual = 1.0 / (jnp.exp2(levels_ref[0:1, :1]) + levels_ref[1:2, :1])
+    likely = (norm > 0.0) & (curve > 1e-6 * norm)
+    guess = jnp.where(likely, norm / jnp.where(likely, curve, 1.0), usual)
+    guess = jnp.clip(guess, 1e-6, 1e3).astype(BF16)
+    for b, (image, right) in enumerate(zip(images, rights)):
+        out_ref[0, b * probes : (b + 1) * probes, :] = (right - guess.astype(F32) * image).astype(BF16)
+    parts = [part.astype(F32) for part in (*three_parts(norm), *three_parts(curve), guess)]
     lane = lax.broadcasted_iota(jnp.int32, (probes, 128), 1)
-    both = jnp.where(lane == 0, norm, jnp.where(lane == 1, curve, 0.0))
-    flat = jnp.concatenate([both, jnp.zeros((128 - probes, 128), F32)], axis=0).T
-    out_ref[0, len(images) * probes :, :] = jnp.concatenate([flat[:8], jnp.zeros((8, slots - 128), F32)], axis=1)
+    flat = jnp.zeros((probes, 128), F32)
+    for at, part in enumerate(parts):
+        flat = jnp.where(lane == at, part, flat)
+    flat = jnp.concatenate([flat, jnp.zeros((128 - probes, 128), F32)], axis=0).T[:TAIL]
+    flat = jnp.concatenate([flat, jnp.zeros((TAIL, slots - 128), F32)], axis=1)
+    out_ref[0, len(images) * probes :, :] = flat.astype(BF16)
 
 
 def apply_first(near, far, levels, so_far, feat, group, keep, last=False):
     copies, slots, probes = near.shape[0], near.shape[2], far[0].shape[1] - 2 * feat
     wide, steps, begin = group * slots, far[0].shape[0] // group, so_far is None
-    outs = [pltpu.VMEM((1, copies * probes + 8, slots) if last else (probes, copies * slots), F32)]
+    outs = [pltpu.VMEM((probes, copies * slots), F32)]
     if last:
+        outs = [pltpu.VMEM((1, copies * probes + TAIL, slots), BF16)]
         outs = outs + [pltpu.VMEM((probes, slots), F32)]
     if keep:
         outs = [pltpu.VMEM((steps, wide, copies * slots), BF16)] * len(far) + outs
@@ -187,55 +196,77 @@
     points, images, refs = refs[:PIECES], refs[PIECES : 2 * PIECES], refs[2 * PIECES :]
     if keep:
         kept, refs = refs[:PIECES], refs[PIECES:]
-    (partial_ref, solution_ref, residual_ref, own_dir_ref, own_image_ref, norm_ref, product_ref, dirs_ref) = refs[:8]
+    (partial_ref, solution_ref, residual_ref, own_dir_ref, own_image_ref, norm_ref, product_ref, dirs_ref, scale_ref) = refs[:9]
     if not keep:
-        right_ref, left_ref = refs[8:]
+        right_ref, left_ref = refs[9:]
     slots, probes = images[0].shape[2], own_image_in_ref.shape[0]
     pairs = list(zip(points, images))
+    groups = images[0].shape[0]
 
     def over_blocks(visit, start):
         carry = start
-        for x_ref, w_ref in pairs:
+        for piece, (x_ref, _) in enumerate(pairs):
             blocks = x_ref.shape[0]
-            carry = lax.fori_loop(0, blocks, functools.partial(visit, x_ref, w_ref), carry, unroll=min(blocks, 8))
+            carry = lax.fori_loop(0, blocks, functools.partial(visit, piece), carry, unroll=min(blocks, 8))
         return carry
 
     def column(wide):
         return jnp.sum(wide, axis=1, keepdims=True)
 
-    def residual_of(x_ref, w_ref, b):
-        first = x_ref[b, 2 * feat :, :].astype(F32)
-        image = w_ref[b // copies, pl.ds(pl.multiple_of(b % copies * probes, probes), probes), :]
-        return first - step_size * image, first
-
-    sums = jnp.zeros((8, 128), F32)
-    for w_ref in images:
-        for g in range(w_ref.shape[0]):
-            sums = sums + w_ref[g, copies * probes :, :128]
-    sums = jnp.concatenate([sums, jnp.zeros((120, 128), F32)], axis=0).T[:probes]
-    norm_now = sums[:, 0:1]
-    step_size = norm_now / sums[:, 1:2]
-
-    def next_sum(x_ref, w_ref, b, norm):
-        residual, _ = residual_of(x_ref, w_ref, b)
+    per = 128 // TAIL
+    tails = [(piece, g) for piece in range(PIECES) for g in range(groups)]
+    norm_now = curve = jnp.zeros((probes, 1), F32)
+    for start in range(0, len(tails), per):
+        flat = [images[piece][g, copies * probes :, :128].astype(F32) for piece, g in tails[start : start + per]]
+        flat = jnp.concatenate(flat + [jnp.zeros((TAIL, 128), F32)] * (per - len(flat)), axis=0).T[:probes]
+        for at in range(min(per, len(tails) - start)):
+            norm_now = norm_now + column(flat[:, TAIL * at : TAIL * at + 3])
+            curve = curve + column(flat[:, TAIL * at + 3 : TAIL * at + 6])
+            scale_ref[start + at] = jnp.broadcast_to(flat[:, TAIL * at + 6 : TAIL * at + 7], (probes, 128))
+    step_size = norm_now / curve
+    for start in range(len(tails)):
+        scale_ref[start] = step_size / scale_ref[start]
+
+    def residual_of(piece, b):
+        first = points[piece][b, 2 * feat :, :].astype(F32)
+        sent = images[piece][b // copies, pl.ds(pl.multiple_of(b % copies * probes, probes), probes), :].astype(F32)
+        return first + scale_ref[piece * groups + b // copies][:, :1] * (sent - first), first
+
+    def next_sum(piece, b, norm):
+        residual, _ = residual_of(piece, b)
         return norm + residual * residual
 
     norm_next = column(over_blocks(next_sum, jnp.zeros((probes, slots), F32)))
     ratio = norm_next / norm_now
 
-    def direct(x_ref, w_ref, b):
-        residual, first = residual_of(x_ref, w_ref, b)
+    def direct(piece, b):
+        residual, first = residual_of(piece, b)
         return (residual + ratio * first).astype(BF16)
 
+    first = own_ref[0, 2 * feat : 2 * feat + probes, :].astype(F32)
+    right = first + own_ref[0, 2 * feat + probes :, :].astype(F32)
+    residual = right - step_size * own_image_in_ref[...]
+    own_direction = (residual + ratio * first).astype(BF16)
+    solution_ref[...] = step_size * first
+    residual_ref[...] = residual
+    own_dir_ref[...] = own_direction.astype(F32)
     product_ref[...] = jnp.zeros_like(product_ref)
     if not keep:
         fill_right(points[0], levels_ref, right_ref, feat)
-    for piece, (x_ref, w_ref) in enumerate(pairs):
-
-        def step(g, carry, piece=piece, x_ref=x_ref, w_ref=w_ref):
+    for piece, (x_ref, _) in enumerate(pairs):
+
+        def step(g, carry, piece=piece, x_ref=x_ref):
             for b in range(group):
                 place = slice(b * slots, (b + 1) * slots)
-                dirs_ref[:, place] = direct(x_ref, w_ref, g * group + b)
+                dirs_ref[:, place] = direct(piece, g * group + b)
+            if piece == 0:
+
+                @pl.when(g == 0)
+                def own_block():
+                    dirs_ref[:, :slots] = own_direction
+
+            for b in range(group):
+                place = slice(b * slots, (b + 1) * slots)
                 if not keep:
                     left_ref[:, place] = features(x_ref[g * group + b, : 2 * feat, :], None, True)
             block = kept[piece][g] if keep else entries(left_ref[...], right_ref[...])
@@ -246,17 +277,14 @@
 
     curve = jnp.zeros((probes, slots), F32)
     for b in range(copies):
-        direction = direct(points[0], images[0], b).astype(F32)
-        curve = curve + direction * (product_ref[:, b * slots : (b + 1) * slots] + levels_ref[1:2, :] * direction)
-    first = own_ref[0, 2 * feat : 2 * feat + probes, :].astype(F32)
-    right = first + own_ref[0, 2 * feat + probes :, :].astype(F32)
-    residual = right - step_size * own_image_in_ref[...]
-    direction = (residual + ratio * first).astype(BF16).astype(F32)
-    solution_ref[...] = step_size * first
-    residual_ref[...] = residual
-    own_dir_ref[...] = direction
-    own_image_ref[...] = product_ref[:, :slots] + levels_ref[1:2, :] * direction
-    partial_ref[...] = jnp.broadcast_to(column(curve), partial_ref.shape)
+        direction = (direct(0, b) if b else own_direction).astype(F32)
+        image = product_ref[:, b * slots : (b + 1) * slots] + levels_ref[1:2, :] * direction
+        curve = curve + direction * image
+        if b == 0:
+            own_image_ref[...] = image
+    lane = lax.broadcasted_iota(jnp.int32, (probes, 128), 1)
+    flat = jnp.where(lane == 0, column(curve), 0.0)
+    partial_ref[...] = jnp.concatenate([flat, jnp.zeros((128 - probes, 128), F32)], axis=0).T[:8]
     norm_ref[...] = jnp.broadcast_to(norm_next, norm_ref.shape)
 
 
@@ -264,7 +292,11 @@
     keep = kept is not None
     slots, probes = own_image.shape[1], own_image.shape[0]
     one, small, wide = pltpu.VMEM((probes, slots), F32), pltpu.VMEM((probes, 128), F32), group * slots
-    scratch = [pltpu.VMEM((probes, copies * slots), F32), pltpu.VMEM((probes, wide), BF16)]
+    scratch = [
+        pltpu.VMEM((probes, copies * slots), F32),
+        pltpu.VMEM((probes, wide), BF16),
+        pltpu.VMEM((PIECES * images[0].shape[0], probes, 128), F32),
+    ]
     arrays = [levels, own, own_image, *points, *images, *(kept or ())]
     if keep:
         arrays = [stay(array) for array in arrays]
@@ -272,7 +304,7 @@
         scratch += [pltpu.VMEM((feature_rows(feat), copies * slots), BF16), pltpu.VMEM((feature_rows(feat), wide), BF16)]
     return pl.pallas_call(
         functools.partial(second_kernel, feat, group, keep, copies),
-        out_shape=[small, one, one, one, one, small],
+        out_shape=[pltpu.VMEM((8, 128), F32), one, one, one, one, small],
         in_specs=[VMEM] * len(arrays),
         out_specs=[VMEM] * 6,
         scratch_shapes=scratch,
@@ -281,7 +313,9 @@
 
 
 def finish_kernel(curve_ref, norm_ref, solution_ref, residual_ref, direction_ref, image_ref, out_ref, left_ref):
-    step_size = norm_ref[:, :1] / curve_ref[:, :1]
+    probes = norm_ref.shape[0]
+    curve = jnp.concatenate([curve_ref[...], jnp.zeros((120, 128), F32)], axis=0).T[:probes, :1]
+    step_size = norm_ref[:, :1] / curve
     out_ref[...] = solution_ref[...] + step_size * direction_ref[...]
     left_ref[...] = residual_ref[...] - step_size * image_ref[...]
 

time: 51.9 us -> 49.1 us (0.946)
  waiting for transfers between devices: 16.8 us -> 13.8 us
    ppermute x21, waiting for transfers between devices: 16.8 us -> 13.8 us  [swap(): return lax.ppermute(array, AXES, [(i, i ^ bit) for i in range(count)])]
  transfers between devices with their start and end apart: 21 -> 21, of which waited for: 13 -> 14; matrix products, arithmetic and copies ran while one was open for 0% -> 0% of each run, Pallas kernels for 14% -> 14%
where the time goes in v6:
time: 49.1 us; the launch traced here: 48.8 us
  starting transfers between devices  18.4 us (37%)
  waiting for transfers between devices  13.8 us (28%)
  Pallas kernels  13.7 us (28%)
  between operations  2.68 us (5%)
    ppermute x21, starting transfers between devices, swap(): return lax.ppermute(array, AXES, [(i, i ^ bit) for i in range(count)])  18.4 us
    ppermute x21, waiting for transfers between devices, swap(): return lax.ppermute(array, AXES, [(i, i ^ bit) for i in range(count)])  13.8 us
    pallas_call x5, Pallas kernels, apply_first(): pl.pallas_call(functools.partial(apply_kernel, feat, group, keep, begin,...  8.36 us
    pallas_call x1, Pallas kernels, second(): pl.pallas_call(functools.partial(second_kernel, feat, group, keep, copies...  3.77 us
  transfers between devices with their start and end apart: 21, of which 14 were waited for; matrix products, arithmetic and copies ran while one was open for 0% of the time, Pallas kernels for 14%

profile of v6, /device:TPU:0, one launch (start us, length us, event | category | flops | bytes accessed | tf_op | source)
XLA Modules:
  0.0 48.8 jit_solution(15793969045992706986)
XLA Ops:
  1.3 0.8 %shard_map.77.own_ref = bf16[1,96,256]{2,1,0:T(8,128)(2,1)S(1)} custom-call(f32[16,256]{1,0:T(8,128)} %bitcast.5, f32[16]{0:T(128)} %inv_ref.1, f32[32,256]{1,0:T(8,128)} %bitcast.4, s32[1]{0:T(128)S(6)} %copy.10.count_ref), custom_call_target="tpu_custom_call" | custom-call | tf_op jit(solution)/shard_map/pallas_call | solution.py:77
  2.1 5.1 %collective-permute-start.2 = (bf16[1,96,256]{2,1,0:T(8,128)(2,1)S(1)}, bf16[1,96,256]{2,1,0:T(8,128)(2,1)S(1)}, u32[]{:S(2)}, u32[]{:S(2)}) collective-permute-start(bf16[1,96,256]{2,1,0:T(8,128)(2,1)S(1)} %shard_map.77.own_ref), channel_id=1, source_target_pairs={{0,24},{1,25},{2,26},{3,27},{4,28},{5,29},{6,30},{7,31},{8,16},{9,... | collective-permute-start | bytes 147464 | tf_op jit(solution)/shard_map/ppermute | solution.py:27
  7.2 0.0 collective-permute-start.1
  7.2 0.6 %collective-permute-start = (bf16[1,96,256]{2,1,0:T(8,128)(2,1)S(1)}, bf16[1,96,256]{2,1,0:T(8,128)(2,1)S(1)}, u32[]{:S(2)}, u32[]{:S(2)}) collective-permute-start(bf16[1,96,256]{2,1,0:T(8,128)(2,1)S(1)} %shard_map.77.own_ref), channel_id=1, source_target_pairs={{0,16},{1,17},{2,18},{3,19},{4,20},{5,21},{6,22},{7,23},{8,24},{9,... | collective-permute-start | bytes 147464 | tf_op jit(solution)/shard_map/ppermute | solution.py:27
  9.2 0.1 pad_maximum_fusion.1
  9.3 0.2 collective-permute-done.2
  9.5 1.8 %collective-permute-done.1 = bf16[1,96,256]{2,1,0:T(8,128)(2,1)S(1)} collective-permute-done((bf16[1,96,256]{2,1,0:T(8,128)(2,1)S(1)}, bf16[1,96,256]{2,1,0:T(8,128)(2,1)S(1)}, u32[]{:S(2)}, u32[]{:S(2)}) %collective-permute-start.1) | collective-permute-done | bytes 49184 | tf_op jit(solution)/shard_map/ppermute | solution.py:27
  11.3 1.2 %collective-permute-done = bf16[1,96,256]{2,1,0:T(8,128)(2,1)S(1)} collective-permute-done((bf16[1,96,256]{2,1,0:T(8,128)(2,1)S(1)}, bf16[1,96,256]{2,1,0:T(8,128)(2,1)S(1)}, u32[]{:S(2)}, u32[]{:S(2)}) %collective-permute-start) | collective-permute-done | bytes 49184 | tf_op jit(solution)/shard_map/ppermute | solution.py:27
  12.5 0.1 broadcast_in_dim.2.levels_ref
  12.6 0.1 collective-permute-start.4
  12.7 1.6 %collective-permute-start.3 = (bf16[4,64,256]{2,1,0:T(8,128)(2,1)S(1)}, bf16[4,64,256]{2,1,0:T(8,128)(2,1)S(1)}, u32[]{:S(2)}, u32[]{:S(2)}) collective-permute-start(bf16[4,64,256]{2,1,0:T(8,128)(2,1)S(1)} %slice.3.refs_0_), channel_id=1, source_target_pairs={{0,4},{1,5},{2,6},{3,7},{4,0},{5,1},{6,2},{7,3},{8,12},{9,13},{10,... | collective-permute-start | bytes 393224 | tf_op jit(solution)/shard_map/ppermute | solution.py:27
  14.3 1.5 %collective-permute-start.6 = (bf16[4,64,256]{2,1,0:T(8,128)(2,1)S(1)}, bf16[4,64,256]{2,1,0:T(8,128)(2,1)S(1)}, u32[]{:S(2)}, u32[]{:S(2)}) collective-permute-start(bf16[4,64,256]{2,1,0:T(8,128)(2,1)S(1)} %slice.3.refs_0_), channel_id=1, source_target_pairs={{0,2},{1,3},{2,0},{3,1},{4,6},{5,7},{6,4},{7,5},{8,10},{9,11},{10,... | collective-permute-start | bytes 393224 | tf_op jit(solution)/shard_map/ppermute | solution.py:27
  15.8 0.0 collective-permute-done.4.refs_1_
  15.8 2.0 %shard_map.78 = (bf16[1,1024,1024]{2,1,0:T(8,128)(2,1)S(1)}, bf16[1,1024,1024]{2,1,0:T(8,128)(2,1)S(1)}, f32[32,1024]{1,0:T(8,128)S(1)}, bf16[80,1024]{1,0:T(8,128)(2,1)S(1)}) custom-call(bf16[4,96,256]{2,1,0:T(8,128)(2,1)S(1)} %pad_maximum_fusion.near_ref, f32[2,256]{1,0:T(2,128)S(1)} %broadcast_in_dim.2.levels_ref, bf16[4,64,256]{2,1,0:T(8,128)(2,1)S(1)} %slice.3.refs_0_, ...), custom_call_target="tpu_custom_call" | custom-call | flops 1073741824 | bytes 262144 | tf_op jit(solution)/shard_map/pallas_call | solution.py:172
  17.8 0.9 %collective-permute-done.3.refs_0_.refs_2_ = bf16[4,64,256]{2,1,0:T(8,128)(2,1)S(1)} collective-permute-done((bf16[4,64,256]{2,1,0:T(8,128)(2,1)S(1)}, bf16[4,64,256]{2,1,0:T(8,128)(2,1)S(1)}, u32[]{:S(2)}, u32[]{:S(2)}) %collective-permute-start.3) | collective-permute-done | bytes 131104 | tf_op jit(solution)/shard_map/ppermute | solution.py:27
  18.6 0.0 collective-permute-start.7
  18.6 1.5 %collective-permute-start.5 = (bf16[4,64,256]{2,1,0:T(8,128)(2,1)S(1)}, bf16[4,64,256]{2,1,0:T(8,128)(2,1)S(1)}, u32[]{:S(2)}, u32[]{:S(2)}) collective-permute-start(bf16[4,64,256]{2,1,0:T(8,128)(2,1)S(1)} %collective-permute-done.3.refs_0_.refs_2_), channel_id=1, source_target_pairs={{0,2},{1,3},{2,0},{3,1},{4,6},{5,7},{6,4},{7,5},{8,10},{9,11},{10,... | collective-permute-start | bytes 393224 | tf_op jit(solution)/shard_map/ppermute | solution.py:27
  20.1 1.1 %shard_map.79 = (bf16[1,1024,1024]{2,1,0:T(8,128)(2,1)S(1)}, f32[32,1024]{1,0:T(8,128)S(1)}) custom-call(bf16[4,96,256]{2,1,0:T(8,128)(2,1)S(1)} %pad_maximum_fusion.near_ref, f32[2,256]{1,0:T(2,128)S(1)} %broadcast_in_dim.2.levels_ref, bf16[4,64,256]{2,1,0:T(8,128)(2,1)S(1)} %collective-permute-done.3.refs_0_.refs_2_, ...), custom_call_target="tpu_custom_call" | custom-call | flops 536870912 | bytes 262144 | tf_op jit(solution)/shard_map/pallas_call | solution.py:172
  21.2 0.0 collective-permute-done.6.refs_1_.refs_4_
  21.2 0.3 collective-permute-start.9
  21.5 2.0 %shard_map.80 = (bf16[1,1024,1024]{2,1,0:T(8,128)(2,1)S(1)}, bf16[1,1024,1024]{2,1,0:T(8,128)(2,1)S(1)}, f32[32,1024]{1,0:T(8,128)S(1)}) custom-call(bf16[4,96,256]{2,1,0:T(8,128)(2,1)S(1)} %pad_maximum_fusion.near_ref, f32[2,256]{1,0:T(2,128)S(1)} %broadcast_in_dim.2.levels_ref, bf16[4,64,256]{2,1,0:T(8,128)(2,1)S(1)} %collective-permute-done.7.refs_0_.refs_3_, ...), custom_call_target="tpu_custom_call" | custom-call | flops 1073741824 | bytes 262144 | tf_op jit(solution)/shard_map/pallas_call | solution.py:172
  23.5 1.0 %collective-permute-done.5.refs_1_.refs_6_ = bf16[4,64,256]{2,1,0:T(8,128)(2,1)S(1)} collective-permute-done((bf16[4,64,256]{2,1,0:T(8,128)(2,1)S(1)}, bf16[4,64,256]{2,1,0:T(8,128)(2,1)S(1)}, u32[]{:S(2)}, u32[]{:S(2)}) %collective-permute-start.5) | collective-permute-done | bytes 131104 | tf_op jit(solution)/shard_map/ppermute | solution.py:27
  24.5 0.0 collective-permute-start.8
  24.5 0.0 collective-permute-done.9.refs_0_.refs_5_
  24.5 2.0 %shard_map.81 = (bf16[1,1024,1024]{2,1,0:T(8,128)(2,1)S(1)}, bf16[1,1024,1024]{2,1,0:T(8,128)(2,1)S(1)}, f32[32,1024]{1,0:T(8,128)S(1)}) custom-call(bf16[4,96,256]{2,1,0:T(8,128)(2,1)S(1)} %pad_maximum_fusion.near_ref, f32[2,256]{1,0:T(2,128)S(1)} %broadcast_in_dim.2.levels_ref, bf16[4,64,256]{2,1,0:T(8,128)(2,1)S(1)} %collective-permute-done.9.refs_0_.refs_5_, ...), custom_call_target="tpu_custom_call" | custom-call | flops 1073741824 | bytes 262144 | tf_op jit(solution)/shard_map/pallas_call | solution.py:172
  26.5 0.0 collective-permute-done.8.refs_0_.refs_7_
  26.5 1.3 %shard_map.82 = (bf16[1,1024,1024]{2,1,0:T(8,128)(2,1)S(1)}, bf16[1,144,256]{2,1,0:T(8,128)(2,1)S(1)}, f32[32,256]{1,0:T(8,128)S(1)}) custom-call(bf16[4,96,256]{2,1,0:T(8,128)(2,1)S(1)} %pad_maximum_fusion.near_ref, f32[2,256]{1,0:T(2,128)S(1)} %broadcast_in_dim.2.levels_ref, bf16[4,64,256]{2,1,0:T(8,128)(2,1)S(1)} %collective-permute-done.8.refs_0_.refs_7_, ...), custom_call_target="tpu_custom_call" | custom-call | flops 536870912 | bytes 262144 | tf_op jit(solution)/shard_map/pallas_call | solution.py:172
  27.9 2.5 %collective-permute-start.15 = (bf16[1,144,256]{2,1,0:T(8,128)(2,1)S(1)}, bf16[1,144,256]{2,1,0:T(8,128)(2,1)S(1)}, u32[]{:S(2)}, u32[]{:S(2)}) collective-permute-start(bf16[1,144,256]{2,1,0:T(8,128)(2,1)S(1)} %get-tuple-element.59.refs_8_), channel_id=1, source_target_pairs={{0,6},{1,7},{2,4},{3,5},{4,2},{5,3},{6,0},{7,1},{8,14},{9,15},{10,... | collective-permute-start | bytes 221192 | tf_op jit(solution)/shard_map/ppermute | solution.py:27
  30.3 0.5 %collective-permute-start.13 = (bf16[1,144,256]{2,1,0:T(8,128)(2,1)S(1)}, bf16[1,144,256]{2,1,0:T(8,128)(2,1)S(1)}, u32[]{:S(2)}, u32[]{:S(2)}) collective-permute-start(bf16[1,144,256]{2,1,0:T(8,128)(2,1)S(1)} %get-tuple-element.59.refs_8_), channel_id=1, source_target_pairs={{0,2},{1,3},{2,0},{3,1},{4,6},{5,7},{6,4},{7,5},{8,10},{9,11},{10,... | collective-permute-start | bytes 221192 | tf_op jit(solution)/shard_map/ppermute | solution.py:27
  30.9 0.5 %collective-permute-start.11 = (bf16[1,144,256]{2,1,0:T(8,128)(2,1)S(1)}, bf16[1,144,256]{2,1,0:T(8,128)(2,1)S(1)}, u32[]{:S(2)}, u32[]{:S(2)}) collective-permute-start(bf16[1,144,256]{2,1,0:T(8,128)(2,1)S(1)} %get-tuple-element.59.refs_8_), channel_id=1, source_target_pairs={{0,4},{1,5},{2,6},{3,7},{4,0},{5,1},{6,2},{7,3},{8,12},{9,13},{10,... | collective-permute-start | bytes 221192 | tf_op jit(solution)/shard_map/ppermute | solution.py:27
  31.4 2.5 %collective-permute-done.15.refs_14_ = bf16[1,144,256]{2,1,0:T(8,128)(2,1)S(1)} collective-permute-done((bf16[1,144,256]{2,1,0:T(8,128)(2,1)S(1)}, bf16[1,144,256]{2,1,0:T(8,128)(2,1)S(1)}, u32[]{:S(2)}, u32[]{:S(2)}) %collective-permute-start.15) | collective-permute-done | bytes 73760 | tf_op jit(solution)/shard_map/ppermute | solution.py:27
  33.9 1.2 %collective-permute-done.13.refs_12_ = bf16[1,144,256]{2,1,0:T(8,128)(2,1)S(1)} collective-permute-done((bf16[1,144,256]{2,1,0:T(8,128)(2,1)S(1)}, bf16[1,144,256]{2,1,0:T(8,128)(2,1)S(1)}, u32[]{:S(2)}, u32[]{:S(2)}) %collective-permute-start.13) | collective-permute-done | bytes 73760 | tf_op jit(solution)/shard_map/ppermute | solution.py:27
  35.1 0.0 collective-permute-start.14
  35.1 0.1 collective-permute-done.11.refs_10_
  35.2 0.4 collective-permute-start.12
  35.6 0.0 collective-permute-done.10.refs_9_
  35.6 0.7 %collective-permute-done.14.refs_13_ = bf16[1,144,256]{2,1,0:T(8,128)(2,1)S(1)} collective-permute-done((bf16[1,144,256]{2,1,0:T(8,128)(2,1)S(1)}, bf16[1,144,256]{2,1,0:T(8,128)(2,1)S(1)}, u32[]{:S(2)}, u32[]{:S(2)}) %collective-permute-start.14) | collective-permute-done | bytes 73760 | tf_op jit(solution)/shard_map/ppermute | solution.py:27
  36.4 0.2 collective-permute-done.12.refs_11_
  36.5 3.8 %shard_map.83 = (f32[8,128]{1,0:T(8,128)S(1)}, f32[32,256]{1,0:T(8,128)S(1)}, f32[32,256]{1,0:T(8,128)S(1)}, f32[32,256]{1,0:T(8,128)S(1)}, f32[32,256]{1,0:T(8,128)S(1)}, /*index=5*/f32[32,128]{1,0:T(8,128)S(1)}) custom-call(f32[2,256]{1,0:T(2,128)S(1)} %broadcast_in_dim.2.levels_ref, bf16[1,96,256]{2,1,0:T(8,128)(2,1)S(1)} %shard_map.77.own_ref, ...), custom_call_target="tpu_custom_call" | custom-call | tf_op jit(solution)/shard_map/pallas_call | solution.py:305
  40.3 0.4 collective-permute-start.17
  40.6 0.8 %collective-permute-done.17 = f32[8,128]{1,0:T(8,128)S(1)} collective-permute-done((f32[8,128]{1,0:T(8,128)S(1)}, f32[8,128]{1,0:T(8,128)S(1)}, u32[]{:S(2)}, u32[]{:S(2)}) %collective-permute-start.17) | collective-permute-done | bytes 4128 | tf_op jit(solution)/shard_map/ppermute | solution.py:27
  41.5 2.2 %collective-permute-start.20 = (f32[8,128]{1,0:T(8,128)S(1)}, f32[8,128]{1,0:T(8,128)S(1)}, u32[]{:S(2)}, u32[]{:S(2)}) collective-permute-start(f32[8,128]{1,0:T(8,128)S(1)} %add.12), channel_id=1, source_target_pairs={{0,6},{1,7},{2,4},{3,5},{4,2},{5,3},{6,0},{7,1},{8,14},{9,15},{10,... | collective-permute-start | bytes 12296 | tf_op jit(solution)/shard_map/ppermute | solution.py:27
  43.7 0.7 %collective-permute-start.19 = (f32[8,128]{1,0:T(8,128)S(1)}, f32[8,128]{1,0:T(8,128)S(1)}, u32[]{:S(2)}, u32[]{:S(2)}) collective-permute-start(f32[8,128]{1,0:T(8,128)S(1)} %add.12), channel_id=1, source_target_pairs={{0,4},{1,5},{2,6},{3,7},{4,0},{5,1},{6,2},{7,3},{8,12},{9,13},{10,... | collective-permute-start | bytes 12296 | tf_op jit(solution)/shard_map/ppermute | solution.py:27
  44.4 0.5 %collective-permute-start.18 = (f32[8,128]{1,0:T(8,128)S(1)}, f32[8,128]{1,0:T(8,128)S(1)}, u32[]{:S(2)}, u32[]{:S(2)}) collective-permute-start(f32[8,128]{1,0:T(8,128)S(1)} %add.12), channel_id=1, source_target_pairs={{0,2},{1,3},{2,0},{3,1},{4,6},{5,7},{6,4},{7,5},{8,10},{9,11},{10,... | collective-permute-start | bytes 12296 | tf_op jit(solution)/shard_map/ppermute | solution.py:27
  45.0 1.0 %collective-permute-done.20 = f32[8,128]{1,0:T(8,128)S(1)} collective-permute-done((f32[8,128]{1,0:T(8,128)S(1)}, f32[8,128]{1,0:T(8,128)S(1)}, u32[]{:S(2)}, u32[]{:S(2)}) %collective-permute-start.20) | collective-permute-done | bytes 4128 | tf_op jit(solution)/shard_map/ppermute | solution.py:27
  46.0 1.3 %collective-permute-done.19 = f32[8,128]{1,0:T(8,128)S(1)} collective-permute-done((f32[8,128]{1,0:T(8,128)S(1)}, f32[8,128]{1,0:T(8,128)S(1)}, u32[]{:S(2)}, u32[]{:S(2)}) %collective-permute-start.19) | collective-permute-done | bytes 4128 | tf_op jit(solution)/shard_map/ppermute | solution.py:27
  47.3 0.7 %collective-permute-done.18 = f32[8,128]{1,0:T(8,128)S(1)} collective-permute-done((f32[8,128]{1,0:T(8,128)S(1)}, f32[8,128]{1,0:T(8,128)S(1)}, u32[]{:S(2)}, u32[]{:S(2)}) %collective-permute-start.18) | collective-permute-done | bytes 4128 | tf_op jit(solution)/shard_map/ppermute | solution.py:27
  48.1 0.8 %shard_map.84 = (f32[32,256]{1,0:T(8,128)}, f32[32,256]{1,0:T(8,128)}) custom-call(f32[8,128]{1,0:T(8,128)S(1)} %add_add_fusion.curve_ref, f32[32,128]{1,0:T(8,128)S(1)} %get-tuple-element.69.norm_ref, f32[32,256]{1,0:T(8,128)S(1)} %get-tuple-element.70.solution_ref, f32[32,256]{1,0:T(8,128)S(1)} %get-tuple-element.71.residual_ref, ...), custom_call_target="tpu_custom_call" | custom-call | tf_op jit(solution)/shard_map/pallas_call | solution.py:384
  (8 shorter events, 0.1 us)
Async XLA Ops:
  2.1 7.4 %collective-permute-start.2 = (bf16[1,96,256]{2,1,0:T(8,128)(2,1)S(1)}, bf16[1,96,256]{2,1,0:T(8,128)(2,1)S(1)}, u32[]{:S(2)}, u32[]{:S(2)}) collective-permute-start(bf16[1,96,256]{2,1,0:T(8,128)(2,1)S(1)} %shard_map.77.own_ref), channel_id=1, source_target_pairs={{0,24},{1,25},{2,26},{3,27},{4,28},{5,29},{6,30},{7,31},{8,16},{9,... | collective-permute-start | bytes 147464 | tf_op jit(solution)/shard_map/ppermute | solution.py:27
  7.2 4.1 %collective-permute-start.1 = (bf16[1,96,256]{2,1,0:T(8,128)(2,1)S(1)}, bf16[1,96,256]{2,1,0:T(8,128)(2,1)S(1)}, u32[]{:S(2)}, u32[]{:S(2)}) collective-permute-start(bf16[1,96,256]{2,1,0:T(8,128)(2,1)S(1)} %shard_map.77.own_ref), channel_id=1, source_target_pairs={{0,8},{1,9},{2,10},{3,11},{4,12},{5,13},{6,14},{7,15},{8,0},{9,1},... | collective-permute-start | bytes 147464 | tf_op jit(solution)/shard_map/ppermute | solution.py:27
  7.2 5.3 %collective-permute-start = (bf16[1,96,256]{2,1,0:T(8,128)(2,1)S(1)}, bf16[1,96,256]{2,1,0:T(8,128)(2,1)S(1)}, u32[]{:S(2)}, u32[]{:S(2)}) collective-permute-start(bf16[1,96,256]{2,1,0:T(8,128)(2,1)S(1)} %shard_map.77.own_ref), channel_id=1, source_target_pairs={{0,16},{1,17},{2,18},{3,19},{4,20},{5,21},{6,22},{7,23},{8,24},{9,... | collective-permute-start | bytes 147464 | tf_op jit(solution)/shard_map/ppermute | solution.py:27
  12.6 3.2 %collective-permute-start.4 = (bf16[4,64,256]{2,1,0:T(8,128)(2,1)S(1)}, bf16[4,64,256]{2,1,0:T(8,128)(2,1)S(1)}, u32[]{:S(2)}, u32[]{:S(2)}) collective-permute-start(bf16[4,64,256]{2,1,0:T(8,128)(2,1)S(1)} %slice.3.refs_0_), channel_id=1, source_target_pairs={{0,1},{1,0},{2,3},{3,2},{4,5},{5,4},{6,7},{7,6},{8,9},{9,8},{10,11... | collective-permute-start | bytes 393224 | tf_op jit(solution)/shard_map/ppermute | solution.py:27
  12.7 5.9 %collective-permute-start.3 = (bf16[4,64,256]{2,1,0:T(8,128)(2,1)S(1)}, bf16[4,64,256]{2,1,0:T(8,128)(2,1)S(1)}, u32[]{:S(2)}, u32[]{:S(2)}) collective-permute-start(bf16[4,64,256]{2,1,0:T(8,128)(2,1)S(1)} %slice.3.refs_0_), channel_id=1, source_target_pairs={{0,4},{1,5},{2,6},{3,7},{4,0},{5,1},{6,2},{7,3},{8,12},{9,13},{10,... | collective-permute-start | bytes 393224 | tf_op jit(solution)/shard_map/ppermute | solution.py:27
  14.3 6.9 %collective-permute-start.6 = (bf16[4,64,256]{2,1,0:T(8,128)(2,1)S(1)}, bf16[4,64,256]{2,1,0:T(8,128)(2,1)S(1)}, u32[]{:S(2)}, u32[]{:S(2)}) collective-permute-start(bf16[4,64,256]{2,1,0:T(8,128)(2,1)S(1)} %slice.3.refs_0_), channel_id=1, source_target_pairs={{0,2},{1,3},{2,0},{3,1},{4,6},{5,7},{6,4},{7,5},{8,10},{9,11},{10,... | collective-permute-start | bytes 393224 | tf_op jit(solution)/shard_map/ppermute | solution.py:27
  18.6 2.9 %collective-permute-start.7 = (bf16[4,64,256]{2,1,0:T(8,128)(2,1)S(1)}, bf16[4,64,256]{2,1,0:T(8,128)(2,1)S(1)}, u32[]{:S(2)}, u32[]{:S(2)}) collective-permute-start(bf16[4,64,256]{2,1,0:T(8,128)(2,1)S(1)} %collective-permute-done.3.refs_0_.refs_2_), channel_id=1, source_target_pairs={{0,1},{1,0},{2,3},{3,2},{4,5},{5,4},{6,7},{7,6},{8,9},{9,8},{10,11... | collective-permute-start | bytes 393224 | tf_op jit(solution)/shard_map/ppermute | solution.py:27
  18.6 5.9 %collective-permute-start.5 = (bf16[4,64,256]{2,1,0:T(8,128)(2,1)S(1)}, bf16[4,64,256]{2,1,0:T(8,128)(2,1)S(1)}, u32[]{:S(2)}, u32[]{:S(2)}) collective-permute-start(bf16[4,64,256]{2,1,0:T(8,128)(2,1)S(1)} %collective-permute-done.3.refs_0_.refs_2_), channel_id=1, source_target_pairs={{0,2},{1,3},{2,0},{3,1},{4,6},{5,7},{6,4},{7,5},{8,10},{9,11},{10,... | collective-permute-start | bytes 393224 | tf_op jit(solution)/shard_map/ppermute | solution.py:27
  21.2 3.3 %collective-permute-start.9 = (bf16[4,64,256]{2,1,0:T(8,128)(2,1)S(1)}, bf16[4,64,256]{2,1,0:T(8,128)(2,1)S(1)}, u32[]{:S(2)}, u32[]{:S(2)}) collective-permute-start(bf16[4,64,256]{2,1,0:T(8,128)(2,1)S(1)} %collective-permute-done.6.refs_1_.refs_4_), channel_id=1, source_target_pairs={{0,1},{1,0},{2,3},{3,2},{4,5},{5,4},{6,7},{7,6},{8,9},{9,8},{10,11... | collective-permute-start | bytes 393224 | tf_op jit(solution)/shard_map/ppermute | solution.py:27
  24.5 2.0 %collective-permute-start.8 = (bf16[4,64,256]{2,1,0:T(8,128)(2,1)S(1)}, bf16[4,64,256]{2,1,0:T(8,128)(2,1)S(1)}, u32[]{:S(2)}, u32[]{:S(2)}) collective-permute-start(bf16[4,64,256]{2,1,0:T(8,128)(2,1)S(1)} %collective-permute-done.5.refs_1_.refs_6_), channel_id=1, source_target_pairs={{0,1},{1,0},{2,3},{3,2},{4,5},{5,4},{6,7},{7,6},{8,9},{9,8},{10,11... | collective-permute-start | bytes 393224 | tf_op jit(solution)/shard_map/ppermute | solution.py:27
  27.9 6.0 %collective-permute-start.15 = (bf16[1,144,256]{2,1,0:T(8,128)(2,1)S(1)}, bf16[1,144,256]{2,1,0:T(8,128)(2,1)S(1)}, u32[]{:S(2)}, u32[]{:S(2)}) collective-permute-start(bf16[1,144,256]{2,1,0:T(8,128)(2,1)S(1)} %get-tuple-element.59.refs_8_), channel_id=1, source_target_pairs={{0,6},{1,7},{2,4},{3,5},{4,2},{5,3},{6,0},{7,1},{8,14},{9,15},{10,... | collective-permute-start | bytes 221192 | tf_op jit(solution)/shard_map/ppermute | solution.py:27
  30.3 4.8 %collective-permute-start.13 = (bf16[1,144,256]{2,1,0:T(8,128)(2,1)S(1)}, bf16[1,144,256]{2,1,0:T(8,128)(2,1)S(1)}, u32[]{:S(2)}, u32[]{:S(2)}) collective-permute-start(bf16[1,144,256]{2,1,0:T(8,128)(2,1)S(1)} %get-tuple-element.59.refs_8_), channel_id=1, source_target_pairs={{0,2},{1,3},{2,0},{3,1},{4,6},{5,7},{6,4},{7,5},{8,10},{9,11},{10,... | collective-permute-start | bytes 221192 | tf_op jit(solution)/shard_map/ppermute | solution.py:27
  30.9 4.4 %collective-permute-start.11 = (bf16[1,144,256]{2,1,0:T(8,128)(2,1)S(1)}, bf16[1,144,256]{2,1,0:T(8,128)(2,1)S(1)}, u32[]{:S(2)}, u32[]{:S(2)}) collective-permute-start(bf16[1,144,256]{2,1,0:T(8,128)(2,1)S(1)} %get-tuple-element.59.refs_8_), channel_id=1, source_target_pairs={{0,4},{1,5},{2,6},{3,7},{4,0},{5,1},{6,2},{7,3},{8,12},{9,13},{10,... | collective-permute-start | bytes 221192 | tf_op jit(solution)/shard_map/ppermute | solution.py:27
  31.4 4.2 %collective-permute-start.10 = (bf16[1,144,256]{2,1,0:T(8,128)(2,1)S(1)}, bf16[1,144,256]{2,1,0:T(8,128)(2,1)S(1)}, u32[]{:S(2)}, u32[]{:S(2)}) collective-permute-start(bf16[1,144,256]{2,1,0:T(8,128)(2,1)S(1)} %get-tuple-element.59.refs_8_), channel_id=1, source_target_pairs={{0,1},{1,0},{2,3},{3,2},{4,5},{5,4},{6,7},{7,6},{8,9},{9,8},{10,11... | collective-permute-start | bytes 221192 | tf_op jit(solution)/shard_map/ppermute | solution.py:27
  33.9 1.8 %collective-permute-start.16 = (bf16[1,144,256]{2,1,0:T(8,128)(2,1)S(1)}, bf16[1,144,256]{2,1,0:T(8,128)(2,1)S(1)}, u32[]{:S(2)}, u32[]{:S(2)}) collective-permute-start(bf16[1,144,256]{2,1,0:T(8,128)(2,1)S(1)} %collective-permute-done.15.refs_14_), channel_id=1, source_target_pairs={{0,1},{1,0},{2,3},{3,2},{4,5},{5,4},{6,7},{7,6},{8,9},{9,8},{10,11... | collective-permute-start | bytes 221192 | tf_op jit(solution)/shard_map/ppermute | solution.py:27
  35.1 1.3 %collective-permute-start.14 = (bf16[1,144,256]{2,1,0:T(8,128)(2,1)S(1)}, bf16[1,144,256]{2,1,0:T(8,128)(2,1)S(1)}, u32[]{:S(2)}, u32[]{:S(2)}) collective-permute-start(bf16[1,144,256]{2,1,0:T(8,128)(2,1)S(1)} %collective-permute-done.13.refs_12_), channel_id=1, source_target_pairs={{0,1},{1,0},{2,3},{3,2},{4,5},{5,4},{6,7},{7,6},{8,9},{9,8},{10,11... | collective-permute-start | bytes 221192 | tf_op jit(solution)/shard_map/ppermute | solution.py:27
  35.2 1.3 %collective-permute-start.12 = (bf16[1,144,256]{2,1,0:T(8,128)(2,1)S(1)}, bf16[1,144,256]{2,1,0:T(8,128)(2,1)S(1)}, u32[]{:S(2)}, u32[]{:S(2)}) collective-permute-start(bf16[1,144,256]{2,1,0:T(8,128)(2,1)S(1)} %collective-permute-done.11.refs_10_), channel_id=1, source_target_pairs={{0,1},{1,0},{2,3},{3,2},{4,5},{5,4},{6,7},{7,6},{8,9},{9,8},{10,11... | collective-permute-start | bytes 221192 | tf_op jit(solution)/shard_map/ppermute | solution.py:27
  40.3 1.2 %collective-permute-start.17 = (f32[8,128]{1,0:T(8,128)S(1)}, f32[8,128]{1,0:T(8,128)S(1)}, u32[]{:S(2)}, u32[]{:S(2)}) collective-permute-start(f32[8,128]{1,0:T(8,128)S(1)} %get-tuple-element.68), channel_id=1, source_target_pairs={{0,1},{1,0},{2,3},{3,2},{4,5},{5,4},{6,7},{7,6},{8,9},{9,8},{10,11... | collective-permute-start | bytes 12296 | tf_op jit(solution)/shard_map/ppermute | solution.py:27
  41.5 4.5 %collective-permute-start.20 = (f32[8,128]{1,0:T(8,128)S(1)}, f32[8,128]{1,0:T(8,128)S(1)}, u32[]{:S(2)}, u32[]{:S(2)}) collective-permute-start(f32[8,128]{1,0:T(8,128)S(1)} %add.12), channel_id=1, source_target_pairs={{0,6},{1,7},{2,4},{3,5},{4,2},{5,3},{6,0},{7,1},{8,14},{9,15},{10,... | collective-permute-start | bytes 12296 | tf_op jit(solution)/shard_map/ppermute | solution.py:27
  43.7 3.6 %collective-permute-start.19 = (f32[8,128]{1,0:T(8,128)S(1)}, f32[8,128]{1,0:T(8,128)S(1)}, u32[]{:S(2)}, u32[]{:S(2)}) collective-permute-start(f32[8,128]{1,0:T(8,128)S(1)} %add.12), channel_id=1, source_target_pairs={{0,4},{1,5},{2,6},{3,7},{4,0},{5,1},{6,2},{7,3},{8,12},{9,13},{10,... | collective-permute-start | bytes 12296 | tf_op jit(solution)/shard_map/ppermute | solution.py:27
  44.4 3.6 %collective-permute-start.18 = (f32[8,128]{1,0:T(8,128)S(1)}, f32[8,128]{1,0:T(8,128)S(1)}, u32[]{:S(2)}, u32[]{:S(2)}) collective-permute-start(f32[8,128]{1,0:T(8,128)S(1)} %add.12), channel_id=1, source_target_pairs={{0,2},{1,3},{2,0},{3,1},{4,6},{5,7},{6,4},{7,5},{8,10},{9,11},{10,... | collective-permute-start | bytes 12296 | tf_op jit(solution)/shard_map/ppermute | solution.py:27

commit v7 on v6

--- a/solution.py
+++ b/solution.py
@@ -88,6 +88,12 @@
         right_ref[:, b * slots : (b + 1) * slots] = features(near_ref[b, : 2 * feat, :], levels_ref[0:1, :], False)
 
 
+def turned(rows, height):
+    if rows.shape[0] < height:
+        rows = jnp.concatenate([rows, jnp.zeros((height - rows.shape[0], rows.shape[1]), F32)], axis=0)
+    return rows.T
+
+
 def entries(left, right):
     powers = lax.dot_general(left, right, (((0,), (0,)), ((), ())), preferred_element_type=F32)
     return jnp.exp2(powers).astype(BF16)
@@ -96,43 +102,53 @@
 def apply_kernel(feat, group, keep, begin, last, count, near_ref, levels_ref, *refs):
     far, refs = refs[:count], refs[count:]
     if begin:
-        right_ref, refs = refs[-4], refs[:-4] + refs[-3:]
+        right_ref, refs = refs[-2], refs[:-2] + refs[-1:]
     else:
         right_ref, so_far_ref, refs = refs[0], refs[1], refs[2:]
     kept, refs = (refs[:count], refs[count:]) if keep else ((), refs)
     own_ref = None
     if last:
         own_ref, refs = refs[1], refs[:1] + refs[2:]
-    out_ref, left_ref, dirs_ref, sum_ref = refs
-    slots, probes = near_ref.shape[2], dirs_ref.shape[0]
+    out_ref, sum_ref = refs
+    slots, probes = near_ref.shape[2], sum_ref.shape[0]
     if begin:
         fill_right(near_ref, levels_ref, right_ref, feat)
-        sum_ref[...] = jnp.zeros_like(sum_ref)
+        product = jnp.zeros(sum_ref.shape, F32)
     else:
-        sum_ref[...] = so_far_ref[...]
-    for piece, far_ref in enumerate(far):
-
-        def step(g, carry, piece=piece, far_ref=far_ref):
-            for b in range(group):
-                place = slice(b * slots, (b + 1) * slots)
-                left_ref[:, place] = features(far_ref[g * group + b, : 2 * feat, :], None, True)
-                dirs_ref[:, place] = far_ref[g * group + b, 2 * feat :, :]
-            block = entries(left_ref[...], right_ref[...])
-            if keep:
-                kept[piece][g] = block
-            sum_ref[...] += jnp.dot(dirs_ref[...], block, preferred_element_type=F32)
+        product = so_far_ref[...]
+
+    def step(piece, g):
+        blocks = [far[piece][g * group + b] for b in range(group)]
+        left = jnp.concatenate([features(block[: 2 * feat], None, True) for block in blocks], axis=1)
+        directions = jnp.concatenate([block[2 * feat :] for block in blocks], axis=1)
+        block = entries(left, right_ref[...])
+        if keep:
+            kept[piece][g] = block
+        return jnp.dot(directions, block, preferred_element_type=F32)
+
+    steps = far[0].shape[0] // group
+    if steps == 1:
+        for piece in range(count):
+            product = product + step(piece, 0)
+    else:
+        sum_ref[...] = product
+
+        def add(piece, g, carry):
+            sum_ref[...] += step(piece, g)
             return carry
 
-        lax.fori_loop(0, far_ref.shape[0] // group, step, 0)
+        for piece in range(count):
+            lax.fori_loop(0, steps, functools.partial(add, piece), 0)
+        product = sum_ref[...]
     if not last:
-        out_ref[...] = sum_ref[...]
+        out_ref[...] = product
         return
     images, rights = [], []
     norm = curve = jnp.zeros((probes, slots), F32)
     for b in range(near_ref.shape[0]):
         direction = near_ref[b, 2 * feat : 2 * feat + probes, :].astype(F32)
         right = direction + near_ref[b, 2 * feat + probes :, :].astype(F32)
-        image = sum_ref[:, b * slots : (b + 1) * slots] + levels_ref[1:2, :] * direction
+        image = product[:, b * slots : (b + 1) * slots] + levels_ref[1:2, :] * direction
         norm = norm + right * right
         curve = curve + direction * image
         images.append(image)
@@ -143,16 +159,20 @@
     likely = (norm > 0.0) & (curve > 1e-6 * norm)
     guess = jnp.where(likely, norm / jnp.where(likely, curve, 1.0), usual)
     guess = jnp.clip(guess, 1e-6, 1e3).astype(BF16)
-    for b, (image, right) in enumerate(zip(images, rights)):
-        out_ref[0, b * probes : (b + 1) * probes, :] = (right - guess.astype(F32) * image).astype(BF16)
-    parts = [part.astype(F32) for part in (*three_parts(norm), *three_parts(curve), guess)]
+    steps = [right - guess.astype(F32) * image for image, right in zip(images, rights)]
+    for b, after in enumerate(steps):
+        out_ref[0, b * probes : (b + 1) * probes, :] = after.astype(BF16)
+    products = [[x * y for x, y in zip(*pair)] for pair in ((steps, steps), (steps, images), (images, images))]
+    sums = [norm, curve] + [jnp.sum(sum(each), axis=1, keepdims=True) for each in products]
     lane = lax.broadcasted_iota(jnp.int32, (probes, 128), 1)
     flat = jnp.zeros((probes, 128), F32)
-    for at, part in enumerate(parts):
-        flat = jnp.where(lane == at, part, flat)
-    flat = jnp.concatenate([flat, jnp.zeros((128 - probes, 128), F32)], axis=0).T[:TAIL]
-    flat = jnp.concatenate([flat, jnp.zeros((TAIL, slots - 128), F32)], axis=1)
-    out_ref[0, len(images) * probes :, :] = flat.astype(BF16)
+    for at, each in enumerate([*sums, guess.astype(F32)]):
+        flat = jnp.where(lane == at, each, flat)
+    high, middle, low = (part.astype(F32) for part in three_parts(turned(flat, 128)[:8]))
+    rows = jnp.concatenate([jnp.concatenate([high, middle], axis=1), jnp.concatenate([low, jnp.zeros_like(low)], axis=1)])
+    if slots > 256:
+        rows = jnp.concatenate([rows, jnp.zeros((TAIL, slots - 256), F32)], axis=1)
+    out_ref[0, len(images) * probes :, :] = rows.astype(BF16)
 
 
 def apply_first(near, far, levels, so_far, feat, group, keep, last=False):
@@ -174,11 +194,7 @@
         out_shape=outs,
         in_specs=[VMEM] * len(arrays),
         out_specs=[VMEM] * len(outs),
-        scratch_shapes=[
-            pltpu.VMEM((feature_rows(feat), wide), BF16),
-            pltpu.VMEM((probes, wide), BF16),
-            pltpu.VMEM((probes, copies * slots), F32),
-        ],
+        scratch_shapes=[pltpu.VMEM((probes, copies * slots), F32)],
         compiler_params=pltpu.CompilerParams(vmem_limit_bytes=(16 if keep else 40) * 2**20),
         cost_estimate=pl.CostEstimate(
             flops=2 * copies * slots * len(far) * far[0].shape[0] * slots * 256,
@@ -196,48 +212,40 @@
     points, images, refs = refs[:PIECES], refs[PIECES : 2 * PIECES], refs[2 * PIECES :]
     if keep:
         kept, refs = refs[:PIECES], refs[PIECES:]
-    (partial_ref, solution_ref, residual_ref, own_dir_ref, own_image_ref, norm_ref, product_ref, dirs_ref, scale_ref) = refs[:9]
+    (partial_ref, solution_ref, residual_ref, own_dir_ref, own_image_ref, norm_ref, product_ref, scale_ref) = refs[:8]
     if not keep:
-        right_ref, left_ref = refs[9:]
+        right_ref = refs[8]
     slots, probes = images[0].shape[2], own_image_in_ref.shape[0]
     pairs = list(zip(points, images))
     groups = images[0].shape[0]
 
-    def over_blocks(visit, start):
-        carry = start
-        for piece, (x_ref, _) in enumerate(pairs):
-            blocks = x_ref.shape[0]
-            carry = lax.fori_loop(0, blocks, functools.partial(visit, piece), carry, unroll=min(blocks, 8))
-        return carry
-
     def column(wide):
         return jnp.sum(wide, axis=1, keepdims=True)
 
-    per = 128 // TAIL
-    tails = [(piece, g) for piece in range(PIECES) for g in range(groups)]
-    norm_now = curve = jnp.zeros((probes, 1), F32)
-    for start in range(0, len(tails), per):
-        flat = [images[piece][g, copies * probes :, :128].astype(F32) for piece, g in tails[start : start + per]]
-        flat = jnp.concatenate(flat + [jnp.zeros((TAIL, 128), F32)] * (per - len(flat)), axis=0).T[:probes]
-        for at in range(min(per, len(tails) - start)):
-            norm_now = norm_now + column(flat[:, TAIL * at : TAIL * at + 3])
-            curve = curve + column(flat[:, TAIL * at + 3 : TAIL * at + 6])
-            scale_ref[start + at] = jnp.broadcast_to(flat[:, TAIL * at + 6 : TAIL * at + 7], (probes, 128))
+    tails = []
+    for w_ref in images:
+        for g in range(groups):
+            parts = w_ref[g, copies * probes :, :].astype(F32)
+            tails.append(parts[:8, :128] + parts[:8, 128:256] + parts[8:, :128])
+    norm_now, curve = (sum(tail[at : at + 1] for tail in tails) for at in range(2))
     step_size = norm_now / curve
-    for start in range(len(tails)):
-        scale_ref[start] = step_size / scale_ref[start]
+    norm_next = jnp.zeros_like(norm_now)
+    guesses = [tail[5:6] for tail in tails]
+    for tail, guess in zip(tails, guesses):
+        apart = guess - step_size
+        norm_next = norm_next + (tail[2:3] + apart * (2.0 * tail[3:4] + apart * tail[4:5]))
+    few = jnp.concatenate([step_size, norm_next / norm_now, norm_next, jnp.zeros((5, 128), F32)], axis=0)
+    for start in range(0, len(guesses), 120):
+        some = guesses[start : start + 120]
+        columns = turned(jnp.concatenate([few] + [step_size / guess for guess in some], axis=0), 128)[:probes]
+        for at in range(len(some)):
+            scale_ref[start + at] = jnp.broadcast_to(columns[:, at + 8 : at + 9], (probes, 128))
+    step_size, ratio, norm_next = (columns[:, at : at + 1] for at in range(3))
 
     def residual_of(piece, b):
         first = points[piece][b, 2 * feat :, :].astype(F32)
         sent = images[piece][b // copies, pl.ds(pl.multiple_of(b % copies * probes, probes), probes), :].astype(F32)
         return first + scale_ref[piece * groups + b // copies][:, :1] * (sent - first), first
-
-    def next_sum(piece, b, norm):
-        residual, _ = residual_of(piece, b)
-        return norm + residual * residual
-
-    norm_next = column(over_blocks(next_sum, jnp.zeros((probes, slots), F32)))
-    ratio = norm_next / norm_now
 
     def direct(piece, b):
         residual, first = residual_of(piece, b)
@@ -250,58 +258,61 @@
     solution_ref[...] = step_size * first
     residual_ref[...] = residual
     own_dir_ref[...] = own_direction.astype(F32)
-    product_ref[...] = jnp.zeros_like(product_ref)
     if not keep:
         fill_right(points[0], levels_ref, right_ref, feat)
-    for piece, (x_ref, _) in enumerate(pairs):
-
-        def step(g, carry, piece=piece, x_ref=x_ref):
-            for b in range(group):
-                place = slice(b * slots, (b + 1) * slots)
-                dirs_ref[:, place] = direct(piece, g * group + b)
-            if piece == 0:
-
-                @pl.when(g == 0)
-                def own_block():
-                    dirs_ref[:, :slots] = own_direction
-
-            for b in range(group):
-                place = slice(b * slots, (b + 1) * slots)
-                if not keep:
-                    left_ref[:, place] = features(x_ref[g * group + b, : 2 * feat, :], None, True)
-            block = kept[piece][g] if keep else entries(left_ref[...], right_ref[...])
-            product_ref[...] += jnp.dot(dirs_ref[...], block, preferred_element_type=F32)
+
+    def step(piece, g):
+        directions = [direct(piece, g * group + b) for b in range(group)]
+        if piece == 0:
+            directions[0] = jnp.where(g == 0, own_direction, directions[0])
+        if keep:
+            block = kept[piece][g]
+        else:
+            blocks = [points[piece][g * group + b, : 2 * feat, :] for b in range(group)]
+            left = jnp.concatenate([features(block, None, True) for block in blocks], axis=1)
+            block = entries(left, right_ref[...])
+        return jnp.dot(jnp.concatenate(directions, axis=1), block, preferred_element_type=F32)
+
+    steps = points[0].shape[0] // group
+    if steps == 1:
+        product = sum(step(piece, 0) for piece in range(PIECES))
+    else:
+        product_ref[...] = jnp.zeros_like(product_ref)
+
+        def add(piece, g, carry):
+            product_ref[...] += step(piece, g)
             return carry
 
-        lax.fori_loop(0, x_ref.shape[0] // group, step, 0)
+        for piece in range(PIECES):
+            lax.fori_loop(0, steps, functools.partial(add, piece), 0)
+        product = product_ref[...]
 
     curve = jnp.zeros((probes, slots), F32)
     for b in range(copies):
         direction = (direct(0, b) if b else own_direction).astype(F32)
-        image = product_ref[:, b * slots : (b + 1) * slots] + levels_ref[1:2, :] * direction
+        image = product[:, b * slots : (b + 1) * slots] + levels_ref[1:2, :] * direction
         curve = curve + direction * image
         if b == 0:
             own_image_ref[...] = image
     lane = lax.broadcasted_iota(jnp.int32, (probes, 128), 1)
     flat = jnp.where(lane == 0, column(curve), 0.0)
-    partial_ref[...] = jnp.concatenate([flat, jnp.zeros((128 - probes, 128), F32)], axis=0).T[:8]
+    partial_ref[...] = turned(flat, 128)[:8]
     norm_ref[...] = jnp.broadcast_to(norm_next, norm_ref.shape)
 
 
 def second(levels, own, own_image, points, images, kept, copies, feat, group):
     keep = kept is not None
     slots, probes = own_image.shape[1], own_image.shape[0]
-    one, small, wide = pltpu.VMEM((probes, slots), F32), pltpu.VMEM((probes, 128), F32), group * slots
+    one, small = pltpu.VMEM((probes, slots), F32), pltpu.VMEM((probes, 128), F32)
     scratch = [
         pltpu.VMEM((probes, copies * slots), F32),
-        pltpu.VMEM((probes, wide), BF16),
         pltpu.VMEM((PIECES * images[0].shape[0], probes, 128), F32),
     ]
     arrays = [levels, own, own_image, *points, *images, *(kept or ())]
     if keep:
         arrays = [stay(array) for array in arrays]
     else:
-        scratch += [pltpu.VMEM((feature_rows(feat), copies * slots), BF16), pltpu.VMEM((feature_rows(feat), wide), BF16)]
+        scratch.append(pltpu.VMEM((feature_rows(feat), copies * slots), BF16))
     return pl.pallas_call(
         functools.partial(second_kernel, feat, group, keep, copies),
         out_shape=[pltpu.VMEM((8, 128), F32), one, one, one, one, small],
@@ -314,7 +325,7 @@
 
 def finish_kernel(curve_ref, norm_ref, solution_ref, residual_ref, direction_ref, image_ref, out_ref, left_ref):
     probes = norm_ref.shape[0]
-    curve = jnp.concatenate([curve_ref[...], jnp.zeros((120, 128), F32)], axis=0).T[:probes, :1]
+    curve = turned(curve_ref[...], 128)[:probes, :1]
     step_size = norm_ref[:, :1] / curve
     out_ref[...] = solution_ref[...] + step_size * direction_ref[...]
     left_ref[...] = residual_ref[...] - step_size * image_ref[...]
@@ -360,17 +371,18 @@
     beside, up, over = (swap(held, bit, count) for bit in (core, one, two))
     kept_0, product = first(near, [held, beside], levels, None)
     up, product = lax.optimization_barrier((up, product))
-    corner, up_beside = swap(up, two, count), swap(up, core, count)
+    corner = swap(up, two, count)
+    up_beside = swap(up, core, count)
     kept_1, product = first(near, [up], levels, product)
-    over, product = lax.optimization_barrier((over, product))
     over_beside = swap(over, core, count)
     kept_2, product = first(near, [up_beside, over], levels, product)
+    kept_3, product = first(near, [over_beside], levels, product)
     corner, product = lax.optimization_barrier((corner, product))
     corner_beside = swap(corner, core, count)
-    kept_3, product = first(near, [over_beside, corner], levels, product)
-    kept_4, (image, own_image) = first(near, [corner_beside], levels, product, last=True)
+    kept_4, product = first(near, [corner], levels, product)
+    kept_5, (image, own_image) = first(near, [corner_beside], levels, product, last=True)
     pieces = [held, beside, up, up_beside, over, over_beside, corner, corner_beside]
-    kept = [*kept_0, *kept_1, *kept_2, *kept_3, *kept_4]
+    kept = [*kept_0, *kept_1, *kept_2, *kept_3, *kept_4, *kept_5]
 
     held = gather(image, later[:-3], count)
     up, over, corner = (swap(held, bit, count) for bit in (one, two, one | two))

time: 49.1 us -> 48.1 us (0.980)
  waiting for transfers between devices: 13.8 us -> 13.1 us
    ppermute x21, waiting for transfers between devices: 13.8 us -> 13.1 us  [swap(): return lax.ppermute(array, AXES, [(i, i ^ bit) for i in range(count)])]
    pallas_call x5 -> x6, Pallas kernels: 8.36 us -> 8.58 us  [apply_first(): pl.pallas_call(functools.partial(apply_kernel, feat, group, keep, begin,...]
  transfers between devices with their start and end apart: 21 -> 21, of which waited for: 14 -> 13; matrix products, arithmetic and copies ran while one was open for 0% -> 0% of each run, Pallas kernels for 14% -> 15%
where the time goes in v7:
time: 48.1 us; the launch traced here: 47.9 us
  starting transfers between devices  18.3 us (38%)
  Pallas kernels  13.6 us (28%)
  waiting for transfers between devices  13.1 us (27%)
  between operations  2.69 us (6%)
    ppermute x21, starting transfers between devices, swap(): return lax.ppermute(array, AXES, [(i, i ^ bit) for i in range(count)])  18.3 us
    ppermute x21, waiting for transfers between devices, swap(): return lax.ppermute(array, AXES, [(i, i ^ bit) for i in range(count)])  13.1 us
    pallas_call x6, Pallas kernels, apply_first(): pl.pallas_call(functools.partial(apply_kernel, feat, group, keep, begin,...  8.58 us
    pallas_call x1, Pallas kernels, second(): pl.pallas_call(functools.partial(second_kernel, feat, group, keep, copies...  3.43 us
  transfers between devices with their start and end apart: 21, of which 13 were waited for; matrix products, arithmetic and copies ran while one was open for 0% of the time, Pallas kernels for 15%

profile of v7, /device:TPU:0, one launch (start us, length us, event | category | flops | bytes accessed | tf_op | source)
XLA Modules:
  0.0 47.9 jit_solution(7863282004476407505)
XLA Ops:
  1.3 0.8 %shard_map.77.own_ref = bf16[1,96,256]{2,1,0:T(8,128)(2,1)S(1)} custom-call(f32[16,256]{1,0:T(8,128)} %bitcast.5, f32[16]{0:T(128)} %inv_ref.1, f32[32,256]{1,0:T(8,128)} %bitcast.4, s32[1]{0:T(128)S(6)} %copy.10.count_ref), custom_call_target="tpu_custom_call" | custom-call | tf_op jit(solution)/shard_map/pallas_call | solution.py:77
  2.1 5.1 %collective-permute-start.2 = (bf16[1,96,256]{2,1,0:T(8,128)(2,1)S(1)}, bf16[1,96,256]{2,1,0:T(8,128)(2,1)S(1)}, u32[]{:S(2)}, u32[]{:S(2)}) collective-permute-start(bf16[1,96,256]{2,1,0:T(8,128)(2,1)S(1)} %shard_map.77.own_ref), channel_id=1, source_target_pairs={{0,24},{1,25},{2,26},{3,27},{4,28},{5,29},{6,30},{7,31},{8,16},{9,... | collective-permute-start | bytes 147464 | tf_op jit(solution)/shard_map/ppermute | solution.py:27
  7.2 0.0 collective-permute-start.1
  7.2 0.6 %collective-permute-start = (bf16[1,96,256]{2,1,0:T(8,128)(2,1)S(1)}, bf16[1,96,256]{2,1,0:T(8,128)(2,1)S(1)}, u32[]{:S(2)}, u32[]{:S(2)}) collective-permute-start(bf16[1,96,256]{2,1,0:T(8,128)(2,1)S(1)} %shard_map.77.own_ref), channel_id=1, source_target_pairs={{0,16},{1,17},{2,18},{3,19},{4,20},{5,21},{6,22},{7,23},{8,24},{9,... | collective-permute-start | bytes 147464 | tf_op jit(solution)/shard_map/ppermute | solution.py:27
  9.2 0.1 pad_maximum_fusion.1
  9.3 0.2 collective-permute-done.2
  9.5 1.8 %collective-permute-done.1 = bf16[1,96,256]{2,1,0:T(8,128)(2,1)S(1)} collective-permute-done((bf16[1,96,256]{2,1,0:T(8,128)(2,1)S(1)}, bf16[1,96,256]{2,1,0:T(8,128)(2,1)S(1)}, u32[]{:S(2)}, u32[]{:S(2)}) %collective-permute-start.1) | collective-permute-done | bytes 49184 | tf_op jit(solution)/shard_map/ppermute | solution.py:27
  11.3 1.2 %collective-permute-done = bf16[1,96,256]{2,1,0:T(8,128)(2,1)S(1)} collective-permute-done((bf16[1,96,256]{2,1,0:T(8,128)(2,1)S(1)}, bf16[1,96,256]{2,1,0:T(8,128)(2,1)S(1)}, u32[]{:S(2)}, u32[]{:S(2)}) %collective-permute-start) | collective-permute-done | bytes 49184 | tf_op jit(solution)/shard_map/ppermute | solution.py:27
  12.5 0.1 broadcast_in_dim.2.levels_ref
  12.6 0.1 collective-permute-start.4
  12.7 1.6 %collective-permute-start.3 = (bf16[4,64,256]{2,1,0:T(8,128)(2,1)S(1)}, bf16[4,64,256]{2,1,0:T(8,128)(2,1)S(1)}, u32[]{:S(2)}, u32[]{:S(2)}) collective-permute-start(bf16[4,64,256]{2,1,0:T(8,128)(2,1)S(1)} %slice.3.refs_0_), channel_id=1, source_target_pairs={{0,4},{1,5},{2,6},{3,7},{4,0},{5,1},{6,2},{7,3},{8,12},{9,13},{10,... | collective-permute-start | bytes 393224 | tf_op jit(solution)/shard_map/ppermute | solution.py:27
  14.3 1.5 %collective-permute-start.6 = (bf16[4,64,256]{2,1,0:T(8,128)(2,1)S(1)}, bf16[4,64,256]{2,1,0:T(8,128)(2,1)S(1)}, u32[]{:S(2)}, u32[]{:S(2)}) collective-permute-start(bf16[4,64,256]{2,1,0:T(8,128)(2,1)S(1)} %slice.3.refs_0_), channel_id=1, source_target_pairs={{0,2},{1,3},{2,0},{3,1},{4,6},{5,7},{6,4},{7,5},{8,10},{9,11},{10,... | collective-permute-start | bytes 393224 | tf_op jit(solution)/shard_map/ppermute | solution.py:27
  15.8 0.0 collective-permute-done.4.refs_1_
  15.8 2.0 %shard_map.78 = (bf16[1,1024,1024]{2,1,0:T(8,128)(2,1)S(1)}, bf16[1,1024,1024]{2,1,0:T(8,128)(2,1)S(1)}, f32[32,1024]{1,0:T(8,128)S(1)}, bf16[80,1024]{1,0:T(8,128)(2,1)S(1)}) custom-call(bf16[4,96,256]{2,1,0:T(8,128)(2,1)S(1)} %pad_maximum_fusion.near_ref, f32[2,256]{1,0:T(2,128)S(1)} %broadcast_in_dim.2.levels_ref, bf16[4,64,256]{2,1,0:T(8,128)(2,1)S(1)} %slice.3.refs_0_, ...), custom_call_target="tpu_custom_call" | custom-call | flops 1073741824 | bytes 262144 | tf_op jit(solution)/shard_map/pallas_call | solution.py:192
  17.8 0.8 %collective-permute-done.3.refs_0_.refs_2_ = bf16[4,64,256]{2,1,0:T(8,128)(2,1)S(1)} collective-permute-done((bf16[4,64,256]{2,1,0:T(8,128)(2,1)S(1)}, bf16[4,64,256]{2,1,0:T(8,128)(2,1)S(1)}, u32[]{:S(2)}, u32[]{:S(2)}) %collective-permute-start.3) | collective-permute-done | bytes 131104 | tf_op jit(solution)/shard_map/ppermute | solution.py:27
  18.6 0.0 collective-permute-start.8
  18.6 1.5 %collective-permute-start.5 = (bf16[4,64,256]{2,1,0:T(8,128)(2,1)S(1)}, bf16[4,64,256]{2,1,0:T(8,128)(2,1)S(1)}, u32[]{:S(2)}, u32[]{:S(2)}) collective-permute-start(bf16[4,64,256]{2,1,0:T(8,128)(2,1)S(1)} %collective-permute-done.3.refs_0_.refs_2_), channel_id=1, source_target_pairs={{0,2},{1,3},{2,0},{3,1},{4,6},{5,7},{6,4},{7,5},{8,10},{9,11},{10,... | collective-permute-start | bytes 393224 | tf_op jit(solution)/shard_map/ppermute | solution.py:27
  20.1 0.2 collective-permute-start.7
  20.3 1.1 %shard_map.79 = (bf16[1,1024,1024]{2,1,0:T(8,128)(2,1)S(1)}, f32[32,1024]{1,0:T(8,128)S(1)}) custom-call(bf16[4,96,256]{2,1,0:T(8,128)(2,1)S(1)} %pad_maximum_fusion.near_ref, f32[2,256]{1,0:T(2,128)S(1)} %broadcast_in_dim.2.levels_ref, bf16[4,64,256]{2,1,0:T(8,128)(2,1)S(1)} %collective-permute-done.3.refs_0_.refs_2_, ...), custom_call_target="tpu_custom_call" | custom-call | flops 536870912 | bytes 262144 | tf_op jit(solution)/shard_map/pallas_call | solution.py:192
  21.4 0.0 collective-permute-done.8.refs_0_.refs_3_
  21.4 2.0 %shard_map.80 = (bf16[1,1024,1024]{2,1,0:T(8,128)(2,1)S(1)}, bf16[1,1024,1024]{2,1,0:T(8,128)(2,1)S(1)}, f32[32,1024]{1,0:T(8,128)S(1)}) custom-call(bf16[4,96,256]{2,1,0:T(8,128)(2,1)S(1)} %pad_maximum_fusion.near_ref, f32[2,256]{1,0:T(2,128)S(1)} %broadcast_in_dim.2.levels_ref, bf16[4,64,256]{2,1,0:T(8,128)(2,1)S(1)} %collective-permute-done.8.refs_0_.refs_3_, ...), custom_call_target="tpu_custom_call" | custom-call | flops 1073741824 | bytes 262144 | tf_op jit(solution)/shard_map/pallas_call | solution.py:192
  23.4 0.0 collective-permute-done.7.refs_0_.refs_5_
  23.4 1.1 %shard_map.81 = (bf16[1,1024,1024]{2,1,0:T(8,128)(2,1)S(1)}, f32[32,1024]{1,0:T(8,128)S(1)}) custom-call(bf16[4,96,256]{2,1,0:T(8,128)(2,1)S(1)} %pad_maximum_fusion.near_ref, f32[2,256]{1,0:T(2,128)S(1)} %broadcast_in_dim.2.levels_ref, bf16[4,64,256]{2,1,0:T(8,128)(2,1)S(1)} %collective-permute-done.7.refs_0_.refs_5_, ...), custom_call_target="tpu_custom_call" | custom-call | flops 536870912 | bytes 262144 | tf_op jit(solution)/shard_map/pallas_call | solution.py:192
  24.5 0.0 collective-permute-done.5.refs_0_.refs_6_
  24.5 0.3 collective-permute-start.9
  24.8 1.1 %shard_map.82 = (bf16[1,1024,1024]{2,1,0:T(8,128)(2,1)S(1)}, f32[32,1024]{1,0:T(8,128)S(1)}) custom-call(bf16[4,96,256]{2,1,0:T(8,128)(2,1)S(1)} %pad_maximum_fusion.near_ref, f32[2,256]{1,0:T(2,128)S(1)} %broadcast_in_dim.2.levels_ref, bf16[4,64,256]{2,1,0:T(8,128)(2,1)S(1)} %collective-permute-done.5.refs_0_.refs_6_, ...), custom_call_target="tpu_custom_call" | custom-call | flops 536870912 | bytes 262144 | tf_op jit(solution)/shard_map/pallas_call | solution.py:192
  25.9 0.0 collective-permute-done.9.refs_0_.refs_7_
  25.9 1.4 %shard_map.83 = (bf16[1,1024,1024]{2,1,0:T(8,128)(2,1)S(1)}, bf16[1,144,256]{2,1,0:T(8,128)(2,1)S(1)}, f32[32,256]{1,0:T(8,128)S(1)}) custom-call(bf16[4,96,256]{2,1,0:T(8,128)(2,1)S(1)} %pad_maximum_fusion.near_ref, f32[2,256]{1,0:T(2,128)S(1)} %broadcast_in_dim.2.levels_ref, bf16[4,64,256]{2,1,0:T(8,128)(2,1)S(1)} %collective-permute-done.9.refs_0_.refs_7_, ...), custom_call_target="tpu_custom_call" | custom-call | flops 536870912 | bytes 262144 | tf_op jit(solution)/shard_map/pallas_call | solution.py:192
  27.3 2.4 %collective-permute-start.15 = (bf16[1,144,256]{2,1,0:T(8,128)(2,1)S(1)}, bf16[1,144,256]{2,1,0:T(8,128)(2,1)S(1)}, u32[]{:S(2)}, u32[]{:S(2)}) collective-permute-start(bf16[1,144,256]{2,1,0:T(8,128)(2,1)S(1)} %get-tuple-element.55.refs_8_), channel_id=1, source_target_pairs={{0,6},{1,7},{2,4},{3,5},{4,2},{5,3},{6,0},{7,1},{8,14},{9,15},{10,... | collective-permute-start | bytes 221192 | tf_op jit(solution)/shard_map/ppermute | solution.py:27
  29.8 0.6 %collective-permute-start.13 = (bf16[1,144,256]{2,1,0:T(8,128)(2,1)S(1)}, bf16[1,144,256]{2,1,0:T(8,128)(2,1)S(1)}, u32[]{:S(2)}, u32[]{:S(2)}) collective-permute-start(bf16[1,144,256]{2,1,0:T(8,128)(2,1)S(1)} %get-tuple-element.55.refs_8_), channel_id=1, source_target_pairs={{0,2},{1,3},{2,0},{3,1},{4,6},{5,7},{6,4},{7,5},{8,10},{9,11},{10,... | collective-permute-start | bytes 221192 | tf_op jit(solution)/shard_map/ppermute | solution.py:27
  30.3 0.5 %collective-permute-start.11 = (bf16[1,144,256]{2,1,0:T(8,128)(2,1)S(1)}, bf16[1,144,256]{2,1,0:T(8,128)(2,1)S(1)}, u32[]{:S(2)}, u32[]{:S(2)}) collective-permute-start(bf16[1,144,256]{2,1,0:T(8,128)(2,1)S(1)} %get-tuple-element.55.refs_8_), channel_id=1, source_target_pairs={{0,4},{1,5},{2,6},{3,7},{4,0},{5,1},{6,2},{7,3},{8,12},{9,13},{10,... | collective-permute-start | bytes 221192 | tf_op jit(solution)/shard_map/ppermute | solution.py:27
  30.8 0.0 collective-permute-start.10
  30.8 2.3 %collective-permute-done.15.refs_14_ = bf16[1,144,256]{2,1,0:T(8,128)(2,1)S(1)} collective-permute-done((bf16[1,144,256]{2,1,0:T(8,128)(2,1)S(1)}, bf16[1,144,256]{2,1,0:T(8,128)(2,1)S(1)}, u32[]{:S(2)}, u32[]{:S(2)}) %collective-permute-start.15) | collective-permute-done | bytes 73760 | tf_op jit(solution)/shard_map/ppermute | solution.py:27
  33.1 1.2 %collective-permute-done.13.refs_12_ = bf16[1,144,256]{2,1,0:T(8,128)(2,1)S(1)} collective-permute-done((bf16[1,144,256]{2,1,0:T(8,128)(2,1)S(1)}, bf16[1,144,256]{2,1,0:T(8,128)(2,1)S(1)}, u32[]{:S(2)}, u32[]{:S(2)}) %collective-permute-start.13) | collective-permute-done | bytes 73760 | tf_op jit(solution)/shard_map/ppermute | solution.py:27
  34.3 0.4 collective-permute-done.11.refs_10_
  34.7 0.2 collective-permute-start.12
  34.9 0.7 %collective-permute-done.14.refs_13_ = bf16[1,144,256]{2,1,0:T(8,128)(2,1)S(1)} collective-permute-done((bf16[1,144,256]{2,1,0:T(8,128)(2,1)S(1)}, bf16[1,144,256]{2,1,0:T(8,128)(2,1)S(1)}, u32[]{:S(2)}, u32[]{:S(2)}) %collective-permute-start.14) | collective-permute-done | bytes 73760 | tf_op jit(solution)/shard_map/ppermute | solution.py:27
  35.6 0.4 collective-permute-done.12.refs_11_
  36.0 3.4 %shard_map.84 = (f32[8,128]{1,0:T(8,128)S(1)}, f32[32,256]{1,0:T(8,128)S(1)}, f32[32,256]{1,0:T(8,128)S(1)}, f32[32,256]{1,0:T(8,128)S(1)}, f32[32,256]{1,0:T(8,128)S(1)}, /*index=5*/f32[32,128]{1,0:T(8,128)S(1)}) custom-call(f32[2,256]{1,0:T(2,128)S(1)} %broadcast_in_dim.2.levels_ref, bf16[1,96,256]{2,1,0:T(8,128)(2,1)S(1)} %shard_map.77.own_ref, ...), custom_call_target="tpu_custom_call" | custom-call | tf_op jit(solution)/shard_map/pallas_call | solution.py:316
  39.4 0.2 collective-permute-start.17
  39.6 1.0 %collective-permute-done.17 = f32[8,128]{1,0:T(8,128)S(1)} collective-permute-done((f32[8,128]{1,0:T(8,128)S(1)}, f32[8,128]{1,0:T(8,128)S(1)}, u32[]{:S(2)}, u32[]{:S(2)}) %collective-permute-start.17) | collective-permute-done | bytes 4128 | tf_op jit(solution)/shard_map/ppermute | solution.py:27
  40.6 2.0 %collective-permute-start.20 = (f32[8,128]{1,0:T(8,128)S(1)}, f32[8,128]{1,0:T(8,128)S(1)}, u32[]{:S(2)}, u32[]{:S(2)}) collective-permute-start(f32[8,128]{1,0:T(8,128)S(1)} %add.12), channel_id=1, source_target_pairs={{0,6},{1,7},{2,4},{3,5},{4,2},{5,3},{6,0},{7,1},{8,14},{9,15},{10,... | collective-permute-start | bytes 12296 | tf_op jit(solution)/shard_map/ppermute | solution.py:27
  42.5 0.9 %collective-permute-start.19 = (f32[8,128]{1,0:T(8,128)S(1)}, f32[8,128]{1,0:T(8,128)S(1)}, u32[]{:S(2)}, u32[]{:S(2)}) collective-permute-start(f32[8,128]{1,0:T(8,128)S(1)} %add.12), channel_id=1, source_target_pairs={{0,4},{1,5},{2,6},{3,7},{4,0},{5,1},{6,2},{7,3},{8,12},{9,13},{10,... | collective-permute-start | bytes 12296 | tf_op jit(solution)/shard_map/ppermute | solution.py:27
  43.5 0.6 %collective-permute-start.18 = (f32[8,128]{1,0:T(8,128)S(1)}, f32[8,128]{1,0:T(8,128)S(1)}, u32[]{:S(2)}, u32[]{:S(2)}) collective-permute-start(f32[8,128]{1,0:T(8,128)S(1)} %add.12), channel_id=1, source_target_pairs={{0,2},{1,3},{2,0},{3,1},{4,6},{5,7},{6,4},{7,5},{8,10},{9,11},{10,... | collective-permute-start | bytes 12296 | tf_op jit(solution)/shard_map/ppermute | solution.py:27
  44.1 1.0 %collective-permute-done.20 = f32[8,128]{1,0:T(8,128)S(1)} collective-permute-done((f32[8,128]{1,0:T(8,128)S(1)}, f32[8,128]{1,0:T(8,128)S(1)}, u32[]{:S(2)}, u32[]{:S(2)}) %collective-permute-start.20) | collective-permute-done | bytes 4128 | tf_op jit(solution)/shard_map/ppermute | solution.py:27
  45.1 1.0 %collective-permute-done.19 = f32[8,128]{1,0:T(8,128)S(1)} collective-permute-done((f32[8,128]{1,0:T(8,128)S(1)}, f32[8,128]{1,0:T(8,128)S(1)}, u32[]{:S(2)}, u32[]{:S(2)}) %collective-permute-start.19) | collective-permute-done | bytes 4128 | tf_op jit(solution)/shard_map/ppermute | solution.py:27
  46.1 0.9 %collective-permute-done.18 = f32[8,128]{1,0:T(8,128)S(1)} collective-permute-done((f32[8,128]{1,0:T(8,128)S(1)}, f32[8,128]{1,0:T(8,128)S(1)}, u32[]{:S(2)}, u32[]{:S(2)}) %collective-permute-start.18) | collective-permute-done | bytes 4128 | tf_op jit(solution)/shard_map/ppermute | solution.py:27
  47.1 0.8 %shard_map.85 = (f32[32,256]{1,0:T(8,128)}, f32[32,256]{1,0:T(8,128)}) custom-call(f32[8,128]{1,0:T(8,128)S(1)} %add_add_fusion.curve_ref, f32[32,128]{1,0:T(8,128)S(1)} %get-tuple-element.65.norm_ref, f32[32,256]{1,0:T(8,128)S(1)} %get-tuple-element.66.solution_ref, f32[32,256]{1,0:T(8,128)S(1)} %get-tuple-element.67.residual_ref, ...), custom_call_target="tpu_custom_call" | custom-call | tf_op jit(solution)/shard_map/pallas_call | solution.py:396
  (9 shorter events, 0.1 us)
Async XLA Ops:
  2.1 7.4 %collective-permute-start.2 = (bf16[1,96,256]{2,1,0:T(8,128)(2,1)S(1)}, bf16[1,96,256]{2,1,0:T(8,128)(2,1)S(1)}, u32[]{:S(2)}, u32[]{:S(2)}) collective-permute-start(bf16[1,96,256]{2,1,0:T(8,128)(2,1)S(1)} %shard_map.77.own_ref), channel_id=1, source_target_pairs={{0,24},{1,25},{2,26},{3,27},{4,28},{5,29},{6,30},{7,31},{8,16},{9,... | collective-permute-start | bytes 147464 | tf_op jit(solution)/shard_map/ppermute | solution.py:27
  7.2 4.1 %collective-permute-start.1 = (bf16[1,96,256]{2,1,0:T(8,128)(2,1)S(1)}, bf16[1,96,256]{2,1,0:T(8,128)(2,1)S(1)}, u32[]{:S(2)}, u32[]{:S(2)}) collective-permute-start(bf16[1,96,256]{2,1,0:T(8,128)(2,1)S(1)} %shard_map.77.own_ref), channel_id=1, source_target_pairs={{0,8},{1,9},{2,10},{3,11},{4,12},{5,13},{6,14},{7,15},{8,0},{9,1},... | collective-permute-start | bytes 147464 | tf_op jit(solution)/shard_map/ppermute | solution.py:27
  7.2 5.3 %collective-permute-start = (bf16[1,96,256]{2,1,0:T(8,128)(2,1)S(1)}, bf16[1,96,256]{2,1,0:T(8,128)(2,1)S(1)}, u32[]{:S(2)}, u32[]{:S(2)}) collective-permute-start(bf16[1,96,256]{2,1,0:T(8,128)(2,1)S(1)} %shard_map.77.own_ref), channel_id=1, source_target_pairs={{0,16},{1,17},{2,18},{3,19},{4,20},{5,21},{6,22},{7,23},{8,24},{9,... | collective-permute-start | bytes 147464 | tf_op jit(solution)/shard_map/ppermute | solution.py:27
  12.6 3.2 %collective-permute-start.4 = (bf16[4,64,256]{2,1,0:T(8,128)(2,1)S(1)}, bf16[4,64,256]{2,1,0:T(8,128)(2,1)S(1)}, u32[]{:S(2)}, u32[]{:S(2)}) collective-permute-start(bf16[4,64,256]{2,1,0:T(8,128)(2,1)S(1)} %slice.3.refs_0_), channel_id=1, source_target_pairs={{0,1},{1,0},{2,3},{3,2},{4,5},{5,4},{6,7},{7,6},{8,9},{9,8},{10,11... | collective-permute-start | bytes 393224 | tf_op jit(solution)/shard_map/ppermute | solution.py:27
  12.7 5.9 %collective-permute-start.3 = (bf16[4,64,256]{2,1,0:T(8,128)(2,1)S(1)}, bf16[4,64,256]{2,1,0:T(8,128)(2,1)S(1)}, u32[]{:S(2)}, u32[]{:S(2)}) collective-permute-start(bf16[4,64,256]{2,1,0:T(8,128)(2,1)S(1)} %slice.3.refs_0_), channel_id=1, source_target_pairs={{0,4},{1,5},{2,6},{3,7},{4,0},{5,1},{6,2},{7,3},{8,12},{9,13},{10,... | collective-permute-start | bytes 393224 | tf_op jit(solution)/shard_map/ppermute | solution.py:27
  14.3 5.8 %collective-permute-start.6 = (bf16[4,64,256]{2,1,0:T(8,128)(2,1)S(1)}, bf16[4,64,256]{2,1,0:T(8,128)(2,1)S(1)}, u32[]{:S(2)}, u32[]{:S(2)}) collective-permute-start(bf16[4,64,256]{2,1,0:T(8,128)(2,1)S(1)} %slice.3.refs_0_), channel_id=1, source_target_pairs={{0,2},{1,3},{2,0},{3,1},{4,6},{5,7},{6,4},{7,5},{8,10},{9,11},{10,... | collective-permute-start | bytes 393224 | tf_op jit(solution)/shard_map/ppermute | solution.py:27
  18.6 2.8 %collective-permute-start.8 = (bf16[4,64,256]{2,1,0:T(8,128)(2,1)S(1)}, bf16[4,64,256]{2,1,0:T(8,128)(2,1)S(1)}, u32[]{:S(2)}, u32[]{:S(2)}) collective-permute-start(bf16[4,64,256]{2,1,0:T(8,128)(2,1)S(1)} %collective-permute-done.3.refs_0_.refs_2_), channel_id=1, source_target_pairs={{0,1},{1,0},{2,3},{3,2},{4,5},{5,4},{6,7},{7,6},{8,9},{9,8},{10,11... | collective-permute-start | bytes 393224 | tf_op jit(solution)/shard_map/ppermute | solution.py:27
  18.6 5.9 %collective-permute-start.5 = (bf16[4,64,256]{2,1,0:T(8,128)(2,1)S(1)}, bf16[4,64,256]{2,1,0:T(8,128)(2,1)S(1)}, u32[]{:S(2)}, u32[]{:S(2)}) collective-permute-start(bf16[4,64,256]{2,1,0:T(8,128)(2,1)S(1)} %collective-permute-done.3.refs_0_.refs_2_), channel_id=1, source_target_pairs={{0,2},{1,3},{2,0},{3,1},{4,6},{5,7},{6,4},{7,5},{8,10},{9,11},{10,... | collective-permute-start | bytes 393224 | tf_op jit(solution)/shard_map/ppermute | solution.py:27
  20.1 3.3 %collective-permute-start.7 = (bf16[4,64,256]{2,1,0:T(8,128)(2,1)S(1)}, bf16[4,64,256]{2,1,0:T(8,128)(2,1)S(1)}, u32[]{:S(2)}, u32[]{:S(2)}) collective-permute-start(bf16[4,64,256]{2,1,0:T(8,128)(2,1)S(1)} %collective-permute-done.6.refs_1_.refs_4_), channel_id=1, source_target_pairs={{0,1},{1,0},{2,3},{3,2},{4,5},{5,4},{6,7},{7,6},{8,9},{9,8},{10,11... | collective-permute-start | bytes 393224 | tf_op jit(solution)/shard_map/ppermute | solution.py:27
  24.5 1.4 %collective-permute-start.9 = (bf16[4,64,256]{2,1,0:T(8,128)(2,1)S(1)}, bf16[4,64,256]{2,1,0:T(8,128)(2,1)S(1)}, u32[]{:S(2)}, u32[]{:S(2)}) collective-permute-start(bf16[4,64,256]{2,1,0:T(8,128)(2,1)S(1)} %collective-permute-done.5.refs_0_.refs_6_), channel_id=1, source_target_pairs={{0,1},{1,0},{2,3},{3,2},{4,5},{5,4},{6,7},{7,6},{8,9},{9,8},{10,11... | collective-permute-start | bytes 393224 | tf_op jit(solution)/shard_map/ppermute | solution.py:27
  27.3 5.8 %collective-permute-start.15 = (bf16[1,144,256]{2,1,0:T(8,128)(2,1)S(1)}, bf16[1,144,256]{2,1,0:T(8,128)(2,1)S(1)}, u32[]{:S(2)}, u32[]{:S(2)}) collective-permute-start(bf16[1,144,256]{2,1,0:T(8,128)(2,1)S(1)} %get-tuple-element.55.refs_8_), channel_id=1, source_target_pairs={{0,6},{1,7},{2,4},{3,5},{4,2},{5,3},{6,0},{7,1},{8,14},{9,15},{10,... | collective-permute-start | bytes 221192 | tf_op jit(solution)/shard_map/ppermute | solution.py:27
  29.8 4.6 %collective-permute-start.13 = (bf16[1,144,256]{2,1,0:T(8,128)(2,1)S(1)}, bf16[1,144,256]{2,1,0:T(8,128)(2,1)S(1)}, u32[]{:S(2)}, u32[]{:S(2)}) collective-permute-start(bf16[1,144,256]{2,1,0:T(8,128)(2,1)S(1)} %get-tuple-element.55.refs_8_), channel_id=1, source_target_pairs={{0,2},{1,3},{2,0},{3,1},{4,6},{5,7},{6,4},{7,5},{8,10},{9,11},{10,... | collective-permute-start | bytes 221192 | tf_op jit(solution)/shard_map/ppermute | solution.py:27
  30.3 4.4 %collective-permute-start.11 = (bf16[1,144,256]{2,1,0:T(8,128)(2,1)S(1)}, bf16[1,144,256]{2,1,0:T(8,128)(2,1)S(1)}, u32[]{:S(2)}, u32[]{:S(2)}) collective-permute-start(bf16[1,144,256]{2,1,0:T(8,128)(2,1)S(1)} %get-tuple-element.55.refs_8_), channel_id=1, source_target_pairs={{0,4},{1,5},{2,6},{3,7},{4,0},{5,1},{6,2},{7,3},{8,12},{9,13},{10,... | collective-permute-start | bytes 221192 | tf_op jit(solution)/shard_map/ppermute | solution.py:27
  30.8 4.0 %collective-permute-start.10 = (bf16[1,144,256]{2,1,0:T(8,128)(2,1)S(1)}, bf16[1,144,256]{2,1,0:T(8,128)(2,1)S(1)}, u32[]{:S(2)}, u32[]{:S(2)}) collective-permute-start(bf16[1,144,256]{2,1,0:T(8,128)(2,1)S(1)} %get-tuple-element.55.refs_8_), channel_id=1, source_target_pairs={{0,1},{1,0},{2,3},{3,2},{4,5},{5,4},{6,7},{7,6},{8,9},{9,8},{10,11... | collective-permute-start | bytes 221192 | tf_op jit(solution)/shard_map/ppermute | solution.py:27
  33.1 1.7 %collective-permute-start.16 = (bf16[1,144,256]{2,1,0:T(8,128)(2,1)S(1)}, bf16[1,144,256]{2,1,0:T(8,128)(2,1)S(1)}, u32[]{:S(2)}, u32[]{:S(2)}) collective-permute-start(bf16[1,144,256]{2,1,0:T(8,128)(2,1)S(1)} %collective-permute-done.15.refs_14_), channel_id=1, source_target_pairs={{0,1},{1,0},{2,3},{3,2},{4,5},{5,4},{6,7},{7,6},{8,9},{9,8},{10,11... | collective-permute-start | bytes 221192 | tf_op jit(solution)/shard_map/ppermute | solution.py:27
  34.3 1.3 %collective-permute-start.14 = (bf16[1,144,256]{2,1,0:T(8,128)(2,1)S(1)}, bf16[1,144,256]{2,1,0:T(8,128)(2,1)S(1)}, u32[]{:S(2)}, u32[]{:S(2)}) collective-permute-start(bf16[1,144,256]{2,1,0:T(8,128)(2,1)S(1)} %collective-permute-done.13.refs_12_), channel_id=1, source_target_pairs={{0,1},{1,0},{2,3},{3,2},{4,5},{5,4},{6,7},{7,6},{8,9},{9,8},{10,11... | collective-permute-start | bytes 221192 | tf_op jit(solution)/shard_map/ppermute | solution.py:27
  34.7 1.3 %collective-permute-start.12 = (bf16[1,144,256]{2,1,0:T(8,128)(2,1)S(1)}, bf16[1,144,256]{2,1,0:T(8,128)(2,1)S(1)}, u32[]{:S(2)}, u32[]{:S(2)}) collective-permute-start(bf16[1,144,256]{2,1,0:T(8,128)(2,1)S(1)} %collective-permute-done.11.refs_10_), channel_id=1, source_target_pairs={{0,1},{1,0},{2,3},{3,2},{4,5},{5,4},{6,7},{7,6},{8,9},{9,8},{10,11... | collective-permute-start | bytes 221192 | tf_op jit(solution)/shard_map/ppermute | solution.py:27
  39.4 1.2 %collective-permute-start.17 = (f32[8,128]{1,0:T(8,128)S(1)}, f32[8,128]{1,0:T(8,128)S(1)}, u32[]{:S(2)}, u32[]{:S(2)}) collective-permute-start(f32[8,128]{1,0:T(8,128)S(1)} %get-tuple-element.64), channel_id=1, source_target_pairs={{0,1},{1,0},{2,3},{3,2},{4,5},{5,4},{6,7},{7,6},{8,9},{9,8},{10,11... | collective-permute-start | bytes 12296 | tf_op jit(solution)/shard_map/ppermute | solution.py:27
  40.6 4.5 %collective-permute-start.20 = (f32[8,128]{1,0:T(8,128)S(1)}, f32[8,128]{1,0:T(8,128)S(1)}, u32[]{:S(2)}, u32[]{:S(2)}) collective-permute-start(f32[8,128]{1,0:T(8,128)S(1)} %add.12), channel_id=1, source_target_pairs={{0,6},{1,7},{2,4},{3,5},{4,2},{5,3},{6,0},{7,1},{8,14},{9,15},{10,... | collective-permute-start | bytes 12296 | tf_op jit(solution)/shard_map/ppermute | solution.py:27
  42.5 3.6 %collective-permute-start.19 = (f32[8,128]{1,0:T(8,128)S(1)}, f32[8,128]{1,0:T(8,128)S(1)}, u32[]{:S(2)}, u32[]{:S(2)}) collective-permute-start(f32[8,128]{1,0:T(8,128)S(1)} %add.12), channel_id=1, source_target_pairs={{0,4},{1,5},{2,6},{3,7},{4,0},{5,1},{6,2},{7,3},{8,12},{9,13},{10,... | collective-permute-start | bytes 12296 | tf_op jit(solution)/shard_map/ppermute | solution.py:27
  43.5 3.6 %collective-permute-start.18 = (f32[8,128]{1,0:T(8,128)S(1)}, f32[8,128]{1,0:T(8,128)S(1)}, u32[]{:S(2)}, u32[]{:S(2)}) collective-permute-start(f32[8,128]{1,0:T(8,128)S(1)} %add.12), channel_id=1, source_target_pairs={{0,2},{1,3},{2,0},{3,1},{4,6},{5,7},{6,4},{7,5},{8,10},{9,11},{10,... | collective-permute-start | bytes 12296 | tf_op jit(solution)/shard_map/ppermute | solution.py:27

commit v8 on v7

--- a/solution.py
+++ b/solution.py
@@ -15,6 +15,7 @@
 COPIES = 4
 PIECES = 8
 TAIL = 16
+LATE = 2
 F32, BF16 = jnp.float32, jnp.bfloat16
 VMEM = pl.BlockSpec(memory_space=pltpu.VMEM)
 
@@ -30,6 +31,11 @@
 def two_parts(wide):
     high = wide.astype(BF16)
     return high, (wide - high.astype(F32)).astype(BF16)
+
+
+def swap_apart(array, bits, count):
+    one, two, core = bits
+    return lax.ppermute(array, AXES, [(i, i ^ (one | two if i & core else one)) for i in range(count)])
 
 
 def three_parts(wide):
@@ -99,23 +105,18 @@
     return jnp.exp2(powers).astype(BF16)
 
 
-def apply_kernel(feat, group, keep, begin, last, count, near_ref, levels_ref, *refs):
+def apply_kernel(feat, group, keep, begin, last, count, earlier, near_ref, levels_ref, *refs):
     far, refs = refs[:count], refs[count:]
     if begin:
         right_ref, refs = refs[-2], refs[:-2] + refs[-1:]
+        fill_right(near_ref, levels_ref, right_ref, feat)
     else:
-        right_ref, so_far_ref, refs = refs[0], refs[1], refs[2:]
+        right_ref, refs = refs[0], refs[1:]
+    sum_ref, refs = refs[-1], refs[:-1]
+    before, refs = refs[:earlier], refs[earlier:]
     kept, refs = (refs[:count], refs[count:]) if keep else ((), refs)
-    own_ref = None
-    if last:
-        own_ref, refs = refs[1], refs[:1] + refs[2:]
-    out_ref, sum_ref = refs
+    products, refs = refs[: count if keep else 1 - last], refs[count if keep else 1 - last :]
     slots, probes = near_ref.shape[2], sum_ref.shape[0]
-    if begin:
-        fill_right(near_ref, levels_ref, right_ref, feat)
-        product = jnp.zeros(sum_ref.shape, F32)
-    else:
-        product = so_far_ref[...]
 
     def step(piece, g):
         blocks = [far[piece][g * group + b] for b in range(group)]
@@ -127,11 +128,15 @@
         return jnp.dot(directions, block, preferred_element_type=F32)
 
     steps = far[0].shape[0] // group
-    if steps == 1:
-        for piece in range(count):
-            product = product + step(piece, 0)
+    if keep:
+        done = [step(piece, 0) for piece in range(count)]
+        for product_ref, product in zip(products, done):
+            product_ref[...] = product
+        if not last:
+            return
+        product = sum([before_ref[...] for before_ref in before], sum(done))
     else:
-        sum_ref[...] = product
+        sum_ref[...] = sum([before_ref[...] for before_ref in before], jnp.zeros(sum_ref.shape, F32))
 
         def add(piece, g, carry):
             sum_ref[...] += step(piece, g)
@@ -140,9 +145,10 @@
         for piece in range(count):
             lax.fori_loop(0, steps, functools.partial(add, piece), 0)
         product = sum_ref[...]
-    if not last:
-        out_ref[...] = product
-        return
+        if not last:
+            products[0][...] = product
+            return
+    out_ref, own_ref = refs
     images, rights = [], []
     norm = curve = jnp.zeros((probes, slots), F32)
     for b in range(near_ref.shape[0]):
@@ -175,56 +181,40 @@
     out_ref[0, len(images) * probes :, :] = rows.astype(BF16)
 
 
-def apply_first(near, far, levels, so_far, feat, group, keep, last=False):
+def apply_first(near, far, levels, right, products, feat, group, keep, last=False):
     copies, slots, probes = near.shape[0], near.shape[2], far[0].shape[1] - 2 * feat
-    wide, steps, begin = group * slots, far[0].shape[0] // group, so_far is None
-    outs = [pltpu.VMEM((probes, copies * slots), F32)]
+    wide, steps, begin = group * slots, far[0].shape[0] // group, right is None
+    product = pltpu.VMEM((probes, copies * slots), F32)
+    outs = [product] * (len(far) if keep else 1 - last)
+    if keep:
+        outs = [pltpu.VMEM((steps, wide, copies * slots), BF16)] * len(far) + outs
     if last:
-        outs = [pltpu.VMEM((1, copies * probes + TAIL, slots), BF16)]
-        outs = outs + [pltpu.VMEM((probes, slots), F32)]
-    if keep:
-        outs = [pltpu.VMEM((steps, wide, copies * slots), BF16)] * len(far) + outs
+        outs = outs + [pltpu.VMEM((1, copies * probes + TAIL, slots), BF16), pltpu.VMEM((probes, slots), F32)]
     if begin:
         outs = outs + [pltpu.VMEM((feature_rows(feat), copies * slots), BF16)]
-    arrays = [near, levels, *far, *([] if begin else so_far)]
+    before = products if last or not keep else products[-1:]
+    arrays = [near, levels, *far, *([] if begin else [right]), *before]
     if keep:
         arrays = [stay(array) for array in arrays]
     done = pl.pallas_call(
-        functools.partial(apply_kernel, feat, group, keep, begin, last, len(far)),
+        functools.partial(apply_kernel, feat, group, keep, begin, last, len(far), len(before)),
         out_shape=outs,
         in_specs=[VMEM] * len(arrays),
         out_specs=[VMEM] * len(outs),
         scratch_shapes=[pltpu.VMEM((probes, copies * slots), F32)],
         compiler_params=pltpu.CompilerParams(vmem_limit_bytes=(16 if keep else 40) * 2**20),
-        cost_estimate=pl.CostEstimate(
-            flops=2 * copies * slots * len(far) * far[0].shape[0] * slots * 256,
-            bytes_accessed=far[0].size * 4,
-            transcendentals=0,
-        ),
     )(*arrays)
-    kept, rest = (done[: len(far)], done[len(far) :]) if keep else ([None] * len(far), done)
-    if begin:
-        return kept, (rest[1], rest[0])
-    return kept, rest if last else (so_far[0], rest[0])
-
-
-def second_kernel(feat, group, keep, copies, levels_ref, own_ref, own_image_in_ref, *refs):
-    points, images, refs = refs[:PIECES], refs[PIECES : 2 * PIECES], refs[2 * PIECES :]
-    if keep:
-        kept, refs = refs[:PIECES], refs[PIECES:]
-    (partial_ref, solution_ref, residual_ref, own_dir_ref, own_image_ref, norm_ref, product_ref, scale_ref) = refs[:8]
-    if not keep:
-        right_ref = refs[8]
-    slots, probes = images[0].shape[2], own_image_in_ref.shape[0]
-    pairs = list(zip(points, images))
-    groups = images[0].shape[0]
-
-    def column(wide):
-        return jnp.sum(wide, axis=1, keepdims=True)
-
+    done = list(done)
+    kept, done = (done[: len(far)], done[len(far) :]) if keep else ([None] * len(far), done)
+    parts = len(far) if keep else 1 - last
+    products = products + done[:parts] if keep else done[:parts]
+    return kept, products, done[parts:] if last else done[parts] if begin else right
+
+
+def step_sums(images, copies, probes):
     tails = []
     for w_ref in images:
-        for g in range(groups):
+        for g in range(w_ref.shape[0]):
             parts = w_ref[g, copies * probes :, :].astype(F32)
             tails.append(parts[:8, :128] + parts[:8, 128:256] + parts[8:, :128])
     norm_now, curve = (sum(tail[at : at + 1] for tail in tails) for at in range(2))
@@ -235,12 +225,31 @@
         apart = guess - step_size
         norm_next = norm_next + (tail[2:3] + apart * (2.0 * tail[3:4] + apart * tail[4:5]))
     few = jnp.concatenate([step_size, norm_next / norm_now, norm_next, jnp.zeros((5, 128), F32)], axis=0)
+    scales = []
     for start in range(0, len(guesses), 120):
         some = guesses[start : start + 120]
         columns = turned(jnp.concatenate([few] + [step_size / guess for guess in some], axis=0), 128)[:probes]
-        for at in range(len(some)):
-            scale_ref[start + at] = jnp.broadcast_to(columns[:, at + 8 : at + 9], (probes, 128))
-    step_size, ratio, norm_next = (columns[:, at : at + 1] for at in range(3))
+        scales += [columns[:, at + 8 : at + 9] for at in range(len(some))]
+    return *(columns[:, at : at + 1] for at in range(3)), scales
+
+
+def second_kernel(feat, group, keep, copies, levels_ref, own_ref, own_image_in_ref, *refs):
+    points, images, refs = refs[:PIECES], refs[PIECES : 2 * PIECES], refs[2 * PIECES :]
+    if keep:
+        kept, refs = refs[:PIECES], refs[PIECES:]
+    (partial_ref, solution_ref, residual_ref, own_dir_ref, own_image_ref, norm_ref, product_ref, scale_ref) = refs[:8]
+    if not keep:
+        right_ref = refs[8]
+    slots, probes = images[0].shape[2], own_image_in_ref.shape[0]
+    pairs = list(zip(points, images))
+    groups = images[0].shape[0]
+
+    def column(wide):
+        return jnp.sum(wide, axis=1, keepdims=True)
+
+    step_size, ratio, norm_next, scales = step_sums(images, copies, probes)
+    for at, scale in enumerate(scales):
+        scale_ref[at] = jnp.broadcast_to(scale, (probes, 128))
 
     def residual_of(piece, b):
         first = points[piece][b, 2 * feat :, :].astype(F32)
@@ -300,6 +309,81 @@
     norm_ref[...] = jnp.broadcast_to(norm_next, norm_ref.shape)
 
 
+def sent_product(sent_ref, kept_ref, copies):
+    probes = (sent_ref.shape[1] - TAIL) // copies
+    sent = jnp.concatenate([sent_ref[0, b * probes : (b + 1) * probes, :] for b in range(copies)], axis=1)
+    return jnp.dot(sent, kept_ref[0], preferred_element_type=F32)
+
+
+def again_kernel(copies, count, *refs):
+    for sent_ref, kept_ref, out_ref in zip(refs[:count], refs[count : 2 * count], refs[2 * count :]):
+        out_ref[...] = sent_product(sent_ref, kept_ref, copies)
+
+
+def apply_again(sent, kept, copies):
+    outs = [pltpu.VMEM(((sent[0].shape[1] - TAIL) // copies, kept[0].shape[2]), F32)] * len(sent)
+    done = pl.pallas_call(
+        functools.partial(again_kernel, copies, len(sent)),
+        out_shape=outs,
+        in_specs=[VMEM] * (2 * len(sent)),
+        out_specs=[VMEM] * len(sent),
+        compiler_params=pltpu.CompilerParams(vmem_limit_bytes=16 * 2**20),
+    )(*[stay(array) for array in (*sent, *kept)])
+    return list(done)
+
+
+def combine_kernel(feat, copies, levels_ref, own_ref, own_image_in_ref, near_ref, kept_near_ref, *refs):
+    images, firsts, refs = refs[:PIECES], refs[PIECES : 2 * PIECES], refs[2 * PIECES :]
+    late = LATE
+    agains, kept, outs = refs[: PIECES - late], refs[PIECES - late : PIECES], refs[PIECES:]
+    partial_ref, solution_ref, residual_ref, own_dir_ref, own_image_ref, norm_ref = outs
+    slots, probes = images[0].shape[2], own_image_in_ref.shape[0]
+    agains = [again_ref[...] for again_ref in agains]
+    for image_ref, kept_ref in zip(images[PIECES - late :], kept):
+        agains.append(sent_product(image_ref, kept_ref, copies))
+    step_size, ratio, norm_next, scales = step_sums(images, copies, probes)
+    product = jnp.zeros((probes, copies * slots), F32)
+    for first_ref, again, scale in zip(firsts, agains, scales):
+        product = product + ((1.0 - scale + ratio) * first_ref[...] + scale * again)
+
+    first = own_ref[0, 2 * feat : 2 * feat + probes, :].astype(F32)
+    right = first + own_ref[0, 2 * feat + probes :, :].astype(F32)
+    residual = right - step_size * own_image_in_ref[...]
+    directions = [(residual + ratio * first).astype(BF16).astype(F32)]
+    solution_ref[...] = step_size * first
+    residual_ref[...] = residual
+    own_dir_ref[...] = directions[0]
+    for b in range(copies):
+        first = near_ref[b, 2 * feat :, :].astype(F32)
+        sent = images[0][0, b * probes : (b + 1) * probes, :].astype(F32)
+        directions.append((1.0 - scales[0] + ratio) * first + scales[0] * sent)
+    exact, formed = directions[:2]
+    product = product + jnp.dot((exact - formed).astype(BF16), kept_near_ref[0, :slots, :], preferred_element_type=F32)
+    curve = jnp.zeros((probes, slots), F32)
+    for b, direction in enumerate([exact] + directions[2:]):
+        image = product[:, b * slots : (b + 1) * slots] + levels_ref[1:2, :] * direction
+        curve = curve + direction * image
+        if b == 0:
+            own_image_ref[...] = image
+    lane = lax.broadcasted_iota(jnp.int32, (probes, 128), 1)
+    flat = jnp.where(lane == 0, jnp.sum(curve, axis=1, keepdims=True), 0.0)
+    partial_ref[...] = turned(flat, 128)[:8]
+    norm_ref[...] = jnp.broadcast_to(norm_next, norm_ref.shape)
+
+
+def combine(levels, own, own_image, near, images, products, agains, kept, copies, feat):
+    probes, slots = own_image.shape
+    one, small = pltpu.VMEM((probes, slots), F32), pltpu.VMEM((probes, 128), F32)
+    arrays = [levels, own, own_image, near, kept[0], *images, *products, *agains, *kept[len(agains) :]]
+    return pl.pallas_call(
+        functools.partial(combine_kernel, feat, copies),
+        out_shape=[pltpu.VMEM((8, 128), F32), one, one, one, one, small],
+        in_specs=[VMEM] * len(arrays),
+        out_specs=[VMEM] * 6,
+        compiler_params=pltpu.CompilerParams(vmem_limit_bytes=16 * 2**20),
+    )(*[stay(array) for array in arrays])
+
+
 def second(levels, own, own_image, points, images, kept, copies, feat, group):
     keep = kept is not None
     slots, probes = own_image.shape[1], own_image.shape[0]
@@ -335,7 +419,7 @@
     for at in range(0, len(bits), 2):
         pair = bits[at : at + 2]
         flips = pair if len(pair) == 1 else [pair[0], pair[1], sum(pair)]
-        held = jnp.concatenate([held] + [swap(held, flip, count) for flip in flips], axis=0)
+        held = jnp.concatenate([held] + [swap(held, flip, count) for flip in reversed(flips)], axis=0)
     return held
 
 
@@ -343,7 +427,7 @@
     for at in range(0, len(bits), 2):
         pair = bits[at : at + 2]
         flips = pair if len(pair) == 1 else [pair[0], pair[1], sum(pair)]
-        held = sum([swap(held, flip, count) for flip in flips], held)
+        held = sum([swap(held, flip, count) for flip in reversed(flips)], held)
     return held
 
 
@@ -352,9 +436,9 @@
     probes = right_sides.shape[1]
     copies = COPIES
     while copies > 1 and (copies * PIECES > count or copies * count * slots * slots * 2 > KEEP_BYTES):
-        copies //= 2
-    keep = copies * count * slots * slots * 2 <= KEEP_BYTES
+        copies //= 4
     group = math.gcd(count // PIECES, 8)
+    keep = copies == group == count // PIECES and copies * count * slots * slots * 2 <= KEEP_BYTES
     bits = [1 << k for k in reversed(range(count.bit_length() - 1))]
     later = bits[copies.bit_length() - 1 :]
     one, two, core = bits[-3:]
@@ -369,29 +453,45 @@
     near = held[:copies]
     held = held[:, : 2 * feat + probes]
     beside, up, over = (swap(held, bit, count) for bit in (core, one, two))
-    kept_0, product = first(near, [held, beside], levels, None)
-    up, product = lax.optimization_barrier((up, product))
-    corner = swap(up, two, count)
-    up_beside = swap(up, core, count)
-    kept_1, product = first(near, [up], levels, product)
+    kept_0, products, near_features = first(near, [held, beside], levels, None, [])
+    up, products[-1] = lax.optimization_barrier((up, products[-1]))
+    corner, up_beside = swap(up, two, count), swap(up, core, count)
+    kept_1, products, _ = first(near, [up], levels, near_features, products)
+    over, products[-1] = lax.optimization_barrier((over, products[-1]))
     over_beside = swap(over, core, count)
-    kept_2, product = first(near, [up_beside, over], levels, product)
-    kept_3, product = first(near, [over_beside], levels, product)
-    corner, product = lax.optimization_barrier((corner, product))
+    kept_2, products, _ = first(near, [up_beside, over], levels, near_features, products)
+    corner, products[-1] = lax.optimization_barrier((corner, products[-1]))
     corner_beside = swap(corner, core, count)
-    kept_4, product = first(near, [corner], levels, product)
-    kept_5, (image, own_image) = first(near, [corner_beside], levels, product, last=True)
+    kept_3, products, _ = first(near, [over_beside, corner], levels, near_features, products)
+    kept_4, products, (message, own_image) = first(near, [corner_beside], levels, near_features, products, last=True)
     pieces = [held, beside, up, up_beside, over, over_beside, corner, corner_beside]
-    kept = [*kept_0, *kept_1, *kept_2, *kept_3, *kept_4, *kept_5]
-
-    held = gather(image, later[:-3], count)
-    up, over, corner = (swap(held, bit, count) for bit in (one, two, one | two))
-    beside, up_beside, over_beside, corner_beside = (swap(array, core, count) for array in (held, up, over, corner))
-    images = [held, beside, up, up_beside, over, over_beside, corner, corner_beside]
-    partial, solution, residual, direction, second_image, norm = second(
-        levels, own, own_image, pieces, images, kept if keep else None, copies, feat, group
-    )
-    partial = total(partial + swap(partial, core, count), later[:-1][::-1], count)
+    kept = [*kept_0, *kept_1, *kept_2, *kept_3, *kept_4]
+
+    held = gather(message, later[:-3], count)
+    beside, up, over, corner = (swap(held, bit, count) for bit in (core, one, two, one | two))
+    if keep:
+        corner_beside = swap(corner, core, count)
+        again_0 = apply_again([held, beside], kept[:2], copies)
+        over, up, again_0[0] = lax.optimization_barrier((over, up, again_0[0]))
+    else:
+        corner_beside = swap(corner, core, count)
+    up_beside, over_beside = (swap(array, core, count) for array in (up, over))
+    if keep:
+        again_1 = apply_again([corner, corner_beside], kept[6:], copies)
+        again_2 = apply_again([up, over], [kept[2], kept[4]], copies)
+        images = [held, beside, corner, corner_beside, up, over, up_beside, over_beside]
+        order = [0, 1, 6, 7, 2, 4, 3, 5]
+        kept, products = ([each[at] for at in order] for each in (kept, products))
+        agains = [*again_0, *again_1, *again_2]
+        done = combine(levels, own, own_image, pieces[0], images, products, agains, kept, copies, feat)
+    else:
+        images = [held, beside, up, up_beside, over, over_beside, corner, corner_beside]
+        done = second(levels, own, own_image, pieces, images, None, copies, feat, group)
+    partial, solution, residual, direction, second_image, norm = done
+    partial = partial + swap(partial, core, count)
+    apart = swap_apart(partial, bits[-3:], count)
+    partial = partial + swap(partial, two, count) + (apart + swap(apart, core, count))
+    partial = total(partial, later[:-3], count)
     done = jax.ShapeDtypeStruct((probes, slots), F32)
     solution, residual = pl.pallas_call(
         finish_kernel,

time: 48.1 us -> 45.9 us (0.954)
  waiting for transfers between devices: 13.1 us -> 11.6 us
  starting transfers between devices: 18.3 us -> 17.5 us
    ppermute x21 -> x20, waiting for transfers between devices: 13.1 us -> 10.6 us  [swap(): return lax.ppermute(array, AXES, [(i, i ^ bit) for i in range(count)])]
    ppermute x21 -> x20, starting transfers between devices: 18.3 us -> 16.4 us  [swap(): return lax.ppermute(array, AXES, [(i, i ^ bit) for i in range(count)])]
    ppermute x0 -> x1, starting transfers between devices: none -> 1.12 us  [swap_apart(): lax.ppermute(array, AXES, [(i, i ^ (one | two if i & core else one)) for...]
    ppermute x0 -> x1, waiting for transfers between devices: none -> 0.99 us  [swap_apart(): lax.ppermute(array, AXES, [(i, i ^ (one | two if i & core else one)) for...]
    pallas_call x1 -> x4, Pallas kernels: 3.43 us -> 3.63 us  [the longest x3 2.46 us: apply_again(): pl.pallas_call(functools.partial(again_kernel, copies, len(sent)), out_sh...]
    pallas_call x6 -> x5, Pallas kernels: 8.58 us -> 8.43 us  [apply_first(): pl.pallas_call(functools.partial(apply_kernel, feat, group, keep, begin,...]
  transfers between devices with their start and end apart: 21 -> 21, of which waited for: 13 -> 12; matrix products, arithmetic and copies ran while one was open for 0% -> 0% of each run, Pallas kernels for 15% -> 21%
where the time goes in v8:
time: 45.9 us; the launch traced here: 45.6 us
  starting transfers between devices  17.5 us (38%)
  Pallas kernels  13.7 us (30%)
  waiting for transfers between devices  11.6 us (25%)
  between operations  2.68 us (6%)
    ppermute x20, starting transfers between devices, swap(): return lax.ppermute(array, AXES, [(i, i ^ bit) for i in range(count)])  16.4 us
    ppermute x20, waiting for transfers between devices, swap(): return lax.ppermute(array, AXES, [(i, i ^ bit) for i in range(count)])  10.6 us
    pallas_call x5, Pallas kernels, apply_first(): pl.pallas_call(functools.partial(apply_kernel, feat, group, keep, begin,...  8.43 us
    pallas_call x3, Pallas kernels, apply_again(): pl.pallas_call(functools.partial(again_kernel, copies, len(sent)), out_sh...  2.46 us
    pallas_call x1, Pallas kernels, combine(): pl.pallas_call(functools.partial(combine_kernel, feat, copies), out_shape...  1.17 us
    ppermute x1, starting transfers between devices, swap_apart(): lax.ppermute(array, AXES, [(i, i ^ (one | two if i & core else one)) for...  1.12 us
    ppermute x1, waiting for transfers between devices, swap_apart(): lax.ppermute(array, AXES, [(i, i ^ (one | two if i & core else one)) for...  0.99 us
  transfers between devices with their start and end apart: 21, of which 12 were waited for; matrix products, arithmetic and copies ran while one was open for 0% of the time, Pallas kernels for 21%

profile of v8, /device:TPU:0, one launch (start us, length us, event | category | flops | bytes accessed | tf_op | source)
XLA Modules:
  0.0 45.6 jit_solution(942639299240538348)
XLA Ops:
  1.3 0.8 %shard_map.77.own_ref = bf16[1,96,256]{2,1,0:T(8,128)(2,1)S(1)} custom-call(f32[16,256]{1,0:T(8,128)} %bitcast.5, f32[16]{0:T(128)} %inv_ref.1, f32[32,256]{1,0:T(8,128)} %bitcast.4, s32[1]{0:T(128)S(6)} %copy.10.count_ref), custom_call_target="tpu_custom_call" | custom-call | tf_op jit(solution)/shard_map/pallas_call | solution.py:83
  2.1 5.1 %collective-permute-start = (bf16[1,96,256]{2,1,0:T(8,128)(2,1)S(1)}, bf16[1,96,256]{2,1,0:T(8,128)(2,1)S(1)}, u32[]{:S(2)}, u32[]{:S(2)}) collective-permute-start(bf16[1,96,256]{2,1,0:T(8,128)(2,1)S(1)} %shard_map.77.own_ref), channel_id=1, source_target_pairs={{0,24},{1,25},{2,26},{3,27},{4,28},{5,29},{6,30},{7,31},{8,16},{9,... | collective-permute-start | bytes 147464 | tf_op jit(solution)/shard_map/ppermute | solution.py:28
  7.2 0.0 collective-permute-start.1
  7.2 0.6 %collective-permute-start.2 = (bf16[1,96,256]{2,1,0:T(8,128)(2,1)S(1)}, bf16[1,96,256]{2,1,0:T(8,128)(2,1)S(1)}, u32[]{:S(2)}, u32[]{:S(2)}) collective-permute-start(bf16[1,96,256]{2,1,0:T(8,128)(2,1)S(1)} %shard_map.77.own_ref), channel_id=1, source_target_pairs={{0,16},{1,17},{2,18},{3,19},{4,20},{5,21},{6,22},{7,23},{8,24},{9,... | collective-permute-start | bytes 147464 | tf_op jit(solution)/shard_map/ppermute | solution.py:28
  9.2 0.1 pad_maximum_fusion.1
  9.3 0.2 collective-permute-done
  9.5 1.8 %collective-permute-done.1 = bf16[1,96,256]{2,1,0:T(8,128)(2,1)S(1)} collective-permute-done((bf16[1,96,256]{2,1,0:T(8,128)(2,1)S(1)}, bf16[1,96,256]{2,1,0:T(8,128)(2,1)S(1)}, u32[]{:S(2)}, u32[]{:S(2)}) %collective-permute-start.1) | collective-permute-done | bytes 49184 | tf_op jit(solution)/shard_map/ppermute | solution.py:28
  11.3 1.2 %collective-permute-done.2 = bf16[1,96,256]{2,1,0:T(8,128)(2,1)S(1)} collective-permute-done((bf16[1,96,256]{2,1,0:T(8,128)(2,1)S(1)}, bf16[1,96,256]{2,1,0:T(8,128)(2,1)S(1)}, u32[]{:S(2)}, u32[]{:S(2)}) %collective-permute-start.2) | collective-permute-done | bytes 49184 | tf_op jit(solution)/shard_map/ppermute | solution.py:28
  12.5 0.1 broadcast_in_dim.2.levels_ref
  12.6 0.1 collective-permute-start.4
  12.7 1.6 %collective-permute-start.3 = (bf16[4,64,256]{2,1,0:T(8,128)(2,1)S(1)}, bf16[4,64,256]{2,1,0:T(8,128)(2,1)S(1)}, u32[]{:S(2)}, u32[]{:S(2)}) collective-permute-start(bf16[4,64,256]{2,1,0:T(8,128)(2,1)S(1)} %slice.3.refs_0_.near_ref), channel_id=1, source_target_pairs={{0,4},{1,5},{2,6},{3,7},{4,0},{5,1},{6,2},{7,3},{8,12},{9,13},{10,... | collective-permute-start | bytes 393224 | tf_op jit(solution)/shard_map/ppermute | solution.py:28
  14.3 1.5 %collective-permute-start.7 = (bf16[4,64,256]{2,1,0:T(8,128)(2,1)S(1)}, bf16[4,64,256]{2,1,0:T(8,128)(2,1)S(1)}, u32[]{:S(2)}, u32[]{:S(2)}) collective-permute-start(bf16[4,64,256]{2,1,0:T(8,128)(2,1)S(1)} %slice.3.refs_0_.near_ref), channel_id=1, source_target_pairs={{0,2},{1,3},{2,0},{3,1},{4,6},{5,7},{6,4},{7,5},{8,10},{9,11},{10,... | collective-permute-start | bytes 393224 | tf_op jit(solution)/shard_map/ppermute | solution.py:28
  15.8 2.0 %shard_map.78 = (bf16[1,1024,1024]{2,1,0:T(8,128)(2,1)S(1)}, bf16[1,1024,1024]{2,1,0:T(8,128)(2,1)S(1)}, f32[32,1024]{1,0:T(8,128)S(1)}, f32[32,1024]{1,0:T(8,128)S(1)}, bf16[80,1024]{1,0:T(8,128)(2,1)S(1)}) custom-call(bf16[4,96,256]{2,1,0:T(8,128)(2,1)S(1)} %pad_maximum_fusion.near_ref, f32[2,256]{1,0:T(2,128)S(1)} %broadcast_in_dim.2.levels_ref, ...), custom_call_target="tpu_custom_call" | custom-call | tf_op jit(solution)/shard_map/pallas_call | solution.py:199
  17.7 0.9 %collective-permute-done.3.refs_0_ = bf16[4,64,256]{2,1,0:T(8,128)(2,1)S(1)} collective-permute-done((bf16[4,64,256]{2,1,0:T(8,128)(2,1)S(1)}, bf16[4,64,256]{2,1,0:T(8,128)(2,1)S(1)}, u32[]{:S(2)}, u32[]{:S(2)}) %collective-permute-start.3) | collective-permute-done | bytes 131104 | tf_op jit(solution)/shard_map/ppermute | solution.py:28
  18.6 1.5 %collective-permute-start.5 = (bf16[4,64,256]{2,1,0:T(8,128)(2,1)S(1)}, bf16[4,64,256]{2,1,0:T(8,128)(2,1)S(1)}, u32[]{:S(2)}, u32[]{:S(2)}) collective-permute-start(bf16[4,64,256]{2,1,0:T(8,128)(2,1)S(1)} %collective-permute-done.3.refs_0_), channel_id=1, source_target_pairs={{0,2},{1,3},{2,0},{3,1},{4,6},{5,7},{6,4},{7,5},{8,10},{9,11},{10,... | collective-permute-start | bytes 393224 | tf_op jit(solution)/shard_map/ppermute | solution.py:28
  20.1 1.1 %shard_map.79 = (bf16[1,1024,1024]{2,1,0:T(8,128)(2,1)S(1)}, f32[32,1024]{1,0:T(8,128)S(1)}) custom-call(bf16[4,96,256]{2,1,0:T(8,128)(2,1)S(1)} %pad_maximum_fusion.near_ref, f32[2,256]{1,0:T(2,128)S(1)} %broadcast_in_dim.2.levels_ref, bf16[4,64,256]{2,1,0:T(8,128)(2,1)S(1)} %collective-permute-done.3.refs_0_, ...), custom_call_target="tpu_custom_call" | custom-call | tf_op jit(solution)/shard_map/pallas_call | solution.py:199
  21.2 0.0 collective-permute-done.7.refs_1_
  21.2 0.3 collective-permute-start.9
  21.4 2.0 %shard_map.80 = (bf16[1,1024,1024]{2,1,0:T(8,128)(2,1)S(1)}, bf16[1,1024,1024]{2,1,0:T(8,128)(2,1)S(1)}, f32[32,1024]{1,0:T(8,128)S(1)}, f32[32,1024]{1,0:T(8,128)S(1)}) custom-call(bf16[4,96,256]{2,1,0:T(8,128)(2,1)S(1)} %pad_maximum_fusion.near_ref, f32[2,256]{1,0:T(2,128)S(1)} %broadcast_in_dim.2.levels_ref, ...), custom_call_target="tpu_custom_call" | custom-call | tf_op jit(solution)/shard_map/pallas_call | solution.py:199
  23.4 1.1 %collective-permute-done.5.refs_1_ = bf16[4,64,256]{2,1,0:T(8,128)(2,1)S(1)} collective-permute-done((bf16[4,64,256]{2,1,0:T(8,128)(2,1)S(1)}, bf16[4,64,256]{2,1,0:T(8,128)(2,1)S(1)}, u32[]{:S(2)}, u32[]{:S(2)}) %collective-permute-start.5) | collective-permute-done | bytes 131104 | tf_op jit(solution)/shard_map/ppermute | solution.py:28
  24.5 2.0 %shard_map.81 = (bf16[1,1024,1024]{2,1,0:T(8,128)(2,1)S(1)}, bf16[1,1024,1024]{2,1,0:T(8,128)(2,1)S(1)}, f32[32,1024]{1,0:T(8,128)S(1)}, f32[32,1024]{1,0:T(8,128)S(1)}) custom-call(bf16[4,96,256]{2,1,0:T(8,128)(2,1)S(1)} %pad_maximum_fusion.near_ref, f32[2,256]{1,0:T(2,128)S(1)} %broadcast_in_dim.2.levels_ref, ...), custom_call_target="tpu_custom_call" | custom-call | tf_op jit(solution)/shard_map/pallas_call | solution.py:199
  26.5 0.0 collective-permute-done.8.refs_0_
  26.5 1.5 %shard_map.82 = (bf16[1,1024,1024]{2,1,0:T(8,128)(2,1)S(1)}, f32[32,1024]{1,0:T(8,128)S(1)}, bf16[1,144,256]{2,1,0:T(8,128)(2,1)S(1)}, f32[32,256]{1,0:T(8,128)S(1)}) custom-call(bf16[4,96,256]{2,1,0:T(8,128)(2,1)S(1)} %pad_maximum_fusion.near_ref, f32[2,256]{1,0:T(2,128)S(1)} %broadcast_in_dim.2.levels_ref, ...), custom_call_target="tpu_custom_call" | custom-call | tf_op jit(solution)/shard_map/pallas_call | solution.py:199
  28.0 2.5 %collective-permute-start.11 = (bf16[1,144,256]{2,1,0:T(8,128)(2,1)S(1)}, bf16[1,144,256]{2,1,0:T(8,128)(2,1)S(1)}, u32[]{:S(2)}, u32[]{:S(2)}) collective-permute-start(bf16[1,144,256]{2,1,0:T(8,128)(2,1)S(1)} %get-tuple-element.70.refs_0_), channel_id=1, source_target_pairs={{0,6},{1,7},{2,4},{3,5},{4,2},{5,3},{6,0},{7,1},{8,14},{9,15},{10,... | collective-permute-start | bytes 221192 | tf_op jit(solution)/shard_map/ppermute | solution.py:28
  30.4 0.2 collective-permute-start.10
  30.7 0.5 %collective-permute-start.13 = (bf16[1,144,256]{2,1,0:T(8,128)(2,1)S(1)}, bf16[1,144,256]{2,1,0:T(8,128)(2,1)S(1)}, u32[]{:S(2)}, u32[]{:S(2)}) collective-permute-start(bf16[1,144,256]{2,1,0:T(8,128)(2,1)S(1)} %get-tuple-element.70.refs_0_), channel_id=1, source_target_pairs={{0,2},{1,3},{2,0},{3,1},{4,6},{5,7},{6,4},{7,5},{8,10},{9,11},{10,... | collective-permute-start | bytes 221192 | tf_op jit(solution)/shard_map/ppermute | solution.py:28
  31.2 0.5 %collective-permute-start.14 = (bf16[1,144,256]{2,1,0:T(8,128)(2,1)S(1)}, bf16[1,144,256]{2,1,0:T(8,128)(2,1)S(1)}, u32[]{:S(2)}, u32[]{:S(2)}) collective-permute-start(bf16[1,144,256]{2,1,0:T(8,128)(2,1)S(1)} %get-tuple-element.70.refs_0_), channel_id=1, source_target_pairs={{0,4},{1,5},{2,6},{3,7},{4,0},{5,1},{6,2},{7,3},{8,12},{9,13},{10,... | collective-permute-start | bytes 221192 | tf_op jit(solution)/shard_map/ppermute | solution.py:28
  31.7 1.9 %collective-permute-done.11.refs_0_.refs_2_ = bf16[1,144,256]{2,1,0:T(8,128)(2,1)S(1)} collective-permute-done((bf16[1,144,256]{2,1,0:T(8,128)(2,1)S(1)}, bf16[1,144,256]{2,1,0:T(8,128)(2,1)S(1)}, u32[]{:S(2)}, u32[]{:S(2)}) %collective-permute-start.11) | collective-permute-done | bytes 73760 | tf_op jit(solution)/shard_map/ppermute | solution.py:28
  33.6 0.0 collective-permute-start.12
  33.6 0.0 collective-permute-done.10.refs_1_
  33.6 0.8 %shard_map.83 = (f32[32,1024]{1,0:T(8,128)S(1)}, f32[32,1024]{1,0:T(8,128)S(1)}) custom-call(bf16[1,144,256]{2,1,0:T(8,128)(2,1)S(1)} %get-tuple-element.70.refs_0_, bf16[1,144,256]{2,1,0:T(8,128)(2,1)S(1)} %collective-permute-done.10.refs_1_, bf16[1,1024,1024]{2,1,0:T(8,128)(2,1)S(1)} %get-tuple-element.69.refs_2_.kept_near_ref, ...), custom_call_target="tpu_custom_call" | custom-call | tf_op jit(solution)/shard_map/pallas_call | solution.py:325
  34.5 0.7 %collective-permute-done.13.refs_1_.refs_5_ = bf16[1,144,256]{2,1,0:T(8,128)(2,1)S(1)} collective-permute-done((bf16[1,144,256]{2,1,0:T(8,128)(2,1)S(1)}, bf16[1,144,256]{2,1,0:T(8,128)(2,1)S(1)}, u32[]{:S(2)}, u32[]{:S(2)}) %collective-permute-start.13) | collective-permute-done | bytes 73760 | tf_op jit(solution)/shard_map/ppermute | solution.py:28
  35.2 0.3 collective-permute-done.14.refs_0_.refs_4_
  35.5 0.0 collective-permute-start.15
  35.5 0.5 %collective-permute-start.16 = (bf16[1,144,256]{2,1,0:T(8,128)(2,1)S(1)}, bf16[1,144,256]{2,1,0:T(8,128)(2,1)S(1)}, u32[]{:S(2)}, u32[]{:S(2)}) collective-permute-start(bf16[1,144,256]{2,1,0:T(8,128)(2,1)S(1)} %collective-permute-done.13.refs_1_.refs_5_), channel_id=1, source_target_pairs={{0,1},{1,0},{2,3},{3,2},{4,5},{5,4},{6,7},{7,6},{8,9},{9,8},{10,11... | collective-permute-start | bytes 221192 | tf_op jit(solution)/shard_map/ppermute | solution.py:28
  36.0 0.8 %shard_map.85 = (f32[32,1024]{1,0:T(8,128)S(1)}, f32[32,1024]{1,0:T(8,128)S(1)}) custom-call(bf16[1,144,256]{2,1,0:T(8,128)(2,1)S(1)} %collective-permute-done.14.refs_0_.refs_4_, bf16[1,144,256]{2,1,0:T(8,128)(2,1)S(1)} %collective-permute-done.13.refs_1_.refs_5_, bf16[1,1024,1024]{2,1,0:T(8,128)(2,1)S(1)} %get-tuple-element.82.refs_2_, ...), custom_call_target="tpu_custom_call" | custom-call | tf_op jit(solution)/shard_map/pallas_call | solution.py:325
  36.9 0.0 collective-permute-done.12.refs_1_.refs_3_
  36.9 0.8 %shard_map.84 = (f32[32,1024]{1,0:T(8,128)S(1)}, f32[32,1024]{1,0:T(8,128)S(1)}) custom-call(bf16[1,144,256]{2,1,0:T(8,128)(2,1)S(1)} %collective-permute-done.11.refs_0_.refs_2_, bf16[1,144,256]{2,1,0:T(8,128)(2,1)S(1)} %collective-permute-done.12.refs_1_.refs_3_, bf16[1,1024,1024]{2,1,0:T(8,128)(2,1)S(1)} %get-tuple-element.78.refs_2_, ...), custom_call_target="tpu_custom_call" | custom-call | tf_op jit(solution)/shard_map/pallas_call | solution.py:325
  37.7 0.0 collective-permute-done.16.refs_7_
  37.7 1.2 %shard_map.86 = (f32[8,128]{1,0:T(8,128)S(1)}, f32[32,256]{1,0:T(8,128)S(1)}, f32[32,256]{1,0:T(8,128)S(1)}, f32[32,256]{1,0:T(8,128)S(1)}, f32[32,256]{1,0:T(8,128)S(1)}, /*index=5*/f32[32,128]{1,0:T(8,128)S(1)}) custom-call(f32[2,256]{1,0:T(2,128)S(1)} %broadcast_in_dim.2.levels_ref, bf16[1,96,256]{2,1,0:T(8,128)(2,1)S(1)} %shard_map.77.own_ref, ...), custom_call_target="tpu_custom_call" | custom-call | tf_op jit(solution)/shard_map/pallas_call | solution.py:378
  38.9 0.0 collective-permute-start.17
  38.9 1.2 %collective-permute-done.17 = f32[8,128]{1,0:T(8,128)S(1)} collective-permute-done((f32[8,128]{1,0:T(8,128)S(1)}, f32[8,128]{1,0:T(8,128)S(1)}, u32[]{:S(2)}, u32[]{:S(2)}) %collective-permute-start.17) | collective-permute-done | bytes 4128 | tf_op jit(solution)/shard_map/ppermute | solution.py:28
  40.1 1.1 %collective-permute-start.19 = (f32[8,128]{1,0:T(8,128)S(1)}, f32[8,128]{1,0:T(8,128)S(1)}, u32[]{:S(2)}, u32[]{:S(2)}) collective-permute-start(f32[8,128]{1,0:T(8,128)S(1)} %add.12), channel_id=1, source_target_pairs={{0,4},{1,7},{2,6},{3,5},{4,0},{5,3},{6,2},{7,1},{8,12},{9,15},{10,... | collective-permute-start | bytes 12296 | tf_op jit(solution)/shard_map/ppermute | solution.py:38
  41.2 1.5 %collective-permute-start.18 = (f32[8,128]{1,0:T(8,128)S(1)}, f32[8,128]{1,0:T(8,128)S(1)}, u32[]{:S(2)}, u32[]{:S(2)}) collective-permute-start(f32[8,128]{1,0:T(8,128)S(1)} %add.12), channel_id=1, source_target_pairs={{0,2},{1,3},{2,0},{3,1},{4,6},{5,7},{6,4},{7,5},{8,10},{9,11},{10,... | collective-permute-start | bytes 12296 | tf_op jit(solution)/shard_map/ppermute | solution.py:28
  42.7 1.0 %collective-permute-done.19 = f32[8,128]{1,0:T(8,128)S(1)} collective-permute-done((f32[8,128]{1,0:T(8,128)S(1)}, f32[8,128]{1,0:T(8,128)S(1)}, u32[]{:S(2)}, u32[]{:S(2)}) %collective-permute-start.19) | collective-permute-done | bytes 4128 | tf_op jit(solution)/shard_map/ppermute | solution.py:38
  43.7 1.1 %collective-permute-done.18 = f32[8,128]{1,0:T(8,128)S(1)} collective-permute-done((f32[8,128]{1,0:T(8,128)S(1)}, f32[8,128]{1,0:T(8,128)S(1)}, u32[]{:S(2)}, u32[]{:S(2)}) %collective-permute-start.18) | collective-permute-done | bytes 4128 | tf_op jit(solution)/shard_map/ppermute | solution.py:28
  44.8 0.1 collective-permute-done.20
  44.9 0.8 %shard_map.87 = (f32[32,256]{1,0:T(8,128)}, f32[32,256]{1,0:T(8,128)}) custom-call(f32[8,128]{1,0:T(8,128)S(1)} %add_add_fusion.curve_ref, f32[32,128]{1,0:T(8,128)S(1)} %get-tuple-element.89.norm_ref, f32[32,256]{1,0:T(8,128)S(1)} %get-tuple-element.90.solution_ref, f32[32,256]{1,0:T(8,128)S(1)} %get-tuple-element.91.residual_ref, ...), custom_call_target="tpu_custom_call" | custom-call | tf_op jit(solution)/shard_map/pallas_call | solution.py:496
  (11 shorter events, 0.1 us)
Async XLA Ops:
  2.1 7.4 %collective-permute-start = (bf16[1,96,256]{2,1,0:T(8,128)(2,1)S(1)}, bf16[1,96,256]{2,1,0:T(8,128)(2,1)S(1)}, u32[]{:S(2)}, u32[]{:S(2)}) collective-permute-start(bf16[1,96,256]{2,1,0:T(8,128)(2,1)S(1)} %shard_map.77.own_ref), channel_id=1, source_target_pairs={{0,24},{1,25},{2,26},{3,27},{4,28},{5,29},{6,30},{7,31},{8,16},{9,... | collective-permute-start | bytes 147464 | tf_op jit(solution)/shard_map/ppermute | solution.py:28
  7.2 4.1 %collective-permute-start.1 = (bf16[1,96,256]{2,1,0:T(8,128)(2,1)S(1)}, bf16[1,96,256]{2,1,0:T(8,128)(2,1)S(1)}, u32[]{:S(2)}, u32[]{:S(2)}) collective-permute-start(bf16[1,96,256]{2,1,0:T(8,128)(2,1)S(1)} %shard_map.77.own_ref), channel_id=1, source_target_pairs={{0,8},{1,9},{2,10},{3,11},{4,12},{5,13},{6,14},{7,15},{8,0},{9,1},... | collective-permute-start | bytes 147464 | tf_op jit(solution)/shard_map/ppermute | solution.py:28
  7.2 5.3 %collective-permute-start.2 = (bf16[1,96,256]{2,1,0:T(8,128)(2,1)S(1)}, bf16[1,96,256]{2,1,0:T(8,128)(2,1)S(1)}, u32[]{:S(2)}, u32[]{:S(2)}) collective-permute-start(bf16[1,96,256]{2,1,0:T(8,128)(2,1)S(1)} %shard_map.77.own_ref), channel_id=1, source_target_pairs={{0,16},{1,17},{2,18},{3,19},{4,20},{5,21},{6,22},{7,23},{8,24},{9,... | collective-permute-start | bytes 147464 | tf_op jit(solution)/shard_map/ppermute | solution.py:28
  12.6 3.2 %collective-permute-start.4 = (bf16[4,64,256]{2,1,0:T(8,128)(2,1)S(1)}, bf16[4,64,256]{2,1,0:T(8,128)(2,1)S(1)}, u32[]{:S(2)}, u32[]{:S(2)}) collective-permute-start(bf16[4,64,256]{2,1,0:T(8,128)(2,1)S(1)} %slice.3.refs_0_.near_ref), channel_id=1, source_target_pairs={{0,1},{1,0},{2,3},{3,2},{4,5},{5,4},{6,7},{7,6},{8,9},{9,8},{10,11... | collective-permute-start | bytes 393224 | tf_op jit(solution)/shard_map/ppermute | solution.py:28
  12.7 5.9 %collective-permute-start.3 = (bf16[4,64,256]{2,1,0:T(8,128)(2,1)S(1)}, bf16[4,64,256]{2,1,0:T(8,128)(2,1)S(1)}, u32[]{:S(2)}, u32[]{:S(2)}) collective-permute-start(bf16[4,64,256]{2,1,0:T(8,128)(2,1)S(1)} %slice.3.refs_0_.near_ref), channel_id=1, source_target_pairs={{0,4},{1,5},{2,6},{3,7},{4,0},{5,1},{6,2},{7,3},{8,12},{9,13},{10,... | collective-permute-start | bytes 393224 | tf_op jit(solution)/shard_map/ppermute | solution.py:28
  14.3 6.9 %collective-permute-start.7 = (bf16[4,64,256]{2,1,0:T(8,128)(2,1)S(1)}, bf16[4,64,256]{2,1,0:T(8,128)(2,1)S(1)}, u32[]{:S(2)}, u32[]{:S(2)}) collective-permute-start(bf16[4,64,256]{2,1,0:T(8,128)(2,1)S(1)} %slice.3.refs_0_.near_ref), channel_id=1, source_target_pairs={{0,2},{1,3},{2,0},{3,1},{4,6},{5,7},{6,4},{7,5},{8,10},{9,11},{10,... | collective-permute-start | bytes 393224 | tf_op jit(solution)/shard_map/ppermute | solution.py:28
  18.6 2.8 %collective-permute-start.6 = (bf16[4,64,256]{2,1,0:T(8,128)(2,1)S(1)}, bf16[4,64,256]{2,1,0:T(8,128)(2,1)S(1)}, u32[]{:S(2)}, u32[]{:S(2)}) collective-permute-start(bf16[4,64,256]{2,1,0:T(8,128)(2,1)S(1)} %collective-permute-done.3.refs_0_), channel_id=1, source_target_pairs={{0,1},{1,0},{2,3},{3,2},{4,5},{5,4},{6,7},{7,6},{8,9},{9,8},{10,11... | collective-permute-start | bytes 393224 | tf_op jit(solution)/shard_map/ppermute | solution.py:28
  18.6 5.9 %collective-permute-start.5 = (bf16[4,64,256]{2,1,0:T(8,128)(2,1)S(1)}, bf16[4,64,256]{2,1,0:T(8,128)(2,1)S(1)}, u32[]{:S(2)}, u32[]{:S(2)}) collective-permute-start(bf16[4,64,256]{2,1,0:T(8,128)(2,1)S(1)} %collective-permute-done.3.refs_0_), channel_id=1, source_target_pairs={{0,2},{1,3},{2,0},{3,1},{4,6},{5,7},{6,4},{7,5},{8,10},{9,11},{10,... | collective-permute-start | bytes 393224 | tf_op jit(solution)/shard_map/ppermute | solution.py:28
  21.2 3.4 %collective-permute-start.9 = (bf16[4,64,256]{2,1,0:T(8,128)(2,1)S(1)}, bf16[4,64,256]{2,1,0:T(8,128)(2,1)S(1)}, u32[]{:S(2)}, u32[]{:S(2)}) collective-permute-start(bf16[4,64,256]{2,1,0:T(8,128)(2,1)S(1)} %collective-permute-done.7.refs_1_), channel_id=1, source_target_pairs={{0,1},{1,0},{2,3},{3,2},{4,5},{5,4},{6,7},{7,6},{8,9},{9,8},{10,11... | collective-permute-start | bytes 393224 | tf_op jit(solution)/shard_map/ppermute | solution.py:28
  24.5 2.0 %collective-permute-start.8 = (bf16[4,64,256]{2,1,0:T(8,128)(2,1)S(1)}, bf16[4,64,256]{2,1,0:T(8,128)(2,1)S(1)}, u32[]{:S(2)}, u32[]{:S(2)}) collective-permute-start(bf16[4,64,256]{2,1,0:T(8,128)(2,1)S(1)} %collective-permute-done.5.refs_1_), channel_id=1, source_target_pairs={{0,1},{1,0},{2,3},{3,2},{4,5},{5,4},{6,7},{7,6},{8,9},{9,8},{10,11... | collective-permute-start | bytes 393224 | tf_op jit(solution)/shard_map/ppermute | solution.py:28
  28.0 5.7 %collective-permute-start.11 = (bf16[1,144,256]{2,1,0:T(8,128)(2,1)S(1)}, bf16[1,144,256]{2,1,0:T(8,128)(2,1)S(1)}, u32[]{:S(2)}, u32[]{:S(2)}) collective-permute-start(bf16[1,144,256]{2,1,0:T(8,128)(2,1)S(1)} %get-tuple-element.70.refs_0_), channel_id=1, source_target_pairs={{0,6},{1,7},{2,4},{3,5},{4,2},{5,3},{6,0},{7,1},{8,14},{9,15},{10,... | collective-permute-start | bytes 221192 | tf_op jit(solution)/shard_map/ppermute | solution.py:28
  30.4 3.2 %collective-permute-start.10 = (bf16[1,144,256]{2,1,0:T(8,128)(2,1)S(1)}, bf16[1,144,256]{2,1,0:T(8,128)(2,1)S(1)}, u32[]{:S(2)}, u32[]{:S(2)}) collective-permute-start(bf16[1,144,256]{2,1,0:T(8,128)(2,1)S(1)} %get-tuple-element.70.refs_0_), channel_id=1, source_target_pairs={{0,1},{1,0},{2,3},{3,2},{4,5},{5,4},{6,7},{7,6},{8,9},{9,8},{10,11... | collective-permute-start | bytes 221192 | tf_op jit(solution)/shard_map/ppermute | solution.py:28
  30.7 4.5 %collective-permute-start.13 = (bf16[1,144,256]{2,1,0:T(8,128)(2,1)S(1)}, bf16[1,144,256]{2,1,0:T(8,128)(2,1)S(1)}, u32[]{:S(2)}, u32[]{:S(2)}) collective-permute-start(bf16[1,144,256]{2,1,0:T(8,128)(2,1)S(1)} %get-tuple-element.70.refs_0_), channel_id=1, source_target_pairs={{0,2},{1,3},{2,0},{3,1},{4,6},{5,7},{6,4},{7,5},{8,10},{9,11},{10,... | collective-permute-start | bytes 221192 | tf_op jit(solution)/shard_map/ppermute | solution.py:28
  31.2 4.4 %collective-permute-start.14 = (bf16[1,144,256]{2,1,0:T(8,128)(2,1)S(1)}, bf16[1,144,256]{2,1,0:T(8,128)(2,1)S(1)}, u32[]{:S(2)}, u32[]{:S(2)}) collective-permute-start(bf16[1,144,256]{2,1,0:T(8,128)(2,1)S(1)} %get-tuple-element.70.refs_0_), channel_id=1, source_target_pairs={{0,4},{1,5},{2,6},{3,7},{4,0},{5,1},{6,2},{7,3},{8,12},{9,13},{10,... | collective-permute-start | bytes 221192 | tf_op jit(solution)/shard_map/ppermute | solution.py:28
  33.6 3.2 %collective-permute-start.12 = (bf16[1,144,256]{2,1,0:T(8,128)(2,1)S(1)}, bf16[1,144,256]{2,1,0:T(8,128)(2,1)S(1)}, u32[]{:S(2)}, u32[]{:S(2)}) collective-permute-start(bf16[1,144,256]{2,1,0:T(8,128)(2,1)S(1)} %collective-permute-done.11.refs_0_.refs_2_), channel_id=1, source_target_pairs={{0,1},{1,0},{2,3},{3,2},{4,5},{5,4},{6,7},{7,6},{8,9},{9,8},{10,11... | collective-permute-start | bytes 221192 | tf_op jit(solution)/shard_map/ppermute | solution.py:28
  35.5 2.2 %collective-permute-start.15 = (bf16[1,144,256]{2,1,0:T(8,128)(2,1)S(1)}, bf16[1,144,256]{2,1,0:T(8,128)(2,1)S(1)}, u32[]{:S(2)}, u32[]{:S(2)}) collective-permute-start(bf16[1,144,256]{2,1,0:T(8,128)(2,1)S(1)} %collective-permute-done.14.refs_0_.refs_4_), channel_id=1, source_target_pairs={{0,1},{1,0},{2,3},{3,2},{4,5},{5,4},{6,7},{7,6},{8,9},{9,8},{10,11... | collective-permute-start | bytes 221192 | tf_op jit(solution)/shard_map/ppermute | solution.py:28
  35.5 2.2 %collective-permute-start.16 = (bf16[1,144,256]{2,1,0:T(8,128)(2,1)S(1)}, bf16[1,144,256]{2,1,0:T(8,128)(2,1)S(1)}, u32[]{:S(2)}, u32[]{:S(2)}) collective-permute-start(bf16[1,144,256]{2,1,0:T(8,128)(2,1)S(1)} %collective-permute-done.13.refs_1_.refs_5_), channel_id=1, source_target_pairs={{0,1},{1,0},{2,3},{3,2},{4,5},{5,4},{6,7},{7,6},{8,9},{9,8},{10,11... | collective-permute-start | bytes 221192 | tf_op jit(solution)/shard_map/ppermute | solution.py:28
  38.9 1.2 %collective-permute-start.17 = (f32[8,128]{1,0:T(8,128)S(1)}, f32[8,128]{1,0:T(8,128)S(1)}, u32[]{:S(2)}, u32[]{:S(2)}) collective-permute-start(f32[8,128]{1,0:T(8,128)S(1)} %get-tuple-element.88), channel_id=1, source_target_pairs={{0,1},{1,0},{2,3},{3,2},{4,5},{5,4},{6,7},{7,6},{8,9},{9,8},{10,11... | collective-permute-start | bytes 12296 | tf_op jit(solution)/shard_map/ppermute | solution.py:28
  40.1 3.6 %collective-permute-start.19 = (f32[8,128]{1,0:T(8,128)S(1)}, f32[8,128]{1,0:T(8,128)S(1)}, u32[]{:S(2)}, u32[]{:S(2)}) collective-permute-start(f32[8,128]{1,0:T(8,128)S(1)} %add.12), channel_id=1, source_target_pairs={{0,4},{1,7},{2,6},{3,5},{4,0},{5,3},{6,2},{7,1},{8,12},{9,15},{10,... | collective-permute-start | bytes 12296 | tf_op jit(solution)/shard_map/ppermute | solution.py:38
  41.2 3.6 %collective-permute-start.18 = (f32[8,128]{1,0:T(8,128)S(1)}, f32[8,128]{1,0:T(8,128)S(1)}, u32[]{:S(2)}, u32[]{:S(2)}) collective-permute-start(f32[8,128]{1,0:T(8,128)S(1)} %add.12), channel_id=1, source_target_pairs={{0,2},{1,3},{2,0},{3,1},{4,6},{5,7},{6,4},{7,5},{8,10},{9,11},{10,... | collective-permute-start | bytes 12296 | tf_op jit(solution)/shard_map/ppermute | solution.py:28
  43.7 1.2 %collective-permute-start.20 = (f32[8,128]{1,0:T(8,128)S(1)}, f32[8,128]{1,0:T(8,128)S(1)}, u32[]{:S(2)}, u32[]{:S(2)}) collective-permute-start(f32[8,128]{1,0:T(8,128)S(1)} %collective-permute-done.19), channel_id=1, source_target_pairs={{0,1},{1,0},{2,3},{3,2},{4,5},{5,4},{6,7},{7,6},{8,9},{9,8},{10,11... | collective-permute-start | bytes 12296 | tf_op jit(solution)/shard_map/ppermute | solution.py:28

commit v9 on v8

--- a/solution.py
+++ b/solution.py
@@ -33,9 +33,8 @@
     return high, (wide - high.astype(F32)).astype(BF16)
 
 
-def swap_apart(array, bits, count):
-    one, two, core = bits
-    return lax.ppermute(array, AXES, [(i, i ^ (one | two if i & core else one)) for i in range(count)])
+def swap_apart(array, first, second, core, count):
+    return lax.ppermute(array, AXES, [(i, i ^ (second if i & core else first)) for i in range(count)])
 
 
 def three_parts(wide):
@@ -452,10 +451,11 @@
     held, levels = lax.optimization_barrier((held, levels))
     near = held[:copies]
     held = held[:, : 2 * feat + probes]
-    beside, up, over = (swap(held, bit, count) for bit in (core, one, two))
+    beside = swap(held, core, count)
+    up, over = swap_apart(held, one, two, core, count), swap_apart(held, two, one, core, count)
     kept_0, products, near_features = first(near, [held, beside], levels, None, [])
     up, products[-1] = lax.optimization_barrier((up, products[-1]))
-    corner, up_beside = swap(up, two, count), swap(up, core, count)
+    corner, up_beside = swap_apart(up, two, one, core, count), swap(up, core, count)
     kept_1, products, _ = first(near, [up], levels, near_features, products)
     over, products[-1] = lax.optimization_barrier((over, products[-1]))
     over_beside = swap(over, core, count)
@@ -468,7 +468,8 @@
     kept = [*kept_0, *kept_1, *kept_2, *kept_3, *kept_4]
 
     held = gather(message, later[:-3], count)
-    beside, up, over, corner = (swap(held, bit, count) for bit in (core, one, two, one | two))
+    beside, corner = swap(held, core, count), swap(held, one | two, count)
+    up, over = swap_apart(held, one, two, core, count), swap_apart(held, two, one, core, count)
     if keep:
         corner_beside = swap(corner, core, count)
         again_0 = apply_again([held, beside], kept[:2], copies)
@@ -489,7 +490,7 @@
         done = second(levels, own, own_image, pieces, images, None, copies, feat, group)
     partial, solution, residual, direction, second_image, norm = done
     partial = partial + swap(partial, core, count)
-    apart = swap_apart(partial, bits[-3:], count)
+    apart = swap_apart(partial, one, one | two, core, count)
     partial = partial + swap(partial, two, count) + (apart + swap(apart, core, count))
     partial = total(partial, later[:-3], count)
     done = jax.ShapeDtypeStruct((probes, slots), F32)

time: 45.9 us -> 45.1 us (0.983)
  waiting for transfers between devices: 11.6 us -> 10.4 us
    ppermute x1 -> x6, starting transfers between devices: 1.12 us -> 6.82 us  [swap_apart(): lax.ppermute(array, AXES, [(i, i ^ (second if i & core else first)) for i...]
    ppermute x20 -> x15, starting transfers between devices: 16.4 us -> 11.1 us  [swap(): return lax.ppermute(array, AXES, [(i, i ^ bit) for i in range(count)])]
    ppermute x20 -> x15, waiting for transfers between devices: 10.6 us -> 7.36 us  [swap(): return lax.ppermute(array, AXES, [(i, i ^ bit) for i in range(count)])]
    ppermute x1 -> x6, waiting for transfers between devices: 0.99 us -> 3.01 us  [swap_apart(): lax.ppermute(array, AXES, [(i, i ^ (second if i & core else first)) for i...]
where the time goes in v9:
time: 45.1 us; the launch traced here: 44.8 us
  starting transfers between devices  17.9 us (40%)
  Pallas kernels  13.7 us (30%)
  waiting for transfers between devices  10.4 us (23%)
  between operations  2.7 us (6%)
    ppermute x15, starting transfers between devices, swap(): return lax.ppermute(array, AXES, [(i, i ^ bit) for i in range(count)])  11.1 us
    pallas_call x5, Pallas kernels, apply_first(): pl.pallas_call(functools.partial(apply_kernel, feat, group, keep, begin,...  8.43 us
    ppermute x15, waiting for transfers between devices, swap(): return lax.ppermute(array, AXES, [(i, i ^ bit) for i in range(count)])  7.36 us
    ppermute x6, starting transfers between devices, swap_apart(): lax.ppermute(array, AXES, [(i, i ^ (second if i & core else first)) for i...  6.82 us
    ppermute x6, waiting for transfers between devices, swap_apart(): lax.ppermute(array, AXES, [(i, i ^ (second if i & core else first)) for i...  3.01 us
    pallas_call x3, Pallas kernels, apply_again(): pl.pallas_call(functools.partial(again_kernel, copies, len(sent)), out_sh...  2.46 us
    pallas_call x1, Pallas kernels, combine(): pl.pallas_call(functools.partial(combine_kernel, feat, copies), out_shape...  1.17 us
  transfers between devices with their start and end apart: 21, of which 12 were waited for; matrix products, arithmetic and copies ran while one was open for 0% of the time, Pallas kernels for 21%

profile of v9, /device:TPU:0, one launch (start us, length us, event | category | flops | bytes accessed | tf_op | source)
XLA Modules:
  0.0 44.8 jit_solution(2278328309173090586)
XLA Ops:
  1.3 0.8 %shard_map.77.own_ref = bf16[1,96,256]{2,1,0:T(8,128)(2,1)S(1)} custom-call(f32[16,256]{1,0:T(8,128)} %bitcast.5, f32[16]{0:T(128)} %inv_ref.1, f32[32,256]{1,0:T(8,128)} %bitcast.4, s32[1]{0:T(128)S(6)} %copy.10.count_ref), custom_call_target="tpu_custom_call" | custom-call | tf_op jit(solution)/shard_map/pallas_call | solution.py:82
  2.1 5.1 %collective-permute-start = (bf16[1,96,256]{2,1,0:T(8,128)(2,1)S(1)}, bf16[1,96,256]{2,1,0:T(8,128)(2,1)S(1)}, u32[]{:S(2)}, u32[]{:S(2)}) collective-permute-start(bf16[1,96,256]{2,1,0:T(8,128)(2,1)S(1)} %shard_map.77.own_ref), channel_id=1, source_target_pairs={{0,24},{1,25},{2,26},{3,27},{4,28},{5,29},{6,30},{7,31},{8,16},{9,... | collective-permute-start | bytes 147464 | tf_op jit(solution)/shard_map/ppermute | solution.py:28
  7.2 0.0 collective-permute-start.1
  7.2 0.6 %collective-permute-start.2 = (bf16[1,96,256]{2,1,0:T(8,128)(2,1)S(1)}, bf16[1,96,256]{2,1,0:T(8,128)(2,1)S(1)}, u32[]{:S(2)}, u32[]{:S(2)}) collective-permute-start(bf16[1,96,256]{2,1,0:T(8,128)(2,1)S(1)} %shard_map.77.own_ref), channel_id=1, source_target_pairs={{0,16},{1,17},{2,18},{3,19},{4,20},{5,21},{6,22},{7,23},{8,24},{9,... | collective-permute-start | bytes 147464 | tf_op jit(solution)/shard_map/ppermute | solution.py:28
  9.2 0.1 pad_maximum_fusion.1
  9.3 0.2 collective-permute-done
  9.5 1.8 %collective-permute-done.1 = bf16[1,96,256]{2,1,0:T(8,128)(2,1)S(1)} collective-permute-done((bf16[1,96,256]{2,1,0:T(8,128)(2,1)S(1)}, bf16[1,96,256]{2,1,0:T(8,128)(2,1)S(1)}, u32[]{:S(2)}, u32[]{:S(2)}) %collective-permute-start.1) | collective-permute-done | bytes 49184 | tf_op jit(solution)/shard_map/ppermute | solution.py:28
  11.3 1.2 %collective-permute-done.2 = bf16[1,96,256]{2,1,0:T(8,128)(2,1)S(1)} collective-permute-done((bf16[1,96,256]{2,1,0:T(8,128)(2,1)S(1)}, bf16[1,96,256]{2,1,0:T(8,128)(2,1)S(1)}, u32[]{:S(2)}, u32[]{:S(2)}) %collective-permute-start.2) | collective-permute-done | bytes 49184 | tf_op jit(solution)/shard_map/ppermute | solution.py:28
  12.5 0.1 broadcast_in_dim.2.levels_ref
  12.6 0.1 collective-permute-start.4
  12.7 1.6 %collective-permute-start.3 = (bf16[4,64,256]{2,1,0:T(8,128)(2,1)S(1)}, bf16[4,64,256]{2,1,0:T(8,128)(2,1)S(1)}, u32[]{:S(2)}, u32[]{:S(2)}) collective-permute-start(bf16[4,64,256]{2,1,0:T(8,128)(2,1)S(1)} %slice.3.refs_0_.near_ref), channel_id=1, source_target_pairs={{0,4},{1,3},{2,6},{3,1},{4,0},{5,7},{6,2},{7,5},{8,12},{9,11},{10,... | collective-permute-start | bytes 393224 | tf_op jit(solution)/shard_map/ppermute | solution.py:37
  14.3 1.5 %collective-permute-start.7 = (bf16[4,64,256]{2,1,0:T(8,128)(2,1)S(1)}, bf16[4,64,256]{2,1,0:T(8,128)(2,1)S(1)}, u32[]{:S(2)}, u32[]{:S(2)}) collective-permute-start(bf16[4,64,256]{2,1,0:T(8,128)(2,1)S(1)} %slice.3.refs_0_.near_ref), channel_id=1, source_target_pairs={{0,2},{1,5},{2,0},{3,7},{4,6},{5,1},{6,4},{7,3},{8,10},{9,13},{10,... | collective-permute-start | bytes 393224 | tf_op jit(solution)/shard_map/ppermute | solution.py:37
  15.8 2.0 %shard_map.78 = (bf16[1,1024,1024]{2,1,0:T(8,128)(2,1)S(1)}, bf16[1,1024,1024]{2,1,0:T(8,128)(2,1)S(1)}, f32[32,1024]{1,0:T(8,128)S(1)}, f32[32,1024]{1,0:T(8,128)S(1)}, bf16[80,1024]{1,0:T(8,128)(2,1)S(1)}) custom-call(bf16[4,96,256]{2,1,0:T(8,128)(2,1)S(1)} %pad_maximum_fusion.near_ref, f32[2,256]{1,0:T(2,128)S(1)} %broadcast_in_dim.2.levels_ref, ...), custom_call_target="tpu_custom_call" | custom-call | tf_op jit(solution)/shard_map/pallas_call | solution.py:198
  17.7 0.8 %collective-permute-done.3.refs_0_ = bf16[4,64,256]{2,1,0:T(8,128)(2,1)S(1)} collective-permute-done((bf16[4,64,256]{2,1,0:T(8,128)(2,1)S(1)}, bf16[4,64,256]{2,1,0:T(8,128)(2,1)S(1)}, u32[]{:S(2)}, u32[]{:S(2)}) %collective-permute-start.3) | collective-permute-done | bytes 131104 | tf_op jit(solution)/shard_map/ppermute | solution.py:37
  18.5 0.0 collective-permute-start.6
  18.5 1.8 %collective-permute-start.5 = (bf16[4,64,256]{2,1,0:T(8,128)(2,1)S(1)}, bf16[4,64,256]{2,1,0:T(8,128)(2,1)S(1)}, u32[]{:S(2)}, u32[]{:S(2)}) collective-permute-start(bf16[4,64,256]{2,1,0:T(8,128)(2,1)S(1)} %collective-permute-done.3.refs_0_), channel_id=1, source_target_pairs={{0,2},{1,5},{2,0},{3,7},{4,6},{5,1},{6,4},{7,3},{8,10},{9,13},{10,... | collective-permute-start | bytes 393224 | tf_op jit(solution)/shard_map/ppermute | solution.py:37
  20.3 1.1 %shard_map.79 = (bf16[1,1024,1024]{2,1,0:T(8,128)(2,1)S(1)}, f32[32,1024]{1,0:T(8,128)S(1)}) custom-call(bf16[4,96,256]{2,1,0:T(8,128)(2,1)S(1)} %pad_maximum_fusion.near_ref, f32[2,256]{1,0:T(2,128)S(1)} %broadcast_in_dim.2.levels_ref, bf16[4,64,256]{2,1,0:T(8,128)(2,1)S(1)} %collective-permute-done.3.refs_0_, ...), custom_call_target="tpu_custom_call" | custom-call | tf_op jit(solution)/shard_map/pallas_call | solution.py:198
  21.4 0.0 collective-permute-start.9
  21.4 0.0 collective-permute-done.6.refs_0_
  21.5 2.0 %shard_map.80 = (bf16[1,1024,1024]{2,1,0:T(8,128)(2,1)S(1)}, bf16[1,1024,1024]{2,1,0:T(8,128)(2,1)S(1)}, f32[32,1024]{1,0:T(8,128)S(1)}, f32[32,1024]{1,0:T(8,128)S(1)}) custom-call(bf16[4,96,256]{2,1,0:T(8,128)(2,1)S(1)} %pad_maximum_fusion.near_ref, f32[2,256]{1,0:T(2,128)S(1)} %broadcast_in_dim.2.levels_ref, ...), custom_call_target="tpu_custom_call" | custom-call | tf_op jit(solution)/shard_map/pallas_call | solution.py:198
  23.4 0.1 collective-permute-done.5.refs_1_
  23.5 0.5 %collective-permute-start.8 = (bf16[4,64,256]{2,1,0:T(8,128)(2,1)S(1)}, bf16[4,64,256]{2,1,0:T(8,128)(2,1)S(1)}, u32[]{:S(2)}, u32[]{:S(2)}) collective-permute-start(bf16[4,64,256]{2,1,0:T(8,128)(2,1)S(1)} %collective-permute-done.5.refs_1_), channel_id=1, source_target_pairs={{0,1},{1,0},{2,3},{3,2},{4,5},{5,4},{6,7},{7,6},{8,9},{9,8},{10,11... | collective-permute-start | bytes 393224 | tf_op jit(solution)/shard_map/ppermute | solution.py:28
  23.9 2.0 %shard_map.81 = (bf16[1,1024,1024]{2,1,0:T(8,128)(2,1)S(1)}, bf16[1,1024,1024]{2,1,0:T(8,128)(2,1)S(1)}, f32[32,1024]{1,0:T(8,128)S(1)}, f32[32,1024]{1,0:T(8,128)S(1)}) custom-call(bf16[4,96,256]{2,1,0:T(8,128)(2,1)S(1)} %pad_maximum_fusion.near_ref, f32[2,256]{1,0:T(2,128)S(1)} %broadcast_in_dim.2.levels_ref, ...), custom_call_target="tpu_custom_call" | custom-call | tf_op jit(solution)/shard_map/pallas_call | solution.py:198
  25.9 0.0 collective-permute-done.8.refs_0_
  25.9 1.5 %shard_map.82 = (bf16[1,1024,1024]{2,1,0:T(8,128)(2,1)S(1)}, f32[32,1024]{1,0:T(8,128)S(1)}, bf16[1,144,256]{2,1,0:T(8,128)(2,1)S(1)}, f32[32,256]{1,0:T(8,128)S(1)}) custom-call(bf16[4,96,256]{2,1,0:T(8,128)(2,1)S(1)} %pad_maximum_fusion.near_ref, f32[2,256]{1,0:T(2,128)S(1)} %broadcast_in_dim.2.levels_ref, ...), custom_call_target="tpu_custom_call" | custom-call | tf_op jit(solution)/shard_map/pallas_call | solution.py:198
  27.4 2.4 %collective-permute-start.11 = (bf16[1,144,256]{2,1,0:T(8,128)(2,1)S(1)}, bf16[1,144,256]{2,1,0:T(8,128)(2,1)S(1)}, u32[]{:S(2)}, u32[]{:S(2)}) collective-permute-start(bf16[1,144,256]{2,1,0:T(8,128)(2,1)S(1)} %get-tuple-element.70.refs_0_), channel_id=1, source_target_pairs={{0,6},{1,7},{2,4},{3,5},{4,2},{5,3},{6,0},{7,1},{8,14},{9,15},{10,... | collective-permute-start | bytes 221192 | tf_op jit(solution)/shard_map/ppermute | solution.py:28
  29.7 0.2 collective-permute-start.10
  30.0 0.4 collective-permute-start.13
  30.4 0.5 %collective-permute-start.14 = (bf16[1,144,256]{2,1,0:T(8,128)(2,1)S(1)}, bf16[1,144,256]{2,1,0:T(8,128)(2,1)S(1)}, u32[]{:S(2)}, u32[]{:S(2)}) collective-permute-start(bf16[1,144,256]{2,1,0:T(8,128)(2,1)S(1)} %get-tuple-element.70.refs_0_), channel_id=1, source_target_pairs={{0,4},{1,3},{2,6},{3,1},{4,0},{5,7},{6,2},{7,5},{8,12},{9,11},{10,... | collective-permute-start | bytes 221192 | tf_op jit(solution)/shard_map/ppermute | solution.py:37
  30.9 1.8 %collective-permute-done.11.refs_0_.refs_2_ = bf16[1,144,256]{2,1,0:T(8,128)(2,1)S(1)} collective-permute-done((bf16[1,144,256]{2,1,0:T(8,128)(2,1)S(1)}, bf16[1,144,256]{2,1,0:T(8,128)(2,1)S(1)}, u32[]{:S(2)}, u32[]{:S(2)}) %collective-permute-start.11) | collective-permute-done | bytes 73760 | tf_op jit(solution)/shard_map/ppermute | solution.py:28
  32.7 0.8 %shard_map.83 = (f32[32,1024]{1,0:T(8,128)S(1)}, f32[32,1024]{1,0:T(8,128)S(1)}) custom-call(bf16[1,144,256]{2,1,0:T(8,128)(2,1)S(1)} %get-tuple-element.70.refs_0_, bf16[1,144,256]{2,1,0:T(8,128)(2,1)S(1)} %collective-permute-done.10.refs_1_, bf16[1,1024,1024]{2,1,0:T(8,128)(2,1)S(1)} %get-tuple-element.69.refs_2_.kept_near_ref, ...), custom_call_target="tpu_custom_call" | custom-call | tf_op jit(solution)/shard_map/pallas_call | solution.py:324
  33.5 1.1 %collective-permute-done.13.refs_1_.refs_5_ = bf16[1,144,256]{2,1,0:T(8,128)(2,1)S(1)} collective-permute-done((bf16[1,144,256]{2,1,0:T(8,128)(2,1)S(1)}, bf16[1,144,256]{2,1,0:T(8,128)(2,1)S(1)}, u32[]{:S(2)}, u32[]{:S(2)}) %collective-permute-start.13) | collective-permute-done | bytes 73760 | tf_op jit(solution)/shard_map/ppermute | solution.py:37
  34.6 0.1 collective-permute-done.14.refs_0_.refs_4_
  34.7 0.0 collective-permute-start.15
  34.7 0.5 %collective-permute-start.16 = (bf16[1,144,256]{2,1,0:T(8,128)(2,1)S(1)}, bf16[1,144,256]{2,1,0:T(8,128)(2,1)S(1)}, u32[]{:S(2)}, u32[]{:S(2)}) collective-permute-start(bf16[1,144,256]{2,1,0:T(8,128)(2,1)S(1)} %collective-permute-done.13.refs_1_.refs_5_), channel_id=1, source_target_pairs={{0,1},{1,0},{2,3},{3,2},{4,5},{5,4},{6,7},{7,6},{8,9},{9,8},{10,11... | collective-permute-start | bytes 221192 | tf_op jit(solution)/shard_map/ppermute | solution.py:28
  35.2 0.8 %shard_map.85 = (f32[32,1024]{1,0:T(8,128)S(1)}, f32[32,1024]{1,0:T(8,128)S(1)}) custom-call(bf16[1,144,256]{2,1,0:T(8,128)(2,1)S(1)} %collective-permute-done.14.refs_0_.refs_4_, bf16[1,144,256]{2,1,0:T(8,128)(2,1)S(1)} %collective-permute-done.13.refs_1_.refs_5_, bf16[1,1024,1024]{2,1,0:T(8,128)(2,1)S(1)} %get-tuple-element.82.refs_2_, ...), custom_call_target="tpu_custom_call" | custom-call | tf_op jit(solution)/shard_map/pallas_call | solution.py:324
  36.0 0.0 collective-permute-done.12.refs_1_.refs_3_
  36.0 0.8 %shard_map.84 = (f32[32,1024]{1,0:T(8,128)S(1)}, f32[32,1024]{1,0:T(8,128)S(1)}) custom-call(bf16[1,144,256]{2,1,0:T(8,128)(2,1)S(1)} %collective-permute-done.11.refs_0_.refs_2_, bf16[1,144,256]{2,1,0:T(8,128)(2,1)S(1)} %collective-permute-done.12.refs_1_.refs_3_, bf16[1,1024,1024]{2,1,0:T(8,128)(2,1)S(1)} %get-tuple-element.78.refs_2_, ...), custom_call_target="tpu_custom_call" | custom-call | tf_op jit(solution)/shard_map/pallas_call | solution.py:324
  36.9 0.0 collective-permute-done.16.refs_7_
  36.9 1.2 %shard_map.86 = (f32[8,128]{1,0:T(8,128)S(1)}, f32[32,256]{1,0:T(8,128)S(1)}, f32[32,256]{1,0:T(8,128)S(1)}, f32[32,256]{1,0:T(8,128)S(1)}, f32[32,256]{1,0:T(8,128)S(1)}, /*index=5*/f32[32,128]{1,0:T(8,128)S(1)}) custom-call(f32[2,256]{1,0:T(2,128)S(1)} %broadcast_in_dim.2.levels_ref, bf16[1,96,256]{2,1,0:T(8,128)(2,1)S(1)} %shard_map.77.own_ref, ...), custom_call_target="tpu_custom_call" | custom-call | tf_op jit(solution)/shard_map/pallas_call | solution.py:377
  38.1 0.0 collective-permute-start.17
  38.1 1.2 %collective-permute-done.17 = f32[8,128]{1,0:T(8,128)S(1)} collective-permute-done((f32[8,128]{1,0:T(8,128)S(1)}, f32[8,128]{1,0:T(8,128)S(1)}, u32[]{:S(2)}, u32[]{:S(2)}) %collective-permute-start.17) | collective-permute-done | bytes 4128 | tf_op jit(solution)/shard_map/ppermute | solution.py:28
  39.3 1.0 %collective-permute-start.19 = (f32[8,128]{1,0:T(8,128)S(1)}, f32[8,128]{1,0:T(8,128)S(1)}, u32[]{:S(2)}, u32[]{:S(2)}) collective-permute-start(f32[8,128]{1,0:T(8,128)S(1)} %add.12), channel_id=1, source_target_pairs={{0,4},{1,7},{2,6},{3,5},{4,0},{5,3},{6,2},{7,1},{8,12},{9,15},{10,... | collective-permute-start | bytes 12296 | tf_op jit(solution)/shard_map/ppermute | solution.py:37
  40.3 1.7 %collective-permute-start.18 = (f32[8,128]{1,0:T(8,128)S(1)}, f32[8,128]{1,0:T(8,128)S(1)}, u32[]{:S(2)}, u32[]{:S(2)}) collective-permute-start(f32[8,128]{1,0:T(8,128)S(1)} %add.12), channel_id=1, source_target_pairs={{0,2},{1,3},{2,0},{3,1},{4,6},{5,7},{6,4},{7,5},{8,10},{9,11},{10,... | collective-permute-start | bytes 12296 | tf_op jit(solution)/shard_map/ppermute | solution.py:28
  41.9 1.0 %collective-permute-done.19 = f32[8,128]{1,0:T(8,128)S(1)} collective-permute-done((f32[8,128]{1,0:T(8,128)S(1)}, f32[8,128]{1,0:T(8,128)S(1)}, u32[]{:S(2)}, u32[]{:S(2)}) %collective-permute-start.19) | collective-permute-done | bytes 4128 | tf_op jit(solution)/shard_map/ppermute | solution.py:37
  42.9 1.0 %collective-permute-done.18 = f32[8,128]{1,0:T(8,128)S(1)} collective-permute-done((f32[8,128]{1,0:T(8,128)S(1)}, f32[8,128]{1,0:T(8,128)S(1)}, u32[]{:S(2)}, u32[]{:S(2)}) %collective-permute-start.18) | collective-permute-done | bytes 4128 | tf_op jit(solution)/shard_map/ppermute | solution.py:28
  43.9 0.2 collective-permute-done.20
  44.0 0.8 %shard_map.87 = (f32[32,256]{1,0:T(8,128)}, f32[32,256]{1,0:T(8,128)}) custom-call(f32[8,128]{1,0:T(8,128)S(1)} %add_add_fusion.curve_ref, f32[32,128]{1,0:T(8,128)S(1)} %get-tuple-element.89.norm_ref, f32[32,256]{1,0:T(8,128)S(1)} %get-tuple-element.90.solution_ref, f32[32,256]{1,0:T(8,128)S(1)} %get-tuple-element.91.residual_ref, ...), custom_call_target="tpu_custom_call" | custom-call | tf_op jit(solution)/shard_map/pallas_call | solution.py:497
  (11 shorter events, 0.1 us)
Async XLA Ops:
  2.1 7.4 %collective-permute-start = (bf16[1,96,256]{2,1,0:T(8,128)(2,1)S(1)}, bf16[1,96,256]{2,1,0:T(8,128)(2,1)S(1)}, u32[]{:S(2)}, u32[]{:S(2)}) collective-permute-start(bf16[1,96,256]{2,1,0:T(8,128)(2,1)S(1)} %shard_map.77.own_ref), channel_id=1, source_target_pairs={{0,24},{1,25},{2,26},{3,27},{4,28},{5,29},{6,30},{7,31},{8,16},{9,... | collective-permute-start | bytes 147464 | tf_op jit(solution)/shard_map/ppermute | solution.py:28
  7.2 4.1 %collective-permute-start.1 = (bf16[1,96,256]{2,1,0:T(8,128)(2,1)S(1)}, bf16[1,96,256]{2,1,0:T(8,128)(2,1)S(1)}, u32[]{:S(2)}, u32[]{:S(2)}) collective-permute-start(bf16[1,96,256]{2,1,0:T(8,128)(2,1)S(1)} %shard_map.77.own_ref), channel_id=1, source_target_pairs={{0,8},{1,9},{2,10},{3,11},{4,12},{5,13},{6,14},{7,15},{8,0},{9,1},... | collective-permute-start | bytes 147464 | tf_op jit(solution)/shard_map/ppermute | solution.py:28
  7.2 5.3 %collective-permute-start.2 = (bf16[1,96,256]{2,1,0:T(8,128)(2,1)S(1)}, bf16[1,96,256]{2,1,0:T(8,128)(2,1)S(1)}, u32[]{:S(2)}, u32[]{:S(2)}) collective-permute-start(bf16[1,96,256]{2,1,0:T(8,128)(2,1)S(1)} %shard_map.77.own_ref), channel_id=1, source_target_pairs={{0,16},{1,17},{2,18},{3,19},{4,20},{5,21},{6,22},{7,23},{8,24},{9,... | collective-permute-start | bytes 147464 | tf_op jit(solution)/shard_map/ppermute | solution.py:28
  12.6 3.2 %collective-permute-start.4 = (bf16[4,64,256]{2,1,0:T(8,128)(2,1)S(1)}, bf16[4,64,256]{2,1,0:T(8,128)(2,1)S(1)}, u32[]{:S(2)}, u32[]{:S(2)}) collective-permute-start(bf16[4,64,256]{2,1,0:T(8,128)(2,1)S(1)} %slice.3.refs_0_.near_ref), channel_id=1, source_target_pairs={{0,1},{1,0},{2,3},{3,2},{4,5},{5,4},{6,7},{7,6},{8,9},{9,8},{10,11... | collective-permute-start | bytes 393224 | tf_op jit(solution)/shard_map/ppermute | solution.py:28
  12.7 5.8 %collective-permute-start.3 = (bf16[4,64,256]{2,1,0:T(8,128)(2,1)S(1)}, bf16[4,64,256]{2,1,0:T(8,128)(2,1)S(1)}, u32[]{:S(2)}, u32[]{:S(2)}) collective-permute-start(bf16[4,64,256]{2,1,0:T(8,128)(2,1)S(1)} %slice.3.refs_0_.near_ref), channel_id=1, source_target_pairs={{0,4},{1,3},{2,6},{3,1},{4,0},{5,7},{6,2},{7,5},{8,12},{9,11},{10,... | collective-permute-start | bytes 393224 | tf_op jit(solution)/shard_map/ppermute | solution.py:37
  14.3 7.1 %collective-permute-start.7 = (bf16[4,64,256]{2,1,0:T(8,128)(2,1)S(1)}, bf16[4,64,256]{2,1,0:T(8,128)(2,1)S(1)}, u32[]{:S(2)}, u32[]{:S(2)}) collective-permute-start(bf16[4,64,256]{2,1,0:T(8,128)(2,1)S(1)} %slice.3.refs_0_.near_ref), channel_id=1, source_target_pairs={{0,2},{1,5},{2,0},{3,7},{4,6},{5,1},{6,4},{7,3},{8,10},{9,13},{10,... | collective-permute-start | bytes 393224 | tf_op jit(solution)/shard_map/ppermute | solution.py:37
  18.5 2.9 %collective-permute-start.6 = (bf16[4,64,256]{2,1,0:T(8,128)(2,1)S(1)}, bf16[4,64,256]{2,1,0:T(8,128)(2,1)S(1)}, u32[]{:S(2)}, u32[]{:S(2)}) collective-permute-start(bf16[4,64,256]{2,1,0:T(8,128)(2,1)S(1)} %collective-permute-done.3.refs_0_), channel_id=1, source_target_pairs={{0,1},{1,0},{2,3},{3,2},{4,5},{5,4},{6,7},{7,6},{8,9},{9,8},{10,11... | collective-permute-start | bytes 393224 | tf_op jit(solution)/shard_map/ppermute | solution.py:28
  18.5 5.0 %collective-permute-start.5 = (bf16[4,64,256]{2,1,0:T(8,128)(2,1)S(1)}, bf16[4,64,256]{2,1,0:T(8,128)(2,1)S(1)}, u32[]{:S(2)}, u32[]{:S(2)}) collective-permute-start(bf16[4,64,256]{2,1,0:T(8,128)(2,1)S(1)} %collective-permute-done.3.refs_0_), channel_id=1, source_target_pairs={{0,2},{1,5},{2,0},{3,7},{4,6},{5,1},{6,4},{7,3},{8,10},{9,13},{10,... | collective-permute-start | bytes 393224 | tf_op jit(solution)/shard_map/ppermute | solution.py:37
  21.4 2.5 %collective-permute-start.9 = (bf16[4,64,256]{2,1,0:T(8,128)(2,1)S(1)}, bf16[4,64,256]{2,1,0:T(8,128)(2,1)S(1)}, u32[]{:S(2)}, u32[]{:S(2)}) collective-permute-start(bf16[4,64,256]{2,1,0:T(8,128)(2,1)S(1)} %collective-permute-done.7.refs_1_), channel_id=1, source_target_pairs={{0,1},{1,0},{2,3},{3,2},{4,5},{5,4},{6,7},{7,6},{8,9},{9,8},{10,11... | collective-permute-start | bytes 393224 | tf_op jit(solution)/shard_map/ppermute | solution.py:28
  23.5 2.4 %collective-permute-start.8 = (bf16[4,64,256]{2,1,0:T(8,128)(2,1)S(1)}, bf16[4,64,256]{2,1,0:T(8,128)(2,1)S(1)}, u32[]{:S(2)}, u32[]{:S(2)}) collective-permute-start(bf16[4,64,256]{2,1,0:T(8,128)(2,1)S(1)} %collective-permute-done.5.refs_1_), channel_id=1, source_target_pairs={{0,1},{1,0},{2,3},{3,2},{4,5},{5,4},{6,7},{7,6},{8,9},{9,8},{10,11... | collective-permute-start | bytes 393224 | tf_op jit(solution)/shard_map/ppermute | solution.py:28
  27.4 5.3 %collective-permute-start.11 = (bf16[1,144,256]{2,1,0:T(8,128)(2,1)S(1)}, bf16[1,144,256]{2,1,0:T(8,128)(2,1)S(1)}, u32[]{:S(2)}, u32[]{:S(2)}) collective-permute-start(bf16[1,144,256]{2,1,0:T(8,128)(2,1)S(1)} %get-tuple-element.70.refs_0_), channel_id=1, source_target_pairs={{0,6},{1,7},{2,4},{3,5},{4,2},{5,3},{6,0},{7,1},{8,14},{9,15},{10,... | collective-permute-start | bytes 221192 | tf_op jit(solution)/shard_map/ppermute | solution.py:28
  29.7 2.9 %collective-permute-start.10 = (bf16[1,144,256]{2,1,0:T(8,128)(2,1)S(1)}, bf16[1,144,256]{2,1,0:T(8,128)(2,1)S(1)}, u32[]{:S(2)}, u32[]{:S(2)}) collective-permute-start(bf16[1,144,256]{2,1,0:T(8,128)(2,1)S(1)} %get-tuple-element.70.refs_0_), channel_id=1, source_target_pairs={{0,1},{1,0},{2,3},{3,2},{4,5},{5,4},{6,7},{7,6},{8,9},{9,8},{10,11... | collective-permute-start | bytes 221192 | tf_op jit(solution)/shard_map/ppermute | solution.py:28
  30.0 4.7 %collective-permute-start.13 = (bf16[1,144,256]{2,1,0:T(8,128)(2,1)S(1)}, bf16[1,144,256]{2,1,0:T(8,128)(2,1)S(1)}, u32[]{:S(2)}, u32[]{:S(2)}) collective-permute-start(bf16[1,144,256]{2,1,0:T(8,128)(2,1)S(1)} %get-tuple-element.70.refs_0_), channel_id=1, source_target_pairs={{0,2},{1,5},{2,0},{3,7},{4,6},{5,1},{6,4},{7,3},{8,10},{9,13},{10,... | collective-permute-start | bytes 221192 | tf_op jit(solution)/shard_map/ppermute | solution.py:37
  30.4 4.4 %collective-permute-start.14 = (bf16[1,144,256]{2,1,0:T(8,128)(2,1)S(1)}, bf16[1,144,256]{2,1,0:T(8,128)(2,1)S(1)}, u32[]{:S(2)}, u32[]{:S(2)}) collective-permute-start(bf16[1,144,256]{2,1,0:T(8,128)(2,1)S(1)} %get-tuple-element.70.refs_0_), channel_id=1, source_target_pairs={{0,4},{1,3},{2,6},{3,1},{4,0},{5,7},{6,2},{7,5},{8,12},{9,11},{10,... | collective-permute-start | bytes 221192 | tf_op jit(solution)/shard_map/ppermute | solution.py:37
  32.7 3.4 %collective-permute-start.12 = (bf16[1,144,256]{2,1,0:T(8,128)(2,1)S(1)}, bf16[1,144,256]{2,1,0:T(8,128)(2,1)S(1)}, u32[]{:S(2)}, u32[]{:S(2)}) collective-permute-start(bf16[1,144,256]{2,1,0:T(8,128)(2,1)S(1)} %collective-permute-done.11.refs_0_.refs_2_), channel_id=1, source_target_pairs={{0,1},{1,0},{2,3},{3,2},{4,5},{5,4},{6,7},{7,6},{8,9},{9,8},{10,11... | collective-permute-start | bytes 221192 | tf_op jit(solution)/shard_map/ppermute | solution.py:28
  34.7 2.2 %collective-permute-start.15 = (bf16[1,144,256]{2,1,0:T(8,128)(2,1)S(1)}, bf16[1,144,256]{2,1,0:T(8,128)(2,1)S(1)}, u32[]{:S(2)}, u32[]{:S(2)}) collective-permute-start(bf16[1,144,256]{2,1,0:T(8,128)(2,1)S(1)} %collective-permute-done.14.refs_0_.refs_4_), channel_id=1, source_target_pairs={{0,1},{1,0},{2,3},{3,2},{4,5},{5,4},{6,7},{7,6},{8,9},{9,8},{10,11... | collective-permute-start | bytes 221192 | tf_op jit(solution)/shard_map/ppermute | solution.py:28
  34.7 2.2 %collective-permute-start.16 = (bf16[1,144,256]{2,1,0:T(8,128)(2,1)S(1)}, bf16[1,144,256]{2,1,0:T(8,128)(2,1)S(1)}, u32[]{:S(2)}, u32[]{:S(2)}) collective-permute-start(bf16[1,144,256]{2,1,0:T(8,128)(2,1)S(1)} %collective-permute-done.13.refs_1_.refs_5_), channel_id=1, source_target_pairs={{0,1},{1,0},{2,3},{3,2},{4,5},{5,4},{6,7},{7,6},{8,9},{9,8},{10,11... | collective-permute-start | bytes 221192 | tf_op jit(solution)/shard_map/ppermute | solution.py:28
  38.1 1.2 %collective-permute-start.17 = (f32[8,128]{1,0:T(8,128)S(1)}, f32[8,128]{1,0:T(8,128)S(1)}, u32[]{:S(2)}, u32[]{:S(2)}) collective-permute-start(f32[8,128]{1,0:T(8,128)S(1)} %get-tuple-element.88), channel_id=1, source_target_pairs={{0,1},{1,0},{2,3},{3,2},{4,5},{5,4},{6,7},{7,6},{8,9},{9,8},{10,11... | collective-permute-start | bytes 12296 | tf_op jit(solution)/shard_map/ppermute | solution.py:28
  39.3 3.6 %collective-permute-start.19 = (f32[8,128]{1,0:T(8,128)S(1)}, f32[8,128]{1,0:T(8,128)S(1)}, u32[]{:S(2)}, u32[]{:S(2)}) collective-permute-start(f32[8,128]{1,0:T(8,128)S(1)} %add.12), channel_id=1, source_target_pairs={{0,4},{1,7},{2,6},{3,5},{4,0},{5,3},{6,2},{7,1},{8,12},{9,15},{10,... | collective-permute-start | bytes 12296 | tf_op jit(solution)/shard_map/ppermute | solution.py:37
  40.3 3.6 %collective-permute-start.18 = (f32[8,128]{1,0:T(8,128)S(1)}, f32[8,128]{1,0:T(8,128)S(1)}, u32[]{:S(2)}, u32[]{:S(2)}) collective-permute-start(f32[8,128]{1,0:T(8,128)S(1)} %add.12), channel_id=1, source_target_pairs={{0,2},{1,3},{2,0},{3,1},{4,6},{5,7},{6,4},{7,5},{8,10},{9,11},{10,... | collective-permute-start | bytes 12296 | tf_op jit(solution)/shard_map/ppermute | solution.py:28
  42.9 1.2 %collective-permute-start.20 = (f32[8,128]{1,0:T(8,128)S(1)}, f32[8,128]{1,0:T(8,128)S(1)}, u32[]{:S(2)}, u32[]{:S(2)}) collective-permute-start(f32[8,128]{1,0:T(8,128)S(1)} %collective-permute-done.19), channel_id=1, source_target_pairs={{0,1},{1,0},{2,3},{3,2},{4,5},{5,4},{6,7},{7,6},{8,9},{9,8},{10,11... | collective-permute-start | bytes 12296 | tf_op jit(solution)/shard_map/ppermute | solution.py:28

commit v10 on v9

--- a/solution.py
+++ b/solution.py
@@ -417,8 +417,8 @@
 def gather(held, bits, count):
     for at in range(0, len(bits), 2):
         pair = bits[at : at + 2]
-        flips = pair if len(pair) == 1 else [pair[0], pair[1], sum(pair)]
-        held = jnp.concatenate([held] + [swap(held, flip, count) for flip in reversed(flips)], axis=0)
+        flips = pair if len(pair) == 1 else [pair[0], sum(pair), pair[1]]
+        held = jnp.concatenate([held] + [swap(held, flip, count) for flip in flips], axis=0)
     return held
 
 
@@ -452,8 +452,12 @@
     near = held[:copies]
     held = held[:, : 2 * feat + probes]
     beside = swap(held, core, count)
-    up, over = swap_apart(held, one, two, core, count), swap_apart(held, two, one, core, count)
-    kept_0, products, near_features = first(near, [held, beside], levels, None, [])
+    up = swap_apart(held, one, two, core, count)
+    kept_h, products, near_features = first(near, [held], levels, None, [])
+    held_again, products[-1] = lax.optimization_barrier((held, products[-1]))
+    over = swap_apart(held_again, two, one, core, count)
+    kept_0, products, _ = first(near, [beside], levels, near_features, products)
+    kept_0 = [*kept_h, *kept_0]
     up, products[-1] = lax.optimization_barrier((up, products[-1]))
     corner, up_beside = swap_apart(up, two, one, core, count), swap(up, core, count)
     kept_1, products, _ = first(near, [up], levels, near_features, products)

time: 45.1 us -> 44.3 us (0.982)
  waiting for transfers between devices: 10.4 us -> 9.37 us
    ppermute x6, waiting for transfers between devices: 3.01 us -> 2.26 us  [swap_apart(): lax.ppermute(array, AXES, [(i, i ^ (second if i & core else first)) for i...]
    pallas_call x5 -> x6, Pallas kernels: 8.43 us -> 8.57 us  [apply_first(): pl.pallas_call(functools.partial(apply_kernel, feat, group, keep, begin,...]
  transfers between devices with their start and end apart: 21 -> 21, of which waited for: 12 -> 8; matrix products, arithmetic and copies ran while one was open for 0% -> 0% of each run, Pallas kernels for 21% -> 22%
where the time goes in v10:
time: 44.3 us; the launch traced here: 44 us
  starting transfers between devices  18 us (41%)
  Pallas kernels  13.8 us (31%)
  waiting for transfers between devices  9.37 us (21%)
  between operations  2.71 us (6%)
    ppermute x15, starting transfers between devices, swap(): return lax.ppermute(array, AXES, [(i, i ^ bit) for i in range(count)])  11.1 us
    pallas_call x6, Pallas kernels, apply_first(): pl.pallas_call(functools.partial(apply_kernel, feat, group, keep, begin,...  8.57 us
    ppermute x15, waiting for transfers between devices, swap(): return lax.ppermute(array, AXES, [(i, i ^ bit) for i in range(count)])  7.11 us
    ppermute x6, starting transfers between devices, swap_apart(): lax.ppermute(array, AXES, [(i, i ^ (second if i & core else first)) for i...  6.9 us
    pallas_call x3, Pallas kernels, apply_again(): pl.pallas_call(functools.partial(again_kernel, copies, len(sent)), out_sh...  2.46 us
    ppermute x6, waiting for transfers between devices, swap_apart(): lax.ppermute(array, AXES, [(i, i ^ (second if i & core else first)) for i...  2.26 us
    pallas_call x1, Pallas kernels, combine(): pl.pallas_call(functools.partial(combine_kernel, feat, copies), out_shape...  1.18 us
  transfers between devices with their start and end apart: 21, of which 8 were waited for; matrix products, arithmetic and copies ran while one was open for 0% of the time, Pallas kernels for 22%

profile of v10, /device:TPU:0, one launch (start us, length us, event | category | flops | bytes accessed | tf_op | source)
XLA Modules:
  0.0 44.0 jit_solution(8302302047962776822)
XLA Ops:
  1.3 0.8 %shard_map.77.own_ref = bf16[1,96,256]{2,1,0:T(8,128)(2,1)S(1)} custom-call(f32[16,256]{1,0:T(8,128)} %bitcast.5, f32[16]{0:T(128)} %inv_ref.1, f32[32,256]{1,0:T(8,128)} %bitcast.4, s32[1]{0:T(128)S(6)} %copy.10.count_ref), custom_call_target="tpu_custom_call" | custom-call | tf_op jit(solution)/shard_map/pallas_call | solution.py:82
  2.1 4.1 %collective-permute-start = (bf16[1,96,256]{2,1,0:T(8,128)(2,1)S(1)}, bf16[1,96,256]{2,1,0:T(8,128)(2,1)S(1)}, u32[]{:S(2)}, u32[]{:S(2)}) collective-permute-start(bf16[1,96,256]{2,1,0:T(8,128)(2,1)S(1)} %shard_map.77.own_ref), channel_id=1, source_target_pairs={{0,16},{1,17},{2,18},{3,19},{4,20},{5,21},{6,22},{7,23},{8,24},{9,... | collective-permute-start | bytes 147464 | tf_op jit(solution)/shard_map/ppermute | solution.py:28
  6.2 1.3 %collective-permute-start.1 = (bf16[1,96,256]{2,1,0:T(8,128)(2,1)S(1)}, bf16[1,96,256]{2,1,0:T(8,128)(2,1)S(1)}, u32[]{:S(2)}, u32[]{:S(2)}) collective-permute-start(bf16[1,96,256]{2,1,0:T(8,128)(2,1)S(1)} %shard_map.77.own_ref), channel_id=1, source_target_pairs={{0,24},{1,25},{2,26},{3,27},{4,28},{5,29},{6,30},{7,31},{8,16},{9,... | collective-permute-start | bytes 147464 | tf_op jit(solution)/shard_map/ppermute | solution.py:28
  7.6 0.2 collective-permute-start.2
  9.1 0.1 pad_maximum_fusion.1
  9.2 3.0 %collective-permute-done.1 = bf16[1,96,256]{2,1,0:T(8,128)(2,1)S(1)} collective-permute-done((bf16[1,96,256]{2,1,0:T(8,128)(2,1)S(1)}, bf16[1,96,256]{2,1,0:T(8,128)(2,1)S(1)}, u32[]{:S(2)}, u32[]{:S(2)}) %collective-permute-start.1) | collective-permute-done | bytes 49184 | tf_op jit(solution)/shard_map/ppermute | solution.py:28
  12.2 0.1 broadcast_in_dim.2.levels_ref
  12.3 0.1 collective-permute-start.4
  12.4 1.6 %collective-permute-start.3 = (bf16[4,64,256]{2,1,0:T(8,128)(2,1)S(1)}, bf16[4,64,256]{2,1,0:T(8,128)(2,1)S(1)}, u32[]{:S(2)}, u32[]{:S(2)}) collective-permute-start(bf16[4,64,256]{2,1,0:T(8,128)(2,1)S(1)} %slice.3.refs_0_.near_ref), channel_id=1, source_target_pairs={{0,4},{1,3},{2,6},{3,1},{4,0},{5,7},{6,2},{7,5},{8,12},{9,11},{10,... | collective-permute-start | bytes 393224 | tf_op jit(solution)/shard_map/ppermute | solution.py:37
  14.0 1.1 %shard_map.78 = (bf16[1,1024,1024]{2,1,0:T(8,128)(2,1)S(1)}, f32[32,1024]{1,0:T(8,128)S(1)}, bf16[80,1024]{1,0:T(8,128)(2,1)S(1)}) custom-call(bf16[4,96,256]{2,1,0:T(8,128)(2,1)S(1)} %pad_maximum_fusion.near_ref, f32[2,256]{1,0:T(2,128)S(1)} %broadcast_in_dim.2.levels_ref, bf16[4,64,256]{2,1,0:T(8,128)(2,1)S(1)} %slice.3.refs_0_.near_ref), custom_call_target="tpu_custom_call" | custom-call | tf_op jit(solution)/shard_map/pallas_call | solution.py:198
  15.0 1.5 %collective-permute-start.7 = (bf16[4,64,256]{2,1,0:T(8,128)(2,1)S(1)}, bf16[4,64,256]{2,1,0:T(8,128)(2,1)S(1)}, u32[]{:S(2)}, u32[]{:S(2)}) collective-permute-start(bf16[4,64,256]{2,1,0:T(8,128)(2,1)S(1)} %slice.3.refs_0_.near_ref), channel_id=1, source_target_pairs={{0,2},{1,5},{2,0},{3,7},{4,6},{5,1},{6,4},{7,3},{8,10},{9,13},{10,... | collective-permute-start | bytes 393224 | tf_op jit(solution)/shard_map/ppermute | solution.py:37
  16.5 0.0 collective-permute-done.4.refs_0_
  16.5 1.1 %shard_map.79 = (bf16[1,1024,1024]{2,1,0:T(8,128)(2,1)S(1)}, f32[32,1024]{1,0:T(8,128)S(1)}) custom-call(bf16[4,96,256]{2,1,0:T(8,128)(2,1)S(1)} %pad_maximum_fusion.near_ref, f32[2,256]{1,0:T(2,128)S(1)} %broadcast_in_dim.2.levels_ref, bf16[4,64,256]{2,1,0:T(8,128)(2,1)S(1)} %collective-permute-done.4.refs_0_, ...), custom_call_target="tpu_custom_call" | custom-call | tf_op jit(solution)/shard_map/pallas_call | solution.py:198
  17.6 0.0 collective-permute-start.6
  17.6 1.9 %collective-permute-start.5 = (bf16[4,64,256]{2,1,0:T(8,128)(2,1)S(1)}, bf16[4,64,256]{2,1,0:T(8,128)(2,1)S(1)}, u32[]{:S(2)}, u32[]{:S(2)}) collective-permute-start(bf16[4,64,256]{2,1,0:T(8,128)(2,1)S(1)} %collective-permute-done.3.refs_0_), channel_id=1, source_target_pairs={{0,2},{1,5},{2,0},{3,7},{4,6},{5,1},{6,4},{7,3},{8,10},{9,13},{10,... | collective-permute-start | bytes 393224 | tf_op jit(solution)/shard_map/ppermute | solution.py:37
  19.5 1.1 %shard_map.80 = (bf16[1,1024,1024]{2,1,0:T(8,128)(2,1)S(1)}, f32[32,1024]{1,0:T(8,128)S(1)}) custom-call(bf16[4,96,256]{2,1,0:T(8,128)(2,1)S(1)} %pad_maximum_fusion.near_ref, f32[2,256]{1,0:T(2,128)S(1)} %broadcast_in_dim.2.levels_ref, bf16[4,64,256]{2,1,0:T(8,128)(2,1)S(1)} %collective-permute-done.3.refs_0_, ...), custom_call_target="tpu_custom_call" | custom-call | tf_op jit(solution)/shard_map/pallas_call | solution.py:198
  20.6 0.0 collective-permute-done.7.refs_1_
  20.6 0.0 collective-permute-start.9
  20.6 2.0 %shard_map.81 = (bf16[1,1024,1024]{2,1,0:T(8,128)(2,1)S(1)}, bf16[1,1024,1024]{2,1,0:T(8,128)(2,1)S(1)}, f32[32,1024]{1,0:T(8,128)S(1)}, f32[32,1024]{1,0:T(8,128)S(1)}) custom-call(bf16[4,96,256]{2,1,0:T(8,128)(2,1)S(1)} %pad_maximum_fusion.near_ref, f32[2,256]{1,0:T(2,128)S(1)} %broadcast_in_dim.2.levels_ref, ...), custom_call_target="tpu_custom_call" | custom-call | tf_op jit(solution)/shard_map/pallas_call | solution.py:198
  22.6 0.0 collective-permute-done.5.refs_1_
  22.7 0.5 %collective-permute-start.8 = (bf16[4,64,256]{2,1,0:T(8,128)(2,1)S(1)}, bf16[4,64,256]{2,1,0:T(8,128)(2,1)S(1)}, u32[]{:S(2)}, u32[]{:S(2)}) collective-permute-start(bf16[4,64,256]{2,1,0:T(8,128)(2,1)S(1)} %collective-permute-done.5.refs_1_), channel_id=1, source_target_pairs={{0,1},{1,0},{2,3},{3,2},{4,5},{5,4},{6,7},{7,6},{8,9},{9,8},{10,11... | collective-permute-start | bytes 393224 | tf_op jit(solution)/shard_map/ppermute | solution.py:28
  23.1 0.0 collective-permute-done.9.refs_0_
  23.1 2.0 %shard_map.82 = (bf16[1,1024,1024]{2,1,0:T(8,128)(2,1)S(1)}, bf16[1,1024,1024]{2,1,0:T(8,128)(2,1)S(1)}, f32[32,1024]{1,0:T(8,128)S(1)}, f32[32,1024]{1,0:T(8,128)S(1)}) custom-call(bf16[4,96,256]{2,1,0:T(8,128)(2,1)S(1)} %pad_maximum_fusion.near_ref, f32[2,256]{1,0:T(2,128)S(1)} %broadcast_in_dim.2.levels_ref, ...), custom_call_target="tpu_custom_call" | custom-call | tf_op jit(solution)/shard_map/pallas_call | solution.py:198
  25.1 0.0 collective-permute-done.8.refs_0_
  25.1 1.5 %shard_map.83 = (bf16[1,1024,1024]{2,1,0:T(8,128)(2,1)S(1)}, f32[32,1024]{1,0:T(8,128)S(1)}, bf16[1,144,256]{2,1,0:T(8,128)(2,1)S(1)}, f32[32,256]{1,0:T(8,128)S(1)}) custom-call(bf16[4,96,256]{2,1,0:T(8,128)(2,1)S(1)} %pad_maximum_fusion.near_ref, f32[2,256]{1,0:T(2,128)S(1)} %broadcast_in_dim.2.levels_ref, ...), custom_call_target="tpu_custom_call" | custom-call | tf_op jit(solution)/shard_map/pallas_call | solution.py:198
  26.6 2.4 %collective-permute-start.11 = (bf16[1,144,256]{2,1,0:T(8,128)(2,1)S(1)}, bf16[1,144,256]{2,1,0:T(8,128)(2,1)S(1)}, u32[]{:S(2)}, u32[]{:S(2)}) collective-permute-start(bf16[1,144,256]{2,1,0:T(8,128)(2,1)S(1)} %get-tuple-element.74.refs_0_), channel_id=1, source_target_pairs={{0,6},{1,7},{2,4},{3,5},{4,2},{5,3},{6,0},{7,1},{8,14},{9,15},{10,... | collective-permute-start | bytes 221192 | tf_op jit(solution)/shard_map/ppermute | solution.py:28
  28.9 0.2 collective-permute-start.10
  29.1 0.4 collective-permute-start.13
  29.6 0.5 %collective-permute-start.14 = (bf16[1,144,256]{2,1,0:T(8,128)(2,1)S(1)}, bf16[1,144,256]{2,1,0:T(8,128)(2,1)S(1)}, u32[]{:S(2)}, u32[]{:S(2)}) collective-permute-start(bf16[1,144,256]{2,1,0:T(8,128)(2,1)S(1)} %get-tuple-element.74.refs_0_), channel_id=1, source_target_pairs={{0,4},{1,3},{2,6},{3,1},{4,0},{5,7},{6,2},{7,5},{8,12},{9,11},{10,... | collective-permute-start | bytes 221192 | tf_op jit(solution)/shard_map/ppermute | solution.py:37
  30.1 1.8 %collective-permute-done.11.refs_0_.refs_2_ = bf16[1,144,256]{2,1,0:T(8,128)(2,1)S(1)} collective-permute-done((bf16[1,144,256]{2,1,0:T(8,128)(2,1)S(1)}, bf16[1,144,256]{2,1,0:T(8,128)(2,1)S(1)}, u32[]{:S(2)}, u32[]{:S(2)}) %collective-permute-start.11) | collective-permute-done | bytes 73760 | tf_op jit(solution)/shard_map/ppermute | solution.py:28
  31.9 0.0 collective-permute-start.12
  31.9 0.0 collective-permute-done.10.refs_1_
  31.9 0.8 %shard_map.84 = (f32[32,1024]{1,0:T(8,128)S(1)}, f32[32,1024]{1,0:T(8,128)S(1)}) custom-call(bf16[1,144,256]{2,1,0:T(8,128)(2,1)S(1)} %get-tuple-element.74.refs_0_, bf16[1,144,256]{2,1,0:T(8,128)(2,1)S(1)} %collective-permute-done.10.refs_1_, bf16[1,1024,1024]{2,1,0:T(8,128)(2,1)S(1)} %get-tuple-element.73.refs_2_.kept_near_ref, ...), custom_call_target="tpu_custom_call" | custom-call | tf_op jit(solution)/shard_map/pallas_call | solution.py:324
  32.7 1.1 %collective-permute-done.13.refs_1_.refs_5_ = bf16[1,144,256]{2,1,0:T(8,128)(2,1)S(1)} collective-permute-done((bf16[1,144,256]{2,1,0:T(8,128)(2,1)S(1)}, bf16[1,144,256]{2,1,0:T(8,128)(2,1)S(1)}, u32[]{:S(2)}, u32[]{:S(2)}) %collective-permute-start.13) | collective-permute-done | bytes 73760 | tf_op jit(solution)/shard_map/ppermute | solution.py:37
  33.8 0.1 collective-permute-done.14.refs_0_.refs_4_
  33.9 0.5 %collective-permute-start.16 = (bf16[1,144,256]{2,1,0:T(8,128)(2,1)S(1)}, bf16[1,144,256]{2,1,0:T(8,128)(2,1)S(1)}, u32[]{:S(2)}, u32[]{:S(2)}) collective-permute-start(bf16[1,144,256]{2,1,0:T(8,128)(2,1)S(1)} %collective-permute-done.13.refs_1_.refs_5_), channel_id=1, source_target_pairs={{0,1},{1,0},{2,3},{3,2},{4,5},{5,4},{6,7},{7,6},{8,9},{9,8},{10,11... | collective-permute-start | bytes 221192 | tf_op jit(solution)/shard_map/ppermute | solution.py:28
  34.4 0.8 %shard_map.86 = (f32[32,1024]{1,0:T(8,128)S(1)}, f32[32,1024]{1,0:T(8,128)S(1)}) custom-call(bf16[1,144,256]{2,1,0:T(8,128)(2,1)S(1)} %collective-permute-done.14.refs_0_.refs_4_, bf16[1,144,256]{2,1,0:T(8,128)(2,1)S(1)} %collective-permute-done.13.refs_1_.refs_5_, bf16[1,1024,1024]{2,1,0:T(8,128)(2,1)S(1)} %get-tuple-element.86.refs_2_, ...), custom_call_target="tpu_custom_call" | custom-call | tf_op jit(solution)/shard_map/pallas_call | solution.py:324
  35.2 0.8 %shard_map.85 = (f32[32,1024]{1,0:T(8,128)S(1)}, f32[32,1024]{1,0:T(8,128)S(1)}) custom-call(bf16[1,144,256]{2,1,0:T(8,128)(2,1)S(1)} %collective-permute-done.11.refs_0_.refs_2_, bf16[1,144,256]{2,1,0:T(8,128)(2,1)S(1)} %collective-permute-done.12.refs_1_.refs_3_, bf16[1,1024,1024]{2,1,0:T(8,128)(2,1)S(1)} %get-tuple-element.82.refs_2_, ...), custom_call_target="tpu_custom_call" | custom-call | tf_op jit(solution)/shard_map/pallas_call | solution.py:324
  36.1 0.0 collective-permute-done.16.refs_7_
  36.1 1.2 %shard_map.87 = (f32[8,128]{1,0:T(8,128)S(1)}, f32[32,256]{1,0:T(8,128)S(1)}, f32[32,256]{1,0:T(8,128)S(1)}, f32[32,256]{1,0:T(8,128)S(1)}, f32[32,256]{1,0:T(8,128)S(1)}, /*index=5*/f32[32,128]{1,0:T(8,128)S(1)}) custom-call(f32[2,256]{1,0:T(2,128)S(1)} %broadcast_in_dim.2.levels_ref, bf16[1,96,256]{2,1,0:T(8,128)(2,1)S(1)} %shard_map.77.own_ref, ...), custom_call_target="tpu_custom_call" | custom-call | tf_op jit(solution)/shard_map/pallas_call | solution.py:377
  37.3 0.0 collective-permute-start.17
  37.3 1.2 %collective-permute-done.17 = f32[8,128]{1,0:T(8,128)S(1)} collective-permute-done((f32[8,128]{1,0:T(8,128)S(1)}, f32[8,128]{1,0:T(8,128)S(1)}, u32[]{:S(2)}, u32[]{:S(2)}) %collective-permute-start.17) | collective-permute-done | bytes 4128 | tf_op jit(solution)/shard_map/ppermute | solution.py:28
  38.5 1.0 %collective-permute-start.19 = (f32[8,128]{1,0:T(8,128)S(1)}, f32[8,128]{1,0:T(8,128)S(1)}, u32[]{:S(2)}, u32[]{:S(2)}) collective-permute-start(f32[8,128]{1,0:T(8,128)S(1)} %add.12), channel_id=1, source_target_pairs={{0,4},{1,7},{2,6},{3,5},{4,0},{5,3},{6,2},{7,1},{8,12},{9,15},{10,... | collective-permute-start | bytes 12296 | tf_op jit(solution)/shard_map/ppermute | solution.py:37
  39.4 1.7 %collective-permute-start.18 = (f32[8,128]{1,0:T(8,128)S(1)}, f32[8,128]{1,0:T(8,128)S(1)}, u32[]{:S(2)}, u32[]{:S(2)}) collective-permute-start(f32[8,128]{1,0:T(8,128)S(1)} %add.12), channel_id=1, source_target_pairs={{0,2},{1,3},{2,0},{3,1},{4,6},{5,7},{6,4},{7,5},{8,10},{9,11},{10,... | collective-permute-start | bytes 12296 | tf_op jit(solution)/shard_map/ppermute | solution.py:28
  41.1 1.0 %collective-permute-done.19 = f32[8,128]{1,0:T(8,128)S(1)} collective-permute-done((f32[8,128]{1,0:T(8,128)S(1)}, f32[8,128]{1,0:T(8,128)S(1)}, u32[]{:S(2)}, u32[]{:S(2)}) %collective-permute-start.19) | collective-permute-done | bytes 4128 | tf_op jit(solution)/shard_map/ppermute | solution.py:37
  42.1 1.0 %collective-permute-done.18 = f32[8,128]{1,0:T(8,128)S(1)} collective-permute-done((f32[8,128]{1,0:T(8,128)S(1)}, f32[8,128]{1,0:T(8,128)S(1)}, u32[]{:S(2)}, u32[]{:S(2)}) %collective-permute-start.18) | collective-permute-done | bytes 4128 | tf_op jit(solution)/shard_map/ppermute | solution.py:28
  43.1 0.2 collective-permute-done.20
  43.3 0.8 %shard_map.88 = (f32[32,256]{1,0:T(8,128)}, f32[32,256]{1,0:T(8,128)}) custom-call(f32[8,128]{1,0:T(8,128)S(1)} %add_add_fusion.curve_ref, f32[32,128]{1,0:T(8,128)S(1)} %get-tuple-element.93.norm_ref, f32[32,256]{1,0:T(8,128)S(1)} %get-tuple-element.94.solution_ref, f32[32,256]{1,0:T(8,128)S(1)} %get-tuple-element.95.residual_ref, ...), custom_call_target="tpu_custom_call" | custom-call | tf_op jit(solution)/shard_map/pallas_call | solution.py:501
  (12 shorter events, 0.1 us)
Async XLA Ops:
  2.1 7.1 %collective-permute-start = (bf16[1,96,256]{2,1,0:T(8,128)(2,1)S(1)}, bf16[1,96,256]{2,1,0:T(8,128)(2,1)S(1)}, u32[]{:S(2)}, u32[]{:S(2)}) collective-permute-start(bf16[1,96,256]{2,1,0:T(8,128)(2,1)S(1)} %shard_map.77.own_ref), channel_id=1, source_target_pairs={{0,16},{1,17},{2,18},{3,19},{4,20},{5,21},{6,22},{7,23},{8,24},{9,... | collective-permute-start | bytes 147464 | tf_op jit(solution)/shard_map/ppermute | solution.py:28
  6.2 6.0 %collective-permute-start.1 = (bf16[1,96,256]{2,1,0:T(8,128)(2,1)S(1)}, bf16[1,96,256]{2,1,0:T(8,128)(2,1)S(1)}, u32[]{:S(2)}, u32[]{:S(2)}) collective-permute-start(bf16[1,96,256]{2,1,0:T(8,128)(2,1)S(1)} %shard_map.77.own_ref), channel_id=1, source_target_pairs={{0,24},{1,25},{2,26},{3,27},{4,28},{5,29},{6,30},{7,31},{8,16},{9,... | collective-permute-start | bytes 147464 | tf_op jit(solution)/shard_map/ppermute | solution.py:28
  7.6 4.6 %collective-permute-start.2 = (bf16[1,96,256]{2,1,0:T(8,128)(2,1)S(1)}, bf16[1,96,256]{2,1,0:T(8,128)(2,1)S(1)}, u32[]{:S(2)}, u32[]{:S(2)}) collective-permute-start(bf16[1,96,256]{2,1,0:T(8,128)(2,1)S(1)} %shard_map.77.own_ref), channel_id=1, source_target_pairs={{0,8},{1,9},{2,10},{3,11},{4,12},{5,13},{6,14},{7,15},{8,0},{9,1},... | collective-permute-start | bytes 147464 | tf_op jit(solution)/shard_map/ppermute | solution.py:28
  12.3 4.2 %collective-permute-start.4 = (bf16[4,64,256]{2,1,0:T(8,128)(2,1)S(1)}, bf16[4,64,256]{2,1,0:T(8,128)(2,1)S(1)}, u32[]{:S(2)}, u32[]{:S(2)}) collective-permute-start(bf16[4,64,256]{2,1,0:T(8,128)(2,1)S(1)} %slice.3.refs_0_.near_ref), channel_id=1, source_target_pairs={{0,1},{1,0},{2,3},{3,2},{4,5},{5,4},{6,7},{7,6},{8,9},{9,8},{10,11... | collective-permute-start | bytes 393224 | tf_op jit(solution)/shard_map/ppermute | solution.py:28
  12.4 5.2 %collective-permute-start.3 = (bf16[4,64,256]{2,1,0:T(8,128)(2,1)S(1)}, bf16[4,64,256]{2,1,0:T(8,128)(2,1)S(1)}, u32[]{:S(2)}, u32[]{:S(2)}) collective-permute-start(bf16[4,64,256]{2,1,0:T(8,128)(2,1)S(1)} %slice.3.refs_0_.near_ref), channel_id=1, source_target_pairs={{0,4},{1,3},{2,6},{3,1},{4,0},{5,7},{6,2},{7,5},{8,12},{9,11},{10,... | collective-permute-start | bytes 393224 | tf_op jit(solution)/shard_map/ppermute | solution.py:37
  15.0 5.6 %collective-permute-start.7 = (bf16[4,64,256]{2,1,0:T(8,128)(2,1)S(1)}, bf16[4,64,256]{2,1,0:T(8,128)(2,1)S(1)}, u32[]{:S(2)}, u32[]{:S(2)}) collective-permute-start(bf16[4,64,256]{2,1,0:T(8,128)(2,1)S(1)} %slice.3.refs_0_.near_ref), channel_id=1, source_target_pairs={{0,2},{1,5},{2,0},{3,7},{4,6},{5,1},{6,4},{7,3},{8,10},{9,13},{10,... | collective-permute-start | bytes 393224 | tf_op jit(solution)/shard_map/ppermute | solution.py:37
  17.6 3.0 %collective-permute-start.6 = (bf16[4,64,256]{2,1,0:T(8,128)(2,1)S(1)}, bf16[4,64,256]{2,1,0:T(8,128)(2,1)S(1)}, u32[]{:S(2)}, u32[]{:S(2)}) collective-permute-start(bf16[4,64,256]{2,1,0:T(8,128)(2,1)S(1)} %collective-permute-done.3.refs_0_), channel_id=1, source_target_pairs={{0,1},{1,0},{2,3},{3,2},{4,5},{5,4},{6,7},{7,6},{8,9},{9,8},{10,11... | collective-permute-start | bytes 393224 | tf_op jit(solution)/shard_map/ppermute | solution.py:28
  17.6 5.0 %collective-permute-start.5 = (bf16[4,64,256]{2,1,0:T(8,128)(2,1)S(1)}, bf16[4,64,256]{2,1,0:T(8,128)(2,1)S(1)}, u32[]{:S(2)}, u32[]{:S(2)}) collective-permute-start(bf16[4,64,256]{2,1,0:T(8,128)(2,1)S(1)} %collective-permute-done.3.refs_0_), channel_id=1, source_target_pairs={{0,2},{1,5},{2,0},{3,7},{4,6},{5,1},{6,4},{7,3},{8,10},{9,13},{10,... | collective-permute-start | bytes 393224 | tf_op jit(solution)/shard_map/ppermute | solution.py:37
  20.6 2.5 %collective-permute-start.9 = (bf16[4,64,256]{2,1,0:T(8,128)(2,1)S(1)}, bf16[4,64,256]{2,1,0:T(8,128)(2,1)S(1)}, u32[]{:S(2)}, u32[]{:S(2)}) collective-permute-start(bf16[4,64,256]{2,1,0:T(8,128)(2,1)S(1)} %collective-permute-done.7.refs_1_), channel_id=1, source_target_pairs={{0,1},{1,0},{2,3},{3,2},{4,5},{5,4},{6,7},{7,6},{8,9},{9,8},{10,11... | collective-permute-start | bytes 393224 | tf_op jit(solution)/shard_map/ppermute | solution.py:28
  22.7 2.4 %collective-permute-start.8 = (bf16[4,64,256]{2,1,0:T(8,128)(2,1)S(1)}, bf16[4,64,256]{2,1,0:T(8,128)(2,1)S(1)}, u32[]{:S(2)}, u32[]{:S(2)}) collective-permute-start(bf16[4,64,256]{2,1,0:T(8,128)(2,1)S(1)} %collective-permute-done.5.refs_1_), channel_id=1, source_target_pairs={{0,1},{1,0},{2,3},{3,2},{4,5},{5,4},{6,7},{7,6},{8,9},{9,8},{10,11... | collective-permute-start | bytes 393224 | tf_op jit(solution)/shard_map/ppermute | solution.py:28
  26.6 5.3 %collective-permute-start.11 = (bf16[1,144,256]{2,1,0:T(8,128)(2,1)S(1)}, bf16[1,144,256]{2,1,0:T(8,128)(2,1)S(1)}, u32[]{:S(2)}, u32[]{:S(2)}) collective-permute-start(bf16[1,144,256]{2,1,0:T(8,128)(2,1)S(1)} %get-tuple-element.74.refs_0_), channel_id=1, source_target_pairs={{0,6},{1,7},{2,4},{3,5},{4,2},{5,3},{6,0},{7,1},{8,14},{9,15},{10,... | collective-permute-start | bytes 221192 | tf_op jit(solution)/shard_map/ppermute | solution.py:28
  28.9 2.9 %collective-permute-start.10 = (bf16[1,144,256]{2,1,0:T(8,128)(2,1)S(1)}, bf16[1,144,256]{2,1,0:T(8,128)(2,1)S(1)}, u32[]{:S(2)}, u32[]{:S(2)}) collective-permute-start(bf16[1,144,256]{2,1,0:T(8,128)(2,1)S(1)} %get-tuple-element.74.refs_0_), channel_id=1, source_target_pairs={{0,1},{1,0},{2,3},{3,2},{4,5},{5,4},{6,7},{7,6},{8,9},{9,8},{10,11... | collective-permute-start | bytes 221192 | tf_op jit(solution)/shard_map/ppermute | solution.py:28
  29.1 4.7 %collective-permute-start.13 = (bf16[1,144,256]{2,1,0:T(8,128)(2,1)S(1)}, bf16[1,144,256]{2,1,0:T(8,128)(2,1)S(1)}, u32[]{:S(2)}, u32[]{:S(2)}) collective-permute-start(bf16[1,144,256]{2,1,0:T(8,128)(2,1)S(1)} %get-tuple-element.74.refs_0_), channel_id=1, source_target_pairs={{0,2},{1,5},{2,0},{3,7},{4,6},{5,1},{6,4},{7,3},{8,10},{9,13},{10,... | collective-permute-start | bytes 221192 | tf_op jit(solution)/shard_map/ppermute | solution.py:37
  29.6 4.4 %collective-permute-start.14 = (bf16[1,144,256]{2,1,0:T(8,128)(2,1)S(1)}, bf16[1,144,256]{2,1,0:T(8,128)(2,1)S(1)}, u32[]{:S(2)}, u32[]{:S(2)}) collective-permute-start(bf16[1,144,256]{2,1,0:T(8,128)(2,1)S(1)} %get-tuple-element.74.refs_0_), channel_id=1, source_target_pairs={{0,4},{1,3},{2,6},{3,1},{4,0},{5,7},{6,2},{7,5},{8,12},{9,11},{10,... | collective-permute-start | bytes 221192 | tf_op jit(solution)/shard_map/ppermute | solution.py:37
  31.9 3.4 %collective-permute-start.12 = (bf16[1,144,256]{2,1,0:T(8,128)(2,1)S(1)}, bf16[1,144,256]{2,1,0:T(8,128)(2,1)S(1)}, u32[]{:S(2)}, u32[]{:S(2)}) collective-permute-start(bf16[1,144,256]{2,1,0:T(8,128)(2,1)S(1)} %collective-permute-done.11.refs_0_.refs_2_), channel_id=1, source_target_pairs={{0,1},{1,0},{2,3},{3,2},{4,5},{5,4},{6,7},{7,6},{8,9},{9,8},{10,11... | collective-permute-start | bytes 221192 | tf_op jit(solution)/shard_map/ppermute | solution.py:28
  33.9 2.2 %collective-permute-start.15 = (bf16[1,144,256]{2,1,0:T(8,128)(2,1)S(1)}, bf16[1,144,256]{2,1,0:T(8,128)(2,1)S(1)}, u32[]{:S(2)}, u32[]{:S(2)}) collective-permute-start(bf16[1,144,256]{2,1,0:T(8,128)(2,1)S(1)} %collective-permute-done.14.refs_0_.refs_4_), channel_id=1, source_target_pairs={{0,1},{1,0},{2,3},{3,2},{4,5},{5,4},{6,7},{7,6},{8,9},{9,8},{10,11... | collective-permute-start | bytes 221192 | tf_op jit(solution)/shard_map/ppermute | solution.py:28
  33.9 2.2 %collective-permute-start.16 = (bf16[1,144,256]{2,1,0:T(8,128)(2,1)S(1)}, bf16[1,144,256]{2,1,0:T(8,128)(2,1)S(1)}, u32[]{:S(2)}, u32[]{:S(2)}) collective-permute-start(bf16[1,144,256]{2,1,0:T(8,128)(2,1)S(1)} %collective-permute-done.13.refs_1_.refs_5_), channel_id=1, source_target_pairs={{0,1},{1,0},{2,3},{3,2},{4,5},{5,4},{6,7},{7,6},{8,9},{9,8},{10,11... | collective-permute-start | bytes 221192 | tf_op jit(solution)/shard_map/ppermute | solution.py:28
  37.3 1.2 %collective-permute-start.17 = (f32[8,128]{1,0:T(8,128)S(1)}, f32[8,128]{1,0:T(8,128)S(1)}, u32[]{:S(2)}, u32[]{:S(2)}) collective-permute-start(f32[8,128]{1,0:T(8,128)S(1)} %get-tuple-element.92), channel_id=1, source_target_pairs={{0,1},{1,0},{2,3},{3,2},{4,5},{5,4},{6,7},{7,6},{8,9},{9,8},{10,11... | collective-permute-start | bytes 12296 | tf_op jit(solution)/shard_map/ppermute | solution.py:28
  38.5 3.6 %collective-permute-start.19 = (f32[8,128]{1,0:T(8,128)S(1)}, f32[8,128]{1,0:T(8,128)S(1)}, u32[]{:S(2)}, u32[]{:S(2)}) collective-permute-start(f32[8,128]{1,0:T(8,128)S(1)} %add.12), channel_id=1, source_target_pairs={{0,4},{1,7},{2,6},{3,5},{4,0},{5,3},{6,2},{7,1},{8,12},{9,15},{10,... | collective-permute-start | bytes 12296 | tf_op jit(solution)/shard_map/ppermute | solution.py:37
  39.4 3.6 %collective-permute-start.18 = (f32[8,128]{1,0:T(8,128)S(1)}, f32[8,128]{1,0:T(8,128)S(1)}, u32[]{:S(2)}, u32[]{:S(2)}) collective-permute-start(f32[8,128]{1,0:T(8,128)S(1)} %add.12), channel_id=1, source_target_pairs={{0,2},{1,3},{2,0},{3,1},{4,6},{5,7},{6,4},{7,5},{8,10},{9,11},{10,... | collective-permute-start | bytes 12296 | tf_op jit(solution)/shard_map/ppermute | solution.py:28
  42.1 1.2 %collective-permute-start.20 = (f32[8,128]{1,0:T(8,128)S(1)}, f32[8,128]{1,0:T(8,128)S(1)}, u32[]{:S(2)}, u32[]{:S(2)}) collective-permute-start(f32[8,128]{1,0:T(8,128)S(1)} %collective-permute-done.19), channel_id=1, source_target_pairs={{0,1},{1,0},{2,3},{3,2},{4,5},{5,4},{6,7},{7,6},{8,9},{9,8},{10,11... | collective-permute-start | bytes 12296 | tf_op jit(solution)/shard_map/ppermute | solution.py:28

commit v11 on v10

--- a/solution.py
+++ b/solution.py
@@ -475,15 +475,15 @@
     beside, corner = swap(held, core, count), swap(held, one | two, count)
     up, over = swap_apart(held, one, two, core, count), swap_apart(held, two, one, core, count)
     if keep:
-        corner_beside = swap(corner, core, count)
-        again_0 = apply_again([held, beside], kept[:2], copies)
-        over, up, again_0[0] = lax.optimization_barrier((over, up, again_0[0]))
-    else:
-        corner_beside = swap(corner, core, count)
+        again_0 = apply_again([held], kept[:1], copies)
+        corner, again_0[0] = lax.optimization_barrier((corner, again_0[0]))
+    corner_beside = swap(corner, core, count)
+    if keep:
+        again_1 = apply_again([beside, corner], [kept[1], kept[6]], copies)
+        over, up, again_1[0] = lax.optimization_barrier((over, up, again_1[0]))
     up_beside, over_beside = (swap(array, core, count) for array in (up, over))
     if keep:
-        again_1 = apply_again([corner, corner_beside], kept[6:], copies)
-        again_2 = apply_again([up, over], [kept[2], kept[4]], copies)
+        again_2 = apply_again([corner_beside, up, over], [kept[7], kept[2], kept[4]], copies)
         images = [held, beside, corner, corner_beside, up, over, up_beside, over_beside]
         order = [0, 1, 6, 7, 2, 4, 3, 5]
         kept, products = ([each[at] for at in order] for each in (kept, products))

time: 44.3 us -> 43.8 us (0.989)
  waiting for transfers between devices: 9.37 us -> 8.86 us
    ppermute x15, waiting for transfers between devices: 7.11 us -> 6.62 us  [swap(): return lax.ppermute(array, AXES, [(i, i ^ bit) for i in range(count)])]
where the time goes in v11:
time: 43.8 us; the launch traced here: 43.5 us
  starting transfers between devices  18 us (41%)
  Pallas kernels  13.8 us (32%)
  waiting for transfers between devices  8.86 us (20%)
  between operations  2.7 us (6%)
    ppermute x15, starting transfers between devices, swap(): return lax.ppermute(array, AXES, [(i, i ^ bit) for i in range(count)])  11.1 us
    pallas_call x6, Pallas kernels, apply_first(): pl.pallas_call(functools.partial(apply_kernel, feat, group, keep, begin,...  8.57 us
    ppermute x6, starting transfers between devices, swap_apart(): lax.ppermute(array, AXES, [(i, i ^ (second if i & core else first)) for i...  6.91 us
    ppermute x15, waiting for transfers between devices, swap(): return lax.ppermute(array, AXES, [(i, i ^ bit) for i in range(count)])  6.62 us
    pallas_call x3, Pallas kernels, apply_again(): pl.pallas_call(functools.partial(again_kernel, copies, len(sent)), out_sh...  2.44 us
    ppermute x6, waiting for transfers between devices, swap_apart(): lax.ppermute(array, AXES, [(i, i ^ (second if i & core else first)) for i...  2.25 us
    pallas_call x1, Pallas kernels, combine(): pl.pallas_call(functools.partial(combine_kernel, feat, copies), out_shape...  1.17 us
  transfers between devices with their start and end apart: 21, of which 8 were waited for; matrix products, arithmetic and copies ran while one was open for 0% of the time, Pallas kernels for 22%

profile of v11, /device:TPU:0, one launch (start us, length us, event | category | flops | bytes accessed | tf_op | source)
XLA Modules:
  0.0 43.5 jit_solution(9109229265603808808)
XLA Ops:
  1.3 0.8 %shard_map.77.own_ref = bf16[1,96,256]{2,1,0:T(8,128)(2,1)S(1)} custom-call(f32[16,256]{1,0:T(8,128)} %bitcast.5, f32[16]{0:T(128)} %inv_ref.1, f32[32,256]{1,0:T(8,128)} %bitcast.4, s32[1]{0:T(128)S(6)} %copy.10.count_ref), custom_call_target="tpu_custom_call" | custom-call | tf_op jit(solution)/shard_map/pallas_call | solution.py:82
  2.1 4.1 %collective-permute-start = (bf16[1,96,256]{2,1,0:T(8,128)(2,1)S(1)}, bf16[1,96,256]{2,1,0:T(8,128)(2,1)S(1)}, u32[]{:S(2)}, u32[]{:S(2)}) collective-permute-start(bf16[1,96,256]{2,1,0:T(8,128)(2,1)S(1)} %shard_map.77.own_ref), channel_id=1, source_target_pairs={{0,16},{1,17},{2,18},{3,19},{4,20},{5,21},{6,22},{7,23},{8,24},{9,... | collective-permute-start | bytes 147464 | tf_op jit(solution)/shard_map/ppermute | solution.py:28
  6.2 1.3 %collective-permute-start.1 = (bf16[1,96,256]{2,1,0:T(8,128)(2,1)S(1)}, bf16[1,96,256]{2,1,0:T(8,128)(2,1)S(1)}, u32[]{:S(2)}, u32[]{:S(2)}) collective-permute-start(bf16[1,96,256]{2,1,0:T(8,128)(2,1)S(1)} %shard_map.77.own_ref), channel_id=1, source_target_pairs={{0,24},{1,25},{2,26},{3,27},{4,28},{5,29},{6,30},{7,31},{8,16},{9,... | collective-permute-start | bytes 147464 | tf_op jit(solution)/shard_map/ppermute | solution.py:28
  7.6 0.2 collective-permute-start.2
  9.1 0.1 pad_maximum_fusion.1
  9.2 3.0 %collective-permute-done.1 = bf16[1,96,256]{2,1,0:T(8,128)(2,1)S(1)} collective-permute-done((bf16[1,96,256]{2,1,0:T(8,128)(2,1)S(1)}, bf16[1,96,256]{2,1,0:T(8,128)(2,1)S(1)}, u32[]{:S(2)}, u32[]{:S(2)}) %collective-permute-start.1) | collective-permute-done | bytes 49184 | tf_op jit(solution)/shard_map/ppermute | solution.py:28
  12.2 0.0 collective-permute-done.2
  12.2 0.1 broadcast_in_dim.2.levels_ref
  12.3 0.1 collective-permute-start.4
  12.4 1.6 %collective-permute-start.3 = (bf16[4,64,256]{2,1,0:T(8,128)(2,1)S(1)}, bf16[4,64,256]{2,1,0:T(8,128)(2,1)S(1)}, u32[]{:S(2)}, u32[]{:S(2)}) collective-permute-start(bf16[4,64,256]{2,1,0:T(8,128)(2,1)S(1)} %slice.3.refs_0_.near_ref), channel_id=1, source_target_pairs={{0,4},{1,3},{2,6},{3,1},{4,0},{5,7},{6,2},{7,5},{8,12},{9,11},{10,... | collective-permute-start | bytes 393224 | tf_op jit(solution)/shard_map/ppermute | solution.py:37
  14.0 1.1 %shard_map.78 = (bf16[1,1024,1024]{2,1,0:T(8,128)(2,1)S(1)}, f32[32,1024]{1,0:T(8,128)S(1)}, bf16[80,1024]{1,0:T(8,128)(2,1)S(1)}) custom-call(bf16[4,96,256]{2,1,0:T(8,128)(2,1)S(1)} %pad_maximum_fusion.near_ref, f32[2,256]{1,0:T(2,128)S(1)} %broadcast_in_dim.2.levels_ref, bf16[4,64,256]{2,1,0:T(8,128)(2,1)S(1)} %slice.3.refs_0_.near_ref), custom_call_target="tpu_custom_call" | custom-call | tf_op jit(solution)/shard_map/pallas_call | solution.py:198
  15.0 1.5 %collective-permute-start.7 = (bf16[4,64,256]{2,1,0:T(8,128)(2,1)S(1)}, bf16[4,64,256]{2,1,0:T(8,128)(2,1)S(1)}, u32[]{:S(2)}, u32[]{:S(2)}) collective-permute-start(bf16[4,64,256]{2,1,0:T(8,128)(2,1)S(1)} %slice.3.refs_0_.near_ref), channel_id=1, source_target_pairs={{0,2},{1,5},{2,0},{3,7},{4,6},{5,1},{6,4},{7,3},{8,10},{9,13},{10,... | collective-permute-start | bytes 393224 | tf_op jit(solution)/shard_map/ppermute | solution.py:37
  16.5 0.0 collective-permute-done.4.refs_0_
  16.5 1.1 %shard_map.79 = (bf16[1,1024,1024]{2,1,0:T(8,128)(2,1)S(1)}, f32[32,1024]{1,0:T(8,128)S(1)}) custom-call(bf16[4,96,256]{2,1,0:T(8,128)(2,1)S(1)} %pad_maximum_fusion.near_ref, f32[2,256]{1,0:T(2,128)S(1)} %broadcast_in_dim.2.levels_ref, bf16[4,64,256]{2,1,0:T(8,128)(2,1)S(1)} %collective-permute-done.4.refs_0_, ...), custom_call_target="tpu_custom_call" | custom-call | tf_op jit(solution)/shard_map/pallas_call | solution.py:198
  17.6 0.0 collective-permute-start.6
  17.6 1.9 %collective-permute-start.5 = (bf16[4,64,256]{2,1,0:T(8,128)(2,1)S(1)}, bf16[4,64,256]{2,1,0:T(8,128)(2,1)S(1)}, u32[]{:S(2)}, u32[]{:S(2)}) collective-permute-start(bf16[4,64,256]{2,1,0:T(8,128)(2,1)S(1)} %collective-permute-done.3.refs_0_), channel_id=1, source_target_pairs={{0,2},{1,5},{2,0},{3,7},{4,6},{5,1},{6,4},{7,3},{8,10},{9,13},{10,... | collective-permute-start | bytes 393224 | tf_op jit(solution)/shard_map/ppermute | solution.py:37
  19.5 1.1 %shard_map.80 = (bf16[1,1024,1024]{2,1,0:T(8,128)(2,1)S(1)}, f32[32,1024]{1,0:T(8,128)S(1)}) custom-call(bf16[4,96,256]{2,1,0:T(8,128)(2,1)S(1)} %pad_maximum_fusion.near_ref, f32[2,256]{1,0:T(2,128)S(1)} %broadcast_in_dim.2.levels_ref, bf16[4,64,256]{2,1,0:T(8,128)(2,1)S(1)} %collective-permute-done.3.refs_0_, ...), custom_call_target="tpu_custom_call" | custom-call | tf_op jit(solution)/shard_map/pallas_call | solution.py:198
  20.6 0.0 collective-permute-done.7.refs_1_
  20.6 0.0 collective-permute-start.9
  20.6 0.0 collective-permute-done.6.refs_0_
  20.6 2.0 %shard_map.81 = (bf16[1,1024,1024]{2,1,0:T(8,128)(2,1)S(1)}, bf16[1,1024,1024]{2,1,0:T(8,128)(2,1)S(1)}, f32[32,1024]{1,0:T(8,128)S(1)}, f32[32,1024]{1,0:T(8,128)S(1)}) custom-call(bf16[4,96,256]{2,1,0:T(8,128)(2,1)S(1)} %pad_maximum_fusion.near_ref, f32[2,256]{1,0:T(2,128)S(1)} %broadcast_in_dim.2.levels_ref, ...), custom_call_target="tpu_custom_call" | custom-call | tf_op jit(solution)/shard_map/pallas_call | solution.py:198
  22.6 0.1 collective-permute-done.5.refs_1_
  22.7 0.5 %collective-permute-start.8 = (bf16[4,64,256]{2,1,0:T(8,128)(2,1)S(1)}, bf16[4,64,256]{2,1,0:T(8,128)(2,1)S(1)}, u32[]{:S(2)}, u32[]{:S(2)}) collective-permute-start(bf16[4,64,256]{2,1,0:T(8,128)(2,1)S(1)} %collective-permute-done.5.refs_1_), channel_id=1, source_target_pairs={{0,1},{1,0},{2,3},{3,2},{4,5},{5,4},{6,7},{7,6},{8,9},{9,8},{10,11... | collective-permute-start | bytes 393224 | tf_op jit(solution)/shard_map/ppermute | solution.py:28
  23.1 0.0 collective-permute-done.9.refs_0_
  23.1 2.0 %shard_map.82 = (bf16[1,1024,1024]{2,1,0:T(8,128)(2,1)S(1)}, bf16[1,1024,1024]{2,1,0:T(8,128)(2,1)S(1)}, f32[32,1024]{1,0:T(8,128)S(1)}, f32[32,1024]{1,0:T(8,128)S(1)}) custom-call(bf16[4,96,256]{2,1,0:T(8,128)(2,1)S(1)} %pad_maximum_fusion.near_ref, f32[2,256]{1,0:T(2,128)S(1)} %broadcast_in_dim.2.levels_ref, ...), custom_call_target="tpu_custom_call" | custom-call | tf_op jit(solution)/shard_map/pallas_call | solution.py:198
  25.1 1.5 %shard_map.83 = (bf16[1,1024,1024]{2,1,0:T(8,128)(2,1)S(1)}, f32[32,1024]{1,0:T(8,128)S(1)}, bf16[1,144,256]{2,1,0:T(8,128)(2,1)S(1)}, f32[32,256]{1,0:T(8,128)S(1)}) custom-call(bf16[4,96,256]{2,1,0:T(8,128)(2,1)S(1)} %pad_maximum_fusion.near_ref, f32[2,256]{1,0:T(2,128)S(1)} %broadcast_in_dim.2.levels_ref, ...), custom_call_target="tpu_custom_call" | custom-call | tf_op jit(solution)/shard_map/pallas_call | solution.py:198
  26.6 2.4 %collective-permute-start.11 = (bf16[1,144,256]{2,1,0:T(8,128)(2,1)S(1)}, bf16[1,144,256]{2,1,0:T(8,128)(2,1)S(1)}, u32[]{:S(2)}, u32[]{:S(2)}) collective-permute-start(bf16[1,144,256]{2,1,0:T(8,128)(2,1)S(1)} %get-tuple-element.75.refs_0_), channel_id=1, source_target_pairs={{0,6},{1,7},{2,4},{3,5},{4,2},{5,3},{6,0},{7,1},{8,14},{9,15},{10,... | collective-permute-start | bytes 221192 | tf_op jit(solution)/shard_map/ppermute | solution.py:28
  28.9 0.2 collective-permute-start.10
  29.1 0.4 collective-permute-start.13
  29.6 0.5 %collective-permute-start.14 = (bf16[1,144,256]{2,1,0:T(8,128)(2,1)S(1)}, bf16[1,144,256]{2,1,0:T(8,128)(2,1)S(1)}, u32[]{:S(2)}, u32[]{:S(2)}) collective-permute-start(bf16[1,144,256]{2,1,0:T(8,128)(2,1)S(1)} %get-tuple-element.75.refs_0_), channel_id=1, source_target_pairs={{0,4},{1,3},{2,6},{3,1},{4,0},{5,7},{6,2},{7,5},{8,12},{9,11},{10,... | collective-permute-start | bytes 221192 | tf_op jit(solution)/shard_map/ppermute | solution.py:37
  30.1 0.5 %shard_map.84.refs_16_ = f32[32,1024]{1,0:T(8,128)S(1)} custom-call(bf16[1,144,256]{2,1,0:T(8,128)(2,1)S(1)} %get-tuple-element.75.refs_0_, bf16[1,1024,1024]{2,1,0:T(8,128)(2,1)S(1)} %get-tuple-element.74.refs_1_.kept_near_ref), custom_call_target="tpu_custom_call" | custom-call | tf_op jit(solution)/shard_map/pallas_call | solution.py:324
  30.5 1.3 %collective-permute-done.11.refs_1_.refs_2_ = bf16[1,144,256]{2,1,0:T(8,128)(2,1)S(1)} collective-permute-done((bf16[1,144,256]{2,1,0:T(8,128)(2,1)S(1)}, bf16[1,144,256]{2,1,0:T(8,128)(2,1)S(1)}, u32[]{:S(2)}, u32[]{:S(2)}) %collective-permute-start.11) | collective-permute-done | bytes 73760 | tf_op jit(solution)/shard_map/ppermute | solution.py:28
  31.9 0.0 collective-permute-start.12
  31.9 0.8 %shard_map.85 = (f32[32,1024]{1,0:T(8,128)S(1)}, f32[32,1024]{1,0:T(8,128)S(1)}) custom-call(bf16[1,144,256]{2,1,0:T(8,128)(2,1)S(1)} %collective-permute-done.10.refs_0_.refs_1_, bf16[1,144,256]{2,1,0:T(8,128)(2,1)S(1)} %collective-permute-done.11.refs_1_.refs_2_, bf16[1,1024,1024]{2,1,0:T(8,128)(2,1)S(1)} %get-tuple-element.77.refs_2_, ...), custom_call_target="tpu_custom_call" | custom-call | tf_op jit(solution)/shard_map/pallas_call | solution.py:324
  32.7 1.2 %collective-permute-done.13.refs_2_.refs_5_ = bf16[1,144,256]{2,1,0:T(8,128)(2,1)S(1)} collective-permute-done((bf16[1,144,256]{2,1,0:T(8,128)(2,1)S(1)}, bf16[1,144,256]{2,1,0:T(8,128)(2,1)S(1)}, u32[]{:S(2)}, u32[]{:S(2)}) %collective-permute-start.13) | collective-permute-done | bytes 73760 | tf_op jit(solution)/shard_map/ppermute | solution.py:37
  33.8 0.1 collective-permute-done.14.refs_1_.refs_4_
  33.9 0.5 %collective-permute-start.16 = (bf16[1,144,256]{2,1,0:T(8,128)(2,1)S(1)}, bf16[1,144,256]{2,1,0:T(8,128)(2,1)S(1)}, u32[]{:S(2)}, u32[]{:S(2)}) collective-permute-start(bf16[1,144,256]{2,1,0:T(8,128)(2,1)S(1)} %collective-permute-done.13.refs_2_.refs_5_), channel_id=1, source_target_pairs={{0,1},{1,0},{2,3},{3,2},{4,5},{5,4},{6,7},{7,6},{8,9},{9,8},{10,11... | collective-permute-start | bytes 221192 | tf_op jit(solution)/shard_map/ppermute | solution.py:28
  34.4 1.2 %shard_map.86 = (f32[32,1024]{1,0:T(8,128)S(1)}, f32[32,1024]{1,0:T(8,128)S(1)}, f32[32,1024]{1,0:T(8,128)S(1)}) custom-call(bf16[1,144,256]{2,1,0:T(8,128)(2,1)S(1)} %collective-permute-done.12.refs_0_.refs_3_, bf16[1,144,256]{2,1,0:T(8,128)(2,1)S(1)} %collective-permute-done.14.refs_1_.refs_4_, ...), custom_call_target="tpu_custom_call" | custom-call | tf_op jit(solution)/shard_map/pallas_call | solution.py:324
  35.6 0.0 collective-permute-done.16.refs_7_
  35.6 1.2 %shard_map.87 = (f32[8,128]{1,0:T(8,128)S(1)}, f32[32,256]{1,0:T(8,128)S(1)}, f32[32,256]{1,0:T(8,128)S(1)}, f32[32,256]{1,0:T(8,128)S(1)}, f32[32,256]{1,0:T(8,128)S(1)}, /*index=5*/f32[32,128]{1,0:T(8,128)S(1)}) custom-call(f32[2,256]{1,0:T(2,128)S(1)} %broadcast_in_dim.2.levels_ref, bf16[1,96,256]{2,1,0:T(8,128)(2,1)S(1)} %shard_map.77.own_ref, ...), custom_call_target="tpu_custom_call" | custom-call | tf_op jit(solution)/shard_map/pallas_call | solution.py:377
  36.8 0.1 collective-permute-start.17
  36.9 1.1 %collective-permute-done.17 = f32[8,128]{1,0:T(8,128)S(1)} collective-permute-done((f32[8,128]{1,0:T(8,128)S(1)}, f32[8,128]{1,0:T(8,128)S(1)}, u32[]{:S(2)}, u32[]{:S(2)}) %collective-permute-start.17) | collective-permute-done | bytes 4128 | tf_op jit(solution)/shard_map/ppermute | solution.py:28
  38.0 1.0 %collective-permute-start.19 = (f32[8,128]{1,0:T(8,128)S(1)}, f32[8,128]{1,0:T(8,128)S(1)}, u32[]{:S(2)}, u32[]{:S(2)}) collective-permute-start(f32[8,128]{1,0:T(8,128)S(1)} %add.12), channel_id=1, source_target_pairs={{0,4},{1,7},{2,6},{3,5},{4,0},{5,3},{6,2},{7,1},{8,12},{9,15},{10,... | collective-permute-start | bytes 12296 | tf_op jit(solution)/shard_map/ppermute | solution.py:37
  39.0 1.7 %collective-permute-start.18 = (f32[8,128]{1,0:T(8,128)S(1)}, f32[8,128]{1,0:T(8,128)S(1)}, u32[]{:S(2)}, u32[]{:S(2)}) collective-permute-start(f32[8,128]{1,0:T(8,128)S(1)} %add.12), channel_id=1, source_target_pairs={{0,2},{1,3},{2,0},{3,1},{4,6},{5,7},{6,4},{7,5},{8,10},{9,11},{10,... | collective-permute-start | bytes 12296 | tf_op jit(solution)/shard_map/ppermute | solution.py:28
  40.6 1.0 %collective-permute-done.19 = f32[8,128]{1,0:T(8,128)S(1)} collective-permute-done((f32[8,128]{1,0:T(8,128)S(1)}, f32[8,128]{1,0:T(8,128)S(1)}, u32[]{:S(2)}, u32[]{:S(2)}) %collective-permute-start.19) | collective-permute-done | bytes 4128 | tf_op jit(solution)/shard_map/ppermute | solution.py:37
  41.6 1.0 %collective-permute-done.18 = f32[8,128]{1,0:T(8,128)S(1)} collective-permute-done((f32[8,128]{1,0:T(8,128)S(1)}, f32[8,128]{1,0:T(8,128)S(1)}, u32[]{:S(2)}, u32[]{:S(2)}) %collective-permute-start.18) | collective-permute-done | bytes 4128 | tf_op jit(solution)/shard_map/ppermute | solution.py:28
  42.6 0.2 collective-permute-done.20
  42.8 0.8 %shard_map.88 = (f32[32,256]{1,0:T(8,128)}, f32[32,256]{1,0:T(8,128)}) custom-call(f32[8,128]{1,0:T(8,128)S(1)} %add_add_fusion.curve_ref, f32[32,128]{1,0:T(8,128)S(1)} %get-tuple-element.95.norm_ref, f32[32,256]{1,0:T(8,128)S(1)} %get-tuple-element.96.solution_ref, f32[32,256]{1,0:T(8,128)S(1)} %get-tuple-element.97.residual_ref, ...), custom_call_target="tpu_custom_call" | custom-call | tf_op jit(solution)/shard_map/pallas_call | solution.py:501
  (12 shorter events, 0.1 us)
Async XLA Ops:
  2.1 7.1 %collective-permute-start = (bf16[1,96,256]{2,1,0:T(8,128)(2,1)S(1)}, bf16[1,96,256]{2,1,0:T(8,128)(2,1)S(1)}, u32[]{:S(2)}, u32[]{:S(2)}) collective-permute-start(bf16[1,96,256]{2,1,0:T(8,128)(2,1)S(1)} %shard_map.77.own_ref), channel_id=1, source_target_pairs={{0,16},{1,17},{2,18},{3,19},{4,20},{5,21},{6,22},{7,23},{8,24},{9,... | collective-permute-start | bytes 147464 | tf_op jit(solution)/shard_map/ppermute | solution.py:28
  6.2 6.0 %collective-permute-start.1 = (bf16[1,96,256]{2,1,0:T(8,128)(2,1)S(1)}, bf16[1,96,256]{2,1,0:T(8,128)(2,1)S(1)}, u32[]{:S(2)}, u32[]{:S(2)}) collective-permute-start(bf16[1,96,256]{2,1,0:T(8,128)(2,1)S(1)} %shard_map.77.own_ref), channel_id=1, source_target_pairs={{0,24},{1,25},{2,26},{3,27},{4,28},{5,29},{6,30},{7,31},{8,16},{9,... | collective-permute-start | bytes 147464 | tf_op jit(solution)/shard_map/ppermute | solution.py:28
  7.6 4.6 %collective-permute-start.2 = (bf16[1,96,256]{2,1,0:T(8,128)(2,1)S(1)}, bf16[1,96,256]{2,1,0:T(8,128)(2,1)S(1)}, u32[]{:S(2)}, u32[]{:S(2)}) collective-permute-start(bf16[1,96,256]{2,1,0:T(8,128)(2,1)S(1)} %shard_map.77.own_ref), channel_id=1, source_target_pairs={{0,8},{1,9},{2,10},{3,11},{4,12},{5,13},{6,14},{7,15},{8,0},{9,1},... | collective-permute-start | bytes 147464 | tf_op jit(solution)/shard_map/ppermute | solution.py:28
  12.3 4.2 %collective-permute-start.4 = (bf16[4,64,256]{2,1,0:T(8,128)(2,1)S(1)}, bf16[4,64,256]{2,1,0:T(8,128)(2,1)S(1)}, u32[]{:S(2)}, u32[]{:S(2)}) collective-permute-start(bf16[4,64,256]{2,1,0:T(8,128)(2,1)S(1)} %slice.3.refs_0_.near_ref), channel_id=1, source_target_pairs={{0,1},{1,0},{2,3},{3,2},{4,5},{5,4},{6,7},{7,6},{8,9},{9,8},{10,11... | collective-permute-start | bytes 393224 | tf_op jit(solution)/shard_map/ppermute | solution.py:28
  12.4 5.2 %collective-permute-start.3 = (bf16[4,64,256]{2,1,0:T(8,128)(2,1)S(1)}, bf16[4,64,256]{2,1,0:T(8,128)(2,1)S(1)}, u32[]{:S(2)}, u32[]{:S(2)}) collective-permute-start(bf16[4,64,256]{2,1,0:T(8,128)(2,1)S(1)} %slice.3.refs_0_.near_ref), channel_id=1, source_target_pairs={{0,4},{1,3},{2,6},{3,1},{4,0},{5,7},{6,2},{7,5},{8,12},{9,11},{10,... | collective-permute-start | bytes 393224 | tf_op jit(solution)/shard_map/ppermute | solution.py:37
  15.0 5.6 %collective-permute-start.7 = (bf16[4,64,256]{2,1,0:T(8,128)(2,1)S(1)}, bf16[4,64,256]{2,1,0:T(8,128)(2,1)S(1)}, u32[]{:S(2)}, u32[]{:S(2)}) collective-permute-start(bf16[4,64,256]{2,1,0:T(8,128)(2,1)S(1)} %slice.3.refs_0_.near_ref), channel_id=1, source_target_pairs={{0,2},{1,5},{2,0},{3,7},{4,6},{5,1},{6,4},{7,3},{8,10},{9,13},{10,... | collective-permute-start | bytes 393224 | tf_op jit(solution)/shard_map/ppermute | solution.py:37
  17.6 3.0 %collective-permute-start.6 = (bf16[4,64,256]{2,1,0:T(8,128)(2,1)S(1)}, bf16[4,64,256]{2,1,0:T(8,128)(2,1)S(1)}, u32[]{:S(2)}, u32[]{:S(2)}) collective-permute-start(bf16[4,64,256]{2,1,0:T(8,128)(2,1)S(1)} %collective-permute-done.3.refs_0_), channel_id=1, source_target_pairs={{0,1},{1,0},{2,3},{3,2},{4,5},{5,4},{6,7},{7,6},{8,9},{9,8},{10,11... | collective-permute-start | bytes 393224 | tf_op jit(solution)/shard_map/ppermute | solution.py:28
  17.6 5.0 %collective-permute-start.5 = (bf16[4,64,256]{2,1,0:T(8,128)(2,1)S(1)}, bf16[4,64,256]{2,1,0:T(8,128)(2,1)S(1)}, u32[]{:S(2)}, u32[]{:S(2)}) collective-permute-start(bf16[4,64,256]{2,1,0:T(8,128)(2,1)S(1)} %collective-permute-done.3.refs_0_), channel_id=1, source_target_pairs={{0,2},{1,5},{2,0},{3,7},{4,6},{5,1},{6,4},{7,3},{8,10},{9,13},{10,... | collective-permute-start | bytes 393224 | tf_op jit(solution)/shard_map/ppermute | solution.py:37
  20.6 2.5 %collective-permute-start.9 = (bf16[4,64,256]{2,1,0:T(8,128)(2,1)S(1)}, bf16[4,64,256]{2,1,0:T(8,128)(2,1)S(1)}, u32[]{:S(2)}, u32[]{:S(2)}) collective-permute-start(bf16[4,64,256]{2,1,0:T(8,128)(2,1)S(1)} %collective-permute-done.7.refs_1_), channel_id=1, source_target_pairs={{0,1},{1,0},{2,3},{3,2},{4,5},{5,4},{6,7},{7,6},{8,9},{9,8},{10,11... | collective-permute-start | bytes 393224 | tf_op jit(solution)/shard_map/ppermute | solution.py:28
  22.7 2.4 %collective-permute-start.8 = (bf16[4,64,256]{2,1,0:T(8,128)(2,1)S(1)}, bf16[4,64,256]{2,1,0:T(8,128)(2,1)S(1)}, u32[]{:S(2)}, u32[]{:S(2)}) collective-permute-start(bf16[4,64,256]{2,1,0:T(8,128)(2,1)S(1)} %collective-permute-done.5.refs_1_), channel_id=1, source_target_pairs={{0,1},{1,0},{2,3},{3,2},{4,5},{5,4},{6,7},{7,6},{8,9},{9,8},{10,11... | collective-permute-start | bytes 393224 | tf_op jit(solution)/shard_map/ppermute | solution.py:28
  26.6 5.3 %collective-permute-start.11 = (bf16[1,144,256]{2,1,0:T(8,128)(2,1)S(1)}, bf16[1,144,256]{2,1,0:T(8,128)(2,1)S(1)}, u32[]{:S(2)}, u32[]{:S(2)}) collective-permute-start(bf16[1,144,256]{2,1,0:T(8,128)(2,1)S(1)} %get-tuple-element.75.refs_0_), channel_id=1, source_target_pairs={{0,6},{1,7},{2,4},{3,5},{4,2},{5,3},{6,0},{7,1},{8,14},{9,15},{10,... | collective-permute-start | bytes 221192 | tf_op jit(solution)/shard_map/ppermute | solution.py:28
  28.9 2.9 %collective-permute-start.10 = (bf16[1,144,256]{2,1,0:T(8,128)(2,1)S(1)}, bf16[1,144,256]{2,1,0:T(8,128)(2,1)S(1)}, u32[]{:S(2)}, u32[]{:S(2)}) collective-permute-start(bf16[1,144,256]{2,1,0:T(8,128)(2,1)S(1)} %get-tuple-element.75.refs_0_), channel_id=1, source_target_pairs={{0,1},{1,0},{2,3},{3,2},{4,5},{5,4},{6,7},{7,6},{8,9},{9,8},{10,11... | collective-permute-start | bytes 221192 | tf_op jit(solution)/shard_map/ppermute | solution.py:28
  29.1 4.7 %collective-permute-start.13 = (bf16[1,144,256]{2,1,0:T(8,128)(2,1)S(1)}, bf16[1,144,256]{2,1,0:T(8,128)(2,1)S(1)}, u32[]{:S(2)}, u32[]{:S(2)}) collective-permute-start(bf16[1,144,256]{2,1,0:T(8,128)(2,1)S(1)} %get-tuple-element.75.refs_0_), channel_id=1, source_target_pairs={{0,2},{1,5},{2,0},{3,7},{4,6},{5,1},{6,4},{7,3},{8,10},{9,13},{10,... | collective-permute-start | bytes 221192 | tf_op jit(solution)/shard_map/ppermute | solution.py:37
  29.6 4.4 %collective-permute-start.14 = (bf16[1,144,256]{2,1,0:T(8,128)(2,1)S(1)}, bf16[1,144,256]{2,1,0:T(8,128)(2,1)S(1)}, u32[]{:S(2)}, u32[]{:S(2)}) collective-permute-start(bf16[1,144,256]{2,1,0:T(8,128)(2,1)S(1)} %get-tuple-element.75.refs_0_), channel_id=1, source_target_pairs={{0,4},{1,3},{2,6},{3,1},{4,0},{5,7},{6,2},{7,5},{8,12},{9,11},{10,... | collective-permute-start | bytes 221192 | tf_op jit(solution)/shard_map/ppermute | solution.py:37
  31.9 2.6 %collective-permute-start.12 = (bf16[1,144,256]{2,1,0:T(8,128)(2,1)S(1)}, bf16[1,144,256]{2,1,0:T(8,128)(2,1)S(1)}, u32[]{:S(2)}, u32[]{:S(2)}) collective-permute-start(bf16[1,144,256]{2,1,0:T(8,128)(2,1)S(1)} %collective-permute-done.11.refs_1_.refs_2_), channel_id=1, source_target_pairs={{0,1},{1,0},{2,3},{3,2},{4,5},{5,4},{6,7},{7,6},{8,9},{9,8},{10,11... | collective-permute-start | bytes 221192 | tf_op jit(solution)/shard_map/ppermute | solution.py:28
  33.9 1.7 %collective-permute-start.15 = (bf16[1,144,256]{2,1,0:T(8,128)(2,1)S(1)}, bf16[1,144,256]{2,1,0:T(8,128)(2,1)S(1)}, u32[]{:S(2)}, u32[]{:S(2)}) collective-permute-start(bf16[1,144,256]{2,1,0:T(8,128)(2,1)S(1)} %collective-permute-done.14.refs_1_.refs_4_), channel_id=1, source_target_pairs={{0,1},{1,0},{2,3},{3,2},{4,5},{5,4},{6,7},{7,6},{8,9},{9,8},{10,11... | collective-permute-start | bytes 221192 | tf_op jit(solution)/shard_map/ppermute | solution.py:28
  33.9 1.7 %collective-permute-start.16 = (bf16[1,144,256]{2,1,0:T(8,128)(2,1)S(1)}, bf16[1,144,256]{2,1,0:T(8,128)(2,1)S(1)}, u32[]{:S(2)}, u32[]{:S(2)}) collective-permute-start(bf16[1,144,256]{2,1,0:T(8,128)(2,1)S(1)} %collective-permute-done.13.refs_2_.refs_5_), channel_id=1, source_target_pairs={{0,1},{1,0},{2,3},{3,2},{4,5},{5,4},{6,7},{7,6},{8,9},{9,8},{10,11... | collective-permute-start | bytes 221192 | tf_op jit(solution)/shard_map/ppermute | solution.py:28
  36.8 1.2 %collective-permute-start.17 = (f32[8,128]{1,0:T(8,128)S(1)}, f32[8,128]{1,0:T(8,128)S(1)}, u32[]{:S(2)}, u32[]{:S(2)}) collective-permute-start(f32[8,128]{1,0:T(8,128)S(1)} %get-tuple-element.94), channel_id=1, source_target_pairs={{0,1},{1,0},{2,3},{3,2},{4,5},{5,4},{6,7},{7,6},{8,9},{9,8},{10,11... | collective-permute-start | bytes 12296 | tf_op jit(solution)/shard_map/ppermute | solution.py:28
  38.0 3.6 %collective-permute-start.19 = (f32[8,128]{1,0:T(8,128)S(1)}, f32[8,128]{1,0:T(8,128)S(1)}, u32[]{:S(2)}, u32[]{:S(2)}) collective-permute-start(f32[8,128]{1,0:T(8,128)S(1)} %add.12), channel_id=1, source_target_pairs={{0,4},{1,7},{2,6},{3,5},{4,0},{5,3},{6,2},{7,1},{8,12},{9,15},{10,... | collective-permute-start | bytes 12296 | tf_op jit(solution)/shard_map/ppermute | solution.py:37
  39.0 3.6 %collective-permute-start.18 = (f32[8,128]{1,0:T(8,128)S(1)}, f32[8,128]{1,0:T(8,128)S(1)}, u32[]{:S(2)}, u32[]{:S(2)}) collective-permute-start(f32[8,128]{1,0:T(8,128)S(1)} %add.12), channel_id=1, source_target_pairs={{0,2},{1,3},{2,0},{3,1},{4,6},{5,7},{6,4},{7,5},{8,10},{9,11},{10,... | collective-permute-start | bytes 12296 | tf_op jit(solution)/shard_map/ppermute | solution.py:28
  41.6 1.2 %collective-permute-start.20 = (f32[8,128]{1,0:T(8,128)S(1)}, f32[8,128]{1,0:T(8,128)S(1)}, u32[]{:S(2)}, u32[]{:S(2)}) collective-permute-start(f32[8,128]{1,0:T(8,128)S(1)} %collective-permute-done.19), channel_id=1, source_target_pairs={{0,1},{1,0},{2,3},{3,2},{4,5},{5,4},{6,7},{7,6},{8,9},{9,8},{10,11... | collective-permute-start | bytes 12296 | tf_op jit(solution)/shard_map/ppermute | solution.py:28

commit v12 on v11

--- a/solution.py
+++ b/solution.py
@@ -126,6 +126,22 @@
             kept[piece][g] = block
         return jnp.dot(directions, block, preferred_element_type=F32)
 
+    if last:
+        rough = sum([before_ref[...] for before_ref in before])
+        firsts, rights = [], []
+        norm = curve = jnp.zeros((probes, slots), F32)
+        for b in range(near_ref.shape[0]):
+            direction = near_ref[b, 2 * feat : 2 * feat + probes, :].astype(F32)
+            right = direction + near_ref[b, 2 * feat + probes :, :].astype(F32)
+            norm = norm + right * right
+            curve = curve + direction * (rough[:, b * slots : (b + 1) * slots] + levels_ref[1:2, :] * direction)
+            firsts.append(direction)
+            rights.append(right)
+        norm, curve = (jnp.sum(each, axis=1, keepdims=True) for each in (norm, curve))
+        usual = 1.0 / (jnp.exp2(levels_ref[0:1, :1]) + levels_ref[1:2, :1])
+        likely = (norm > 0.0) & (curve > 1e-6 * norm)
+        guess = jnp.where(likely, norm / jnp.where(likely, curve, 1.0), usual)
+        guess = jnp.clip(guess, 1e-6, 1e3).astype(BF16)
     steps = far[0].shape[0] // group
     if keep:
         done = [step(piece, 0) for piece in range(count)]
@@ -148,27 +164,15 @@
             products[0][...] = product
             return
     out_ref, own_ref = refs
-    images, rights = [], []
-    norm = curve = jnp.zeros((probes, slots), F32)
-    for b in range(near_ref.shape[0]):
-        direction = near_ref[b, 2 * feat : 2 * feat + probes, :].astype(F32)
-        right = direction + near_ref[b, 2 * feat + probes :, :].astype(F32)
-        image = product[:, b * slots : (b + 1) * slots] + levels_ref[1:2, :] * direction
-        norm = norm + right * right
-        curve = curve + direction * image
-        images.append(image)
-        rights.append(right)
+    images = [product[:, b * slots : (b + 1) * slots] + levels_ref[1:2, :] * first for b, first in enumerate(firsts)]
     own_ref[...] = images[0]
-    norm, curve = (jnp.sum(each, axis=1, keepdims=True) for each in (norm, curve))
-    usual = 1.0 / (jnp.exp2(levels_ref[0:1, :1]) + levels_ref[1:2, :1])
-    likely = (norm > 0.0) & (curve > 1e-6 * norm)
-    guess = jnp.where(likely, norm / jnp.where(likely, curve, 1.0), usual)
-    guess = jnp.clip(guess, 1e-6, 1e3).astype(BF16)
     steps = [right - guess.astype(F32) * image for image, right in zip(images, rights)]
     for b, after in enumerate(steps):
         out_ref[0, b * probes : (b + 1) * probes, :] = after.astype(BF16)
     products = [[x * y for x, y in zip(*pair)] for pair in ((steps, steps), (steps, images), (images, images))]
-    sums = [norm, curve] + [jnp.sum(sum(each), axis=1, keepdims=True) for each in products]
+    products.append([first * image for first, image in zip(firsts, images)])
+    after_after, after_image, image_image, curve = (jnp.sum(sum(each), axis=1, keepdims=True) for each in products)
+    sums = [norm, curve, after_after, after_image, image_image]
     lane = lax.broadcasted_iota(jnp.int32, (probes, 128), 1)
     flat = jnp.zeros((probes, 128), F32)
     for at, each in enumerate([*sums, guess.astype(F32)]):

time: 43.8 us -> 43.7 us (level)
  no operation moved by 1% of the time
where the time goes in v12:
time: 43.7 us; the launch traced here: 43.5 us
  starting transfers between devices  18 us (41%)
  Pallas kernels  13.7 us (31%)
  waiting for transfers between devices  8.86 us (20%)
  between operations  2.7 us (6%)
    ppermute x15, starting transfers between devices, swap(): return lax.ppermute(array, AXES, [(i, i ^ bit) for i in range(count)])  11.1 us
    pallas_call x6, Pallas kernels, apply_first(): pl.pallas_call(functools.partial(apply_kernel, feat, group, keep, begin,...  8.48 us
    ppermute x6, starting transfers between devices, swap_apart(): lax.ppermute(array, AXES, [(i, i ^ (second if i & core else first)) for i...  6.91 us
    ppermute x15, waiting for transfers between devices, swap(): return lax.ppermute(array, AXES, [(i, i ^ bit) for i in range(count)])  6.62 us
    pallas_call x3, Pallas kernels, apply_again(): pl.pallas_call(functools.partial(again_kernel, copies, len(sent)), out_sh...  2.44 us
    ppermute x6, waiting for transfers between devices, swap_apart(): lax.ppermute(array, AXES, [(i, i ^ (second if i & core else first)) for i...  2.24 us
    pallas_call x1, Pallas kernels, combine(): pl.pallas_call(functools.partial(combine_kernel, feat, copies), out_shape...  1.17 us
  transfers between devices with their start and end apart: 21, of which 8 were waited for; matrix products, arithmetic and copies ran while one was open for 0% of the time, Pallas kernels for 22%

profile of v12, /device:TPU:0, one launch (start us, length us, event | category | flops | bytes accessed | tf_op | source)
XLA Modules:
  0.0 43.5 jit_solution(6755711800440981517)
XLA Ops:
  1.3 0.8 %shard_map.77.own_ref = bf16[1,96,256]{2,1,0:T(8,128)(2,1)S(1)} custom-call(f32[16,256]{1,0:T(8,128)} %bitcast.5, f32[16]{0:T(128)} %inv_ref.1, f32[32,256]{1,0:T(8,128)} %bitcast.4, s32[1]{0:T(128)S(6)} %copy.10.count_ref), custom_call_target="tpu_custom_call" | custom-call | tf_op jit(solution)/shard_map/pallas_call | solution.py:82
  2.1 4.1 %collective-permute-start = (bf16[1,96,256]{2,1,0:T(8,128)(2,1)S(1)}, bf16[1,96,256]{2,1,0:T(8,128)(2,1)S(1)}, u32[]{:S(2)}, u32[]{:S(2)}) collective-permute-start(bf16[1,96,256]{2,1,0:T(8,128)(2,1)S(1)} %shard_map.77.own_ref), channel_id=1, source_target_pairs={{0,16},{1,17},{2,18},{3,19},{4,20},{5,21},{6,22},{7,23},{8,24},{9,... | collective-permute-start | bytes 147464 | tf_op jit(solution)/shard_map/ppermute | solution.py:28
  6.2 1.3 %collective-permute-start.1 = (bf16[1,96,256]{2,1,0:T(8,128)(2,1)S(1)}, bf16[1,96,256]{2,1,0:T(8,128)(2,1)S(1)}, u32[]{:S(2)}, u32[]{:S(2)}) collective-permute-start(bf16[1,96,256]{2,1,0:T(8,128)(2,1)S(1)} %shard_map.77.own_ref), channel_id=1, source_target_pairs={{0,24},{1,25},{2,26},{3,27},{4,28},{5,29},{6,30},{7,31},{8,16},{9,... | collective-permute-start | bytes 147464 | tf_op jit(solution)/shard_map/ppermute | solution.py:28
  7.6 0.2 collective-permute-start.2
  9.1 0.1 pad_maximum_fusion.1
  9.2 3.0 %collective-permute-done.1 = bf16[1,96,256]{2,1,0:T(8,128)(2,1)S(1)} collective-permute-done((bf16[1,96,256]{2,1,0:T(8,128)(2,1)S(1)}, bf16[1,96,256]{2,1,0:T(8,128)(2,1)S(1)}, u32[]{:S(2)}, u32[]{:S(2)}) %collective-permute-start.1) | collective-permute-done | bytes 49184 | tf_op jit(solution)/shard_map/ppermute | solution.py:28
  12.2 0.0 collective-permute-done.2
  12.2 0.1 broadcast_in_dim.2.levels_ref
  12.3 0.1 collective-permute-start.4
  12.4 1.6 %collective-permute-start.3 = (bf16[4,64,256]{2,1,0:T(8,128)(2,1)S(1)}, bf16[4,64,256]{2,1,0:T(8,128)(2,1)S(1)}, u32[]{:S(2)}, u32[]{:S(2)}) collective-permute-start(bf16[4,64,256]{2,1,0:T(8,128)(2,1)S(1)} %slice.3.refs_0_.near_ref), channel_id=1, source_target_pairs={{0,4},{1,3},{2,6},{3,1},{4,0},{5,7},{6,2},{7,5},{8,12},{9,11},{10,... | collective-permute-start | bytes 393224 | tf_op jit(solution)/shard_map/ppermute | solution.py:37
  14.0 1.1 %shard_map.78 = (bf16[1,1024,1024]{2,1,0:T(8,128)(2,1)S(1)}, f32[32,1024]{1,0:T(8,128)S(1)}, bf16[80,1024]{1,0:T(8,128)(2,1)S(1)}) custom-call(bf16[4,96,256]{2,1,0:T(8,128)(2,1)S(1)} %pad_maximum_fusion.near_ref, f32[2,256]{1,0:T(2,128)S(1)} %broadcast_in_dim.2.levels_ref, bf16[4,64,256]{2,1,0:T(8,128)(2,1)S(1)} %slice.3.refs_0_.near_ref), custom_call_target="tpu_custom_call" | custom-call | tf_op jit(solution)/shard_map/pallas_call | solution.py:202
  15.0 1.5 %collective-permute-start.7 = (bf16[4,64,256]{2,1,0:T(8,128)(2,1)S(1)}, bf16[4,64,256]{2,1,0:T(8,128)(2,1)S(1)}, u32[]{:S(2)}, u32[]{:S(2)}) collective-permute-start(bf16[4,64,256]{2,1,0:T(8,128)(2,1)S(1)} %slice.3.refs_0_.near_ref), channel_id=1, source_target_pairs={{0,2},{1,5},{2,0},{3,7},{4,6},{5,1},{6,4},{7,3},{8,10},{9,13},{10,... | collective-permute-start | bytes 393224 | tf_op jit(solution)/shard_map/ppermute | solution.py:37
  16.5 0.0 collective-permute-done.4.refs_0_
  16.5 1.1 %shard_map.79 = (bf16[1,1024,1024]{2,1,0:T(8,128)(2,1)S(1)}, f32[32,1024]{1,0:T(8,128)S(1)}) custom-call(bf16[4,96,256]{2,1,0:T(8,128)(2,1)S(1)} %pad_maximum_fusion.near_ref, f32[2,256]{1,0:T(2,128)S(1)} %broadcast_in_dim.2.levels_ref, bf16[4,64,256]{2,1,0:T(8,128)(2,1)S(1)} %collective-permute-done.4.refs_0_, ...), custom_call_target="tpu_custom_call" | custom-call | tf_op jit(solution)/shard_map/pallas_call | solution.py:202
  17.6 0.0 collective-permute-start.6
  17.6 1.9 %collective-permute-start.5 = (bf16[4,64,256]{2,1,0:T(8,128)(2,1)S(1)}, bf16[4,64,256]{2,1,0:T(8,128)(2,1)S(1)}, u32[]{:S(2)}, u32[]{:S(2)}) collective-permute-start(bf16[4,64,256]{2,1,0:T(8,128)(2,1)S(1)} %collective-permute-done.3.refs_0_), channel_id=1, source_target_pairs={{0,2},{1,5},{2,0},{3,7},{4,6},{5,1},{6,4},{7,3},{8,10},{9,13},{10,... | collective-permute-start | bytes 393224 | tf_op jit(solution)/shard_map/ppermute | solution.py:37
  19.5 1.1 %shard_map.80 = (bf16[1,1024,1024]{2,1,0:T(8,128)(2,1)S(1)}, f32[32,1024]{1,0:T(8,128)S(1)}) custom-call(bf16[4,96,256]{2,1,0:T(8,128)(2,1)S(1)} %pad_maximum_fusion.near_ref, f32[2,256]{1,0:T(2,128)S(1)} %broadcast_in_dim.2.levels_ref, bf16[4,64,256]{2,1,0:T(8,128)(2,1)S(1)} %collective-permute-done.3.refs_0_, ...), custom_call_target="tpu_custom_call" | custom-call | tf_op jit(solution)/shard_map/pallas_call | solution.py:202
  20.6 0.0 collective-permute-done.7.refs_1_
  20.6 0.0 collective-permute-start.9
  20.6 0.0 collective-permute-done.6.refs_0_
  20.6 2.0 %shard_map.81 = (bf16[1,1024,1024]{2,1,0:T(8,128)(2,1)S(1)}, bf16[1,1024,1024]{2,1,0:T(8,128)(2,1)S(1)}, f32[32,1024]{1,0:T(8,128)S(1)}, f32[32,1024]{1,0:T(8,128)S(1)}) custom-call(bf16[4,96,256]{2,1,0:T(8,128)(2,1)S(1)} %pad_maximum_fusion.near_ref, f32[2,256]{1,0:T(2,128)S(1)} %broadcast_in_dim.2.levels_ref, ...), custom_call_target="tpu_custom_call" | custom-call | tf_op jit(solution)/shard_map/pallas_call | solution.py:202
  22.6 0.1 collective-permute-done.5.refs_1_
  22.7 0.5 %collective-permute-start.8 = (bf16[4,64,256]{2,1,0:T(8,128)(2,1)S(1)}, bf16[4,64,256]{2,1,0:T(8,128)(2,1)S(1)}, u32[]{:S(2)}, u32[]{:S(2)}) collective-permute-start(bf16[4,64,256]{2,1,0:T(8,128)(2,1)S(1)} %collective-permute-done.5.refs_1_), channel_id=1, source_target_pairs={{0,1},{1,0},{2,3},{3,2},{4,5},{5,4},{6,7},{7,6},{8,9},{9,8},{10,11... | collective-permute-start | bytes 393224 | tf_op jit(solution)/shard_map/ppermute | solution.py:28
  23.1 0.0 collective-permute-done.9.refs_0_
  23.1 2.0 %shard_map.82 = (bf16[1,1024,1024]{2,1,0:T(8,128)(2,1)S(1)}, bf16[1,1024,1024]{2,1,0:T(8,128)(2,1)S(1)}, f32[32,1024]{1,0:T(8,128)S(1)}, f32[32,1024]{1,0:T(8,128)S(1)}) custom-call(bf16[4,96,256]{2,1,0:T(8,128)(2,1)S(1)} %pad_maximum_fusion.near_ref, f32[2,256]{1,0:T(2,128)S(1)} %broadcast_in_dim.2.levels_ref, ...), custom_call_target="tpu_custom_call" | custom-call | tf_op jit(solution)/shard_map/pallas_call | solution.py:202
  25.1 1.4 %shard_map.83 = (bf16[1,1024,1024]{2,1,0:T(8,128)(2,1)S(1)}, f32[32,1024]{1,0:T(8,128)S(1)}, bf16[1,144,256]{2,1,0:T(8,128)(2,1)S(1)}, f32[32,256]{1,0:T(8,128)S(1)}) custom-call(bf16[4,96,256]{2,1,0:T(8,128)(2,1)S(1)} %pad_maximum_fusion.near_ref, f32[2,256]{1,0:T(2,128)S(1)} %broadcast_in_dim.2.levels_ref, ...), custom_call_target="tpu_custom_call" | custom-call | tf_op jit(solution)/shard_map/pallas_call | solution.py:202
  26.5 2.4 %collective-permute-start.11 = (bf16[1,144,256]{2,1,0:T(8,128)(2,1)S(1)}, bf16[1,144,256]{2,1,0:T(8,128)(2,1)S(1)}, u32[]{:S(2)}, u32[]{:S(2)}) collective-permute-start(bf16[1,144,256]{2,1,0:T(8,128)(2,1)S(1)} %get-tuple-element.75.refs_0_), channel_id=1, source_target_pairs={{0,6},{1,7},{2,4},{3,5},{4,2},{5,3},{6,0},{7,1},{8,14},{9,15},{10,... | collective-permute-start | bytes 221192 | tf_op jit(solution)/shard_map/ppermute | solution.py:28
  28.8 0.2 collective-permute-start.10
  29.0 0.4 collective-permute-start.13
  29.5 0.5 %collective-permute-start.14 = (bf16[1,144,256]{2,1,0:T(8,128)(2,1)S(1)}, bf16[1,144,256]{2,1,0:T(8,128)(2,1)S(1)}, u32[]{:S(2)}, u32[]{:S(2)}) collective-permute-start(bf16[1,144,256]{2,1,0:T(8,128)(2,1)S(1)} %get-tuple-element.75.refs_0_), channel_id=1, source_target_pairs={{0,4},{1,3},{2,6},{3,1},{4,0},{5,7},{6,2},{7,5},{8,12},{9,11},{10,... | collective-permute-start | bytes 221192 | tf_op jit(solution)/shard_map/ppermute | solution.py:37
  30.0 0.5 %shard_map.84.refs_16_ = f32[32,1024]{1,0:T(8,128)S(1)} custom-call(bf16[1,144,256]{2,1,0:T(8,128)(2,1)S(1)} %get-tuple-element.75.refs_0_, bf16[1,1024,1024]{2,1,0:T(8,128)(2,1)S(1)} %get-tuple-element.74.refs_1_.kept_near_ref), custom_call_target="tpu_custom_call" | custom-call | tf_op jit(solution)/shard_map/pallas_call | solution.py:328
  30.4 1.3 %collective-permute-done.11.refs_1_.refs_2_ = bf16[1,144,256]{2,1,0:T(8,128)(2,1)S(1)} collective-permute-done((bf16[1,144,256]{2,1,0:T(8,128)(2,1)S(1)}, bf16[1,144,256]{2,1,0:T(8,128)(2,1)S(1)}, u32[]{:S(2)}, u32[]{:S(2)}) %collective-permute-start.11) | collective-permute-done | bytes 73760 | tf_op jit(solution)/shard_map/ppermute | solution.py:28
  31.8 0.0 collective-permute-start.12
  31.8 0.8 %shard_map.85 = (f32[32,1024]{1,0:T(8,128)S(1)}, f32[32,1024]{1,0:T(8,128)S(1)}) custom-call(bf16[1,144,256]{2,1,0:T(8,128)(2,1)S(1)} %collective-permute-done.10.refs_0_.refs_1_, bf16[1,144,256]{2,1,0:T(8,128)(2,1)S(1)} %collective-permute-done.11.refs_1_.refs_2_, bf16[1,1024,1024]{2,1,0:T(8,128)(2,1)S(1)} %get-tuple-element.77.refs_2_, ...), custom_call_target="tpu_custom_call" | custom-call | tf_op jit(solution)/shard_map/pallas_call | solution.py:328
  32.6 1.1 %collective-permute-done.13.refs_2_.refs_5_ = bf16[1,144,256]{2,1,0:T(8,128)(2,1)S(1)} collective-permute-done((bf16[1,144,256]{2,1,0:T(8,128)(2,1)S(1)}, bf16[1,144,256]{2,1,0:T(8,128)(2,1)S(1)}, u32[]{:S(2)}, u32[]{:S(2)}) %collective-permute-start.13) | collective-permute-done | bytes 73760 | tf_op jit(solution)/shard_map/ppermute | solution.py:37
  33.7 0.1 collective-permute-done.14.refs_1_.refs_4_
  33.8 0.5 %collective-permute-start.16 = (bf16[1,144,256]{2,1,0:T(8,128)(2,1)S(1)}, bf16[1,144,256]{2,1,0:T(8,128)(2,1)S(1)}, u32[]{:S(2)}, u32[]{:S(2)}) collective-permute-start(bf16[1,144,256]{2,1,0:T(8,128)(2,1)S(1)} %collective-permute-done.13.refs_2_.refs_5_), channel_id=1, source_target_pairs={{0,1},{1,0},{2,3},{3,2},{4,5},{5,4},{6,7},{7,6},{8,9},{9,8},{10,11... | collective-permute-start | bytes 221192 | tf_op jit(solution)/shard_map/ppermute | solution.py:28
  34.3 1.2 %shard_map.86 = (f32[32,1024]{1,0:T(8,128)S(1)}, f32[32,1024]{1,0:T(8,128)S(1)}, f32[32,1024]{1,0:T(8,128)S(1)}) custom-call(bf16[1,144,256]{2,1,0:T(8,128)(2,1)S(1)} %collective-permute-done.12.refs_0_.refs_3_, bf16[1,144,256]{2,1,0:T(8,128)(2,1)S(1)} %collective-permute-done.14.refs_1_.refs_4_, ...), custom_call_target="tpu_custom_call" | custom-call | tf_op jit(solution)/shard_map/pallas_call | solution.py:328
  35.5 0.0 collective-permute-done.16.refs_7_
  35.5 1.2 %shard_map.87 = (f32[8,128]{1,0:T(8,128)S(1)}, f32[32,256]{1,0:T(8,128)S(1)}, f32[32,256]{1,0:T(8,128)S(1)}, f32[32,256]{1,0:T(8,128)S(1)}, f32[32,256]{1,0:T(8,128)S(1)}, /*index=5*/f32[32,128]{1,0:T(8,128)S(1)}) custom-call(f32[2,256]{1,0:T(2,128)S(1)} %broadcast_in_dim.2.levels_ref, bf16[1,96,256]{2,1,0:T(8,128)(2,1)S(1)} %shard_map.77.own_ref, ...), custom_call_target="tpu_custom_call" | custom-call | tf_op jit(solution)/shard_map/pallas_call | solution.py:381
  36.7 0.1 collective-permute-start.17
  36.8 1.1 %collective-permute-done.17 = f32[8,128]{1,0:T(8,128)S(1)} collective-permute-done((f32[8,128]{1,0:T(8,128)S(1)}, f32[8,128]{1,0:T(8,128)S(1)}, u32[]{:S(2)}, u32[]{:S(2)}) %collective-permute-start.17) | collective-permute-done | bytes 4128 | tf_op jit(solution)/shard_map/ppermute | solution.py:28
  37.9 1.0 %collective-permute-start.19 = (f32[8,128]{1,0:T(8,128)S(1)}, f32[8,128]{1,0:T(8,128)S(1)}, u32[]{:S(2)}, u32[]{:S(2)}) collective-permute-start(f32[8,128]{1,0:T(8,128)S(1)} %add.12), channel_id=1, source_target_pairs={{0,4},{1,7},{2,6},{3,5},{4,0},{5,3},{6,2},{7,1},{8,12},{9,15},{10,... | collective-permute-start | bytes 12296 | tf_op jit(solution)/shard_map/ppermute | solution.py:37
  38.9 1.7 %collective-permute-start.18 = (f32[8,128]{1,0:T(8,128)S(1)}, f32[8,128]{1,0:T(8,128)S(1)}, u32[]{:S(2)}, u32[]{:S(2)}) collective-permute-start(f32[8,128]{1,0:T(8,128)S(1)} %add.12), channel_id=1, source_target_pairs={{0,2},{1,3},{2,0},{3,1},{4,6},{5,7},{6,4},{7,5},{8,10},{9,11},{10,... | collective-permute-start | bytes 12296 | tf_op jit(solution)/shard_map/ppermute | solution.py:28
  40.6 0.9 %collective-permute-done.19 = f32[8,128]{1,0:T(8,128)S(1)} collective-permute-done((f32[8,128]{1,0:T(8,128)S(1)}, f32[8,128]{1,0:T(8,128)S(1)}, u32[]{:S(2)}, u32[]{:S(2)}) %collective-permute-start.19) | collective-permute-done | bytes 4128 | tf_op jit(solution)/shard_map/ppermute | solution.py:37
  41.5 1.0 %collective-permute-done.18 = f32[8,128]{1,0:T(8,128)S(1)} collective-permute-done((f32[8,128]{1,0:T(8,128)S(1)}, f32[8,128]{1,0:T(8,128)S(1)}, u32[]{:S(2)}, u32[]{:S(2)}) %collective-permute-start.18) | collective-permute-done | bytes 4128 | tf_op jit(solution)/shard_map/ppermute | solution.py:28
  42.5 0.2 collective-permute-done.20
  42.7 0.8 %shard_map.88 = (f32[32,256]{1,0:T(8,128)}, f32[32,256]{1,0:T(8,128)}) custom-call(f32[8,128]{1,0:T(8,128)S(1)} %add_add_fusion.curve_ref, f32[32,128]{1,0:T(8,128)S(1)} %get-tuple-element.95.norm_ref, f32[32,256]{1,0:T(8,128)S(1)} %get-tuple-element.96.solution_ref, f32[32,256]{1,0:T(8,128)S(1)} %get-tuple-element.97.residual_ref, ...), custom_call_target="tpu_custom_call" | custom-call | tf_op jit(solution)/shard_map/pallas_call | solution.py:505
  (12 shorter events, 0.1 us)
Async XLA Ops:
  2.1 7.1 %collective-permute-start = (bf16[1,96,256]{2,1,0:T(8,128)(2,1)S(1)}, bf16[1,96,256]{2,1,0:T(8,128)(2,1)S(1)}, u32[]{:S(2)}, u32[]{:S(2)}) collective-permute-start(bf16[1,96,256]{2,1,0:T(8,128)(2,1)S(1)} %shard_map.77.own_ref), channel_id=1, source_target_pairs={{0,16},{1,17},{2,18},{3,19},{4,20},{5,21},{6,22},{7,23},{8,24},{9,... | collective-permute-start | bytes 147464 | tf_op jit(solution)/shard_map/ppermute | solution.py:28
  6.2 6.0 %collective-permute-start.1 = (bf16[1,96,256]{2,1,0:T(8,128)(2,1)S(1)}, bf16[1,96,256]{2,1,0:T(8,128)(2,1)S(1)}, u32[]{:S(2)}, u32[]{:S(2)}) collective-permute-start(bf16[1,96,256]{2,1,0:T(8,128)(2,1)S(1)} %shard_map.77.own_ref), channel_id=1, source_target_pairs={{0,24},{1,25},{2,26},{3,27},{4,28},{5,29},{6,30},{7,31},{8,16},{9,... | collective-permute-start | bytes 147464 | tf_op jit(solution)/shard_map/ppermute | solution.py:28
  7.6 4.6 %collective-permute-start.2 = (bf16[1,96,256]{2,1,0:T(8,128)(2,1)S(1)}, bf16[1,96,256]{2,1,0:T(8,128)(2,1)S(1)}, u32[]{:S(2)}, u32[]{:S(2)}) collective-permute-start(bf16[1,96,256]{2,1,0:T(8,128)(2,1)S(1)} %shard_map.77.own_ref), channel_id=1, source_target_pairs={{0,8},{1,9},{2,10},{3,11},{4,12},{5,13},{6,14},{7,15},{8,0},{9,1},... | collective-permute-start | bytes 147464 | tf_op jit(solution)/shard_map/ppermute | solution.py:28
  12.3 4.2 %collective-permute-start.4 = (bf16[4,64,256]{2,1,0:T(8,128)(2,1)S(1)}, bf16[4,64,256]{2,1,0:T(8,128)(2,1)S(1)}, u32[]{:S(2)}, u32[]{:S(2)}) collective-permute-start(bf16[4,64,256]{2,1,0:T(8,128)(2,1)S(1)} %slice.3.refs_0_.near_ref), channel_id=1, source_target_pairs={{0,1},{1,0},{2,3},{3,2},{4,5},{5,4},{6,7},{7,6},{8,9},{9,8},{10,11... | collective-permute-start | bytes 393224 | tf_op jit(solution)/shard_map/ppermute | solution.py:28
  12.4 5.2 %collective-permute-start.3 = (bf16[4,64,256]{2,1,0:T(8,128)(2,1)S(1)}, bf16[4,64,256]{2,1,0:T(8,128)(2,1)S(1)}, u32[]{:S(2)}, u32[]{:S(2)}) collective-permute-start(bf16[4,64,256]{2,1,0:T(8,128)(2,1)S(1)} %slice.3.refs_0_.near_ref), channel_id=1, source_target_pairs={{0,4},{1,3},{2,6},{3,1},{4,0},{5,7},{6,2},{7,5},{8,12},{9,11},{10,... | collective-permute-start | bytes 393224 | tf_op jit(solution)/shard_map/ppermute | solution.py:37
  15.0 5.6 %collective-permute-start.7 = (bf16[4,64,256]{2,1,0:T(8,128)(2,1)S(1)}, bf16[4,64,256]{2,1,0:T(8,128)(2,1)S(1)}, u32[]{:S(2)}, u32[]{:S(2)}) collective-permute-start(bf16[4,64,256]{2,1,0:T(8,128)(2,1)S(1)} %slice.3.refs_0_.near_ref), channel_id=1, source_target_pairs={{0,2},{1,5},{2,0},{3,7},{4,6},{5,1},{6,4},{7,3},{8,10},{9,13},{10,... | collective-permute-start | bytes 393224 | tf_op jit(solution)/shard_map/ppermute | solution.py:37
  17.6 3.0 %collective-permute-start.6 = (bf16[4,64,256]{2,1,0:T(8,128)(2,1)S(1)}, bf16[4,64,256]{2,1,0:T(8,128)(2,1)S(1)}, u32[]{:S(2)}, u32[]{:S(2)}) collective-permute-start(bf16[4,64,256]{2,1,0:T(8,128)(2,1)S(1)} %collective-permute-done.3.refs_0_), channel_id=1, source_target_pairs={{0,1},{1,0},{2,3},{3,2},{4,5},{5,4},{6,7},{7,6},{8,9},{9,8},{10,11... | collective-permute-start | bytes 393224 | tf_op jit(solution)/shard_map/ppermute | solution.py:28
  17.6 5.0 %collective-permute-start.5 = (bf16[4,64,256]{2,1,0:T(8,128)(2,1)S(1)}, bf16[4,64,256]{2,1,0:T(8,128)(2,1)S(1)}, u32[]{:S(2)}, u32[]{:S(2)}) collective-permute-start(bf16[4,64,256]{2,1,0:T(8,128)(2,1)S(1)} %collective-permute-done.3.refs_0_), channel_id=1, source_target_pairs={{0,2},{1,5},{2,0},{3,7},{4,6},{5,1},{6,4},{7,3},{8,10},{9,13},{10,... | collective-permute-start | bytes 393224 | tf_op jit(solution)/shard_map/ppermute | solution.py:37
  20.6 2.5 %collective-permute-start.9 = (bf16[4,64,256]{2,1,0:T(8,128)(2,1)S(1)}, bf16[4,64,256]{2,1,0:T(8,128)(2,1)S(1)}, u32[]{:S(2)}, u32[]{:S(2)}) collective-permute-start(bf16[4,64,256]{2,1,0:T(8,128)(2,1)S(1)} %collective-permute-done.7.refs_1_), channel_id=1, source_target_pairs={{0,1},{1,0},{2,3},{3,2},{4,5},{5,4},{6,7},{7,6},{8,9},{9,8},{10,11... | collective-permute-start | bytes 393224 | tf_op jit(solution)/shard_map/ppermute | solution.py:28
  22.7 2.4 %collective-permute-start.8 = (bf16[4,64,256]{2,1,0:T(8,128)(2,1)S(1)}, bf16[4,64,256]{2,1,0:T(8,128)(2,1)S(1)}, u32[]{:S(2)}, u32[]{:S(2)}) collective-permute-start(bf16[4,64,256]{2,1,0:T(8,128)(2,1)S(1)} %collective-permute-done.5.refs_1_), channel_id=1, source_target_pairs={{0,1},{1,0},{2,3},{3,2},{4,5},{5,4},{6,7},{7,6},{8,9},{9,8},{10,11... | collective-permute-start | bytes 393224 | tf_op jit(solution)/shard_map/ppermute | solution.py:28
  26.5 5.3 %collective-permute-start.11 = (bf16[1,144,256]{2,1,0:T(8,128)(2,1)S(1)}, bf16[1,144,256]{2,1,0:T(8,128)(2,1)S(1)}, u32[]{:S(2)}, u32[]{:S(2)}) collective-permute-start(bf16[1,144,256]{2,1,0:T(8,128)(2,1)S(1)} %get-tuple-element.75.refs_0_), channel_id=1, source_target_pairs={{0,6},{1,7},{2,4},{3,5},{4,2},{5,3},{6,0},{7,1},{8,14},{9,15},{10,... | collective-permute-start | bytes 221192 | tf_op jit(solution)/shard_map/ppermute | solution.py:28
  28.8 2.9 %collective-permute-start.10 = (bf16[1,144,256]{2,1,0:T(8,128)(2,1)S(1)}, bf16[1,144,256]{2,1,0:T(8,128)(2,1)S(1)}, u32[]{:S(2)}, u32[]{:S(2)}) collective-permute-start(bf16[1,144,256]{2,1,0:T(8,128)(2,1)S(1)} %get-tuple-element.75.refs_0_), channel_id=1, source_target_pairs={{0,1},{1,0},{2,3},{3,2},{4,5},{5,4},{6,7},{7,6},{8,9},{9,8},{10,11... | collective-permute-start | bytes 221192 | tf_op jit(solution)/shard_map/ppermute | solution.py:28
  29.0 4.7 %collective-permute-start.13 = (bf16[1,144,256]{2,1,0:T(8,128)(2,1)S(1)}, bf16[1,144,256]{2,1,0:T(8,128)(2,1)S(1)}, u32[]{:S(2)}, u32[]{:S(2)}) collective-permute-start(bf16[1,144,256]{2,1,0:T(8,128)(2,1)S(1)} %get-tuple-element.75.refs_0_), channel_id=1, source_target_pairs={{0,2},{1,5},{2,0},{3,7},{4,6},{5,1},{6,4},{7,3},{8,10},{9,13},{10,... | collective-permute-start | bytes 221192 | tf_op jit(solution)/shard_map/ppermute | solution.py:37
  29.5 4.4 %collective-permute-start.14 = (bf16[1,144,256]{2,1,0:T(8,128)(2,1)S(1)}, bf16[1,144,256]{2,1,0:T(8,128)(2,1)S(1)}, u32[]{:S(2)}, u32[]{:S(2)}) collective-permute-start(bf16[1,144,256]{2,1,0:T(8,128)(2,1)S(1)} %get-tuple-element.75.refs_0_), channel_id=1, source_target_pairs={{0,4},{1,3},{2,6},{3,1},{4,0},{5,7},{6,2},{7,5},{8,12},{9,11},{10,... | collective-permute-start | bytes 221192 | tf_op jit(solution)/shard_map/ppermute | solution.py:37
  31.8 2.6 %collective-permute-start.12 = (bf16[1,144,256]{2,1,0:T(8,128)(2,1)S(1)}, bf16[1,144,256]{2,1,0:T(8,128)(2,1)S(1)}, u32[]{:S(2)}, u32[]{:S(2)}) collective-permute-start(bf16[1,144,256]{2,1,0:T(8,128)(2,1)S(1)} %collective-permute-done.11.refs_1_.refs_2_), channel_id=1, source_target_pairs={{0,1},{1,0},{2,3},{3,2},{4,5},{5,4},{6,7},{7,6},{8,9},{9,8},{10,11... | collective-permute-start | bytes 221192 | tf_op jit(solution)/shard_map/ppermute | solution.py:28
  33.8 1.7 %collective-permute-start.15 = (bf16[1,144,256]{2,1,0:T(8,128)(2,1)S(1)}, bf16[1,144,256]{2,1,0:T(8,128)(2,1)S(1)}, u32[]{:S(2)}, u32[]{:S(2)}) collective-permute-start(bf16[1,144,256]{2,1,0:T(8,128)(2,1)S(1)} %collective-permute-done.14.refs_1_.refs_4_), channel_id=1, source_target_pairs={{0,1},{1,0},{2,3},{3,2},{4,5},{5,4},{6,7},{7,6},{8,9},{9,8},{10,11... | collective-permute-start | bytes 221192 | tf_op jit(solution)/shard_map/ppermute | solution.py:28
  33.8 1.7 %collective-permute-start.16 = (bf16[1,144,256]{2,1,0:T(8,128)(2,1)S(1)}, bf16[1,144,256]{2,1,0:T(8,128)(2,1)S(1)}, u32[]{:S(2)}, u32[]{:S(2)}) collective-permute-start(bf16[1,144,256]{2,1,0:T(8,128)(2,1)S(1)} %collective-permute-done.13.refs_2_.refs_5_), channel_id=1, source_target_pairs={{0,1},{1,0},{2,3},{3,2},{4,5},{5,4},{6,7},{7,6},{8,9},{9,8},{10,11... | collective-permute-start | bytes 221192 | tf_op jit(solution)/shard_map/ppermute | solution.py:28
  36.7 1.2 %collective-permute-start.17 = (f32[8,128]{1,0:T(8,128)S(1)}, f32[8,128]{1,0:T(8,128)S(1)}, u32[]{:S(2)}, u32[]{:S(2)}) collective-permute-start(f32[8,128]{1,0:T(8,128)S(1)} %get-tuple-element.94), channel_id=1, source_target_pairs={{0,1},{1,0},{2,3},{3,2},{4,5},{5,4},{6,7},{7,6},{8,9},{9,8},{10,11... | collective-permute-start | bytes 12296 | tf_op jit(solution)/shard_map/ppermute | solution.py:28
  37.9 3.6 %collective-permute-start.19 = (f32[8,128]{1,0:T(8,128)S(1)}, f32[8,128]{1,0:T(8,128)S(1)}, u32[]{:S(2)}, u32[]{:S(2)}) collective-permute-start(f32[8,128]{1,0:T(8,128)S(1)} %add.12), channel_id=1, source_target_pairs={{0,4},{1,7},{2,6},{3,5},{4,0},{5,3},{6,2},{7,1},{8,12},{9,15},{10,... | collective-permute-start | bytes 12296 | tf_op jit(solution)/shard_map/ppermute | solution.py:37
  38.9 3.6 %collective-permute-start.18 = (f32[8,128]{1,0:T(8,128)S(1)}, f32[8,128]{1,0:T(8,128)S(1)}, u32[]{:S(2)}, u32[]{:S(2)}) collective-permute-start(f32[8,128]{1,0:T(8,128)S(1)} %add.12), channel_id=1, source_target_pairs={{0,2},{1,3},{2,0},{3,1},{4,6},{5,7},{6,4},{7,5},{8,10},{9,11},{10,... | collective-permute-start | bytes 12296 | tf_op jit(solution)/shard_map/ppermute | solution.py:28
  41.5 1.2 %collective-permute-start.20 = (f32[8,128]{1,0:T(8,128)S(1)}, f32[8,128]{1,0:T(8,128)S(1)}, u32[]{:S(2)}, u32[]{:S(2)}) collective-permute-start(f32[8,128]{1,0:T(8,128)S(1)} %collective-permute-done.19), channel_id=1, source_target_pairs={{0,1},{1,0},{2,3},{3,2},{4,5},{5,4},{6,7},{7,6},{8,9},{9,8},{10,11... | collective-permute-start | bytes 12296 | tf_op jit(solution)/shard_map/ppermute | solution.py:28

commit v13 on v11

--- a/solution.py
+++ b/solution.py
@@ -357,13 +357,14 @@
         sent = images[0][0, b * probes : (b + 1) * probes, :].astype(F32)
         directions.append((1.0 - scales[0] + ratio) * first + scales[0] * sent)
     exact, formed = directions[:2]
-    product = product + jnp.dot((exact - formed).astype(BF16), kept_near_ref[0, :slots, :], preferred_element_type=F32)
+    own = jnp.dot((exact - formed).astype(BF16), kept_near_ref[0, :slots, :slots], preferred_element_type=F32)
     curve = jnp.zeros((probes, slots), F32)
     for b, direction in enumerate([exact] + directions[2:]):
         image = product[:, b * slots : (b + 1) * slots] + levels_ref[1:2, :] * direction
+        if b == 0:
+            image = image + own
+            own_image_ref[...] = image
         curve = curve + direction * image
-        if b == 0:
-            own_image_ref[...] = image
     lane = lax.broadcasted_iota(jnp.int32, (probes, 128), 1)
     flat = jnp.where(lane == 0, jnp.sum(curve, axis=1, keepdims=True), 0.0)
     partial_ref[...] = turned(flat, 128)[:8]

time: 43.8 us -> 43.8 us (level)
  no operation moved by 1% of the time
where the time goes in v13:
time: 43.8 us; the launch traced here: 43.5 us
  starting transfers between devices  18 us (41%)
  Pallas kernels  13.7 us (31%)
  waiting for transfers between devices  8.86 us (20%)
  between operations  2.7 us (6%)
    ppermute x15, starting transfers between devices, swap(): return lax.ppermute(array, AXES, [(i, i ^ bit) for i in range(count)])  11.1 us
    pallas_call x6, Pallas kernels, apply_first(): pl.pallas_call(functools.partial(apply_kernel, feat, group, keep, begin,...  8.57 us
    ppermute x6, starting transfers between devices, swap_apart(): lax.ppermute(array, AXES, [(i, i ^ (second if i & core else first)) for i...  6.91 us
    ppermute x15, waiting for transfers between devices, swap(): return lax.ppermute(array, AXES, [(i, i ^ bit) for i in range(count)])  6.62 us
    pallas_call x3, Pallas kernels, apply_again(): pl.pallas_call(functools.partial(again_kernel, copies, len(sent)), out_sh...  2.44 us
    ppermute x6, waiting for transfers between devices, swap_apart(): lax.ppermute(array, AXES, [(i, i ^ (second if i & core else first)) for i...  2.25 us
    pallas_call x1, Pallas kernels, combine(): pl.pallas_call(functools.partial(combine_kernel, feat, copies), out_shape...  1.13 us
  transfers between devices with their start and end apart: 21, of which 8 were waited for; matrix products, arithmetic and copies ran while one was open for 0% of the time, Pallas kernels for 22%

profile of v13, /device:TPU:0, one launch (start us, length us, event | category | flops | bytes accessed | tf_op | source)
XLA Modules:
  0.0 43.5 jit_solution(6617566738141009111)
XLA Ops:
  1.3 0.8 %shard_map.77.own_ref = bf16[1,96,256]{2,1,0:T(8,128)(2,1)S(1)} custom-call(f32[16,256]{1,0:T(8,128)} %bitcast.5, f32[16]{0:T(128)} %inv_ref.1, f32[32,256]{1,0:T(8,128)} %bitcast.4, s32[1]{0:T(128)S(6)} %copy.10.count_ref), custom_call_target="tpu_custom_call" | custom-call | tf_op jit(solution)/shard_map/pallas_call | solution.py:82
  2.1 4.1 %collective-permute-start = (bf16[1,96,256]{2,1,0:T(8,128)(2,1)S(1)}, bf16[1,96,256]{2,1,0:T(8,128)(2,1)S(1)}, u32[]{:S(2)}, u32[]{:S(2)}) collective-permute-start(bf16[1,96,256]{2,1,0:T(8,128)(2,1)S(1)} %shard_map.77.own_ref), channel_id=1, source_target_pairs={{0,16},{1,17},{2,18},{3,19},{4,20},{5,21},{6,22},{7,23},{8,24},{9,... | collective-permute-start | bytes 147464 | tf_op jit(solution)/shard_map/ppermute | solution.py:28
  6.2 1.3 %collective-permute-start.1 = (bf16[1,96,256]{2,1,0:T(8,128)(2,1)S(1)}, bf16[1,96,256]{2,1,0:T(8,128)(2,1)S(1)}, u32[]{:S(2)}, u32[]{:S(2)}) collective-permute-start(bf16[1,96,256]{2,1,0:T(8,128)(2,1)S(1)} %shard_map.77.own_ref), channel_id=1, source_target_pairs={{0,24},{1,25},{2,26},{3,27},{4,28},{5,29},{6,30},{7,31},{8,16},{9,... | collective-permute-start | bytes 147464 | tf_op jit(solution)/shard_map/ppermute | solution.py:28
  7.6 0.2 collective-permute-start.2
  9.1 0.1 pad_maximum_fusion.1
  9.2 3.0 %collective-permute-done.1 = bf16[1,96,256]{2,1,0:T(8,128)(2,1)S(1)} collective-permute-done((bf16[1,96,256]{2,1,0:T(8,128)(2,1)S(1)}, bf16[1,96,256]{2,1,0:T(8,128)(2,1)S(1)}, u32[]{:S(2)}, u32[]{:S(2)}) %collective-permute-start.1) | collective-permute-done | bytes 49184 | tf_op jit(solution)/shard_map/ppermute | solution.py:28
  12.2 0.0 collective-permute-done.2
  12.2 0.1 broadcast_in_dim.2.levels_ref
  12.3 0.1 collective-permute-start.4
  12.4 1.6 %collective-permute-start.3 = (bf16[4,64,256]{2,1,0:T(8,128)(2,1)S(1)}, bf16[4,64,256]{2,1,0:T(8,128)(2,1)S(1)}, u32[]{:S(2)}, u32[]{:S(2)}) collective-permute-start(bf16[4,64,256]{2,1,0:T(8,128)(2,1)S(1)} %slice.3.refs_0_.near_ref), channel_id=1, source_target_pairs={{0,4},{1,3},{2,6},{3,1},{4,0},{5,7},{6,2},{7,5},{8,12},{9,11},{10,... | collective-permute-start | bytes 393224 | tf_op jit(solution)/shard_map/ppermute | solution.py:37
  14.0 1.1 %shard_map.78 = (bf16[1,1024,1024]{2,1,0:T(8,128)(2,1)S(1)}, f32[32,1024]{1,0:T(8,128)S(1)}, bf16[80,1024]{1,0:T(8,128)(2,1)S(1)}) custom-call(bf16[4,96,256]{2,1,0:T(8,128)(2,1)S(1)} %pad_maximum_fusion.near_ref, f32[2,256]{1,0:T(2,128)S(1)} %broadcast_in_dim.2.levels_ref, bf16[4,64,256]{2,1,0:T(8,128)(2,1)S(1)} %slice.3.refs_0_.near_ref), custom_call_target="tpu_custom_call" | custom-call | tf_op jit(solution)/shard_map/pallas_call | solution.py:198
  15.0 1.5 %collective-permute-start.7 = (bf16[4,64,256]{2,1,0:T(8,128)(2,1)S(1)}, bf16[4,64,256]{2,1,0:T(8,128)(2,1)S(1)}, u32[]{:S(2)}, u32[]{:S(2)}) collective-permute-start(bf16[4,64,256]{2,1,0:T(8,128)(2,1)S(1)} %slice.3.refs_0_.near_ref), channel_id=1, source_target_pairs={{0,2},{1,5},{2,0},{3,7},{4,6},{5,1},{6,4},{7,3},{8,10},{9,13},{10,... | collective-permute-start | bytes 393224 | tf_op jit(solution)/shard_map/ppermute | solution.py:37
  16.5 0.0 collective-permute-done.4.refs_0_
  16.5 1.1 %shard_map.79 = (bf16[1,1024,1024]{2,1,0:T(8,128)(2,1)S(1)}, f32[32,1024]{1,0:T(8,128)S(1)}) custom-call(bf16[4,96,256]{2,1,0:T(8,128)(2,1)S(1)} %pad_maximum_fusion.near_ref, f32[2,256]{1,0:T(2,128)S(1)} %broadcast_in_dim.2.levels_ref, bf16[4,64,256]{2,1,0:T(8,128)(2,1)S(1)} %collective-permute-done.4.refs_0_, ...), custom_call_target="tpu_custom_call" | custom-call | tf_op jit(solution)/shard_map/pallas_call | solution.py:198
  17.6 0.0 collective-permute-start.6
  17.6 1.9 %collective-permute-start.5 = (bf16[4,64,256]{2,1,0:T(8,128)(2,1)S(1)}, bf16[4,64,256]{2,1,0:T(8,128)(2,1)S(1)}, u32[]{:S(2)}, u32[]{:S(2)}) collective-permute-start(bf16[4,64,256]{2,1,0:T(8,128)(2,1)S(1)} %collective-permute-done.3.refs_0_), channel_id=1, source_target_pairs={{0,2},{1,5},{2,0},{3,7},{4,6},{5,1},{6,4},{7,3},{8,10},{9,13},{10,... | collective-permute-start | bytes 393224 | tf_op jit(solution)/shard_map/ppermute | solution.py:37
  19.5 1.1 %shard_map.80 = (bf16[1,1024,1024]{2,1,0:T(8,128)(2,1)S(1)}, f32[32,1024]{1,0:T(8,128)S(1)}) custom-call(bf16[4,96,256]{2,1,0:T(8,128)(2,1)S(1)} %pad_maximum_fusion.near_ref, f32[2,256]{1,0:T(2,128)S(1)} %broadcast_in_dim.2.levels_ref, bf16[4,64,256]{2,1,0:T(8,128)(2,1)S(1)} %collective-permute-done.3.refs_0_, ...), custom_call_target="tpu_custom_call" | custom-call | tf_op jit(solution)/shard_map/pallas_call | solution.py:198
  20.6 0.0 collective-permute-done.7.refs_1_
  20.6 0.0 collective-permute-start.9
  20.6 0.0 collective-permute-done.6.refs_0_
  20.6 2.0 %shard_map.81 = (bf16[1,1024,1024]{2,1,0:T(8,128)(2,1)S(1)}, bf16[1,1024,1024]{2,1,0:T(8,128)(2,1)S(1)}, f32[32,1024]{1,0:T(8,128)S(1)}, f32[32,1024]{1,0:T(8,128)S(1)}) custom-call(bf16[4,96,256]{2,1,0:T(8,128)(2,1)S(1)} %pad_maximum_fusion.near_ref, f32[2,256]{1,0:T(2,128)S(1)} %broadcast_in_dim.2.levels_ref, ...), custom_call_target="tpu_custom_call" | custom-call | tf_op jit(solution)/shard_map/pallas_call | solution.py:198
  22.6 0.1 collective-permute-done.5.refs_1_
  22.7 0.5 %collective-permute-start.8 = (bf16[4,64,256]{2,1,0:T(8,128)(2,1)S(1)}, bf16[4,64,256]{2,1,0:T(8,128)(2,1)S(1)}, u32[]{:S(2)}, u32[]{:S(2)}) collective-permute-start(bf16[4,64,256]{2,1,0:T(8,128)(2,1)S(1)} %collective-permute-done.5.refs_1_), channel_id=1, source_target_pairs={{0,1},{1,0},{2,3},{3,2},{4,5},{5,4},{6,7},{7,6},{8,9},{9,8},{10,11... | collective-permute-start | bytes 393224 | tf_op jit(solution)/shard_map/ppermute | solution.py:28
  23.1 0.0 collective-permute-done.9.refs_0_
  23.1 2.0 %shard_map.82 = (bf16[1,1024,1024]{2,1,0:T(8,128)(2,1)S(1)}, bf16[1,1024,1024]{2,1,0:T(8,128)(2,1)S(1)}, f32[32,1024]{1,0:T(8,128)S(1)}, f32[32,1024]{1,0:T(8,128)S(1)}) custom-call(bf16[4,96,256]{2,1,0:T(8,128)(2,1)S(1)} %pad_maximum_fusion.near_ref, f32[2,256]{1,0:T(2,128)S(1)} %broadcast_in_dim.2.levels_ref, ...), custom_call_target="tpu_custom_call" | custom-call | tf_op jit(solution)/shard_map/pallas_call | solution.py:198
  25.1 1.5 %shard_map.83 = (bf16[1,1024,1024]{2,1,0:T(8,128)(2,1)S(1)}, f32[32,1024]{1,0:T(8,128)S(1)}, bf16[1,144,256]{2,1,0:T(8,128)(2,1)S(1)}, f32[32,256]{1,0:T(8,128)S(1)}) custom-call(bf16[4,96,256]{2,1,0:T(8,128)(2,1)S(1)} %pad_maximum_fusion.near_ref, f32[2,256]{1,0:T(2,128)S(1)} %broadcast_in_dim.2.levels_ref, ...), custom_call_target="tpu_custom_call" | custom-call | tf_op jit(solution)/shard_map/pallas_call | solution.py:198
  26.6 2.4 %collective-permute-start.11 = (bf16[1,144,256]{2,1,0:T(8,128)(2,1)S(1)}, bf16[1,144,256]{2,1,0:T(8,128)(2,1)S(1)}, u32[]{:S(2)}, u32[]{:S(2)}) collective-permute-start(bf16[1,144,256]{2,1,0:T(8,128)(2,1)S(1)} %get-tuple-element.75.refs_0_), channel_id=1, source_target_pairs={{0,6},{1,7},{2,4},{3,5},{4,2},{5,3},{6,0},{7,1},{8,14},{9,15},{10,... | collective-permute-start | bytes 221192 | tf_op jit(solution)/shard_map/ppermute | solution.py:28
  28.9 0.2 collective-permute-start.10
  29.1 0.4 collective-permute-start.13
  29.6 0.5 %collective-permute-start.14 = (bf16[1,144,256]{2,1,0:T(8,128)(2,1)S(1)}, bf16[1,144,256]{2,1,0:T(8,128)(2,1)S(1)}, u32[]{:S(2)}, u32[]{:S(2)}) collective-permute-start(bf16[1,144,256]{2,1,0:T(8,128)(2,1)S(1)} %get-tuple-element.75.refs_0_), channel_id=1, source_target_pairs={{0,4},{1,3},{2,6},{3,1},{4,0},{5,7},{6,2},{7,5},{8,12},{9,11},{10,... | collective-permute-start | bytes 221192 | tf_op jit(solution)/shard_map/ppermute | solution.py:37
  30.1 0.5 %shard_map.84.refs_16_ = f32[32,1024]{1,0:T(8,128)S(1)} custom-call(bf16[1,144,256]{2,1,0:T(8,128)(2,1)S(1)} %get-tuple-element.75.refs_0_, bf16[1,1024,1024]{2,1,0:T(8,128)(2,1)S(1)} %get-tuple-element.74.refs_1_.kept_near_ref), custom_call_target="tpu_custom_call" | custom-call | tf_op jit(solution)/shard_map/pallas_call | solution.py:324
  30.5 1.3 %collective-permute-done.11.refs_1_.refs_2_ = bf16[1,144,256]{2,1,0:T(8,128)(2,1)S(1)} collective-permute-done((bf16[1,144,256]{2,1,0:T(8,128)(2,1)S(1)}, bf16[1,144,256]{2,1,0:T(8,128)(2,1)S(1)}, u32[]{:S(2)}, u32[]{:S(2)}) %collective-permute-start.11) | collective-permute-done | bytes 73760 | tf_op jit(solution)/shard_map/ppermute | solution.py:28
  31.9 0.0 collective-permute-start.12
  31.9 0.8 %shard_map.85 = (f32[32,1024]{1,0:T(8,128)S(1)}, f32[32,1024]{1,0:T(8,128)S(1)}) custom-call(bf16[1,144,256]{2,1,0:T(8,128)(2,1)S(1)} %collective-permute-done.10.refs_0_.refs_1_, bf16[1,144,256]{2,1,0:T(8,128)(2,1)S(1)} %collective-permute-done.11.refs_1_.refs_2_, bf16[1,1024,1024]{2,1,0:T(8,128)(2,1)S(1)} %get-tuple-element.77.refs_2_, ...), custom_call_target="tpu_custom_call" | custom-call | tf_op jit(solution)/shard_map/pallas_call | solution.py:324
  32.7 1.2 %collective-permute-done.13.refs_2_.refs_5_ = bf16[1,144,256]{2,1,0:T(8,128)(2,1)S(1)} collective-permute-done((bf16[1,144,256]{2,1,0:T(8,128)(2,1)S(1)}, bf16[1,144,256]{2,1,0:T(8,128)(2,1)S(1)}, u32[]{:S(2)}, u32[]{:S(2)}) %collective-permute-start.13) | collective-permute-done | bytes 73760 | tf_op jit(solution)/shard_map/ppermute | solution.py:37
  33.8 0.1 collective-permute-done.14.refs_1_.refs_4_
  33.9 0.5 %collective-permute-start.16 = (bf16[1,144,256]{2,1,0:T(8,128)(2,1)S(1)}, bf16[1,144,256]{2,1,0:T(8,128)(2,1)S(1)}, u32[]{:S(2)}, u32[]{:S(2)}) collective-permute-start(bf16[1,144,256]{2,1,0:T(8,128)(2,1)S(1)} %collective-permute-done.13.refs_2_.refs_5_), channel_id=1, source_target_pairs={{0,1},{1,0},{2,3},{3,2},{4,5},{5,4},{6,7},{7,6},{8,9},{9,8},{10,11... | collective-permute-start | bytes 221192 | tf_op jit(solution)/shard_map/ppermute | solution.py:28
  34.4 1.2 %shard_map.86 = (f32[32,1024]{1,0:T(8,128)S(1)}, f32[32,1024]{1,0:T(8,128)S(1)}, f32[32,1024]{1,0:T(8,128)S(1)}) custom-call(bf16[1,144,256]{2,1,0:T(8,128)(2,1)S(1)} %collective-permute-done.12.refs_0_.refs_3_, bf16[1,144,256]{2,1,0:T(8,128)(2,1)S(1)} %collective-permute-done.14.refs_1_.refs_4_, ...), custom_call_target="tpu_custom_call" | custom-call | tf_op jit(solution)/shard_map/pallas_call | solution.py:324
  35.6 0.0 collective-permute-done.16.refs_7_
  35.6 1.1 %shard_map.87 = (f32[8,128]{1,0:T(8,128)S(1)}, f32[32,256]{1,0:T(8,128)S(1)}, f32[32,256]{1,0:T(8,128)S(1)}, f32[32,256]{1,0:T(8,128)S(1)}, f32[32,256]{1,0:T(8,128)S(1)}, /*index=5*/f32[32,128]{1,0:T(8,128)S(1)}) custom-call(f32[2,256]{1,0:T(2,128)S(1)} %broadcast_in_dim.2.levels_ref, bf16[1,96,256]{2,1,0:T(8,128)(2,1)S(1)} %shard_map.77.own_ref, ...), custom_call_target="tpu_custom_call" | custom-call | tf_op jit(solution)/shard_map/pallas_call | solution.py:378
  36.8 0.1 collective-permute-start.17
  36.8 1.1 %collective-permute-done.17 = f32[8,128]{1,0:T(8,128)S(1)} collective-permute-done((f32[8,128]{1,0:T(8,128)S(1)}, f32[8,128]{1,0:T(8,128)S(1)}, u32[]{:S(2)}, u32[]{:S(2)}) %collective-permute-start.17) | collective-permute-done | bytes 4128 | tf_op jit(solution)/shard_map/ppermute | solution.py:28
  37.9 1.0 %collective-permute-start.19 = (f32[8,128]{1,0:T(8,128)S(1)}, f32[8,128]{1,0:T(8,128)S(1)}, u32[]{:S(2)}, u32[]{:S(2)}) collective-permute-start(f32[8,128]{1,0:T(8,128)S(1)} %add.12), channel_id=1, source_target_pairs={{0,4},{1,7},{2,6},{3,5},{4,0},{5,3},{6,2},{7,1},{8,12},{9,15},{10,... | collective-permute-start | bytes 12296 | tf_op jit(solution)/shard_map/ppermute | solution.py:37
  38.9 1.7 %collective-permute-start.18 = (f32[8,128]{1,0:T(8,128)S(1)}, f32[8,128]{1,0:T(8,128)S(1)}, u32[]{:S(2)}, u32[]{:S(2)}) collective-permute-start(f32[8,128]{1,0:T(8,128)S(1)} %add.12), channel_id=1, source_target_pairs={{0,2},{1,3},{2,0},{3,1},{4,6},{5,7},{6,4},{7,5},{8,10},{9,11},{10,... | collective-permute-start | bytes 12296 | tf_op jit(solution)/shard_map/ppermute | solution.py:28
  40.6 1.0 %collective-permute-done.19 = f32[8,128]{1,0:T(8,128)S(1)} collective-permute-done((f32[8,128]{1,0:T(8,128)S(1)}, f32[8,128]{1,0:T(8,128)S(1)}, u32[]{:S(2)}, u32[]{:S(2)}) %collective-permute-start.19) | collective-permute-done | bytes 4128 | tf_op jit(solution)/shard_map/ppermute | solution.py:37
  41.6 1.0 %collective-permute-done.18 = f32[8,128]{1,0:T(8,128)S(1)} collective-permute-done((f32[8,128]{1,0:T(8,128)S(1)}, f32[8,128]{1,0:T(8,128)S(1)}, u32[]{:S(2)}, u32[]{:S(2)}) %collective-permute-start.18) | collective-permute-done | bytes 4128 | tf_op jit(solution)/shard_map/ppermute | solution.py:28
  42.5 0.2 collective-permute-done.20
  42.7 0.8 %shard_map.88 = (f32[32,256]{1,0:T(8,128)}, f32[32,256]{1,0:T(8,128)}) custom-call(f32[8,128]{1,0:T(8,128)S(1)} %add_add_fusion.curve_ref, f32[32,128]{1,0:T(8,128)S(1)} %get-tuple-element.95.norm_ref, f32[32,256]{1,0:T(8,128)S(1)} %get-tuple-element.96.solution_ref, f32[32,256]{1,0:T(8,128)S(1)} %get-tuple-element.97.residual_ref, ...), custom_call_target="tpu_custom_call" | custom-call | tf_op jit(solution)/shard_map/pallas_call | solution.py:502
  (12 shorter events, 0.1 us)
Async XLA Ops:
  2.1 7.1 %collective-permute-start = (bf16[1,96,256]{2,1,0:T(8,128)(2,1)S(1)}, bf16[1,96,256]{2,1,0:T(8,128)(2,1)S(1)}, u32[]{:S(2)}, u32[]{:S(2)}) collective-permute-start(bf16[1,96,256]{2,1,0:T(8,128)(2,1)S(1)} %shard_map.77.own_ref), channel_id=1, source_target_pairs={{0,16},{1,17},{2,18},{3,19},{4,20},{5,21},{6,22},{7,23},{8,24},{9,... | collective-permute-start | bytes 147464 | tf_op jit(solution)/shard_map/ppermute | solution.py:28
  6.2 6.0 %collective-permute-start.1 = (bf16[1,96,256]{2,1,0:T(8,128)(2,1)S(1)}, bf16[1,96,256]{2,1,0:T(8,128)(2,1)S(1)}, u32[]{:S(2)}, u32[]{:S(2)}) collective-permute-start(bf16[1,96,256]{2,1,0:T(8,128)(2,1)S(1)} %shard_map.77.own_ref), channel_id=1, source_target_pairs={{0,24},{1,25},{2,26},{3,27},{4,28},{5,29},{6,30},{7,31},{8,16},{9,... | collective-permute-start | bytes 147464 | tf_op jit(solution)/shard_map/ppermute | solution.py:28
  7.6 4.6 %collective-permute-start.2 = (bf16[1,96,256]{2,1,0:T(8,128)(2,1)S(1)}, bf16[1,96,256]{2,1,0:T(8,128)(2,1)S(1)}, u32[]{:S(2)}, u32[]{:S(2)}) collective-permute-start(bf16[1,96,256]{2,1,0:T(8,128)(2,1)S(1)} %shard_map.77.own_ref), channel_id=1, source_target_pairs={{0,8},{1,9},{2,10},{3,11},{4,12},{5,13},{6,14},{7,15},{8,0},{9,1},... | collective-permute-start | bytes 147464 | tf_op jit(solution)/shard_map/ppermute | solution.py:28
  12.3 4.2 %collective-permute-start.4 = (bf16[4,64,256]{2,1,0:T(8,128)(2,1)S(1)}, bf16[4,64,256]{2,1,0:T(8,128)(2,1)S(1)}, u32[]{:S(2)}, u32[]{:S(2)}) collective-permute-start(bf16[4,64,256]{2,1,0:T(8,128)(2,1)S(1)} %slice.3.refs_0_.near_ref), channel_id=1, source_target_pairs={{0,1},{1,0},{2,3},{3,2},{4,5},{5,4},{6,7},{7,6},{8,9},{9,8},{10,11... | collective-permute-start | bytes 393224 | tf_op jit(solution)/shard_map/ppermute | solution.py:28
  12.4 5.2 %collective-permute-start.3 = (bf16[4,64,256]{2,1,0:T(8,128)(2,1)S(1)}, bf16[4,64,256]{2,1,0:T(8,128)(2,1)S(1)}, u32[]{:S(2)}, u32[]{:S(2)}) collective-permute-start(bf16[4,64,256]{2,1,0:T(8,128)(2,1)S(1)} %slice.3.refs_0_.near_ref), channel_id=1, source_target_pairs={{0,4},{1,3},{2,6},{3,1},{4,0},{5,7},{6,2},{7,5},{8,12},{9,11},{10,... | collective-permute-start | bytes 393224 | tf_op jit(solution)/shard_map/ppermute | solution.py:37
  15.0 5.6 %collective-permute-start.7 = (bf16[4,64,256]{2,1,0:T(8,128)(2,1)S(1)}, bf16[4,64,256]{2,1,0:T(8,128)(2,1)S(1)}, u32[]{:S(2)}, u32[]{:S(2)}) collective-permute-start(bf16[4,64,256]{2,1,0:T(8,128)(2,1)S(1)} %slice.3.refs_0_.near_ref), channel_id=1, source_target_pairs={{0,2},{1,5},{2,0},{3,7},{4,6},{5,1},{6,4},{7,3},{8,10},{9,13},{10,... | collective-permute-start | bytes 393224 | tf_op jit(solution)/shard_map/ppermute | solution.py:37
  17.6 3.0 %collective-permute-start.6 = (bf16[4,64,256]{2,1,0:T(8,128)(2,1)S(1)}, bf16[4,64,256]{2,1,0:T(8,128)(2,1)S(1)}, u32[]{:S(2)}, u32[]{:S(2)}) collective-permute-start(bf16[4,64,256]{2,1,0:T(8,128)(2,1)S(1)} %collective-permute-done.3.refs_0_), channel_id=1, source_target_pairs={{0,1},{1,0},{2,3},{3,2},{4,5},{5,4},{6,7},{7,6},{8,9},{9,8},{10,11... | collective-permute-start | bytes 393224 | tf_op jit(solution)/shard_map/ppermute | solution.py:28
  17.6 5.0 %collective-permute-start.5 = (bf16[4,64,256]{2,1,0:T(8,128)(2,1)S(1)}, bf16[4,64,256]{2,1,0:T(8,128)(2,1)S(1)}, u32[]{:S(2)}, u32[]{:S(2)}) collective-permute-start(bf16[4,64,256]{2,1,0:T(8,128)(2,1)S(1)} %collective-permute-done.3.refs_0_), channel_id=1, source_target_pairs={{0,2},{1,5},{2,0},{3,7},{4,6},{5,1},{6,4},{7,3},{8,10},{9,13},{10,... | collective-permute-start | bytes 393224 | tf_op jit(solution)/shard_map/ppermute | solution.py:37
  20.6 2.5 %collective-permute-start.9 = (bf16[4,64,256]{2,1,0:T(8,128)(2,1)S(1)}, bf16[4,64,256]{2,1,0:T(8,128)(2,1)S(1)}, u32[]{:S(2)}, u32[]{:S(2)}) collective-permute-start(bf16[4,64,256]{2,1,0:T(8,128)(2,1)S(1)} %collective-permute-done.7.refs_1_), channel_id=1, source_target_pairs={{0,1},{1,0},{2,3},{3,2},{4,5},{5,4},{6,7},{7,6},{8,9},{9,8},{10,11... | collective-permute-start | bytes 393224 | tf_op jit(solution)/shard_map/ppermute | solution.py:28
  22.7 2.4 %collective-permute-start.8 = (bf16[4,64,256]{2,1,0:T(8,128)(2,1)S(1)}, bf16[4,64,256]{2,1,0:T(8,128)(2,1)S(1)}, u32[]{:S(2)}, u32[]{:S(2)}) collective-permute-start(bf16[4,64,256]{2,1,0:T(8,128)(2,1)S(1)} %collective-permute-done.5.refs_1_), channel_id=1, source_target_pairs={{0,1},{1,0},{2,3},{3,2},{4,5},{5,4},{6,7},{7,6},{8,9},{9,8},{10,11... | collective-permute-start | bytes 393224 | tf_op jit(solution)/shard_map/ppermute | solution.py:28
  26.6 5.3 %collective-permute-start.11 = (bf16[1,144,256]{2,1,0:T(8,128)(2,1)S(1)}, bf16[1,144,256]{2,1,0:T(8,128)(2,1)S(1)}, u32[]{:S(2)}, u32[]{:S(2)}) collective-permute-start(bf16[1,144,256]{2,1,0:T(8,128)(2,1)S(1)} %get-tuple-element.75.refs_0_), channel_id=1, source_target_pairs={{0,6},{1,7},{2,4},{3,5},{4,2},{5,3},{6,0},{7,1},{8,14},{9,15},{10,... | collective-permute-start | bytes 221192 | tf_op jit(solution)/shard_map/ppermute | solution.py:28
  28.9 2.9 %collective-permute-start.10 = (bf16[1,144,256]{2,1,0:T(8,128)(2,1)S(1)}, bf16[1,144,256]{2,1,0:T(8,128)(2,1)S(1)}, u32[]{:S(2)}, u32[]{:S(2)}) collective-permute-start(bf16[1,144,256]{2,1,0:T(8,128)(2,1)S(1)} %get-tuple-element.75.refs_0_), channel_id=1, source_target_pairs={{0,1},{1,0},{2,3},{3,2},{4,5},{5,4},{6,7},{7,6},{8,9},{9,8},{10,11... | collective-permute-start | bytes 221192 | tf_op jit(solution)/shard_map/ppermute | solution.py:28
  29.1 4.7 %collective-permute-start.13 = (bf16[1,144,256]{2,1,0:T(8,128)(2,1)S(1)}, bf16[1,144,256]{2,1,0:T(8,128)(2,1)S(1)}, u32[]{:S(2)}, u32[]{:S(2)}) collective-permute-start(bf16[1,144,256]{2,1,0:T(8,128)(2,1)S(1)} %get-tuple-element.75.refs_0_), channel_id=1, source_target_pairs={{0,2},{1,5},{2,0},{3,7},{4,6},{5,1},{6,4},{7,3},{8,10},{9,13},{10,... | collective-permute-start | bytes 221192 | tf_op jit(solution)/shard_map/ppermute | solution.py:37
  29.6 4.4 %collective-permute-start.14 = (bf16[1,144,256]{2,1,0:T(8,128)(2,1)S(1)}, bf16[1,144,256]{2,1,0:T(8,128)(2,1)S(1)}, u32[]{:S(2)}, u32[]{:S(2)}) collective-permute-start(bf16[1,144,256]{2,1,0:T(8,128)(2,1)S(1)} %get-tuple-element.75.refs_0_), channel_id=1, source_target_pairs={{0,4},{1,3},{2,6},{3,1},{4,0},{5,7},{6,2},{7,5},{8,12},{9,11},{10,... | collective-permute-start | bytes 221192 | tf_op jit(solution)/shard_map/ppermute | solution.py:37
  31.9 2.6 %collective-permute-start.12 = (bf16[1,144,256]{2,1,0:T(8,128)(2,1)S(1)}, bf16[1,144,256]{2,1,0:T(8,128)(2,1)S(1)}, u32[]{:S(2)}, u32[]{:S(2)}) collective-permute-start(bf16[1,144,256]{2,1,0:T(8,128)(2,1)S(1)} %collective-permute-done.11.refs_1_.refs_2_), channel_id=1, source_target_pairs={{0,1},{1,0},{2,3},{3,2},{4,5},{5,4},{6,7},{7,6},{8,9},{9,8},{10,11... | collective-permute-start | bytes 221192 | tf_op jit(solution)/shard_map/ppermute | solution.py:28
  33.9 1.7 %collective-permute-start.15 = (bf16[1,144,256]{2,1,0:T(8,128)(2,1)S(1)}, bf16[1,144,256]{2,1,0:T(8,128)(2,1)S(1)}, u32[]{:S(2)}, u32[]{:S(2)}) collective-permute-start(bf16[1,144,256]{2,1,0:T(8,128)(2,1)S(1)} %collective-permute-done.14.refs_1_.refs_4_), channel_id=1, source_target_pairs={{0,1},{1,0},{2,3},{3,2},{4,5},{5,4},{6,7},{7,6},{8,9},{9,8},{10,11... | collective-permute-start | bytes 221192 | tf_op jit(solution)/shard_map/ppermute | solution.py:28
  33.9 1.7 %collective-permute-start.16 = (bf16[1,144,256]{2,1,0:T(8,128)(2,1)S(1)}, bf16[1,144,256]{2,1,0:T(8,128)(2,1)S(1)}, u32[]{:S(2)}, u32[]{:S(2)}) collective-permute-start(bf16[1,144,256]{2,1,0:T(8,128)(2,1)S(1)} %collective-permute-done.13.refs_2_.refs_5_), channel_id=1, source_target_pairs={{0,1},{1,0},{2,3},{3,2},{4,5},{5,4},{6,7},{7,6},{8,9},{9,8},{10,11... | collective-permute-start | bytes 221192 | tf_op jit(solution)/shard_map/ppermute | solution.py:28
  36.8 1.2 %collective-permute-start.17 = (f32[8,128]{1,0:T(8,128)S(1)}, f32[8,128]{1,0:T(8,128)S(1)}, u32[]{:S(2)}, u32[]{:S(2)}) collective-permute-start(f32[8,128]{1,0:T(8,128)S(1)} %get-tuple-element.94), channel_id=1, source_target_pairs={{0,1},{1,0},{2,3},{3,2},{4,5},{5,4},{6,7},{7,6},{8,9},{9,8},{10,11... | collective-permute-start | bytes 12296 | tf_op jit(solution)/shard_map/ppermute | solution.py:28
  37.9 3.6 %collective-permute-start.19 = (f32[8,128]{1,0:T(8,128)S(1)}, f32[8,128]{1,0:T(8,128)S(1)}, u32[]{:S(2)}, u32[]{:S(2)}) collective-permute-start(f32[8,128]{1,0:T(8,128)S(1)} %add.12), channel_id=1, source_target_pairs={{0,4},{1,7},{2,6},{3,5},{4,0},{5,3},{6,2},{7,1},{8,12},{9,15},{10,... | collective-permute-start | bytes 12296 | tf_op jit(solution)/shard_map/ppermute | solution.py:37
  38.9 3.6 %collective-permute-start.18 = (f32[8,128]{1,0:T(8,128)S(1)}, f32[8,128]{1,0:T(8,128)S(1)}, u32[]{:S(2)}, u32[]{:S(2)}) collective-permute-start(f32[8,128]{1,0:T(8,128)S(1)} %add.12), channel_id=1, source_target_pairs={{0,2},{1,3},{2,0},{3,1},{4,6},{5,7},{6,4},{7,5},{8,10},{9,11},{10,... | collective-permute-start | bytes 12296 | tf_op jit(solution)/shard_map/ppermute | solution.py:28
  41.6 1.2 %collective-permute-start.20 = (f32[8,128]{1,0:T(8,128)S(1)}, f32[8,128]{1,0:T(8,128)S(1)}, u32[]{:S(2)}, u32[]{:S(2)}) collective-permute-start(f32[8,128]{1,0:T(8,128)S(1)} %collective-permute-done.19), channel_id=1, source_target_pairs={{0,1},{1,0},{2,3},{3,2},{4,5},{5,4},{6,7},{7,6},{8,9},{9,8},{10,11... | collective-permute-start | bytes 12296 | tf_op jit(solution)/shard_map/ppermute | solution.py:28
